TPU v7x, 32 devices: a whole 2x2x4 slice. The times are simulated.
32 devices in a mesh: gx: 4 (over z), gy: 8 (over y, x, core).
Axes of the slice: x: 2, y: 2, z: 4, core: 2. Of those that a mesh axis runs over, the one named last changes fastest.
Arguments:
- initial_state: float32 [9, 4, 16, 1024], P(None, None, 'gx', 'gy'), may hold values from -6 to 6
- lame_lambda: float32 [4, 16, 1024], P(None, 'gx', 'gy'), may hold values from 0.5 to 1.5
- shear_modulus: float32 [4, 16, 1024], P(None, 'gx', 'gy'), may hold values from 0.3 to 1
- buoyancy: float32 [4, 16, 1024], P(None, 'gx', 'gy'), may hold values from 0.5 to 1
- source_cells: int32 [2048], P(('gx', 'gy')), may hold values from 0 to 2047
- source_wavelet: float32 [3, 2048], P(None, ('gx', 'gy')), may hold values from -8 to 8
- segment_start: int32 [65536], P(('gx', 'gy')), may hold values from 0 to 1935
- segment_weight: float32 [2, 65536], P(None, ('gx', 'gy')), may hold values from 0.2 to 1
- partial_owner: int32 [65536, 1], P(('gx', 'gy')), may hold values from 0 to 31; in each aligned block of 2048 rows (0 to 2047, 2048 to 4095, ...) at most 128 rows name the same one
- partial_channel: int32 [65536], P(('gx', 'gy')), may hold values from 0 to 1023
- observed_data: float32 [3, 32768], P(None, ('gx', 'gy')), may hold values from -6 to 6
Outputs:
- residuals: float32 [3, 32768], P(None, ('gx', 'gy'))
- gradients: float32 [2, 4, 16, 1024], P(None, None, 'gx', 'gy')
Inputs may be any that keep to these rules, and one draw needn't show every extreme that they name: `partial_owner`: each row names the device that owns the segment's channel, counted with gx slowest; the rows of one device name one owner at most 128 times. `partial_channel`: the segment's channel among its owner's 1024 channels. `segment_start`: index of the segment's first cell in its device's grid of starts of shape [4, 4, 121], flattened in that order. `source_cells`: index of the source's cell in its device's tile of shape [4, 4, 128], flattened in that order; cells may repeat.
All inputs are finite; a program needn't handle non-finite values.
Results may differ from a plain program's by a relative error of at most 0.00002.
Values sent between devices are 32-bit elements; how exact they have to be, the bound alone decides.
No kernel may reach another device: no remote copies, remote signals or barrier semaphores. Data moves between devices by JAX's collectives and lax.ppermute only.
A program may use at most 64 MiB of HBM per device.

v0:
```python
import functools

import jax
import jax.numpy as jnp
from jax import lax
from jax.experimental import pallas as pl
from jax.experimental.pallas import tpu as pltpu
from jax.sharding import PartitionSpec as P

GAUGE = 8
STEP = 0.25
RIM = 3
LANES = 128
TILE_X = 4
SPAN_X = 16
SPAN_Y = 256
F32, BF16, I32 = jnp.float32, jnp.bfloat16, jnp.int32
NEAR = tuple((dx, dy) for dx in (-1, 0, 1) for dy in (-1, 0, 1))


def call_kernel(body, name, outs, scratch, *args):
    whole = pl.BlockSpec(memory_space=pltpu.VMEM)
    return pl.pallas_call(
        body,
        name=name,
        out_shape=outs,
        in_specs=[whole] * len(args),
        out_specs=[whole] * len(outs),
        scratch_shapes=scratch,
        compiler_params=pltpu.CompilerParams(vmem_limit_bytes=24 * 1024 * 1024),
    )(*args)


def pieces(values):
    high = values.astype(BF16).astype(F32)
    rest = values - high
    middle = rest.astype(BF16).astype(F32)
    return high, middle, rest - middle


def iota(shape, dim):
    return lax.broadcasted_iota(I32, shape, dim)


def times(left, right):
    return lax.dot_general(left, right, (((1,), (0,)), ((), ())), preferred_element_type=F32)


def times_turned(left, right):
    return lax.dot_general(left, right, (((1,), (1,)), ((), ())), preferred_element_type=F32)


def sum_thirds(values):
    third = values.shape[0] // 3
    return values[:third] + values[third : 2 * third] + values[2 * third :]


def neighbour(dx, dy):
    count_x, count_y = lax.axis_size("gx"), lax.axis_size("gy")
    at_x, at_y = lax.axis_index("gx") + dx, lax.axis_index("gy") + dy
    inside = (at_x >= 0) & (at_x < count_x) & (at_y >= 0) & (at_y < count_y)
    return jnp.where(inside, at_x * count_y + at_y, 0), inside


def edge_columns(rows, side_ref):
    groups = rows.shape[0] // LANES
    turned = rows.T
    for side, base in ((0, 0), (1, LANES - RIM)):
        for column in range(RIM):
            for group in range(groups):
                side_ref[side, column * groups + group : column * groups + group + 1, :] = turned[
                    base + column : base + column + 1, group * LANES : (group + 1) * LANES
                ]


def send_sides(side_ref, out_ref, places):
    for dx, dy in places:
        index, inside = neighbour(dx, dy)

        @pl.when(inside)
        def _(index=index, dy=dy):
            out_ref[index] = side_ref[1 if dy > 0 else 0]


def arrived_chunk(recv_ref, dx, dy):
    index, inside = neighbour(dx, dy)
    return jnp.where(inside, recv_ref[index], 0.0)


def rim_rows(recv_ref, dx, groups, turn_ref):
    for dy, base in ((1, 0), (-1, LANES - RIM)):
        chunk = arrived_chunk(recv_ref, dx, dy)
        for column in range(RIM):
            for group in range(groups):
                turn_ref[base + column : base + column + 1, group * LANES : (group + 1) * LANES] = chunk[
                    column * groups + group : column * groups + group + 1, :
                ]
    return turn_ref[...].T


def lay_planes(planes_ref, lane, centre, higher, lower):
    upper_half = iota((8, LANES), 0) < TILE_X
    for pair in range(planes_ref.shape[0] // 2):
        rows = slice(8 * pair, 8 * pair + 8)
        mid, high, low = centre[rows], higher[rows], lower[rows]
        lanes = slice(lane, lane + LANES)
        planes_ref[2 * pair, 0:8, lanes] = jnp.where(upper_half, mid, pltpu.roll(high, 4, 0))
        planes_ref[2 * pair + 1, 0:8, lanes] = jnp.where(upper_half, pltpu.roll(mid, 4, 0), high)
        planes_ref[2 * pair, 8:16, lanes] = jnp.where(upper_half, 0.0, pltpu.roll(low, 4, 0))
        planes_ref[2 * pair + 1, 8:16, lanes] = jnp.where(upper_half, 0.0, low)


def ahead_x(plane):
    return pltpu.roll(plane, SPAN_X - 1, 0) - plane


def behind_x(plane):
    return plane - pltpu.roll(plane, 1, 0)


def ahead_y(plane):
    return pltpu.roll(plane, SPAN_Y - 1, 1) - plane


def behind_y(plane):
    return plane - pltpu.roll(plane, 1, 1)


def advance(field_ref, medium_ref, first, depth, emit, last):
    def field(number, z):
        return field_ref[number * depth + z]

    def ahead_z(number, z):
        here = field(number, z)
        return field(number, z + 1) - here if z + 1 < depth else -here

    def behind_z(number, z):
        here = field(number, z)
        return here - field(number, z - 1) if z else here

    for z in range(depth):
        scale = STEP * medium_ref[first + 2 * depth + z]
        accel = (
            ahead_x(field(3, z)) + behind_y(field(6, z)) + behind_z(7, z),
            behind_x(field(6, z)) + ahead_y(field(4, z)) + behind_z(8, z),
            behind_x(field(7, z)) + behind_y(field(8, z)) + ahead_z(5, z),
        )
        for number in range(3):
            field_ref[number * depth + z] = field(number, z) + scale * accel[number]
    for z in range(depth):
        along_x, along_y, along_z = field(0, z), field(1, z), field(2, z)
        strains = (
            behind_x(along_x),
            behind_y(along_y),
            behind_z(2, z),
            ahead_y(along_x) + ahead_x(along_y),
            ahead_z(0, z) + ahead_x(along_z),
            ahead_z(1, z) + ahead_y(along_z),
        )
        emit(z, strains)
        if not last:
            shear = medium_ref[first + depth + z]
            dilated = medium_ref[first + z] * (strains[0] + strains[1] + strains[2])
            for number in range(3):
                field_ref[(3 + number) * depth + z] = field(3 + number, z) + STEP * (
                    dilated + 2.0 * shear * strains[number]
                )
                field_ref[(6 + number) * depth + z] = (
                    field(6 + number, z) + STEP * shear * strains[3 + number]
                )


def pack_body(fields_ref, cells_ref, wavelet_ref, out_ref, side_ref):
    rows = fields_ref[...]
    spare = 2 * LANES - rows.shape[0]
    edge_columns(jnp.concatenate([rows, jnp.zeros((spare, LANES), F32)], axis=0), side_ref)
    count = cells_ref.shape[1]
    for side in range(2):
        side_ref[side, 6:7, 0:count] = cells_ref[...].astype(F32)
        side_ref[side, 6:7, count : 2 * count] = wavelet_ref[0:1, :]
        side_ref[side, 7:8, 0:count] = wavelet_ref[1:2, :]
        side_ref[side, 7:8, count : 2 * count] = wavelet_ref[2:3, :]
    send_sides(side_ref, out_ref, NEAR)


def slots_body(capacity, devices, cols_y, owner_ref, start_ref, slot_ref, row_ref, cover_ref, place_ref, rank_ref):
    blocks = owner_ref.shape[0]
    group = 32
    before = jnp.where(iota((LANES, 2 * LANES), 0) < iota((LANES, 2 * LANES), 1), 1.0, 0.0).astype(BF16)
    rank_ref[...] = jnp.zeros_like(rank_ref)

    def count_group(number, carry):
        names = iota((group, LANES), 0) + number * group
        hot = [names == owner_ref[b : b + 1, :] for b in range(blocks)]
        marks = jnp.concatenate([jnp.where(h, 1.0, 0.0) for h in hot], axis=0).astype(BF16)
        counts = times(marks, before)
        total = jnp.zeros((group, LANES), F32)
        for b in range(blocks):
            part = counts[b * group : (b + 1) * group]
            rank_ref[b : b + 1, :] = rank_ref[b : b + 1, :] + jnp.sum(
                jnp.where(hot[b], part[:, :LANES] + total, 0.0), axis=0, keepdims=True
            )
            total = total + part[:, LANES:]
        return carry

    if devices == group:
        count_group(0, 0)
    else:
        lax.fori_loop(0, devices // group, count_group, 0)
    slot = owner_ref[...] * capacity + rank_ref[...].astype(I32)
    slot_ref[...] = slot >> 7
    low = slot & (LANES - 1)
    span = cols_y - GAUGE + 1
    start = start_ref[...]
    row = ((start.astype(F32) + 0.5) * (1.0 / span)).astype(I32)
    row_ref[...] = row
    first = start - row * span
    down = iota((LANES, LANES), 0)
    for b in range(blocks):
        lanes = slice(b * LANES, (b + 1) * LANES)
        offset = down - first[b : b + 1, :]
        cover_ref[:, lanes] = jnp.where((offset >= 0) & (offset < GAUGE), 1.0, 0.0).astype(BF16)
        place_ref[:, lanes] = jnp.where(down == low[b : b + 1, :], 1.0, 0.0).astype(BF16)


def source_maps(recv_ref, cols_y, depth, left_ref, right_ref):
    count = LANES // 2
    first_half = iota((1, LANES), 1) < count
    rows_per_step = depth * SPAN_X
    down_rows = iota((rows_per_step, LANES), 0)
    down_lanes = iota((SPAN_Y, LANES), 0)
    halves = []
    for dx, dy in NEAR:
        chunk = arrived_chunk(recv_ref, dx, dy)
        cells = chunk[6:7, :].astype(I32)
        y = cells & (cols_y - 1)
        rest = cells >> (cols_y.bit_length() - 1)
        x = rest & (TILE_X - 1)
        z = rest >> (TILE_X.bit_length() - 1)
        row = z * SPAN_X + x + (TILE_X if dx > 0 else SPAN_X - TILE_X if dx < 0 else 0)
        if dy > 0:
            lane = jnp.where(y < RIM, y + LANES, -1)
        elif dy < 0:
            lane = jnp.where(y >= cols_y - RIM, y + LANES, -1)
        else:
            lane = y
        halves.append((row, lane, chunk[6:7, :], chunk[7:8, :]))
    zero_row = jnp.zeros((1, LANES), F32)
    halves.append((jnp.zeros((1, LANES), I32), jnp.full((1, LANES), -1, I32), zero_row, zero_row))
    for block in range(len(halves) // 2):
        (row_a, lane_a, one_a, two_a), (row_b, lane_b, one_b, two_b) = halves[2 * block : 2 * block + 2]
        row = jnp.where(first_half, row_a, pltpu.roll(row_b, count, 1))
        lane = jnp.where(first_half, lane_a, pltpu.roll(lane_b, count, 1))
        steps = (
            jnp.where(first_half, pltpu.roll(one_a, count, 1), one_b),
            jnp.where(first_half, two_a, pltpu.roll(two_b, count, 1)),
            jnp.where(first_half, pltpu.roll(two_a, count, 1), two_b),
        )
        lanes = slice(block * LANES, (block + 1) * LANES)
        right_ref[:, lanes] = jnp.where(down_lanes == lane, 1.0, 0.0).astype(BF16)
        at_row = down_rows == row
        for step, amplitude in enumerate(steps):
            for third, piece in enumerate(pieces(amplitude)):
                base = (third * 3 + step) * rows_per_step
                left_ref[base : base + rows_per_step, lanes] = jnp.where(at_row, piece, 0.0).astype(BF16)
    return sum_thirds(times_turned(left_ref[...], right_ref[...]))


def forward_body(
    cols_y,
    fields_ref,
    higher_ref,
    lower_ref,
    recv_ref,
    slot_ref,
    row_ref,
    weight_ref,
    channel_ref,
    cover_ref,
    place_ref,
    out_ref,
    strain_ref,
    medium_ref,
    planes_ref,
    turn_ref,
    source_left_ref,
    source_right_ref,
    source_ref,
    spread_ref,
):
    depth = medium_ref.shape[0] // 3
    cells_row = depth * TILE_X
    turn_ref[...] = jnp.zeros_like(turn_ref)
    rims = [rim_rows(recv_ref, dx, 2, turn_ref) for dx in (0, 1, -1)]
    lay_planes(planes_ref, 0, fields_ref, higher_ref, lower_ref)
    lay_planes(planes_ref, LANES, *rims)
    first = 9 * depth
    medium_ref[...] = planes_ref[first:]
    source_ref[...] = source_maps(recv_ref, cols_y, depth, source_left_ref, source_right_ref)
    for step in range(3):
        for z in range(depth):
            base = step * depth * SPAN_X + z * SPAN_X
            load = source_ref[base : base + SPAN_X, :]
            for number in range(3, 6):
                planes_ref[number * depth + z] = planes_ref[number * depth + z] + load

        def emit(z, strains, step=step):
            for number, strain in enumerate(strains):
                base = ((step * 6 + number) * depth + z) * TILE_X
                strain_ref[base : base + TILE_X, :] = strain[0:TILE_X, 0:LANES]

        advance(planes_ref, planes_ref, first, depth, emit, step == 2)
    axial = jnp.concatenate(
        [strain_ref[step * 6 * cells_row : (step * 6 + 2) * cells_row, :] for step in range(3)], axis=0
    )
    axial = jnp.concatenate(pieces(axial), axis=0).astype(BF16)
    rows_down = iota((cells_row, LANES), 0)
    slots_down = iota((LANES, LANES), 0) >> 2
    for block in range(slot_ref.shape[0]):
        lanes = slice(block * LANES, (block + 1) * LANES)
        windows = sum_thirds(times(axial, cover_ref[:, lanes]))
        at_row = rows_down == row_ref[block : block + 1, :]
        weight_x, weight_y = weight_ref[0:1, lanes], weight_ref[1:2, lanes]
        sums = []
        for step in range(3):
            base = 2 * step * cells_row
            both = (
                weight_x * windows[base : base + cells_row]
                + weight_y * windows[base + cells_row : base + 2 * cells_row]
            )
            sums.append(jnp.sum(jnp.where(at_row, both, 0.0), axis=0, keepdims=True))
        sums.append(channel_ref[block : block + 1, :].astype(F32))
        values = jnp.concatenate(sums + sums, axis=0)
        in_slot = slots_down == slot_ref[block : block + 1, :]
        for third, piece in enumerate(pieces(values)):
            spread_ref[third * LANES : (third + 1) * LANES, lanes] = jnp.where(
                in_slot, jnp.concatenate([piece] * (LANES // 8), axis=0), 0.0
            ).astype(BF16)
    out_ref[...] = sum_thirds(times_turned(spread_ref[...], place_ref[...]))


def owner_body(arrived_ref, observed_ref, residual_ref, reply_ref, values_ref, place_ref, held_ref):
    groups = arrived_ref.shape[0] // 4
    parts = observed_ref.shape[1] // LANES
    down = iota((LANES, LANES), 0)
    part_down = iota((parts, LANES), 0)
    nothing = jnp.zeros((parts, LANES), F32)
    numbers = [arrived_ref[4 * s + 3 : 4 * s + 4, :].astype(I32) for s in range(groups)]
    for s in range(groups):
        lanes = slice(s * LANES, (s + 1) * LANES)
        place_ref[:, lanes] = jnp.where(down == (numbers[s] & (LANES - 1)), 1.0, 0.0).astype(BF16)
        at_part = part_down == (numbers[s] >> 7)
        thirds = pieces(arrived_ref[4 * s : 4 * s + 3, :])
        stack = []
        for third in thirds:
            for step in range(3):
                stack.append(jnp.where(at_part, third[step : step + 1, :], 0.0))
            stack.append(nothing)
        values_ref[:, lanes] = jnp.concatenate(stack, axis=0).astype(BF16)
    sums = sum_thirds(times_turned(values_ref[...], place_ref[...]))
    for step in range(3):
        for part in range(parts):
            at = step * parts + part
            held_ref[at : at + 1, :] = observed_ref[step : step + 1, part * LANES : (part + 1) * LANES]
    held_ref[3 * parts :, :] = nothing
    held_ref[...] = sums - held_ref[...]
    for step in range(3):
        for part in range(parts):
            at = step * parts + part
            residual_ref[step : step + 1, part * LANES : (part + 1) * LANES] = held_ref[at : at + 1, :]
    residual = jnp.concatenate(pieces(held_ref[...]), axis=0).astype(BF16)
    for s in range(groups):
        lanes = slice(s * LANES, (s + 1) * LANES)
        found = sum_thirds(times(residual, place_ref[:, lanes]))
        at_part = part_down == (numbers[s] >> 7)
        for step in range(3):
            reply_ref[4 * s + step : 4 * s + step + 1, :] = jnp.sum(
                jnp.where(at_part, found[step * parts : (step + 1) * parts], 0.0), axis=0, keepdims=True
            )
        reply_ref[4 * s + 3 : 4 * s + 4, :] = jnp.zeros((1, LANES), F32)


def load_body(
    arrived_ref,
    slot_ref,
    row_ref,
    weight_ref,
    cover_ref,
    place_ref,
    load_ref,
    out_ref,
    spread_ref,
    side_ref,
):
    cells_row = load_ref.shape[0] // 6
    stack_rows = load_ref.shape[0]
    arrived = jnp.concatenate(pieces(arrived_ref[...]), axis=0).astype(BF16)
    slots_down = iota((LANES, LANES), 0) >> 2
    rows_down = iota((cells_row, LANES), 0)
    for block in range(slot_ref.shape[0]):
        lanes = slice(block * LANES, (block + 1) * LANES)
        found = sum_thirds(times(arrived, place_ref[:, lanes]))
        found = jnp.where(slots_down == slot_ref[block : block + 1, :], found, 0.0)
        folded = found[0:8]
        for part in range(1, LANES // 8):
            folded = folded + found[8 * part : 8 * part + 8]
        folded = folded + pltpu.roll(folded, 4, 0)
        at_row = rows_down == row_ref[block : block + 1, :]
        for turn in range(3):
            back = folded[2 - turn : 3 - turn, :]
            for part in range(2):
                for third, piece in enumerate(pieces(weight_ref[part : part + 1, lanes] * back)):
                    base = third * stack_rows + (2 * turn + part) * cells_row
                    spread_ref[base : base + cells_row, lanes] = jnp.where(at_row, piece, 0.0).astype(BF16)
    load = sum_thirds(times_turned(spread_ref[...], cover_ref[...]))
    load_ref[...] = load
    spare = LANES - stack_rows
    edge_columns(jnp.concatenate([load, jnp.zeros((spare, LANES), F32)], axis=0), side_ref)
    side_ref[:, RIM : RIM + 1, :] = jnp.zeros((2, 1, LANES), F32)
    send_sides(side_ref, out_ref, [(dx, dy) for dx, dy in NEAR if dy])


def adjoint_body(
    load_ref, higher_ref, lower_ref, recv_ref, strain_ref, medium_ref, gradient_ref, load_planes_ref, planes_ref, turn_ref
):
    depth = medium_ref.shape[0] // 3
    turn_ref[...] = jnp.zeros_like(turn_ref)
    rims = [rim_rows(recv_ref, dx, 1, turn_ref) for dx in (0, 1, -1)]
    lay_planes(load_planes_ref, 0, load_ref, higher_ref, lower_ref)
    lay_planes(load_planes_ref, LANES, *rims)
    planes_ref[...] = jnp.zeros_like(planes_ref)
    gradient_ref[...] = jnp.zeros_like(gradient_ref)
    for turn in range(3):
        for part in range(2):
            for z in range(depth):
                at = (3 + part) * depth + z
                planes_ref[at] = planes_ref[at] + load_planes_ref[(2 * turn + part) * depth + z]

        def emit(z, strains, turn=turn):
            forward = []
            for number in range(6):
                base = (((2 - turn) * 6 + number) * depth + z) * TILE_X
                forward.append(strain_ref[base : base + TILE_X, :])
            back = [strain[0:TILE_X, 0:LANES] for strain in strains]
            dilation = (forward[0] + forward[1] + forward[2]) * (back[0] + back[1] + back[2])
            product = [forward[number] * back[number] for number in range(6)]
            shear = 2.0 * (product[0] + product[1] + product[2]) + product[3] + product[4] + product[5]
            for part, term in enumerate((dilation, shear)):
                base = (part * depth + z) * TILE_X
                gradient_ref[base : base + TILE_X, :] = gradient_ref[base : base + TILE_X, :] + term

        advance(planes_ref, medium_ref, 0, depth, emit, turn == 2)


def shards(
    initial_state,
    lame_lambda,
    shear_modulus,
    buoyancy,
    source_cells,
    source_wavelet,
    segment_start,
    segment_weight,
    partial_owner,
    partial_channel,
    observed_data,
):
    depth, rows_x, cols_y = lame_lambda.shape
    part_count = segment_start.shape[0]
    count_x, count_y = lax.axis_size("gx"), lax.axis_size("gy")
    devices = count_x * count_y
    capacity = max(2, 2 * part_count // devices)
    slot_groups = devices * capacity // LANES
    blocks = part_count // LANES
    per_group = LANES // capacity
    cells_row = depth * rows_x
    both = ("gx", "gy")
    up = [(i, i + 1) for i in range(count_x - 1)]
    down = [(j, i) for i, j in up]
    shape = jax.ShapeDtypeStruct

    def exchange(chunks):
        return lax.all_to_all(chunks, both, split_axis=0, concat_axis=0, tiled=True)

    def to_owners(rows):
        chunks = rows.reshape(slot_groups, 4, per_group, capacity).transpose(0, 2, 1, 3)
        back = exchange(chunks.reshape(devices, 4, capacity)).reshape(slot_groups, per_group, 4, capacity)
        return back.transpose(0, 2, 1, 3).reshape(slot_groups * 4, LANES)

    fields = jnp.concatenate(
        [values.reshape(-1, cols_y) for values in (initial_state, lame_lambda, shear_modulus, buoyancy)]
    )
    lower = lax.ppermute(fields, "gx", up)
    higher = lax.ppermute(fields, "gx", down)
    (edges,) = call_kernel(
        pack_body,
        "pack_edges",
        [shape((devices, 8, LANES), F32)],
        [pltpu.VMEM((2, 8, LANES), F32)],
        fields,
        source_cells.reshape(1, -1),
        source_wavelet,
    )
    rims = exchange(edges)
    channels = partial_channel.reshape(blocks, LANES)
    slot, row, cover, place = call_kernel(
        functools.partial(slots_body, capacity, devices, cols_y),
        "segment_slots",
        [
            shape((blocks, LANES), I32),
            shape((blocks, LANES), I32),
            shape((cols_y, part_count), BF16),
            shape((LANES, part_count), BF16),
        ],
        [pltpu.VMEM((blocks, LANES), F32)],
        partial_owner.reshape(blocks, LANES),
        segment_start.reshape(blocks, LANES),
    )
    partials, strains, medium = call_kernel(
        functools.partial(forward_body, cols_y),
        "forward_run",
        [
            shape((slot_groups * 4, LANES), F32),
            shape((18 * cells_row, cols_y), F32),
            shape((3 * depth, SPAN_X, SPAN_Y), F32),
        ],
        [
            pltpu.VMEM((12 * depth, SPAN_X, SPAN_Y), F32),
            pltpu.VMEM((LANES, 2 * LANES), F32),
            pltpu.VMEM((9 * depth * SPAN_X, 5 * LANES), BF16),
            pltpu.VMEM((SPAN_Y, 5 * LANES), BF16),
            pltpu.VMEM((3 * depth * SPAN_X, SPAN_Y), F32),
            pltpu.VMEM((3 * LANES, part_count), BF16),
        ],
        fields,
        higher,
        lower,
        rims,
        slot,
        row,
        segment_weight,
        channels,
        cover,
        place,
    )
    parts = observed_data.shape[1] // LANES
    residuals, reply = call_kernel(
        owner_body,
        "channel_sums",
        [shape(observed_data.shape, F32), shape((slot_groups * 4, LANES), F32)],
        [
            pltpu.VMEM((12 * parts, slot_groups * LANES), BF16),
            pltpu.VMEM((LANES, slot_groups * LANES), BF16),
            pltpu.VMEM((4 * parts, LANES), F32),
        ],
        to_owners(partials),
        observed_data,
    )
    loads, load_edges = call_kernel(
        load_body,
        "segment_loads",
        [shape((6 * cells_row, cols_y), F32), shape((devices, 4, LANES), F32)],
        [pltpu.VMEM((18 * cells_row, part_count), BF16), pltpu.VMEM((2, 4, LANES), F32)],
        to_owners(reply),
        slot,
        row,
        segment_weight,
        cover,
        place,
    )
    load_lower = lax.ppermute(loads, "gx", up)
    load_higher = lax.ppermute(loads, "gx", down)
    load_rims = exchange(load_edges)
    (gradients,) = call_kernel(
        adjoint_body,
        "adjoint_run",
        [shape((2 * cells_row, cols_y), F32)],
        [
            pltpu.VMEM((6 * depth, SPAN_X, SPAN_Y), F32),
            pltpu.VMEM((9 * depth, SPAN_X, SPAN_Y), F32),
            pltpu.VMEM((LANES, LANES), F32),
        ],
        loads,
        load_higher,
        load_lower,
        load_rims,
        strains,
        medium,
    )
    return (residuals, gradients.reshape(2, depth, rows_x, cols_y))


def solution(mesh):
    in_specs = (
        P(None, None, "gx", "gy"),
        P(None, "gx", "gy"),
        P(None, "gx", "gy"),
        P(None, "gx", "gy"),
        P(("gx", "gy")),
        P(None, ("gx", "gy")),
        P(("gx", "gy")),
        P(None, ("gx", "gy")),
        P(("gx", "gy"), None),
        P(("gx", "gy")),
        P(None, ("gx", "gy")),
    )
    out_specs = (P(None, ("gx", "gy")), P(None, None, "gx", "gy"))
    return jax.shard_map(shards, mesh=mesh, in_specs=in_specs, out_specs=out_specs, check_vma=False)
```

profile of v0, /device:TPU:0, one launch (start us, length us, event | category | flops | bytes accessed | tf_op | source)
XLA Modules:
  0.0 60.9 jit_solution(10536183836036387656)
XLA Ops:
  0.6 0.9 %pad_maximum_fusion.fields_ref = f32[192,128]{1,0:T(8,128)S(1)} fusion(f32[16,128]{1,0:T(8,128)} %bitcast.23, f32[16,128]{1,0:T(8,128)} %bitcast.24, f32[16,128]{1,0:T(8,128)} %bitcast.25, f32[144,128]{1,0:T(8,128)} %bitcast.21), kind=kLoop, calls=%fused_computation | loop fusion | flops 73728 | bytes 196608 | tf_op jit(solution)/shard_map/concatenate | solution.py:490
  1.6 0.6 %copy-done.6 = s32[64]{0:T(128)S(1)} copy-done((s32[64]{0:T(128)S(1)}, s32[64]{0:T(128)}, u32[]{:S(2)}) %copy-start.6) | copy-done | bytes 280
  2.2 0.8 %pack_edges.1 = f32[32,8,128]{2,1,0:T(8,128)} custom-call(f32[192,128]{1,0:T(8,128)S(1)} %pad_maximum_fusion.fields_ref, s32[1,64]{1,0:T(1,128)S(1)} %bitcast.20, f32[3,64]{1,0:T(4,128)S(1)} %copy-done.5), custom_call_target="tpu_custom_call" | custom-call | tf_op jit(solution)/shard_map/pack_edges/pallas_call | solution.py:23
  3.1 7.3 %all-to-all-start = ((f32[32,8,128]{2,1,0:T(8,128)}), f32[32,8,128]{2,1,0:T(8,128)S(1)}, u32[]{:S(2)}, u32[]{:S(2)}) async-start(f32[32,8,128]{2,1,0:T(8,128)} %pack_edges.1), calls=%async_computation | async-start | bytes 262144 | tf_op jit(solution)/shard_map/all_to_all | solution.py:483
  10.4 0.0 copy-start
  10.4 3.7 %collective-permute-start.1 = (f32[192,128]{1,0:T(8,128)S(1)}, f32[192,128]{1,0:T(8,128)S(1)}, u32[]{:S(2)}, u32[]{:S(2)}) collective-permute-start(f32[192,128]{1,0:T(8,128)S(1)} %pad_maximum_fusion.fields_ref), channel_id=1, source_target_pairs={{0,8},{8,16},{16,24},{1,9},{9,17},{17,25},{2,10},{10,18},{18,26},{... | collective-permute-start | bytes 294920 | tf_op jit(solution)/shard_map/ppermute | solution.py:493
  14.1 1.3 %collective-permute-start = (f32[192,128]{1,0:T(8,128)S(1)}, f32[192,128]{1,0:T(8,128)S(1)}, u32[]{:S(2)}, u32[]{:S(2)}) collective-permute-start(f32[192,128]{1,0:T(8,128)S(1)} %pad_maximum_fusion.fields_ref), channel_id=1, source_target_pairs={{8,0},{16,8},{24,16},{9,1},{17,9},{25,17},{10,2},{18,10},{26,18},{... | collective-permute-start | bytes 294920 | tf_op jit(solution)/shard_map/ppermute | solution.py:494
  15.4 0.6 %segment_slots.1 = (s32[16,128]{1,0:T(8,128)S(1)}, s32[16,128]{1,0:T(8,128)S(1)}, bf16[128,2048]{1,0:T(8,128)(2,1)S(1)}, bf16[128,2048]{1,0:T(8,128)(2,1)S(1)}) custom-call(s32[16,128]{1,0:T(8,128)S(1)} %bitcast.18, s32[16,128]{1,0:T(8,128)S(1)} %bitcast.19), custom_call_target="tpu_custom_call" | custom-call | tf_op jit(solution)/shard_map/segment_slots/pallas_call | solution.py:23
  16.0 0.0 copy-start.2
  16.0 0.4 collective-permute-done.1.lower_ref
  16.4 4.2 %collective-permute-done.higher_ref = f32[192,128]{1,0:T(8,128)S(1)} collective-permute-done((f32[192,128]{1,0:T(8,128)S(1)}, f32[192,128]{1,0:T(8,128)S(1)}, u32[]{:S(2)}, u32[]{:S(2)}) %collective-permute-start) | collective-permute-done | bytes 98336 | tf_op jit(solution)/shard_map/ppermute | solution.py:494
  20.6 0.0 all-to-all-done.recv_ref
  20.6 2.6 %forward_run.1 = (f32[128,128]{1,0:T(8,128)S(1)}, f32[288,128]{1,0:T(8,128)S(1)}, f32[12,16,256]{2,1,0:T(8,128)S(1)}) custom-call(f32[192,128]{1,0:T(8,128)S(1)} %pad_maximum_fusion.fields_ref, f32[192,128]{1,0:T(8,128)S(1)} %collective-permute-done.higher_ref, f32[192,128]{1,0:T(8,128)S(1)} %collective-permute-done.1.lower_ref, ...), custom_call_target="tpu_custom_call" | custom-call | tf_op jit(solution)/shard_map/forward_run/pallas_call | solution.py:23
  23.2 0.0 copy-start.1
  23.2 11.8 %all_to_all.20 = f32[32,4,128]{2,1,0:T(4,128)S(1)} all-to-all(f32[32,4,128]{2,1,0:T(4,128)S(1)} %bitcast.15), channel_id=1, replica_groups=mesh['gx'=4,'gy'=8] {'gx','gy'}, dimensions={0} | all-to-all | bytes 131072 | tf_op jit(solution)/shard_map/all_to_all | solution.py:483
  35.0 1.5 %channel_sums.1 = (f32[3,1024]{1,0:T(4,128)}, f32[128,128]{1,0:T(8,128)S(1)}) custom-call(f32[128,128]{1,0:T(8,128)S(1)} %bitcast.14, f32[3,1024]{1,0:T(4,128)S(1)} %copy-done.1), custom_call_target="tpu_custom_call" | custom-call | tf_op jit(solution)/shard_map/channel_sums/pallas_call | solution.py:23
  36.5 9.1 %all_to_all.21 = f32[32,4,128]{2,1,0:T(4,128)S(1)} all-to-all(f32[32,4,128]{2,1,0:T(4,128)S(1)} %bitcast.16), channel_id=1, replica_groups=mesh['gx'=4,'gy'=8] {'gx','gy'}, dimensions={0} | all-to-all | bytes 131072 | tf_op jit(solution)/shard_map/all_to_all | solution.py:483
  45.6 1.8 %segment_loads.1 = (f32[96,128]{1,0:T(8,128)S(1)}, f32[32,4,128]{2,1,0:T(4,128)}) custom-call(f32[128,128]{1,0:T(8,128)S(1)} %bitcast.13, s32[16,128]{1,0:T(8,128)S(1)} %get-tuple-element.13.slot_ref, s32[16,128]{1,0:T(8,128)S(1)} %get-tuple-element.14.row_ref, f32[2,2048]{1,0:T(2,128)S(1)} %copy-done, bf16[128,2048]{1,0:T(8,128)(2,1)S(1)} %get-tuple-element.15.cover_ref, ...), custom_call_target="tpu_custom_call" | custom-call | tf_op jit(solution)/shard_map/segment_loads/pallas_call | solution.py:23
  47.4 2.6 %all-to-all-start.3 = ((f32[32,4,128]{2,1,0:T(4,128)}), f32[32,4,128]{2,1,0:T(4,128)S(1)}, u32[]{:S(2)}, u32[]{:S(2)}) async-start(f32[32,4,128]{2,1,0:T(4,128)} %get-tuple-element.21), calls=%async_computation.3 | async-start | bytes 131072 | tf_op jit(solution)/shard_map/all_to_all | solution.py:483
  50.0 3.6 %collective-permute-start.3 = (f32[96,128]{1,0:T(8,128)S(1)}, f32[96,128]{1,0:T(8,128)S(1)}, u32[]{:S(2)}, u32[]{:S(2)}) collective-permute-start(f32[96,128]{1,0:T(8,128)S(1)} %get-tuple-element.20.load_ref), channel_id=1, source_target_pairs={{0,8},{8,16},{16,24},{1,9},{9,17},{17,25},{2,10},{10,18},{18,26},{... | collective-permute-start | bytes 147464 | tf_op jit(solution)/shard_map/ppermute | solution.py:571
  53.6 1.3 %collective-permute-start.2 = (f32[96,128]{1,0:T(8,128)S(1)}, f32[96,128]{1,0:T(8,128)S(1)}, u32[]{:S(2)}, u32[]{:S(2)}) collective-permute-start(f32[96,128]{1,0:T(8,128)S(1)} %get-tuple-element.20.load_ref), channel_id=1, source_target_pairs={{8,0},{16,8},{24,16},{9,1},{17,9},{25,17},{10,2},{18,10},{26,18},{... | collective-permute-start | bytes 147464 | tf_op jit(solution)/shard_map/ppermute | solution.py:572
  54.9 0.4 collective-permute-done.3.lower_ref
  55.3 4.3 %collective-permute-done.2.higher_ref = f32[96,128]{1,0:T(8,128)S(1)} collective-permute-done((f32[96,128]{1,0:T(8,128)S(1)}, f32[96,128]{1,0:T(8,128)S(1)}, u32[]{:S(2)}, u32[]{:S(2)}) %collective-permute-start.2) | collective-permute-done | bytes 49184 | tf_op jit(solution)/shard_map/ppermute | solution.py:572
  59.6 1.3 %adjoint_run.1 = f32[32,128]{1,0:T(8,128)} custom-call(f32[96,128]{1,0:T(8,128)S(1)} %get-tuple-element.20.load_ref, f32[96,128]{1,0:T(8,128)S(1)} %collective-permute-done.2.higher_ref, f32[96,128]{1,0:T(8,128)S(1)} %collective-permute-done.3.lower_ref, f32[32,4,128]{2,1,0:T(4,128)S(1)} %all-to-all-done.3.recv_ref, ...), custom_call_target="tpu_custom_call" | custom-call | tf_op jit(solution)/shard_map/adjoint_run/pallas_call | solution.py:23
  (11 shorter events, 0.0 us)
Async XLA Ops:
  0.6 1.0 %copy-start.5 = (f32[3,64]{1,0:T(4,128)S(1)}, f32[3,64]{1,0:T(4,128)}, u32[]{:S(2)}) copy-start(f32[3,64]{1,0:T(4,128)} %wavelet_ref.1) | copy-start | bytes 2308
  1.6 0.7 %copy-start.6 = (s32[64]{0:T(128)S(1)}, s32[64]{0:T(128)}, u32[]{:S(2)}) copy-start(s32[64]{0:T(128)} %param.15) | copy-start | bytes 772
  3.1 12.3 %copy-start.3 = (s32[2048,1]{0,1:T(1,128)S(1)}, s32[2048,1]{0,1:T(1,128)}, u32[]{:S(2)}) copy-start(s32[2048,1]{0,1:T(1,128)} %param.19) | copy-start | bytes 24580
  3.1 12.3 %copy-start.4 = (s32[2048]{0:T(1024)S(1)}, s32[2048]{0:T(1024)}, u32[]{:S(2)}) copy-start(s32[2048]{0:T(1024)} %param.17) | copy-start | bytes 24580
  3.1 17.5 %all-to-all-start = ((f32[32,8,128]{2,1,0:T(8,128)}), f32[32,8,128]{2,1,0:T(8,128)S(1)}, u32[]{:S(2)}, u32[]{:S(2)}) async-start(f32[32,8,128]{2,1,0:T(8,128)} %pack_edges.1), calls=%async_computation | async-start | bytes 262144 | tf_op jit(solution)/shard_map/all_to_all | solution.py:483
  10.4 10.2 %copy-start = (f32[2,2048]{1,0:T(2,128)S(1)}, f32[2,2048]{1,0:T(2,128)}, u32[]{:S(2)}) copy-start(f32[2,2048]{1,0:T(2,128)} %weight_ref.3) | copy-start | bytes 49156
  10.4 6.0 %collective-permute-start.1 = (f32[192,128]{1,0:T(8,128)S(1)}, f32[192,128]{1,0:T(8,128)S(1)}, u32[]{:S(2)}, u32[]{:S(2)}) collective-permute-start(f32[192,128]{1,0:T(8,128)S(1)} %pad_maximum_fusion.fields_ref), channel_id=1, source_target_pairs={{0,8},{8,16},{16,24},{1,9},{9,17},{17,25},{2,10},{10,18},{18,26},{... | collective-permute-start | bytes 294920 | tf_op jit(solution)/shard_map/ppermute | solution.py:493
  14.1 6.5 %collective-permute-start = (f32[192,128]{1,0:T(8,128)S(1)}, f32[192,128]{1,0:T(8,128)S(1)}, u32[]{:S(2)}, u32[]{:S(2)}) collective-permute-start(f32[192,128]{1,0:T(8,128)S(1)} %pad_maximum_fusion.fields_ref), channel_id=1, source_target_pairs={{8,0},{16,8},{24,16},{9,1},{17,9},{25,17},{10,2},{18,10},{26,18},{... | collective-permute-start | bytes 294920 | tf_op jit(solution)/shard_map/ppermute | solution.py:494
  16.0 4.5 %copy-start.2 = (s32[2048]{0:T(1024)S(1)}, s32[2048]{0:T(1024)}, u32[]{:S(2)}) copy-start(s32[2048]{0:T(1024)} %param.20) | copy-start | bytes 24580
  23.2 11.9 %copy-start.1 = (f32[3,1024]{1,0:T(4,128)S(1)}, f32[3,1024]{1,0:T(4,128)}, u32[]{:S(2)}) copy-start(f32[3,1024]{1,0:T(4,128)} %observed_ref.1) | copy-start | bytes 36868
  47.4 12.2 %all-to-all-start.3 = ((f32[32,4,128]{2,1,0:T(4,128)}), f32[32,4,128]{2,1,0:T(4,128)S(1)}, u32[]{:S(2)}, u32[]{:S(2)}) async-start(f32[32,4,128]{2,1,0:T(4,128)} %get-tuple-element.21), calls=%async_computation.3 | async-start | bytes 131072 | tf_op jit(solution)/shard_map/all_to_all | solution.py:483
  50.0 5.3 %collective-permute-start.3 = (f32[96,128]{1,0:T(8,128)S(1)}, f32[96,128]{1,0:T(8,128)S(1)}, u32[]{:S(2)}, u32[]{:S(2)}) collective-permute-start(f32[96,128]{1,0:T(8,128)S(1)} %get-tuple-element.20.load_ref), channel_id=1, source_target_pairs={{0,8},{8,16},{16,24},{1,9},{9,17},{17,25},{2,10},{10,18},{18,26},{... | collective-permute-start | bytes 147464 | tf_op jit(solution)/shard_map/ppermute | solution.py:571
  53.6 6.0 %collective-permute-start.2 = (f32[96,128]{1,0:T(8,128)S(1)}, f32[96,128]{1,0:T(8,128)S(1)}, u32[]{:S(2)}, u32[]{:S(2)}) collective-permute-start(f32[96,128]{1,0:T(8,128)S(1)} %get-tuple-element.20.load_ref), channel_id=1, source_target_pairs={{8,0},{16,8},{24,16},{9,1},{17,9},{25,17},{10,2},{18,10},{26,18},{... | collective-permute-start | bytes 147464 | tf_op jit(solution)/shard_map/ppermute | solution.py:572
where the time goes:
time: 61.3 us; the launch traced here: 60.9 us
  blocking collectives  20.9 us (34%)
  starting transfers between devices  19.7 us (32%)
  waiting for transfers between devices  9.22 us (15%)
  Pallas kernels  8.59 us (14%)
  other arithmetic  0.95 us (2%)
  between operations  0.77 us (1%)
  local copies, waits for them, and re-layouts  0.67 us (1%)
    all_to_all x2, blocking collectives, exchange(): return lax.all_to_all(chunks, both, split_axis=0, concat_axis=0, tiled=True)  20.9 us
    all_to_all x2, starting transfers between devices, exchange(): return lax.all_to_all(chunks, both, split_axis=0, concat_axis=0, tiled=True)  9.86 us
    pallas_call x6, Pallas kernels, call_kernel(): pl.pallas_call(body, name=name, out_shape=outs, in_specs=[whole] * len(ar...  8.59 us
    ppermute x1, waiting for transfers between devices, shards(): load_higher = lax.ppermute(loads, 'gx', down)  4.25 us
    ppermute x1, waiting for transfers between devices, shards(): higher = lax.ppermute(fields, 'gx', down)  4.17 us
    ppermute x1, starting transfers between devices, shards(): lower = lax.ppermute(fields, 'gx', up)  3.68 us
    ppermute x1, starting transfers between devices, shards(): load_lower = lax.ppermute(loads, 'gx', up)  3.59 us
    ppermute x1, starting transfers between devices, shards(): higher = lax.ppermute(fields, 'gx', down)  1.29 us
  transfers between devices with their start and end apart: 6, of which 4 were waited for; matrix products, arithmetic and copies ran while one was open for 0% of the time, Pallas kernels for 1%

commit v1 on v0

--- a/solution.py
+++ b/solution.py
@@ -108,6 +108,16 @@
         planes_ref[2 * pair + 1, 0:8, lanes] = jnp.where(upper_half, pltpu.roll(mid, 4, 0), high)
         planes_ref[2 * pair, 8:16, lanes] = jnp.where(upper_half, 0.0, pltpu.roll(low, 4, 0))
         planes_ref[2 * pair + 1, 8:16, lanes] = jnp.where(upper_half, 0.0, low)
+
+
+def column_tiles(column_ref):
+    count_x, at_x = lax.axis_size("gx"), lax.axis_index("gx")
+    tiles = [column_ref[at_x]]
+    for move in (1, -1):
+        there = at_x + move
+        inside = (there >= 0) & (there < count_x)
+        tiles.append(jnp.where(inside, column_ref[jnp.where(inside, there, at_x)], 0.0))
+    return tiles
 
 
 def ahead_x(plane):
@@ -268,9 +278,7 @@
 
 def forward_body(
     cols_y,
-    fields_ref,
-    higher_ref,
-    lower_ref,
+    column_ref,
     recv_ref,
     slot_ref,
     row_ref,
@@ -292,7 +300,7 @@
     cells_row = depth * TILE_X
     turn_ref[...] = jnp.zeros_like(turn_ref)
     rims = [rim_rows(recv_ref, dx, 2, turn_ref) for dx in (0, 1, -1)]
-    lay_planes(planes_ref, 0, fields_ref, higher_ref, lower_ref)
+    lay_planes(planes_ref, 0, *column_tiles(column_ref))
     lay_planes(planes_ref, LANES, *rims)
     first = 9 * depth
     medium_ref[...] = planes_ref[first:]
@@ -421,12 +429,12 @@
 
 
 def adjoint_body(
-    load_ref, higher_ref, lower_ref, recv_ref, strain_ref, medium_ref, gradient_ref, load_planes_ref, planes_ref, turn_ref
+    column_ref, recv_ref, strain_ref, medium_ref, gradient_ref, load_planes_ref, planes_ref, turn_ref
 ):
     depth = medium_ref.shape[0] // 3
     turn_ref[...] = jnp.zeros_like(turn_ref)
     rims = [rim_rows(recv_ref, dx, 1, turn_ref) for dx in (0, 1, -1)]
-    lay_planes(load_planes_ref, 0, load_ref, higher_ref, lower_ref)
+    lay_planes(load_planes_ref, 0, *column_tiles(column_ref))
     lay_planes(load_planes_ref, LANES, *rims)
     planes_ref[...] = jnp.zeros_like(planes_ref)
     gradient_ref[...] = jnp.zeros_like(gradient_ref)
@@ -475,8 +483,6 @@
     per_group = LANES // capacity
     cells_row = depth * rows_x
     both = ("gx", "gy")
-    up = [(i, i + 1) for i in range(count_x - 1)]
-    down = [(j, i) for i, j in up]
     shape = jax.ShapeDtypeStruct
 
     def exchange(chunks):
@@ -490,8 +496,7 @@
     fields = jnp.concatenate(
         [values.reshape(-1, cols_y) for values in (initial_state, lame_lambda, shear_modulus, buoyancy)]
     )
-    lower = lax.ppermute(fields, "gx", up)
-    higher = lax.ppermute(fields, "gx", down)
+    column = lax.all_gather(fields, "gx")
     (edges,) = call_kernel(
         pack_body,
         "pack_edges",
@@ -532,9 +537,7 @@
             pltpu.VMEM((3 * depth * SPAN_X, SPAN_Y), F32),
             pltpu.VMEM((3 * LANES, part_count), BF16),
         ],
-        fields,
-        higher,
-        lower,
+        column,
         rims,
         slot,
         row,
@@ -568,8 +571,7 @@
         cover,
         place,
     )
-    load_lower = lax.ppermute(loads, "gx", up)
-    load_higher = lax.ppermute(loads, "gx", down)
+    load_column = lax.all_gather(loads, "gx")
     load_rims = exchange(load_edges)
     (gradients,) = call_kernel(
         adjoint_body,
@@ -580,9 +582,7 @@
             pltpu.VMEM((9 * depth, SPAN_X, SPAN_Y), F32),
             pltpu.VMEM((LANES, LANES), F32),
         ],
-        loads,
-        load_higher,
-        load_lower,
+        load_column,
         load_rims,
         strains,
         medium,

time: 61.3 us -> 73 us (1.19)
  blocking collectives: 20.9 us -> 51.1 us
  starting transfers between devices: 19.7 us -> 9.85 us
  waiting for transfers between devices: 9.22 us -> 0.01 us
    all_gather x0 -> x2, blocking collectives: none -> 29.4 us  [the longest x1 15.4 us: shards(): column = lax.all_gather(fields, 'gx')]
    ppermute x4 -> x0, starting transfers between devices: 9.86 us -> none  [the longest x1 3.68 us: shards(): lower = lax.ppermute(fields, 'gx', up)]
    ppermute x4 -> x0, waiting for transfers between devices: 9.21 us -> none  [the longest x1 4.25 us: shards(): load_higher = lax.ppermute(loads, 'gx', down)]
    all_to_all x2, blocking collectives: 20.9 us -> 21.8 us  [exchange(): return lax.all_to_all(chunks, both, split_axis=0, concat_axis=0, tiled=True)]
  transfers between devices with their start and end apart: 6 -> 2, of which waited for: 4 -> 0; matrix products, arithmetic and copies ran while one was open for 0% -> 0% of each run, Pallas kernels for 1% -> 1%
where the time goes in v1:
time: 73 us; the launch traced here: 72.6 us
  blocking collectives  51.1 us (70%)
  starting transfers between devices  9.85 us (13%)
  Pallas kernels  8.52 us (12%)
  local copies, waits for them, and re-layouts  1.35 us (2%)
  other arithmetic  0.95 us (1%)
  between operations  0.74 us (1%)
    all_to_all x2, blocking collectives, exchange(): return lax.all_to_all(chunks, both, split_axis=0, concat_axis=0, tiled=True)  21.8 us
    all_gather x1, blocking collectives, shards(): column = lax.all_gather(fields, 'gx')  15.4 us
    all_gather x1, blocking collectives, shards(): load_column = lax.all_gather(loads, 'gx')  13.9 us
    all_to_all x2, starting transfers between devices, exchange(): return lax.all_to_all(chunks, both, split_axis=0, concat_axis=0, tiled=True)  9.85 us
    pallas_call x6, Pallas kernels, call_kernel(): pl.pallas_call(body, name=name, out_shape=outs, in_specs=[whole] * len(ar...  8.52 us
  transfers between devices with their start and end apart: 2, of which 0 were waited for; matrix products, arithmetic and copies ran while one was open for 0% of the time, Pallas kernels for 1%

profile of v1, /device:TPU:0, one launch (start us, length us, event | category | flops | bytes accessed | tf_op | source)
XLA Modules:
  0.0 72.6 jit_solution(9768495409345904260)
XLA Ops:
  0.6 0.0 copy-start.5
  0.6 0.9 %pad_maximum_fusion.fields_ref = f32[192,128]{1,0:T(8,128)S(1)} fusion(f32[16,128]{1,0:T(8,128)} %bitcast.27, f32[16,128]{1,0:T(8,128)} %bitcast.28, f32[16,128]{1,0:T(8,128)} %bitcast.29, f32[144,128]{1,0:T(8,128)} %bitcast.25), kind=kLoop, calls=%fused_computation | loop fusion | flops 73728 | bytes 196608 | tf_op jit(solution)/shard_map/concatenate | solution.py:496
  1.6 0.0 copy-done.5
  1.6 0.6 copy-done.6
  2.2 0.8 %pack_edges.1 = f32[32,8,128]{2,1,0:T(8,128)} custom-call(f32[192,128]{1,0:T(8,128)S(1)} %pad_maximum_fusion.fields_ref, s32[1,64]{1,0:T(1,128)S(1)} %bitcast.24, f32[3,64]{1,0:T(4,128)S(1)} %copy-done.5), custom_call_target="tpu_custom_call" | custom-call | tf_op jit(solution)/shard_map/pack_edges/pallas_call | solution.py:23
  3.0 7.3 %all-to-all-start = ((f32[32,8,128]{2,1,0:T(8,128)}), f32[32,8,128]{2,1,0:T(8,128)S(1)}, u32[]{:S(2)}, u32[]{:S(2)}) async-start(f32[32,8,128]{2,1,0:T(8,128)} %pack_edges.1), calls=%async_computation | async-start | bytes 262144 | tf_op jit(solution)/shard_map/all_to_all | solution.py:489
  10.3 0.0 copy-done.3
  10.4 0.0 copy-done.4
  10.4 0.6 segment_slots.1
  11.0 0.0 copy-start
  11.0 15.4 %all-gather = f32[768,128]{1,0:T(8,128)S(1)} all-gather(f32[192,128]{1,0:T(8,128)S(1)} %pad_maximum_fusion.fields_ref), channel_id=2, replica_groups=mesh['gx'=4,'gy'=8] {'gx'}, dimensions={0}, use_global_device_ids=true | all-gather | bytes 491520 | tf_op jit(solution)/shard_map/all_gather | solution.py:499
  26.5 0.0 all-to-all-done.recv_ref
  26.5 0.0 copy-done
  26.5 0.7 copy-done.2
  27.2 2.5 %forward_run.1 = (f32[128,128]{1,0:T(8,128)S(1)}, f32[288,128]{1,0:T(8,128)S(1)}, f32[12,16,256]{2,1,0:T(8,128)S(1)}) custom-call(f32[4,192,128]{2,1,0:T(8,128)S(1)} %bitcast.15, f32[32,8,128]{2,1,0:T(8,128)S(1)} %all-to-all-done.recv_ref, s32[16,128]{1,0:T(8,128)S(1)} %get-tuple-element.13.slot_ref, s32[16,128]{1,0:T(8,128)S(1)} %get-tuple-element.14.row_ref, ...), custom_call_target="tpu_custom_call" | custom-call | tf_op jit(solution)/shard_map/forward_run/pallas_call | solution.py:23
  29.7 0.0 copy-start.1
  29.7 12.7 %all_to_all.20 = f32[32,4,128]{2,1,0:T(4,128)S(1)} all-to-all(f32[32,4,128]{2,1,0:T(4,128)S(1)} %bitcast.19), channel_id=1, replica_groups=mesh['gx'=4,'gy'=8] {'gx','gy'}, dimensions={0} | all-to-all | bytes 131072 | tf_op jit(solution)/shard_map/all_to_all | solution.py:489
  42.4 1.5 %channel_sums.1 = (f32[3,1024]{1,0:T(4,128)}, f32[128,128]{1,0:T(8,128)S(1)}) custom-call(f32[128,128]{1,0:T(8,128)S(1)} %bitcast.18, f32[3,1024]{1,0:T(4,128)S(1)} %copy-done.1), custom_call_target="tpu_custom_call" | custom-call | tf_op jit(solution)/shard_map/channel_sums/pallas_call | solution.py:23
  43.9 9.1 %all_to_all.21 = f32[32,4,128]{2,1,0:T(4,128)S(1)} all-to-all(f32[32,4,128]{2,1,0:T(4,128)S(1)} %bitcast.20), channel_id=1, replica_groups=mesh['gx'=4,'gy'=8] {'gx','gy'}, dimensions={0} | all-to-all | bytes 131072 | tf_op jit(solution)/shard_map/all_to_all | solution.py:489
  53.0 1.8 %segment_loads.1 = (f32[96,128]{1,0:T(8,128)S(1)}, f32[32,4,128]{2,1,0:T(4,128)}) custom-call(f32[128,128]{1,0:T(8,128)S(1)} %bitcast.17, s32[16,128]{1,0:T(8,128)S(1)} %get-tuple-element.13.slot_ref, s32[16,128]{1,0:T(8,128)S(1)} %get-tuple-element.14.row_ref, f32[2,2048]{1,0:T(2,128)S(1)} %copy-done, bf16[128,2048]{1,0:T(8,128)(2,1)S(1)} %get-tuple-element.15.cover_ref, ...), custom_call_target="tpu_custom_call" | custom-call | tf_op jit(solution)/shard_map/segment_loads/pallas_call | solution.py:23
  54.8 2.6 %all-to-all-start.3 = ((f32[32,4,128]{2,1,0:T(4,128)}), f32[32,4,128]{2,1,0:T(4,128)S(1)}, u32[]{:S(2)}, u32[]{:S(2)}) async-start(f32[32,4,128]{2,1,0:T(4,128)} %get-tuple-element.21), calls=%async_computation.3 | async-start | bytes 131072 | tf_op jit(solution)/shard_map/all_to_all | solution.py:489
  57.3 13.9 %all-gather.1 = f32[384,128]{1,0:T(8,128)S(1)} all-gather(f32[96,128]{1,0:T(8,128)S(1)} %get-tuple-element.20), channel_id=3, replica_groups=mesh['gx'=4,'gy'=8] {'gx'}, dimensions={0}, use_global_device_ids=true | all-gather | bytes 245760 | tf_op jit(solution)/shard_map/all_gather | solution.py:574
  71.3 0.0 all-to-all-done.3.recv_ref
  71.3 1.3 %adjoint_run.1 = f32[32,128]{1,0:T(8,128)} custom-call(f32[4,96,128]{2,1,0:T(8,128)S(1)} %bitcast.16, f32[32,4,128]{2,1,0:T(4,128)S(1)} %all-to-all-done.3.recv_ref, f32[288,128]{1,0:T(8,128)S(1)} %get-tuple-element.22.strain_ref, f32[12,16,256]{2,1,0:T(8,128)S(1)} %get-tuple-element.23.medium_ref), custom_call_target="tpu_custom_call" | custom-call | tf_op jit(solution)/shard_map/adjoint_run/pallas_call | solution.py:23
  (5 shorter events, 0.0 us)
Async XLA Ops:
  0.6 1.0 %copy-start.5 = (f32[3,64]{1,0:T(4,128)S(1)}, f32[3,64]{1,0:T(4,128)}, u32[]{:S(2)}) copy-start(f32[3,64]{1,0:T(4,128)} %wavelet_ref.1) | copy-start | bytes 2308
  1.6 0.7 copy-start.6
  3.0 7.3 %copy-start.3 = (s32[2048,1]{0,1:T(1,128)S(1)}, s32[2048,1]{0,1:T(1,128)}, u32[]{:S(2)}) copy-start(s32[2048,1]{0,1:T(1,128)} %param.19) | copy-start | bytes 24580
  3.0 7.3 %copy-start.4 = (s32[2048]{0:T(1024)S(1)}, s32[2048]{0:T(1024)}, u32[]{:S(2)}) copy-start(s32[2048]{0:T(1024)} %param.17) | copy-start | bytes 24580
  3.0 23.4 %all-to-all-start = ((f32[32,8,128]{2,1,0:T(8,128)}), f32[32,8,128]{2,1,0:T(8,128)S(1)}, u32[]{:S(2)}, u32[]{:S(2)}) async-start(f32[32,8,128]{2,1,0:T(8,128)} %pack_edges.1), calls=%async_computation | async-start | bytes 262144 | tf_op jit(solution)/shard_map/all_to_all | solution.py:489
  11.0 15.4 %copy-start = (f32[2,2048]{1,0:T(2,128)S(1)}, f32[2,2048]{1,0:T(2,128)}, u32[]{:S(2)}) copy-start(f32[2,2048]{1,0:T(2,128)} %weight_ref.3) | copy-start | bytes 49156
  26.5 0.7 copy-start.2
  29.7 12.7 %copy-start.1 = (f32[3,1024]{1,0:T(4,128)S(1)}, f32[3,1024]{1,0:T(4,128)}, u32[]{:S(2)}) copy-start(f32[3,1024]{1,0:T(4,128)} %observed_ref.1) | copy-start | bytes 36868
  54.8 16.5 %all-to-all-start.3 = ((f32[32,4,128]{2,1,0:T(4,128)}), f32[32,4,128]{2,1,0:T(4,128)S(1)}, u32[]{:S(2)}, u32[]{:S(2)}) async-start(f32[32,4,128]{2,1,0:T(4,128)} %get-tuple-element.21), calls=%async_computation.3 | async-start | bytes 131072 | tf_op jit(solution)/shard_map/all_to_all | solution.py:489

commit v2 on v0

--- a/solution.py
+++ b/solution.py
@@ -60,6 +60,20 @@
     at_x, at_y = lax.axis_index("gx") + dx, lax.axis_index("gy") + dy
     inside = (at_x >= 0) & (at_x < count_x) & (at_y >= 0) & (at_y < count_y)
     return jnp.where(inside, at_x * count_y + at_y, 0), inside
+
+
+def neighbour_x(move):
+    there = lax.axis_index("gx") + move
+    inside = (there >= 0) & (there < lax.axis_size("gx"))
+    return jnp.where(inside, there, 0), inside
+
+
+def column_rows(depth, move):
+    at = 0
+    for plane in range(6 * depth):
+        height = TILE_X if plane < 2 * depth else 2
+        yield at, plane * TILE_X + (TILE_X - height if move > 0 else 0), height
+        at = at + height
 
 
 def edge_columns(rows, side_ref):
@@ -170,8 +184,9 @@
                 )
 
 
-def pack_body(fields_ref, cells_ref, wavelet_ref, out_ref, side_ref):
-    rows = fields_ref[...]
+def pack_body(state_ref, lambda_ref, shear_ref, buoyancy_ref, cells_ref, wavelet_ref, fields_ref, out_ref, side_ref):
+    rows = jnp.concatenate([state_ref[...], lambda_ref[...], shear_ref[...], buoyancy_ref[...]], axis=0)
+    fields_ref[...] = rows
     spare = 2 * LANES - rows.shape[0]
     edge_columns(jnp.concatenate([rows, jnp.zeros((spare, LANES), F32)], axis=0), side_ref)
     count = cells_ref.shape[1]
@@ -389,6 +404,7 @@
     place_ref,
     load_ref,
     out_ref,
+    column_ref,
     spread_ref,
     side_ref,
 ):
@@ -418,15 +434,40 @@
     edge_columns(jnp.concatenate([load, jnp.zeros((spare, LANES), F32)], axis=0), side_ref)
     side_ref[:, RIM : RIM + 1, :] = jnp.zeros((2, 1, LANES), F32)
     send_sides(side_ref, out_ref, [(dx, dy) for dx, dy in NEAR if dy])
+    for move in (1, -1):
+        there, inside = neighbour_x(move)
+
+        @pl.when(inside)
+        def _(there=there, move=move):
+            for at, source, height in column_rows(cells_row // TILE_X, move):
+                column_ref[there, at : at + height, :] = load_ref[source : source + height, :]
 
 
 def adjoint_body(
-    load_ref, higher_ref, lower_ref, recv_ref, strain_ref, medium_ref, gradient_ref, load_planes_ref, planes_ref, turn_ref
+    load_ref,
+    column_ref,
+    recv_ref,
+    strain_ref,
+    medium_ref,
+    gradient_ref,
+    load_planes_ref,
+    planes_ref,
+    turn_ref,
+    tiles_ref,
 ):
     depth = medium_ref.shape[0] // 3
     turn_ref[...] = jnp.zeros_like(turn_ref)
     rims = [rim_rows(recv_ref, dx, 1, turn_ref) for dx in (0, 1, -1)]
-    lay_planes(load_planes_ref, 0, load_ref, higher_ref, lower_ref)
+    tiles_ref[...] = jnp.zeros_like(tiles_ref)
+    for side, move in enumerate((1, -1)):
+        there, inside = neighbour_x(move)
+
+        @pl.when(inside)
+        def _(there=there, side=side, move=move):
+            for at, target, height in column_rows(depth, -move):
+                tiles_ref[side, target : target + height, :] = column_ref[there, at : at + height, :]
+
+    lay_planes(load_planes_ref, 0, load_ref, tiles_ref[0], tiles_ref[1])
     lay_planes(load_planes_ref, LANES, *rims)
     planes_ref[...] = jnp.zeros_like(planes_ref)
     gradient_ref[...] = jnp.zeros_like(gradient_ref)
@@ -487,20 +528,17 @@
         back = exchange(chunks.reshape(devices, 4, capacity)).reshape(slot_groups, per_group, 4, capacity)
         return back.transpose(0, 2, 1, 3).reshape(slot_groups * 4, LANES)
 
-    fields = jnp.concatenate(
-        [values.reshape(-1, cols_y) for values in (initial_state, lame_lambda, shear_modulus, buoyancy)]
+    fields, edges = call_kernel(
+        pack_body,
+        "pack_edges",
+        [shape((12 * cells_row, cols_y), F32), shape((devices, 8, LANES), F32)],
+        [pltpu.VMEM((2, 8, LANES), F32)],
+        *[values.reshape(-1, cols_y) for values in (initial_state, lame_lambda, shear_modulus, buoyancy)],
+        source_cells.reshape(1, -1),
+        source_wavelet,
     )
     lower = lax.ppermute(fields, "gx", up)
     higher = lax.ppermute(fields, "gx", down)
-    (edges,) = call_kernel(
-        pack_body,
-        "pack_edges",
-        [shape((devices, 8, LANES), F32)],
-        [pltpu.VMEM((2, 8, LANES), F32)],
-        fields,
-        source_cells.reshape(1, -1),
-        source_wavelet,
-    )
     rims = exchange(edges)
     channels = partial_channel.reshape(blocks, LANES)
     slot, row, cover, place = call_kernel(
@@ -556,10 +594,14 @@
         to_owners(partials),
         observed_data,
     )
-    loads, load_edges = call_kernel(
+    loads, load_edges, load_rows = call_kernel(
         load_body,
         "segment_loads",
-        [shape((6 * cells_row, cols_y), F32), shape((devices, 4, LANES), F32)],
+        [
+            shape((6 * cells_row, cols_y), F32),
+            shape((devices, 4, LANES), F32),
+            shape((count_x, 4 * cells_row, cols_y), F32),
+        ],
         [pltpu.VMEM((18 * cells_row, part_count), BF16), pltpu.VMEM((2, 4, LANES), F32)],
         to_owners(reply),
         slot,
@@ -568,9 +610,8 @@
         cover,
         place,
     )
-    load_lower = lax.ppermute(loads, "gx", up)
-    load_higher = lax.ppermute(loads, "gx", down)
     load_rims = exchange(load_edges)
+    load_column = lax.all_to_all(load_rows, "gx", split_axis=0, concat_axis=0, tiled=True)
     (gradients,) = call_kernel(
         adjoint_body,
         "adjoint_run",
@@ -579,10 +620,10 @@
             pltpu.VMEM((6 * depth, SPAN_X, SPAN_Y), F32),
             pltpu.VMEM((9 * depth, SPAN_X, SPAN_Y), F32),
             pltpu.VMEM((LANES, LANES), F32),
+            pltpu.VMEM((2, 6 * cells_row, cols_y), F32),
         ],
         loads,
-        load_higher,
-        load_lower,
+        load_column,
         load_rims,
         strains,
         medium,

time: 61.3 us -> 68.7 us (1.12)
  blocking collectives: 20.9 us -> 38.8 us
  starting transfers between devices: 19.7 us -> 12.3 us
  waiting for transfers between devices: 9.22 us -> 4.53 us
  local copies, waits for them, and re-layouts: 0.67 us -> 3.67 us
  other arithmetic: 0.95 us -> 0 us
    all_to_all x2 -> x3, blocking collectives: 20.9 us -> 30.1 us  [exchange(): return lax.all_to_all(chunks, both, split_axis=0, concat_axis=0, tiled=True)]
    all_to_all x0 -> x1, blocking collectives: none -> 8.8 us  [shards(): lax.all_to_all(load_rows, 'gx', split_axis=0, concat_axis=0, tiled=True)]
    ppermute x2 -> x0, starting transfers between devices: 4.89 us -> none  [the longest x1 3.59 us: shards(): load_lower = lax.ppermute(loads, 'gx', up)]
    ppermute x2 -> x0, waiting for transfers between devices: 4.68 us -> none  [the longest x1 4.25 us: shards(): load_higher = lax.ppermute(loads, 'gx', down)]
    unnamed x14 -> x22, local copies, waits for them, and re-layouts: 0.67 us -> 3.67 us
    all_to_all x2 -> x1, starting transfers between devices: 9.86 us -> 7.3 us  [exchange(): return lax.all_to_all(chunks, both, split_axis=0, concat_axis=0, tiled=True)]
    concatenate x1 -> x0, other arithmetic: 0.95 us -> none  [shards(): jnp.concatenate([values.reshape(-1, cols_y) for values in (initial_state,...]
  transfers between devices with their start and end apart: 6 -> 3, of which waited for: 4 -> 2; matrix products, arithmetic and copies ran while one was open for 0% -> 0% of each run, Pallas kernels for 1% -> 1%
where the time goes in v2:
time: 68.7 us; the launch traced here: 68.1 us
  blocking collectives  38.8 us (56%)
  starting transfers between devices  12.3 us (18%)
  Pallas kernels  7.98 us (12%)
  waiting for transfers between devices  4.53 us (7%)
  local copies, waits for them, and re-layouts  3.67 us (5%)
  between operations  0.76 us (1%)
    all_to_all x3, blocking collectives, exchange(): return lax.all_to_all(chunks, both, split_axis=0, concat_axis=0, tiled=True)  30.1 us
    all_to_all x1, blocking collectives, shards(): lax.all_to_all(load_rows, 'gx', split_axis=0, concat_axis=0, tiled=True)  8.8 us
    pallas_call x6, Pallas kernels, call_kernel(): pl.pallas_call(body, name=name, out_shape=outs, in_specs=[whole] * len(ar...  7.98 us
    all_to_all x1, starting transfers between devices, exchange(): return lax.all_to_all(chunks, both, split_axis=0, concat_axis=0, tiled=True)  7.3 us
    ppermute x1, waiting for transfers between devices, shards(): higher = lax.ppermute(fields, 'gx', down)  4.17 us
    ppermute x1, starting transfers between devices, shards(): lower = lax.ppermute(fields, 'gx', up)  3.68 us
    unnamed x22, local copies, waits for them, and re-layouts  3.67 us
  transfers between devices with their start and end apart: 3, of which 2 were waited for; matrix products, arithmetic and copies ran while one was open for 0% of the time, Pallas kernels for 1%

profile of v2, /device:TPU:0, one launch (start us, length us, event | category | flops | bytes accessed | tf_op | source)
XLA Modules:
  0.0 68.1 jit_solution(1075305244892821945)
XLA Ops:
  0.7 0.7 copy-done.4
  1.3 0.9 %copy-done = f32[9,4,4,128]{3,2,1,0:T(4,128)S(1)} copy-done((f32[9,4,4,128]{3,2,1,0:T(4,128)S(1)}, f32[9,4,4,128]{3,2,1,0:T(4,128)}, u32[]{:S(2)}) %copy-start) | copy-done | bytes 73752
  2.2 0.7 %copy-done.5 = f32[4,4,128]{2,1,0:T(4,128)S(1)} copy-done((f32[4,4,128]{2,1,0:T(4,128)S(1)}, f32[4,4,128]{2,1,0:T(4,128)}, u32[]{:S(2)}) %copy-start.5) | copy-done | bytes 8216
  2.9 0.7 %copy-done.6 = f32[4,4,128]{2,1,0:T(4,128)S(1)} copy-done((f32[4,4,128]{2,1,0:T(4,128)S(1)}, f32[4,4,128]{2,1,0:T(4,128)}, u32[]{:S(2)}) %copy-start.6) | copy-done | bytes 8216
  3.6 0.7 copy-done.9
  4.3 0.8 %pack_edges.1 = (f32[192,128]{1,0:T(8,128)S(1)}, f32[32,8,128]{2,1,0:T(8,128)}) custom-call(f32[144,128]{1,0:T(8,128)S(1)} %bitcast.15, f32[16,128]{1,0:T(8,128)S(1)} %bitcast.19, f32[16,128]{1,0:T(8,128)S(1)} %bitcast.20, f32[16,128]{1,0:T(8,128)S(1)} %bitcast.21, s32[1,64]{1,0:T(1,128)S(1)} %bitcast.24, f32[3,64]{1,0:T(4,128)S(1)} %copy-done.9), custom_call_target="tpu_custom_call" | custom-call | tf_op jit(solution)/shard_map/pack_edges/pallas_call | solution.py:23
  5.1 7.3 %all-to-all-start = ((f32[32,8,128]{2,1,0:T(8,128)}), f32[32,8,128]{2,1,0:T(8,128)S(1)}, u32[]{:S(2)}, u32[]{:S(2)}) async-start(f32[32,8,128]{2,1,0:T(8,128)} %get-tuple-element.17), calls=%async_computation | async-start | bytes 262144 | tf_op jit(solution)/shard_map/all_to_all | solution.py:524
  12.4 0.0 copy-start.1
  12.4 3.7 %collective-permute-start.1 = (f32[192,128]{1,0:T(8,128)S(1)}, f32[192,128]{1,0:T(8,128)S(1)}, u32[]{:S(2)}, u32[]{:S(2)}) collective-permute-start(f32[192,128]{1,0:T(8,128)S(1)} %get-tuple-element.16.fields_ref), channel_id=1, source_target_pairs={{0,8},{8,16},{16,24},{1,9},{9,17},{17,25},{2,10},{10,18},{18,26},{... | collective-permute-start | bytes 294920 | tf_op jit(solution)/shard_map/ppermute | solution.py:540
  16.1 1.3 %collective-permute-start = (f32[192,128]{1,0:T(8,128)S(1)}, f32[192,128]{1,0:T(8,128)S(1)}, u32[]{:S(2)}, u32[]{:S(2)}) collective-permute-start(f32[192,128]{1,0:T(8,128)S(1)} %get-tuple-element.16.fields_ref), channel_id=1, source_target_pairs={{8,0},{16,8},{24,16},{9,1},{17,9},{25,17},{10,2},{18,10},{26,18},{... | collective-permute-start | bytes 294920 | tf_op jit(solution)/shard_map/ppermute | solution.py:541
  17.4 0.6 segment_slots.1
  18.1 0.0 copy-start.3
  18.1 0.4 collective-permute-done.1.lower_ref
  18.4 4.2 %collective-permute-done.higher_ref = f32[192,128]{1,0:T(8,128)S(1)} collective-permute-done((f32[192,128]{1,0:T(8,128)S(1)}, f32[192,128]{1,0:T(8,128)S(1)}, u32[]{:S(2)}, u32[]{:S(2)}) %collective-permute-start) | collective-permute-done | bytes 98336 | tf_op jit(solution)/shard_map/ppermute | solution.py:541
  22.6 0.0 all-to-all-done.recv_ref
  22.6 2.6 %forward_run.1 = (f32[128,128]{1,0:T(8,128)S(1)}, f32[288,128]{1,0:T(8,128)S(1)}, f32[12,16,256]{2,1,0:T(8,128)S(1)}) custom-call(f32[192,128]{1,0:T(8,128)S(1)} %get-tuple-element.16.fields_ref, f32[192,128]{1,0:T(8,128)S(1)} %collective-permute-done.higher_ref, f32[192,128]{1,0:T(8,128)S(1)} %collective-permute-done.1.lower_ref, ...), custom_call_target="tpu_custom_call" | custom-call | tf_op jit(solution)/shard_map/forward_run/pallas_call | solution.py:23
  25.2 0.0 copy-start.2
  25.2 11.8 %all_to_all.25 = f32[32,4,128]{2,1,0:T(4,128)S(1)} all-to-all(f32[32,4,128]{2,1,0:T(4,128)S(1)} %bitcast.16), channel_id=1, replica_groups=mesh['gx'=4,'gy'=8] {'gx','gy'}, dimensions={0} | all-to-all | bytes 131072 | tf_op jit(solution)/shard_map/all_to_all | solution.py:524
  37.1 1.5 %channel_sums.1 = (f32[3,1024]{1,0:T(4,128)}, f32[128,128]{1,0:T(8,128)S(1)}) custom-call(f32[128,128]{1,0:T(8,128)S(1)} %bitcast.14, f32[3,1024]{1,0:T(4,128)S(1)} %copy-done.2), custom_call_target="tpu_custom_call" | custom-call | tf_op jit(solution)/shard_map/channel_sums/pallas_call | solution.py:23
  38.5 9.1 %all_to_all.26 = f32[32,4,128]{2,1,0:T(4,128)S(1)} all-to-all(f32[32,4,128]{2,1,0:T(4,128)S(1)} %bitcast.17), channel_id=1, replica_groups=mesh['gx'=4,'gy'=8] {'gx','gy'}, dimensions={0} | all-to-all | bytes 131072 | tf_op jit(solution)/shard_map/all_to_all | solution.py:524
  47.6 1.2 %segment_loads.1 = (f32[96,128]{1,0:T(8,128)S(1)}, f32[32,4,128]{2,1,0:T(4,128)S(1)}, f32[4,64,128]{2,1,0:T(8,128)S(1)}) custom-call(f32[128,128]{1,0:T(8,128)S(1)} %bitcast.13, s32[16,128]{1,0:T(8,128)S(1)} %get-tuple-element.18.slot_ref, s32[16,128]{1,0:T(8,128)S(1)} %get-tuple-element.19.row_ref, f32[2,2048]{1,0:T(2,128)S(1)} %copy-done.1, ...), custom_call_target="tpu_custom_call" | custom-call | tf_op jit(solution)/shard_map/segment_loads/pallas_call | solution.py:23
  48.8 9.1 %all_to_all.27.recv_ref = f32[32,4,128]{2,1,0:T(4,128)S(1)} all-to-all(f32[32,4,128]{2,1,0:T(4,128)S(1)} %get-tuple-element.27), channel_id=1, replica_groups=mesh['gx'=4,'gy'=8] {'gx','gy'}, dimensions={0} | all-to-all | bytes 131072 | tf_op jit(solution)/shard_map/all_to_all | solution.py:524
  57.9 8.8 %all_to_all.28.column_ref = f32[4,64,128]{2,1,0:T(8,128)S(1)} all-to-all(f32[4,64,128]{2,1,0:T(8,128)S(1)} %get-tuple-element.26), channel_id=1, replica_groups=mesh['gx'=4,'gy'=8] {'gx'}, dimensions={0} | all-to-all | bytes 262144 | tf_op jit(solution)/shard_map/all_to_all | solution.py:614
  66.7 1.3 %adjoint_run.1 = f32[32,128]{1,0:T(8,128)} custom-call(f32[96,128]{1,0:T(8,128)S(1)} %get-tuple-element.25.load_ref, f32[4,64,128]{2,1,0:T(8,128)S(1)} %all_to_all.28.column_ref, f32[32,4,128]{2,1,0:T(4,128)S(1)} %all_to_all.27.recv_ref, f32[288,128]{1,0:T(8,128)S(1)} %get-tuple-element.28.strain_ref, f32[12,16,256]{2,1,0:T(8,128)S(1)} %get-tuple-element.29.medium_ref), custom_call_target="tpu_custom_call" | custom-call | tf_op jit(solution)/shard_map/adjoint_run/pallas_call | solution.py:23
  (14 shorter events, 0.0 us)
Async XLA Ops:
  0.6 0.7 %copy-start.4 = (f32[4,4,128]{2,1,0:T(4,128)S(1)}, f32[4,4,128]{2,1,0:T(4,128)}, u32[]{:S(2)}) copy-start(f32[4,4,128]{2,1,0:T(4,128)} %param.12) | copy-start | bytes 24580
  0.6 0.7 %copy-start.10 = (s32[64]{0:T(128)S(1)}, s32[64]{0:T(128)}, u32[]{:S(2)}) copy-start(s32[64]{0:T(128)} %param.15) | copy-start | bytes 772
  1.3 0.9 %copy-start = (f32[9,4,4,128]{3,2,1,0:T(4,128)S(1)}, f32[9,4,4,128]{3,2,1,0:T(4,128)}, u32[]{:S(2)}) copy-start(f32[9,4,4,128]{3,2,1,0:T(4,128)} %param.11) | copy-start | bytes 221188
  2.2 0.7 %copy-start.5 = (f32[4,4,128]{2,1,0:T(4,128)S(1)}, f32[4,4,128]{2,1,0:T(4,128)}, u32[]{:S(2)}) copy-start(f32[4,4,128]{2,1,0:T(4,128)} %param.13) | copy-start | bytes 24580
  2.9 0.7 %copy-start.6 = (f32[4,4,128]{2,1,0:T(4,128)S(1)}, f32[4,4,128]{2,1,0:T(4,128)}, u32[]{:S(2)}) copy-start(f32[4,4,128]{2,1,0:T(4,128)} %param.14) | copy-start | bytes 24580
  3.6 0.7 %copy-start.9 = (f32[3,64]{1,0:T(4,128)S(1)}, f32[3,64]{1,0:T(4,128)}, u32[]{:S(2)}) copy-start(f32[3,64]{1,0:T(4,128)} %wavelet_ref.1) | copy-start | bytes 2308
  5.1 12.3 %copy-start.7 = (s32[2048,1]{0,1:T(1,128)S(1)}, s32[2048,1]{0,1:T(1,128)}, u32[]{:S(2)}) copy-start(s32[2048,1]{0,1:T(1,128)} %param.19) | copy-start | bytes 24580
  5.1 12.3 %copy-start.8 = (s32[2048]{0:T(1024)S(1)}, s32[2048]{0:T(1024)}, u32[]{:S(2)}) copy-start(s32[2048]{0:T(1024)} %param.17) | copy-start | bytes 24580
  5.1 17.5 %all-to-all-start = ((f32[32,8,128]{2,1,0:T(8,128)}), f32[32,8,128]{2,1,0:T(8,128)S(1)}, u32[]{:S(2)}, u32[]{:S(2)}) async-start(f32[32,8,128]{2,1,0:T(8,128)} %get-tuple-element.17), calls=%async_computation | async-start | bytes 262144 | tf_op jit(solution)/shard_map/all_to_all | solution.py:524
  12.4 10.2 %copy-start.1 = (f32[2,2048]{1,0:T(2,128)S(1)}, f32[2,2048]{1,0:T(2,128)}, u32[]{:S(2)}) copy-start(f32[2,2048]{1,0:T(2,128)} %weight_ref.3) | copy-start | bytes 49156
  12.4 6.0 %collective-permute-start.1 = (f32[192,128]{1,0:T(8,128)S(1)}, f32[192,128]{1,0:T(8,128)S(1)}, u32[]{:S(2)}, u32[]{:S(2)}) collective-permute-start(f32[192,128]{1,0:T(8,128)S(1)} %get-tuple-element.16.fields_ref), channel_id=1, source_target_pairs={{0,8},{8,16},{16,24},{1,9},{9,17},{17,25},{2,10},{10,18},{18,26},{... | collective-permute-start | bytes 294920 | tf_op jit(solution)/shard_map/ppermute | solution.py:540
  16.1 6.5 %collective-permute-start = (f32[192,128]{1,0:T(8,128)S(1)}, f32[192,128]{1,0:T(8,128)S(1)}, u32[]{:S(2)}, u32[]{:S(2)}) collective-permute-start(f32[192,128]{1,0:T(8,128)S(1)} %get-tuple-element.16.fields_ref), channel_id=1, source_target_pairs={{8,0},{16,8},{24,16},{9,1},{17,9},{25,17},{10,2},{18,10},{26,18},{... | collective-permute-start | bytes 294920 | tf_op jit(solution)/shard_map/ppermute | solution.py:541
  18.1 4.5 %copy-start.3 = (s32[2048]{0:T(1024)S(1)}, s32[2048]{0:T(1024)}, u32[]{:S(2)}) copy-start(s32[2048]{0:T(1024)} %param.20) | copy-start | bytes 24580
  25.2 11.9 %copy-start.2 = (f32[3,1024]{1,0:T(4,128)S(1)}, f32[3,1024]{1,0:T(4,128)}, u32[]{:S(2)}) copy-start(f32[3,1024]{1,0:T(4,128)} %observed_ref.1) | copy-start | bytes 36868

commit v3 on v0

--- a/solution.py
+++ b/solution.py
@@ -18,13 +18,13 @@
 NEAR = tuple((dx, dy) for dx in (-1, 0, 1) for dy in (-1, 0, 1))
 
 
-def call_kernel(body, name, outs, scratch, *args):
+def call_kernel(body, name, outs, scratch, *args, place=pltpu.VMEM):
     whole = pl.BlockSpec(memory_space=pltpu.VMEM)
     return pl.pallas_call(
         body,
         name=name,
         out_shape=outs,
-        in_specs=[whole] * len(args),
+        in_specs=[pl.BlockSpec(memory_space=place)] * len(args),
         out_specs=[whole] * len(outs),
         scratch_shapes=scratch,
         compiler_params=pltpu.CompilerParams(vmem_limit_bytes=24 * 1024 * 1024),
@@ -50,6 +50,16 @@
     return lax.dot_general(left, right, (((1,), (1,)), ((), ())), preferred_element_type=F32)
 
 
+def two_pieces(values):
+    high = values.astype(BF16).astype(F32)
+    return high, values - high
+
+
+def sum_halves(values):
+    half = values.shape[0] // 2
+    return values[:half] + values[half:]
+
+
 def sum_thirds(values):
     third = values.shape[0] // 3
     return values[:third] + values[third : 2 * third] + values[2 * third :]
@@ -63,14 +73,11 @@
 
 
 def edge_columns(rows, side_ref):
-    groups = rows.shape[0] // LANES
+    width = rows.shape[0]
     turned = rows.T
     for side, base in ((0, 0), (1, LANES - RIM)):
         for column in range(RIM):
-            for group in range(groups):
-                side_ref[side, column * groups + group : column * groups + group + 1, :] = turned[
-                    base + column : base + column + 1, group * LANES : (group + 1) * LANES
-                ]
+            side_ref[side, 0:1, column * width : (column + 1) * width] = turned[base + column : base + column + 1, :]
 
 
 def send_sides(side_ref, out_ref, places):
@@ -87,14 +94,12 @@
     return jnp.where(inside, recv_ref[index], 0.0)
 
 
-def rim_rows(recv_ref, dx, groups, turn_ref):
+def rim_rows(recv_ref, dx, turn_ref):
+    width = turn_ref.shape[1]
     for dy, base in ((1, 0), (-1, LANES - RIM)):
         chunk = arrived_chunk(recv_ref, dx, dy)
         for column in range(RIM):
-            for group in range(groups):
-                turn_ref[base + column : base + column + 1, group * LANES : (group + 1) * LANES] = chunk[
-                    column * groups + group : column * groups + group + 1, :
-                ]
+            turn_ref[base + column : base + column + 1, :] = chunk[:, column * width : (column + 1) * width]
     return turn_ref[...].T
 
 
@@ -170,16 +175,30 @@
                 )
 
 
-def pack_body(fields_ref, cells_ref, wavelet_ref, out_ref, side_ref):
+def pack_body(*refs):
+    inputs, (fields_ref, out_ref, side_ref, cells_ref, wavelet_ref, arrived) = refs[:6], refs[6:]
+    targets, at = [], 0
+    for source in inputs[:4]:
+        targets.append(fields_ref.at[at : at + source.shape[0]])
+        at = at + source.shape[0]
+    copies = [
+        pltpu.make_async_copy(source, target, arrived.at[number])
+        for number, (source, target) in enumerate(zip(inputs, targets + [cells_ref, wavelet_ref]))
+    ]
+    for copy in copies:
+        copy.start()
+    for copy in copies:
+        copy.wait()
     rows = fields_ref[...]
     spare = 2 * LANES - rows.shape[0]
     edge_columns(jnp.concatenate([rows, jnp.zeros((spare, LANES), F32)], axis=0), side_ref)
     count = cells_ref.shape[1]
+    first = RIM * 2 * LANES
     for side in range(2):
-        side_ref[side, 6:7, 0:count] = cells_ref[...].astype(F32)
-        side_ref[side, 6:7, count : 2 * count] = wavelet_ref[0:1, :]
-        side_ref[side, 7:8, 0:count] = wavelet_ref[1:2, :]
-        side_ref[side, 7:8, count : 2 * count] = wavelet_ref[2:3, :]
+        side_ref[side, 0:1, first : first + count] = cells_ref[...].astype(F32)
+        for step in range(3):
+            at = first + (step + 1) * count
+            side_ref[side, 0:1, at : at + count] = wavelet_ref[step : step + 1, :]
     send_sides(side_ref, out_ref, NEAR)
 
 
@@ -232,7 +251,8 @@
     halves = []
     for dx, dy in NEAR:
         chunk = arrived_chunk(recv_ref, dx, dy)
-        cells = chunk[6:7, :].astype(I32)
+        one, two = chunk[:, 6 * LANES : 7 * LANES], chunk[:, 7 * LANES :]
+        cells = one.astype(I32)
         y = cells & (cols_y - 1)
         rest = cells >> (cols_y.bit_length() - 1)
         x = rest & (TILE_X - 1)
@@ -244,7 +264,7 @@
             lane = jnp.where(y >= cols_y - RIM, y + LANES, -1)
         else:
             lane = y
-        halves.append((row, lane, chunk[6:7, :], chunk[7:8, :]))
+        halves.append((row, lane, one, two))
     zero_row = jnp.zeros((1, LANES), F32)
     halves.append((jnp.zeros((1, LANES), I32), jnp.full((1, LANES), -1, I32), zero_row, zero_row))
     for block in range(len(halves) // 2):
@@ -291,7 +311,7 @@
     depth = medium_ref.shape[0] // 3
     cells_row = depth * TILE_X
     turn_ref[...] = jnp.zeros_like(turn_ref)
-    rims = [rim_rows(recv_ref, dx, 2, turn_ref) for dx in (0, 1, -1)]
+    rims = [rim_rows(recv_ref, dx, turn_ref) for dx in (0, 1, -1)]
     lay_planes(planes_ref, 0, fields_ref, higher_ref, lower_ref)
     lay_planes(planes_ref, LANES, *rims)
     first = 9 * depth
@@ -368,16 +388,15 @@
         for part in range(parts):
             at = step * parts + part
             residual_ref[step : step + 1, part * LANES : (part + 1) * LANES] = held_ref[at : at + 1, :]
-    residual = jnp.concatenate(pieces(held_ref[...]), axis=0).astype(BF16)
+    residual = jnp.concatenate(two_pieces(held_ref[...]), axis=0).astype(BF16)
     for s in range(groups):
         lanes = slice(s * LANES, (s + 1) * LANES)
-        found = sum_thirds(times(residual, place_ref[:, lanes]))
+        found = sum_halves(times(residual, place_ref[:, lanes]))
         at_part = part_down == (numbers[s] >> 7)
         for step in range(3):
-            reply_ref[4 * s + step : 4 * s + step + 1, :] = jnp.sum(
+            reply_ref[s, 0:1, step * LANES : (step + 1) * LANES] = jnp.sum(
                 jnp.where(at_part, found[step * parts : (step + 1) * parts], 0.0), axis=0, keepdims=True
             )
-        reply_ref[4 * s + 3 : 4 * s + 4, :] = jnp.zeros((1, LANES), F32)
 
 
 def load_body(
@@ -391,32 +410,34 @@
     out_ref,
     spread_ref,
     side_ref,
+    rows_ref,
 ):
     cells_row = load_ref.shape[0] // 6
     stack_rows = load_ref.shape[0]
-    arrived = jnp.concatenate(pieces(arrived_ref[...]), axis=0).astype(BF16)
-    slots_down = iota((LANES, LANES), 0) >> 2
+    groups = arrived_ref.shape[0]
+    for step in range(3):
+        for s in range(groups):
+            at = step * groups + s
+            rows_ref[at : at + 1, :] = arrived_ref[s, 0:1, step * LANES : (step + 1) * LANES]
+    arrived = jnp.concatenate(two_pieces(rows_ref[...]), axis=0).astype(BF16)
+    slots_down = iota((groups, LANES), 0)
     rows_down = iota((cells_row, LANES), 0)
     for block in range(slot_ref.shape[0]):
         lanes = slice(block * LANES, (block + 1) * LANES)
-        found = sum_thirds(times(arrived, place_ref[:, lanes]))
-        found = jnp.where(slots_down == slot_ref[block : block + 1, :], found, 0.0)
-        folded = found[0:8]
-        for part in range(1, LANES // 8):
-            folded = folded + found[8 * part : 8 * part + 8]
-        folded = folded + pltpu.roll(folded, 4, 0)
+        found = sum_halves(times(arrived, place_ref[:, lanes]))
+        in_slot = slots_down == slot_ref[block : block + 1, :]
         at_row = rows_down == row_ref[block : block + 1, :]
         for turn in range(3):
-            back = folded[2 - turn : 3 - turn, :]
+            base = (2 - turn) * groups
+            back = jnp.sum(jnp.where(in_slot, found[base : base + groups], 0.0), axis=0, keepdims=True)
             for part in range(2):
-                for third, piece in enumerate(pieces(weight_ref[part : part + 1, lanes] * back)):
-                    base = third * stack_rows + (2 * turn + part) * cells_row
+                for half, piece in enumerate(two_pieces(weight_ref[part : part + 1, lanes] * back)):
+                    base = half * stack_rows + (2 * turn + part) * cells_row
                     spread_ref[base : base + cells_row, lanes] = jnp.where(at_row, piece, 0.0).astype(BF16)
-    load = sum_thirds(times_turned(spread_ref[...], cover_ref[...]))
+    load = sum_halves(times_turned(spread_ref[...], cover_ref[...]))
     load_ref[...] = load
     spare = LANES - stack_rows
     edge_columns(jnp.concatenate([load, jnp.zeros((spare, LANES), F32)], axis=0), side_ref)
-    side_ref[:, RIM : RIM + 1, :] = jnp.zeros((2, 1, LANES), F32)
     send_sides(side_ref, out_ref, [(dx, dy) for dx, dy in NEAR if dy])
 
 
@@ -425,7 +446,7 @@
 ):
     depth = medium_ref.shape[0] // 3
     turn_ref[...] = jnp.zeros_like(turn_ref)
-    rims = [rim_rows(recv_ref, dx, 1, turn_ref) for dx in (0, 1, -1)]
+    rims = [rim_rows(recv_ref, dx, turn_ref) for dx in (0, 1, -1)]
     lay_planes(load_planes_ref, 0, load_ref, higher_ref, lower_ref)
     lay_planes(load_planes_ref, LANES, *rims)
     planes_ref[...] = jnp.zeros_like(planes_ref)
@@ -482,25 +503,29 @@
     def exchange(chunks):
         return lax.all_to_all(chunks, both, split_axis=0, concat_axis=0, tiled=True)
 
-    def to_owners(rows):
-        chunks = rows.reshape(slot_groups, 4, per_group, capacity).transpose(0, 2, 1, 3)
-        back = exchange(chunks.reshape(devices, 4, capacity)).reshape(slot_groups, per_group, 4, capacity)
-        return back.transpose(0, 2, 1, 3).reshape(slot_groups * 4, LANES)
-
-    fields = jnp.concatenate(
-        [values.reshape(-1, cols_y) for values in (initial_state, lame_lambda, shear_modulus, buoyancy)]
+    def route(rows, chunk):
+        parts = rows.reshape(slot_groups, -1, per_group, capacity).transpose(0, 2, 1, 3)
+        back = exchange(parts.reshape((devices,) + chunk)).reshape(slot_groups, per_group, -1, capacity)
+        return back.transpose(0, 2, 1, 3).reshape(rows.shape)
+
+    sources = source_cells.shape[0]
+    fields, edges = call_kernel(
+        pack_body,
+        "pack_edges",
+        [shape((12 * cells_row, cols_y), F32), shape((devices, 1, 8 * LANES), F32)],
+        [
+            pltpu.VMEM((2, 1, 8 * LANES), F32),
+            pltpu.VMEM((1, sources), I32),
+            pltpu.VMEM(source_wavelet.shape, F32),
+            pltpu.SemaphoreType.DMA((6,)),
+        ],
+        *[values.reshape(-1, cols_y) for values in (initial_state, lame_lambda, shear_modulus, buoyancy)],
+        source_cells.reshape(1, -1),
+        source_wavelet,
+        place=pl.ANY,
     )
     lower = lax.ppermute(fields, "gx", up)
     higher = lax.ppermute(fields, "gx", down)
-    (edges,) = call_kernel(
-        pack_body,
-        "pack_edges",
-        [shape((devices, 8, LANES), F32)],
-        [pltpu.VMEM((2, 8, LANES), F32)],
-        fields,
-        source_cells.reshape(1, -1),
-        source_wavelet,
-    )
     rims = exchange(edges)
     channels = partial_channel.reshape(blocks, LANES)
     slot, row, cover, place = call_kernel(
@@ -547,21 +572,25 @@
     residuals, reply = call_kernel(
         owner_body,
         "channel_sums",
-        [shape(observed_data.shape, F32), shape((slot_groups * 4, LANES), F32)],
+        [shape(observed_data.shape, F32), shape((slot_groups, 1, 3 * LANES), F32)],
         [
             pltpu.VMEM((12 * parts, slot_groups * LANES), BF16),
             pltpu.VMEM((LANES, slot_groups * LANES), BF16),
             pltpu.VMEM((4 * parts, LANES), F32),
         ],
-        to_owners(partials),
+        route(partials, (4, capacity)),
         observed_data,
     )
     loads, load_edges = call_kernel(
         load_body,
         "segment_loads",
-        [shape((6 * cells_row, cols_y), F32), shape((devices, 4, LANES), F32)],
-        [pltpu.VMEM((18 * cells_row, part_count), BF16), pltpu.VMEM((2, 4, LANES), F32)],
-        to_owners(reply),
+        [shape((6 * cells_row, cols_y), F32), shape((devices, 1, RIM * LANES), F32)],
+        [
+            pltpu.VMEM((12 * cells_row, part_count), BF16),
+            pltpu.VMEM((2, 1, RIM * LANES), F32),
+            pltpu.VMEM((3 * slot_groups, LANES), F32),
+        ],
+        route(reply, (1, 3 * capacity)),
         slot,
         row,
         segment_weight,

time: 61.3 us -> 63.2 us (1.031)
  local copies, waits for them, and re-layouts: 0.67 us -> 3.67 us
  other arithmetic: 0.95 us -> 0 us
    unnamed x14 -> x22, local copies, waits for them, and re-layouts: 0.67 us -> 3.67 us
    concatenate x1 -> x0, other arithmetic: 0.95 us -> none  [shards(): jnp.concatenate([values.reshape(-1, cols_y) for values in (initial_state,...]
where the time goes in v3:
time: 63.2 us; the launch traced here: 62.6 us
  blocking collectives  20.9 us (33%)
  starting transfers between devices  19.7 us (31%)
  waiting for transfers between devices  9.21 us (15%)
  Pallas kernels  8.32 us (13%)
  local copies, waits for them, and re-layouts  3.67 us (6%)
  between operations  0.8 us (1%)
    all_to_all x2, blocking collectives, exchange(): return lax.all_to_all(chunks, both, split_axis=0, concat_axis=0, tiled=True)  20.9 us
    all_to_all x2, starting transfers between devices, exchange(): return lax.all_to_all(chunks, both, split_axis=0, concat_axis=0, tiled=True)  9.86 us
    pallas_call x6, Pallas kernels, call_kernel(): pl.pallas_call(body, name=name, out_shape=outs, in_specs=[pl.BlockSpec(me...  8.32 us
    ppermute x1, waiting for transfers between devices, shards(): load_higher = lax.ppermute(loads, 'gx', down)  4.25 us
    ppermute x1, waiting for transfers between devices, shards(): higher = lax.ppermute(fields, 'gx', down)  4.17 us
    ppermute x1, starting transfers between devices, shards(): lower = lax.ppermute(fields, 'gx', up)  3.68 us
    unnamed x22, local copies, waits for them, and re-layouts  3.67 us
    ppermute x1, starting transfers between devices, shards(): load_lower = lax.ppermute(loads, 'gx', up)  3.59 us
  transfers between devices with their start and end apart: 6, of which 4 were waited for; matrix products, arithmetic and copies ran while one was open for 0% of the time, Pallas kernels for 1%

profile of v3, /device:TPU:0, one launch (start us, length us, event | category | flops | bytes accessed | tf_op | source)
XLA Modules:
  0.0 62.6 jit_solution(13654525223182739975)
XLA Ops:
  0.7 0.7 %copy-done.4 = f32[4,4,128]{2,1,0:T(4,128)S(1)} copy-done((f32[4,4,128]{2,1,0:T(4,128)S(1)}, f32[4,4,128]{2,1,0:T(4,128)}, u32[]{:S(2)}) %copy-start.4) | copy-done | bytes 8216
  1.3 0.9 %copy-done = f32[9,4,4,128]{3,2,1,0:T(4,128)S(1)} copy-done((f32[9,4,4,128]{3,2,1,0:T(4,128)S(1)}, f32[9,4,4,128]{3,2,1,0:T(4,128)}, u32[]{:S(2)}) %copy-start) | copy-done | bytes 73752
  2.2 0.7 %copy-done.5 = f32[4,4,128]{2,1,0:T(4,128)S(1)} copy-done((f32[4,4,128]{2,1,0:T(4,128)S(1)}, f32[4,4,128]{2,1,0:T(4,128)}, u32[]{:S(2)}) %copy-start.5) | copy-done | bytes 8216
  2.9 0.7 %copy-done.6 = f32[4,4,128]{2,1,0:T(4,128)S(1)} copy-done((f32[4,4,128]{2,1,0:T(4,128)S(1)}, f32[4,4,128]{2,1,0:T(4,128)}, u32[]{:S(2)}) %copy-start.6) | copy-done | bytes 8216
  3.6 0.7 %copy-done.9 = f32[3,64]{1,0:T(4,128)S(1)} copy-done((f32[3,64]{1,0:T(4,128)S(1)}, f32[3,64]{1,0:T(4,128)}, u32[]{:S(2)}) %copy-start.9) | copy-done | bytes 792
  4.3 1.0 %pack_edges.1 = (f32[192,128]{1,0:T(8,128)S(1)}, f32[32,1,1024]{2,1,0:T(1,128)}) custom-call(f32[144,128]{1,0:T(8,128)S(1)} %bitcast.12, f32[16,128]{1,0:T(8,128)S(1)} %bitcast.15, f32[16,128]{1,0:T(8,128)S(1)} %bitcast.16, f32[16,128]{1,0:T(8,128)S(1)} %bitcast.17, s32[1,64]{1,0:T(1,128)S(1)} %bitcast.20, f32[3,64]{1,0:T(4,128)S(1)} %copy-done.9), custom_call_target="tpu_custom_call" | custom-call | tf_op jit(solution)/shard_map/pack_edges/pallas_call | solution.py:23
  5.3 0.0 copy-start.7
  5.3 7.3 %all-to-all-start = ((f32[32,1,1024]{2,1,0:T(1,128)}), f32[32,1,1024]{2,1,0:T(1,128)S(1)}, u32[]{:S(2)}, u32[]{:S(2)}) async-start(f32[32,1,1024]{2,1,0:T(1,128)} %get-tuple-element.16), calls=%async_computation | async-start | bytes 262144 | tf_op jit(solution)/shard_map/all_to_all | solution.py:504
  12.6 3.7 %collective-permute-start.1 = (f32[192,128]{1,0:T(8,128)S(1)}, f32[192,128]{1,0:T(8,128)S(1)}, u32[]{:S(2)}, u32[]{:S(2)}) collective-permute-start(f32[192,128]{1,0:T(8,128)S(1)} %get-tuple-element.15.fields_ref), channel_id=1, source_target_pairs={{0,8},{8,16},{16,24},{1,9},{9,17},{17,25},{2,10},{10,18},{18,26},{... | collective-permute-start | bytes 294920 | tf_op jit(solution)/shard_map/ppermute | solution.py:527
  16.3 1.3 %collective-permute-start = (f32[192,128]{1,0:T(8,128)S(1)}, f32[192,128]{1,0:T(8,128)S(1)}, u32[]{:S(2)}, u32[]{:S(2)}) collective-permute-start(f32[192,128]{1,0:T(8,128)S(1)} %get-tuple-element.15.fields_ref), channel_id=1, source_target_pairs={{8,0},{16,8},{24,16},{9,1},{17,9},{25,17},{10,2},{18,10},{26,18},{... | collective-permute-start | bytes 294920 | tf_op jit(solution)/shard_map/ppermute | solution.py:528
  17.6 0.6 %segment_slots.1 = (s32[16,128]{1,0:T(8,128)S(1)}, s32[16,128]{1,0:T(8,128)S(1)}, bf16[128,2048]{1,0:T(8,128)(2,1)S(1)}, bf16[128,2048]{1,0:T(8,128)(2,1)S(1)}) custom-call(s32[16,128]{1,0:T(8,128)S(1)} %bitcast.18, s32[16,128]{1,0:T(8,128)S(1)} %bitcast.19), custom_call_target="tpu_custom_call" | custom-call | tf_op jit(solution)/shard_map/segment_slots/pallas_call | solution.py:23
  18.3 0.4 collective-permute-done.1.lower_ref
  18.6 4.2 %collective-permute-done.higher_ref = f32[192,128]{1,0:T(8,128)S(1)} collective-permute-done((f32[192,128]{1,0:T(8,128)S(1)}, f32[192,128]{1,0:T(8,128)S(1)}, u32[]{:S(2)}, u32[]{:S(2)}) %collective-permute-start) | collective-permute-done | bytes 98336 | tf_op jit(solution)/shard_map/ppermute | solution.py:528
  22.8 2.5 %forward_run.1 = (f32[128,128]{1,0:T(8,128)S(1)}, f32[288,128]{1,0:T(8,128)S(1)}, f32[12,16,256]{2,1,0:T(8,128)S(1)}) custom-call(f32[192,128]{1,0:T(8,128)S(1)} %get-tuple-element.15.fields_ref, f32[192,128]{1,0:T(8,128)S(1)} %collective-permute-done.higher_ref, f32[192,128]{1,0:T(8,128)S(1)} %collective-permute-done.1.lower_ref, ...), custom_call_target="tpu_custom_call" | custom-call | tf_op jit(solution)/shard_map/forward_run/pallas_call | solution.py:23
  25.4 11.8 %all_to_all.20 = f32[32,4,128]{2,1,0:T(4,128)S(1)} all-to-all(f32[32,4,128]{2,1,0:T(4,128)S(1)} %bitcast.13), channel_id=1, replica_groups=mesh['gx'=4,'gy'=8] {'gx','gy'}, dimensions={0} | all-to-all | bytes 131072 | tf_op jit(solution)/shard_map/all_to_all | solution.py:504
  37.2 1.4 %channel_sums.1 = (f32[3,1024]{1,0:T(4,128)}, f32[32,1,384]{2,1,0:T(1,128)S(1)}) custom-call(f32[128,128]{1,0:T(8,128)S(1)} %bitcast.11, f32[3,1024]{1,0:T(4,128)S(1)} %copy-done.2), custom_call_target="tpu_custom_call" | custom-call | tf_op jit(solution)/shard_map/channel_sums/pallas_call | solution.py:23
  38.7 9.0 %all_to_all.21.arrived_ref = f32[32,1,384]{2,1,0:T(1,128)S(1)} all-to-all(f32[32,1,384]{2,1,0:T(1,128)S(1)} %get-tuple-element.23), channel_id=1, replica_groups=mesh['gx'=4,'gy'=8] {'gx','gy'}, dimensions={0} | all-to-all | bytes 98304 | tf_op jit(solution)/shard_map/all_to_all | solution.py:504
  47.7 1.4 %segment_loads.1 = (f32[96,128]{1,0:T(8,128)S(1)}, f32[32,1,384]{2,1,0:T(1,128)}) custom-call(f32[32,1,384]{2,1,0:T(1,128)S(1)} %all_to_all.21.arrived_ref, s32[16,128]{1,0:T(8,128)S(1)} %get-tuple-element.17.slot_ref, s32[16,128]{1,0:T(8,128)S(1)} %get-tuple-element.18.row_ref, f32[2,2048]{1,0:T(2,128)S(1)} %copy-done.1, ...), custom_call_target="tpu_custom_call" | custom-call | tf_op jit(solution)/shard_map/segment_loads/pallas_call | solution.py:23
  49.1 2.6 %all-to-all-start.3 = ((f32[32,1,384]{2,1,0:T(1,128)}), f32[32,1,384]{2,1,0:T(1,128)S(1)}, u32[]{:S(2)}, u32[]{:S(2)}) async-start(f32[32,1,384]{2,1,0:T(1,128)} %get-tuple-element.25), calls=%async_computation.3 | async-start | bytes 98304 | tf_op jit(solution)/shard_map/all_to_all | solution.py:504
  51.7 3.6 %collective-permute-start.3 = (f32[96,128]{1,0:T(8,128)S(1)}, f32[96,128]{1,0:T(8,128)S(1)}, u32[]{:S(2)}, u32[]{:S(2)}) collective-permute-start(f32[96,128]{1,0:T(8,128)S(1)} %get-tuple-element.24.load_ref), channel_id=1, source_target_pairs={{0,8},{8,16},{16,24},{1,9},{9,17},{17,25},{2,10},{10,18},{18,26},{... | collective-permute-start | bytes 147464 | tf_op jit(solution)/shard_map/ppermute | solution.py:600
  55.3 1.3 %collective-permute-start.2 = (f32[96,128]{1,0:T(8,128)S(1)}, f32[96,128]{1,0:T(8,128)S(1)}, u32[]{:S(2)}, u32[]{:S(2)}) collective-permute-start(f32[96,128]{1,0:T(8,128)S(1)} %get-tuple-element.24.load_ref), channel_id=1, source_target_pairs={{8,0},{16,8},{24,16},{9,1},{17,9},{25,17},{10,2},{18,10},{26,18},{... | collective-permute-start | bytes 147464 | tf_op jit(solution)/shard_map/ppermute | solution.py:601
  56.6 0.4 collective-permute-done.3.lower_ref
  57.0 4.3 %collective-permute-done.2.higher_ref = f32[96,128]{1,0:T(8,128)S(1)} collective-permute-done((f32[96,128]{1,0:T(8,128)S(1)}, f32[96,128]{1,0:T(8,128)S(1)}, u32[]{:S(2)}, u32[]{:S(2)}) %collective-permute-start.2) | collective-permute-done | bytes 49184 | tf_op jit(solution)/shard_map/ppermute | solution.py:601
  61.3 1.3 %adjoint_run.1 = f32[32,128]{1,0:T(8,128)} custom-call(f32[96,128]{1,0:T(8,128)S(1)} %get-tuple-element.24.load_ref, f32[96,128]{1,0:T(8,128)S(1)} %collective-permute-done.2.higher_ref, f32[96,128]{1,0:T(8,128)S(1)} %collective-permute-done.3.lower_ref, f32[32,1,384]{2,1,0:T(1,128)S(1)} %all-to-all-done.3.recv_ref, ...), custom_call_target="tpu_custom_call" | custom-call | tf_op jit(solution)/shard_map/adjoint_run/pallas_call | solution.py:23
  (18 shorter events, 0.0 us)
Async XLA Ops:
  0.6 0.7 %copy-start.4 = (f32[4,4,128]{2,1,0:T(4,128)S(1)}, f32[4,4,128]{2,1,0:T(4,128)}, u32[]{:S(2)}) copy-start(f32[4,4,128]{2,1,0:T(4,128)} %param.12) | copy-start | bytes 24580
  0.6 0.7 %copy-start.10 = (s32[64]{0:T(128)S(1)}, s32[64]{0:T(128)}, u32[]{:S(2)}) copy-start(s32[64]{0:T(128)} %param.15) | copy-start | bytes 772
  1.3 0.9 %copy-start = (f32[9,4,4,128]{3,2,1,0:T(4,128)S(1)}, f32[9,4,4,128]{3,2,1,0:T(4,128)}, u32[]{:S(2)}) copy-start(f32[9,4,4,128]{3,2,1,0:T(4,128)} %param.11) | copy-start | bytes 221188
  2.2 0.7 %copy-start.5 = (f32[4,4,128]{2,1,0:T(4,128)S(1)}, f32[4,4,128]{2,1,0:T(4,128)}, u32[]{:S(2)}) copy-start(f32[4,4,128]{2,1,0:T(4,128)} %param.13) | copy-start | bytes 24580
  2.9 0.7 %copy-start.6 = (f32[4,4,128]{2,1,0:T(4,128)S(1)}, f32[4,4,128]{2,1,0:T(4,128)}, u32[]{:S(2)}) copy-start(f32[4,4,128]{2,1,0:T(4,128)} %param.14) | copy-start | bytes 24580
  3.6 0.7 %copy-start.9 = (f32[3,64]{1,0:T(4,128)S(1)}, f32[3,64]{1,0:T(4,128)}, u32[]{:S(2)}) copy-start(f32[3,64]{1,0:T(4,128)} %refs_5_.1) | copy-start | bytes 2308
  5.3 12.3 %copy-start.7 = (s32[2048,1]{0,1:T(1,128)S(1)}, s32[2048,1]{0,1:T(1,128)}, u32[]{:S(2)}) copy-start(s32[2048,1]{0,1:T(1,128)} %param.19) | copy-start | bytes 24580
  5.3 12.3 %copy-start.8 = (s32[2048]{0:T(1024)S(1)}, s32[2048]{0:T(1024)}, u32[]{:S(2)}) copy-start(s32[2048]{0:T(1024)} %param.17) | copy-start | bytes 24580
  5.3 17.5 %all-to-all-start = ((f32[32,1,1024]{2,1,0:T(1,128)}), f32[32,1,1024]{2,1,0:T(1,128)S(1)}, u32[]{:S(2)}, u32[]{:S(2)}) async-start(f32[32,1,1024]{2,1,0:T(1,128)} %get-tuple-element.16), calls=%async_computation | async-start | bytes 262144 | tf_op jit(solution)/shard_map/all_to_all | solution.py:504
  12.6 10.2 %copy-start.1 = (f32[2,2048]{1,0:T(2,128)S(1)}, f32[2,2048]{1,0:T(2,128)}, u32[]{:S(2)}) copy-start(f32[2,2048]{1,0:T(2,128)} %weight_ref.3) | copy-start | bytes 49156
  12.6 6.0 %collective-permute-start.1 = (f32[192,128]{1,0:T(8,128)S(1)}, f32[192,128]{1,0:T(8,128)S(1)}, u32[]{:S(2)}, u32[]{:S(2)}) collective-permute-start(f32[192,128]{1,0:T(8,128)S(1)} %get-tuple-element.15.fields_ref), channel_id=1, source_target_pairs={{0,8},{8,16},{16,24},{1,9},{9,17},{17,25},{2,10},{10,18},{18,26},{... | collective-permute-start | bytes 294920 | tf_op jit(solution)/shard_map/ppermute | solution.py:527
  16.3 6.5 %collective-permute-start = (f32[192,128]{1,0:T(8,128)S(1)}, f32[192,128]{1,0:T(8,128)S(1)}, u32[]{:S(2)}, u32[]{:S(2)}) collective-permute-start(f32[192,128]{1,0:T(8,128)S(1)} %get-tuple-element.15.fields_ref), channel_id=1, source_target_pairs={{8,0},{16,8},{24,16},{9,1},{17,9},{25,17},{10,2},{18,10},{26,18},{... | collective-permute-start | bytes 294920 | tf_op jit(solution)/shard_map/ppermute | solution.py:528
  18.3 4.5 %copy-start.3 = (s32[2048]{0:T(1024)S(1)}, s32[2048]{0:T(1024)}, u32[]{:S(2)}) copy-start(s32[2048]{0:T(1024)} %param.20) | copy-start | bytes 24580
  25.4 11.9 %copy-start.2 = (f32[3,1024]{1,0:T(4,128)S(1)}, f32[3,1024]{1,0:T(4,128)}, u32[]{:S(2)}) copy-start(f32[3,1024]{1,0:T(4,128)} %observed_ref.1) | copy-start | bytes 36868
  49.1 12.1 %all-to-all-start.3 = ((f32[32,1,384]{2,1,0:T(1,128)}), f32[32,1,384]{2,1,0:T(1,128)S(1)}, u32[]{:S(2)}, u32[]{:S(2)}) async-start(f32[32,1,384]{2,1,0:T(1,128)} %get-tuple-element.25), calls=%async_computation.3 | async-start | bytes 98304 | tf_op jit(solution)/shard_map/all_to_all | solution.py:504
  51.7 5.3 %collective-permute-start.3 = (f32[96,128]{1,0:T(8,128)S(1)}, f32[96,128]{1,0:T(8,128)S(1)}, u32[]{:S(2)}, u32[]{:S(2)}) collective-permute-start(f32[96,128]{1,0:T(8,128)S(1)} %get-tuple-element.24.load_ref), channel_id=1, source_target_pairs={{0,8},{8,16},{16,24},{1,9},{9,17},{17,25},{2,10},{10,18},{18,26},{... | collective-permute-start | bytes 147464 | tf_op jit(solution)/shard_map/ppermute | solution.py:600
  55.3 6.0 %collective-permute-start.2 = (f32[96,128]{1,0:T(8,128)S(1)}, f32[96,128]{1,0:T(8,128)S(1)}, u32[]{:S(2)}, u32[]{:S(2)}) collective-permute-start(f32[96,128]{1,0:T(8,128)S(1)} %get-tuple-element.24.load_ref), channel_id=1, source_target_pairs={{8,0},{16,8},{24,16},{9,1},{17,9},{25,17},{10,2},{18,10},{26,18},{... | collective-permute-start | bytes 147464 | tf_op jit(solution)/shard_map/ppermute | solution.py:601

commit v4 on v3

--- a/solution.py
+++ b/solution.py
@@ -18,7 +18,7 @@
 NEAR = tuple((dx, dy) for dx in (-1, 0, 1) for dy in (-1, 0, 1))
 
 
-def call_kernel(body, name, outs, scratch, *args, place=pltpu.VMEM):
+def call_kernel(body, name, outs, scratch, *args, place=pltpu.VMEM, room=24 * 1024 * 1024):
     whole = pl.BlockSpec(memory_space=pltpu.VMEM)
     return pl.pallas_call(
         body,
@@ -27,7 +27,7 @@
         in_specs=[pl.BlockSpec(memory_space=place)] * len(args),
         out_specs=[whole] * len(outs),
         scratch_shapes=scratch,
-        compiler_params=pltpu.CompilerParams(vmem_limit_bytes=24 * 1024 * 1024),
+        compiler_params=pltpu.CompilerParams(vmem_limit_bytes=room),
     )(*args)
 
 
@@ -131,7 +131,12 @@
     return plane - pltpu.roll(plane, 1, 1)
 
 
-def advance(field_ref, medium_ref, first, depth, emit, last):
+def scaled_medium(medium_ref, first, depth, z):
+    shear = STEP * medium_ref[first + depth + z]
+    return STEP * medium_ref[first + 2 * depth + z], STEP * medium_ref[first + z], shear, 2.0 * shear
+
+
+def advance(field_ref, medium, depth, emit, last):
     def field(number, z):
         return field_ref[number * depth + z]
 
@@ -144,7 +149,7 @@
         return here - field(number, z - 1) if z else here
 
     for z in range(depth):
-        scale = STEP * medium_ref[first + 2 * depth + z]
+        scale = medium(z)[0]
         accel = (
             ahead_x(field(3, z)) + behind_y(field(6, z)) + behind_z(7, z),
             behind_x(field(6, z)) + ahead_y(field(4, z)) + behind_z(8, z),
@@ -164,15 +169,11 @@
         )
         emit(z, strains)
         if not last:
-            shear = medium_ref[first + depth + z]
-            dilated = medium_ref[first + z] * (strains[0] + strains[1] + strains[2])
+            _, dilate, shear, twice = medium(z)
+            dilated = dilate * (strains[0] + strains[1] + strains[2])
             for number in range(3):
-                field_ref[(3 + number) * depth + z] = field(3 + number, z) + STEP * (
-                    dilated + 2.0 * shear * strains[number]
-                )
-                field_ref[(6 + number) * depth + z] = (
-                    field(6 + number, z) + STEP * shear * strains[3 + number]
-                )
+                field_ref[(3 + number) * depth + z] = field(3 + number, z) + (dilated + twice * strains[number])
+                field_ref[(6 + number) * depth + z] = field(6 + number, z) + shear * strains[3 + number]
 
 
 def pack_body(*refs):
@@ -316,6 +317,7 @@
     lay_planes(planes_ref, LANES, *rims)
     first = 9 * depth
     medium_ref[...] = planes_ref[first:]
+    medium = functools.partial(scaled_medium, planes_ref, first, depth)
     source_ref[...] = source_maps(recv_ref, cols_y, depth, source_left_ref, source_right_ref)
     for step in range(3):
         for z in range(depth):
@@ -329,7 +331,7 @@
                 base = ((step * 6 + number) * depth + z) * TILE_X
                 strain_ref[base : base + TILE_X, :] = strain[0:TILE_X, 0:LANES]
 
-        advance(planes_ref, planes_ref, first, depth, emit, step == 2)
+        advance(planes_ref, medium, depth, emit, step == 2)
     axial = jnp.concatenate(
         [strain_ref[step * 6 * cells_row : (step * 6 + 2) * cells_row, :] for step in range(3)], axis=0
     )
@@ -441,10 +443,31 @@
     send_sides(side_ref, out_ref, [(dx, dy) for dx, dy in NEAR if dy])
 
 
+def factors_body(strain_ref, factor_ref):
+    rows = strain_ref.shape[0] // 18
+    for step in range(3):
+        strains = [strain_ref[(step * 6 + n) * rows : (step * 6 + n + 1) * rows, :] for n in range(6)]
+        factors = [2.0 * s for s in strains[:3]] + strains[3:] + [strains[0] + strains[1] + strains[2]]
+        for number, factor in enumerate(factors):
+            base = (step * 7 + number) * rows
+            factor_ref[base : base + rows, :] = factor
+
+
+def medium_body(medium_ref, scaled_ref):
+    depth = medium_ref.shape[0] // 3
+    for z in range(depth):
+        for number, plane in enumerate(scaled_medium(medium_ref, 0, depth, z)):
+            scaled_ref[number * depth + z] = plane
+
+
 def adjoint_body(
     load_ref, higher_ref, lower_ref, recv_ref, strain_ref, medium_ref, gradient_ref, load_planes_ref, planes_ref, turn_ref
 ):
-    depth = medium_ref.shape[0] // 3
+    depth = medium_ref.shape[0] // 4
+
+    def medium(z):
+        return [medium_ref[number * depth + z] for number in range(4)]
+
     turn_ref[...] = jnp.zeros_like(turn_ref)
     rims = [rim_rows(recv_ref, dx, turn_ref) for dx in (0, 1, -1)]
     lay_planes(load_planes_ref, 0, load_ref, higher_ref, lower_ref)
@@ -459,18 +482,18 @@
 
         def emit(z, strains, turn=turn):
             forward = []
-            for number in range(6):
-                base = (((2 - turn) * 6 + number) * depth + z) * TILE_X
+            for number in range(7):
+                base = (((2 - turn) * 7 + number) * depth + z) * TILE_X
                 forward.append(strain_ref[base : base + TILE_X, :])
             back = [strain[0:TILE_X, 0:LANES] for strain in strains]
-            dilation = (forward[0] + forward[1] + forward[2]) * (back[0] + back[1] + back[2])
+            dilation = forward[6] * (back[0] + back[1] + back[2])
             product = [forward[number] * back[number] for number in range(6)]
-            shear = 2.0 * (product[0] + product[1] + product[2]) + product[3] + product[4] + product[5]
+            shear = (product[0] + product[1] + product[2]) + product[3] + product[4] + product[5]
             for part, term in enumerate((dilation, shear)):
                 base = (part * depth + z) * TILE_X
                 gradient_ref[base : base + TILE_X, :] = gradient_ref[base : base + TILE_X, :] + term
 
-        advance(planes_ref, medium_ref, 0, depth, emit, turn == 2)
+        advance(planes_ref, medium, depth, emit, turn == 2)
 
 
 def shards(
@@ -523,6 +546,7 @@
         source_cells.reshape(1, -1),
         source_wavelet,
         place=pl.ANY,
+        room=60 * 1024 * 1024,
     )
     lower = lax.ppermute(fields, "gx", up)
     higher = lax.ppermute(fields, "gx", down)
@@ -568,6 +592,10 @@
         cover,
         place,
     )
+    (factors,) = call_kernel(
+        factors_body, "forward_factors", [shape((21 * cells_row, cols_y), F32)], [], strains
+    )
+    arrived, factors = lax.optimization_barrier((route(partials, (4, capacity)), factors))
     parts = observed_data.shape[1] // LANES
     residuals, reply = call_kernel(
         owner_body,
@@ -578,9 +606,14 @@
             pltpu.VMEM((LANES, slot_groups * LANES), BF16),
             pltpu.VMEM((4 * parts, LANES), F32),
         ],
-        route(partials, (4, capacity)),
+        arrived,
         observed_data,
     )
+    medium, reply = lax.optimization_barrier((medium, reply))
+    (scaled,) = call_kernel(
+        medium_body, "scaled_medium", [shape((4 * depth, SPAN_X, SPAN_Y), F32)], [], medium
+    )
+    returned, scaled = lax.optimization_barrier((route(reply, (1, 3 * capacity)), scaled))
     loads, load_edges = call_kernel(
         load_body,
         "segment_loads",
@@ -590,7 +623,7 @@
             pltpu.VMEM((2, 1, RIM * LANES), F32),
             pltpu.VMEM((3 * slot_groups, LANES), F32),
         ],
-        route(reply, (1, 3 * capacity)),
+        returned,
         slot,
         row,
         segment_weight,
@@ -613,8 +646,8 @@
         load_higher,
         load_lower,
         load_rims,
-        strains,
-        medium,
+        factors,
+        scaled,
     )
     return (residuals, gradients.reshape(2, depth, rows_x, cols_y))
 

time: 63.2 us -> 62.4 us (0.987)
  blocking collectives: 20.9 us -> 0 us
  waiting for transfers between devices: 9.21 us -> 23.9 us
  starting transfers between devices: 19.7 us -> 26.8 us
  local copies, waits for them, and re-layouts: 3.67 us -> 0.04 us
  Pallas kernels: 8.32 us -> 10.4 us
    all_to_all x2 -> x0, blocking collectives: 20.9 us -> none  [exchange(): return lax.all_to_all(chunks, both, split_axis=0, concat_axis=0, tiled=True)]
    all_to_all x2 -> x4, waiting for transfers between devices: 0.01 us -> 14.7 us  [exchange(): return lax.all_to_all(chunks, both, split_axis=0, concat_axis=0, tiled=True)]
    all_to_all x2 -> x4, starting transfers between devices: 9.86 us -> 17 us  [exchange(): return lax.all_to_all(chunks, both, split_axis=0, concat_axis=0, tiled=True)]
    unnamed x22 -> x12, local copies, waits for them, and re-layouts: 3.67 us -> 0.04 us
    pallas_call x6 -> x8, Pallas kernels: 8.32 us -> 10.4 us  [call_kernel(): pl.pallas_call(body, name=name, out_shape=outs, in_specs=[pl.BlockSpec(me...]
  transfers between devices with their start and end apart: 6 -> 8, of which waited for: 4 -> 6; matrix products, arithmetic and copies ran while one was open for 0% -> 0% of each run, Pallas kernels for 1% -> 1%
where the time goes in v4:
time: 62.4 us; the launch traced here: 62 us
  starting transfers between devices  26.8 us (43%)
  waiting for transfers between devices  23.9 us (38%)
  Pallas kernels  10.4 us (17%)
  between operations  0.81 us (1%)
    all_to_all x4, starting transfers between devices, exchange(): return lax.all_to_all(chunks, both, split_axis=0, concat_axis=0, tiled=True)  17 us
    all_to_all x4, waiting for transfers between devices, exchange(): return lax.all_to_all(chunks, both, split_axis=0, concat_axis=0, tiled=True)  14.7 us
    pallas_call x8, Pallas kernels, call_kernel(): pl.pallas_call(body, name=name, out_shape=outs, in_specs=[pl.BlockSpec(me...  10.4 us
    ppermute x1, waiting for transfers between devices, shards(): load_higher = lax.ppermute(loads, 'gx', down)  4.25 us
    ppermute x1, waiting for transfers between devices, shards(): higher = lax.ppermute(fields, 'gx', down)  4.17 us
    ppermute x1, starting transfers between devices, shards(): lower = lax.ppermute(fields, 'gx', up)  3.68 us
    ppermute x1, starting transfers between devices, shards(): load_lower = lax.ppermute(loads, 'gx', up)  3.59 us
    ppermute x1, starting transfers between devices, shards(): higher = lax.ppermute(fields, 'gx', down)  1.29 us
  transfers between devices with their start and end apart: 8, of which 6 were waited for; matrix products, arithmetic and copies ran while one was open for 0% of the time, Pallas kernels for 1%

profile of v4, /device:TPU:0, one launch (start us, length us, event | category | flops | bytes accessed | tf_op | source)
XLA Modules:
  0.0 62.0 jit_solution(16634699550789555803)
XLA Ops:
  0.6 1.8 %pack_edges.1 = (f32[192,128]{1,0:T(8,128)}, f32[32,1,1024]{2,1,0:T(1,128)}) custom-call(f32[144,128]{1,0:T(8,128)} %bitcast.15, f32[16,128]{1,0:T(8,128)} %bitcast.17, f32[16,128]{1,0:T(8,128)} %bitcast.18, f32[16,128]{1,0:T(8,128)} %bitcast.19, s32[1,64]{1,0:T(1,128)} %bitcast.20, f32[3,64]{1,0:T(4,128)} %refs_5_.1), custom_call_target="tpu_custom_call" | custom-call | tf_op jit(solution)/shard_map/pack_edges/pallas_call | solution.py:23
  2.4 0.0 copy-start.4
  2.4 0.0 copy-start.5
  2.4 7.3 %all-to-all-start = ((f32[32,1,1024]{2,1,0:T(1,128)}), f32[32,1,1024]{2,1,0:T(1,128)S(1)}, u32[]{:S(2)}, u32[]{:S(2)}) async-start(f32[32,1,1024]{2,1,0:T(1,128)} %get-tuple-element.22), calls=%async_computation | async-start | bytes 262144 | tf_op jit(solution)/shard_map/all_to_all | solution.py:527
  9.8 0.0 copy-start.1
  9.8 3.7 %collective-permute-start.1 = (f32[192,128]{1,0:T(8,128)S(1)}, f32[192,128]{1,0:T(8,128)S(1)}, u32[]{:S(2)}, u32[]{:S(2)}) collective-permute-start(f32[192,128]{1,0:T(8,128)S(1)} %copy-done), channel_id=1, source_target_pairs={{0,8},{8,16},{16,24},{1,9},{9,17},{17,25},{2,10},{10,18},{18,26},{... | collective-permute-start | bytes 294920 | tf_op jit(solution)/shard_map/ppermute | solution.py:551
  13.5 1.3 %collective-permute-start = (f32[192,128]{1,0:T(8,128)S(1)}, f32[192,128]{1,0:T(8,128)S(1)}, u32[]{:S(2)}, u32[]{:S(2)}) collective-permute-start(f32[192,128]{1,0:T(8,128)S(1)} %copy-done), channel_id=1, source_target_pairs={{8,0},{16,8},{24,16},{9,1},{17,9},{25,17},{10,2},{18,10},{26,18},{... | collective-permute-start | bytes 294920 | tf_op jit(solution)/shard_map/ppermute | solution.py:552
  14.8 0.6 %segment_slots.1 = (s32[16,128]{1,0:T(8,128)S(1)}, s32[16,128]{1,0:T(8,128)S(1)}, bf16[128,2048]{1,0:T(8,128)(2,1)S(1)}, bf16[128,2048]{1,0:T(8,128)(2,1)S(1)}) custom-call(s32[16,128]{1,0:T(8,128)S(1)} %bitcast.13, s32[16,128]{1,0:T(8,128)S(1)} %bitcast.14), custom_call_target="tpu_custom_call" | custom-call | tf_op jit(solution)/shard_map/segment_slots/pallas_call | solution.py:23
  15.5 0.4 collective-permute-done.1.lower_ref
  15.8 4.2 %collective-permute-done.higher_ref = f32[192,128]{1,0:T(8,128)S(1)} collective-permute-done((f32[192,128]{1,0:T(8,128)S(1)}, f32[192,128]{1,0:T(8,128)S(1)}, u32[]{:S(2)}, u32[]{:S(2)}) %collective-permute-start) | collective-permute-done | bytes 98336 | tf_op jit(solution)/shard_map/ppermute | solution.py:552
  20.0 3.2 %forward_run.1 = (f32[128,128]{1,0:T(8,128)}, f32[288,128]{1,0:T(8,128)S(1)}, f32[12,16,256]{2,1,0:T(8,128)S(1)}) custom-call(f32[192,128]{1,0:T(8,128)S(1)} %copy-done, f32[192,128]{1,0:T(8,128)S(1)} %collective-permute-done.higher_ref, f32[192,128]{1,0:T(8,128)S(1)} %collective-permute-done.1.lower_ref, f32[32,1,1024]{2,1,0:T(1,128)S(1)} %all-to-all-done.recv_ref, ...), custom_call_target="tpu_custom_call" | custom-call | tf_op jit(solution)/shard_map/forward_run/pallas_call | solution.py:23
  23.2 4.6 %all-to-all-start.1 = ((f32[32,4,128]{2,1,0:T(4,128)}), f32[32,4,128]{2,1,0:T(4,128)S(1)}, u32[]{:S(2)}, u32[]{:S(2)}) async-start(f32[32,4,128]{2,1,0:T(4,128)} %bitcast.8), calls=%async_computation.1 | async-start | bytes 131072 | tf_op jit(solution)/shard_map/all_to_all | solution.py:527
  27.8 0.0 copy-start.2
  27.8 7.4 %all-to-all-done.1 = f32[32,4,128]{2,1,0:T(4,128)S(1)} async-done(((f32[32,4,128]{2,1,0:T(4,128)}), f32[32,4,128]{2,1,0:T(4,128)S(1)}, u32[]{:S(2)}, u32[]{:S(2)}) %all-to-all-start.1) | async-done | bytes 65568 | tf_op jit(solution)/shard_map/all_to_all | solution.py:527
  35.2 2.0 %channel_sums.1 = (f32[3,1024]{1,0:T(4,128)}, f32[32,1,384]{2,1,0:T(1,128)}) custom-call(f32[128,128]{1,0:T(8,128)S(1)} %bitcast.11, f32[3,1024]{1,0:T(4,128)S(1)} %copy-done.2), custom_call_target="tpu_custom_call" | custom-call | tf_op jit(solution)/shard_map/channel_sums/pallas_call | solution.py:23
  37.3 2.5 %all-to-all-start.2 = ((f32[32,1,384]{2,1,0:T(1,128)}), f32[32,1,384]{2,1,0:T(1,128)S(1)}, u32[]{:S(2)}, u32[]{:S(2)}) async-start(f32[32,1,384]{2,1,0:T(1,128)} %get-tuple-element.33), calls=%async_computation.2 | async-start | bytes 98304 | tf_op jit(solution)/shard_map/all_to_all | solution.py:527
  39.8 7.3 %all-to-all-done.2.arrived_ref = f32[32,1,384]{2,1,0:T(1,128)S(1)} async-done(((f32[32,1,384]{2,1,0:T(1,128)}), f32[32,1,384]{2,1,0:T(1,128)S(1)}, u32[]{:S(2)}, u32[]{:S(2)}) %all-to-all-start.2) | async-done | bytes 49184 | tf_op jit(solution)/shard_map/all_to_all | solution.py:527
  47.1 1.4 %segment_loads.1 = (f32[96,128]{1,0:T(8,128)S(1)}, f32[32,1,384]{2,1,0:T(1,128)}) custom-call(f32[32,1,384]{2,1,0:T(1,128)S(1)} %all-to-all-done.2.arrived_ref, s32[16,128]{1,0:T(8,128)S(1)} %get-tuple-element.23.slot_ref, s32[16,128]{1,0:T(8,128)S(1)} %get-tuple-element.24.row_ref, f32[2,2048]{1,0:T(2,128)S(1)} %copy-done.1, ...), custom_call_target="tpu_custom_call" | custom-call | tf_op jit(solution)/shard_map/segment_loads/pallas_call | solution.py:23
  48.6 2.5 %all-to-all-start.3 = ((f32[32,1,384]{2,1,0:T(1,128)}), f32[32,1,384]{2,1,0:T(1,128)S(1)}, u32[]{:S(2)}, u32[]{:S(2)}) async-start(f32[32,1,384]{2,1,0:T(1,128)} %get-tuple-element.37), calls=%async_computation.3 | async-start | bytes 98304 | tf_op jit(solution)/shard_map/all_to_all | solution.py:527
  51.1 3.6 %collective-permute-start.3 = (f32[96,128]{1,0:T(8,128)S(1)}, f32[96,128]{1,0:T(8,128)S(1)}, u32[]{:S(2)}, u32[]{:S(2)}) collective-permute-start(f32[96,128]{1,0:T(8,128)S(1)} %get-tuple-element.36.load_ref), channel_id=1, source_target_pairs={{0,8},{8,16},{16,24},{1,9},{9,17},{17,25},{2,10},{10,18},{18,26},{... | collective-permute-start | bytes 147464 | tf_op jit(solution)/shard_map/ppermute | solution.py:633
  54.7 1.3 %collective-permute-start.2 = (f32[96,128]{1,0:T(8,128)S(1)}, f32[96,128]{1,0:T(8,128)S(1)}, u32[]{:S(2)}, u32[]{:S(2)}) collective-permute-start(f32[96,128]{1,0:T(8,128)S(1)} %get-tuple-element.36.load_ref), channel_id=1, source_target_pairs={{8,0},{16,8},{24,16},{9,1},{17,9},{25,17},{10,2},{18,10},{26,18},{... | collective-permute-start | bytes 147464 | tf_op jit(solution)/shard_map/ppermute | solution.py:634
  56.0 0.4 collective-permute-done.3.lower_ref
  56.4 4.3 %collective-permute-done.2.higher_ref = f32[96,128]{1,0:T(8,128)S(1)} collective-permute-done((f32[96,128]{1,0:T(8,128)S(1)}, f32[96,128]{1,0:T(8,128)S(1)}, u32[]{:S(2)}, u32[]{:S(2)}) %collective-permute-start.2) | collective-permute-done | bytes 49184 | tf_op jit(solution)/shard_map/ppermute | solution.py:634
  60.7 1.3 %adjoint_run.1 = f32[32,128]{1,0:T(8,128)} custom-call(f32[96,128]{1,0:T(8,128)S(1)} %get-tuple-element.36.load_ref, f32[96,128]{1,0:T(8,128)S(1)} %collective-permute-done.2.higher_ref, f32[96,128]{1,0:T(8,128)S(1)} %collective-permute-done.3.lower_ref, f32[32,1,384]{2,1,0:T(1,128)S(1)} %all-to-all-done.3.recv_ref, ...), custom_call_target="tpu_custom_call" | custom-call | tf_op jit(solution)/shard_map/adjoint_run/pallas_call | solution.py:23
  (12 shorter events, 0.1 us)
Async XLA Ops:
  2.4 7.4 %copy-start = (f32[192,128]{1,0:T(8,128)S(1)}, f32[192,128]{1,0:T(8,128)}, u32[]{:S(2)}) copy-start(f32[192,128]{1,0:T(8,128)} %get-tuple-element.21.fields_ref) | copy-start | bytes 294916
  2.4 12.3 %copy-start.4 = (s32[2048,1]{0,1:T(1,128)S(1)}, s32[2048,1]{0,1:T(1,128)}, u32[]{:S(2)}) copy-start(s32[2048,1]{0,1:T(1,128)} %param.19) | copy-start | bytes 24580
  2.4 12.3 %copy-start.5 = (s32[2048]{0:T(1024)S(1)}, s32[2048]{0:T(1024)}, u32[]{:S(2)}) copy-start(s32[2048]{0:T(1024)} %param.17) | copy-start | bytes 24580
  2.4 17.5 %all-to-all-start = ((f32[32,1,1024]{2,1,0:T(1,128)}), f32[32,1,1024]{2,1,0:T(1,128)S(1)}, u32[]{:S(2)}, u32[]{:S(2)}) async-start(f32[32,1,1024]{2,1,0:T(1,128)} %get-tuple-element.22), calls=%async_computation | async-start | bytes 262144 | tf_op jit(solution)/shard_map/all_to_all | solution.py:527
  9.8 10.2 %copy-start.1 = (f32[2,2048]{1,0:T(2,128)S(1)}, f32[2,2048]{1,0:T(2,128)}, u32[]{:S(2)}) copy-start(f32[2,2048]{1,0:T(2,128)} %weight_ref.3) | copy-start | bytes 49156
  9.8 6.0 %collective-permute-start.1 = (f32[192,128]{1,0:T(8,128)S(1)}, f32[192,128]{1,0:T(8,128)S(1)}, u32[]{:S(2)}, u32[]{:S(2)}) collective-permute-start(f32[192,128]{1,0:T(8,128)S(1)} %copy-done), channel_id=1, source_target_pairs={{0,8},{8,16},{16,24},{1,9},{9,17},{17,25},{2,10},{10,18},{18,26},{... | collective-permute-start | bytes 294920 | tf_op jit(solution)/shard_map/ppermute | solution.py:551
  13.5 6.5 %collective-permute-start = (f32[192,128]{1,0:T(8,128)S(1)}, f32[192,128]{1,0:T(8,128)S(1)}, u32[]{:S(2)}, u32[]{:S(2)}) collective-permute-start(f32[192,128]{1,0:T(8,128)S(1)} %copy-done), channel_id=1, source_target_pairs={{8,0},{16,8},{24,16},{9,1},{17,9},{25,17},{10,2},{18,10},{26,18},{... | collective-permute-start | bytes 294920 | tf_op jit(solution)/shard_map/ppermute | solution.py:552
  15.4 4.5 %copy-start.3 = (s32[2048]{0:T(1024)S(1)}, s32[2048]{0:T(1024)}, u32[]{:S(2)}) copy-start(s32[2048]{0:T(1024)} %param.20) | copy-start | bytes 24580
  23.2 12.0 %all-to-all-start.1 = ((f32[32,4,128]{2,1,0:T(4,128)}), f32[32,4,128]{2,1,0:T(4,128)S(1)}, u32[]{:S(2)}, u32[]{:S(2)}) async-start(f32[32,4,128]{2,1,0:T(4,128)} %bitcast.8), calls=%async_computation.1 | async-start | bytes 131072 | tf_op jit(solution)/shard_map/all_to_all | solution.py:527
  27.8 7.4 %copy-start.2 = (f32[3,1024]{1,0:T(4,128)S(1)}, f32[3,1024]{1,0:T(4,128)}, u32[]{:S(2)}) copy-start(f32[3,1024]{1,0:T(4,128)} %observed_ref.1) | copy-start | bytes 36868
  37.3 9.9 %all-to-all-start.2 = ((f32[32,1,384]{2,1,0:T(1,128)}), f32[32,1,384]{2,1,0:T(1,128)S(1)}, u32[]{:S(2)}, u32[]{:S(2)}) async-start(f32[32,1,384]{2,1,0:T(1,128)} %get-tuple-element.33), calls=%async_computation.2 | async-start | bytes 98304 | tf_op jit(solution)/shard_map/all_to_all | solution.py:527
  48.6 12.1 %all-to-all-start.3 = ((f32[32,1,384]{2,1,0:T(1,128)}), f32[32,1,384]{2,1,0:T(1,128)S(1)}, u32[]{:S(2)}, u32[]{:S(2)}) async-start(f32[32,1,384]{2,1,0:T(1,128)} %get-tuple-element.37), calls=%async_computation.3 | async-start | bytes 98304 | tf_op jit(solution)/shard_map/all_to_all | solution.py:527
  51.1 5.3 %collective-permute-start.3 = (f32[96,128]{1,0:T(8,128)S(1)}, f32[96,128]{1,0:T(8,128)S(1)}, u32[]{:S(2)}, u32[]{:S(2)}) collective-permute-start(f32[96,128]{1,0:T(8,128)S(1)} %get-tuple-element.36.load_ref), channel_id=1, source_target_pairs={{0,8},{8,16},{16,24},{1,9},{9,17},{17,25},{2,10},{10,18},{18,26},{... | collective-permute-start | bytes 147464 | tf_op jit(solution)/shard_map/ppermute | solution.py:633
  54.7 6.0 %collective-permute-start.2 = (f32[96,128]{1,0:T(8,128)S(1)}, f32[96,128]{1,0:T(8,128)S(1)}, u32[]{:S(2)}, u32[]{:S(2)}) collective-permute-start(f32[96,128]{1,0:T(8,128)S(1)} %get-tuple-element.36.load_ref), channel_id=1, source_target_pairs={{8,0},{16,8},{24,16},{9,1},{17,9},{25,17},{10,2},{18,10},{26,18},{... | collective-permute-start | bytes 147464 | tf_op jit(solution)/shard_map/ppermute | solution.py:634

commit v5 on v3

v5 whole, which is shorter than its diff:
```python
import functools

import jax
import jax.numpy as jnp
from jax import lax
from jax.experimental import pallas as pl
from jax.experimental.pallas import tpu as pltpu
from jax.sharding import PartitionSpec as P

GAUGE = 8
STEP = 0.25
RIM = 3
LANES = 128
TILE_X = 4
SPAN_X = 16
SPAN_NEAR = 8
SPAN_Y = 256
F32, BF16, I32 = jnp.float32, jnp.bfloat16, jnp.int32
NEAR = tuple((dx, dy) for dx in (-1, 0, 1) for dy in (-1, 0, 1))


def call_kernel(body, name, outs, scratch, *args, place=pltpu.VMEM, room=24 * 1024 * 1024):
    whole = pl.BlockSpec(memory_space=pltpu.VMEM)
    return pl.pallas_call(
        body,
        name=name,
        out_shape=outs,
        in_specs=[pl.BlockSpec(memory_space=place)] * len(args),
        out_specs=[whole] * len(outs),
        scratch_shapes=scratch,
        compiler_params=pltpu.CompilerParams(vmem_limit_bytes=room),
    )(*args)


def pieces(values):
    high = values.astype(BF16).astype(F32)
    rest = values - high
    middle = rest.astype(BF16).astype(F32)
    return high, middle, rest - middle


def iota(shape, dim):
    return lax.broadcasted_iota(I32, shape, dim)


def times(left, right):
    return lax.dot_general(left, right, (((1,), (0,)), ((), ())), preferred_element_type=F32)


def times_turned(left, right):
    return lax.dot_general(left, right, (((1,), (1,)), ((), ())), preferred_element_type=F32)


def two_pieces(values):
    high = values.astype(BF16).astype(F32)
    return high, values - high


def sum_halves(values):
    half = values.shape[0] // 2
    return values[:half] + values[half:]


def sum_thirds(values):
    third = values.shape[0] // 3
    return values[:third] + values[third : 2 * third] + values[2 * third :]


def neighbour(dx, dy):
    count_x, count_y = lax.axis_size("gx"), lax.axis_size("gy")
    at_x, at_y = lax.axis_index("gx") + dx, lax.axis_index("gy") + dy
    inside = (at_x >= 0) & (at_x < count_x) & (at_y >= 0) & (at_y < count_y)
    return jnp.where(inside, at_x * count_y + at_y, 0), inside


def edge_columns(rows, side_ref):
    width = rows.shape[0]
    turned = rows.T
    for side, base in ((0, 0), (1, LANES - RIM)):
        for column in range(RIM):
            side_ref[side, 0:1, column * width : (column + 1) * width] = turned[base + column : base + column + 1, :]


def send_sides(side_ref, out_ref, places):
    for dx, dy in places:
        index, inside = neighbour(dx, dy)

        @pl.when(inside)
        def _(index=index, dy=dy):
            out_ref[index] = side_ref[1 if dy > 0 else 0]


def arrived_chunk(recv_ref, dx, dy):
    index, inside = neighbour(dx, dy)
    return jnp.where(inside, recv_ref[index], 0.0)


def rim_rows(recv_ref, dx, turn_ref):
    width = turn_ref.shape[1]
    for dy, base in ((1, 0), (-1, LANES - RIM)):
        chunk = arrived_chunk(recv_ref, dx, dy)
        for column in range(RIM):
            turn_ref[base + column : base + column + 1, :] = chunk[:, column * width : (column + 1) * width]
    return turn_ref[...].T


def lay_planes(wide_ref, narrow_ref, lane, centre, higher, lower):
    row = iota((8, LANES), 0)
    wide = wide_ref.shape[0]
    lanes = slice(lane, lane + LANES)
    for plane in range(wide + narrow_ref.shape[0]):
        rows = slice(8 * (plane // 2), 8 * (plane // 2) + 8)
        mid, high, low = centre[rows], higher[rows], lower[rows]
        if plane % 2:
            mid = pltpu.roll(mid, TILE_X, 0)
        else:
            high, low = pltpu.roll(high, TILE_X, 0), pltpu.roll(low, TILE_X, 0)
        near = jnp.where(row < TILE_X, mid, high)
        if plane < wide:
            wide_ref[plane, 0:8, lanes] = near
            wide_ref[plane, 8:16, lanes] = jnp.where(row < TILE_X, 0.0, low)
        else:
            narrow_ref[plane - wide, :, lanes] = jnp.where(row < SPAN_NEAR - 2, near, low)


def narrowed(plane):
    row = iota((SPAN_NEAR, plane.shape[1]), 0)
    return jnp.where(row < SPAN_NEAR - 2, plane[:SPAN_NEAR], plane[SPAN_NEAR:])


def ahead_x(plane):
    return pltpu.roll(plane, plane.shape[0] - 1, 0) - plane


def behind_x(plane):
    return plane - pltpu.roll(plane, 1, 0)


def ahead_y(plane):
    return pltpu.roll(plane, SPAN_Y - 1, 1) - plane


def behind_y(plane):
    return plane - pltpu.roll(plane, 1, 1)


def ahead_z(planes, z):
    return planes[z + 1] - planes[z] if z + 1 < len(planes) else -planes[z]


def behind_z(planes, z):
    return planes[z] - planes[z - 1] if z else planes[z]


class Planes:
    def __init__(self, ref, first, depth):
        self.ref, self.first, self.depth = ref, first, depth

    def __len__(self):
        return self.depth

    def __getitem__(self, z):
        return self.ref[self.first + z]

    def __setitem__(self, z, plane):
        self.ref[self.first + z] = plane


def fields_of(ref, count, depth, first=0):
    return [Planes(ref, (first + number) * depth, depth) for number in range(count)]


def strain_rates(velocity, z):
    along_x, along_y, along_z = [field[z] for field in velocity]
    return (
        behind_x(along_x),
        behind_y(along_y),
        behind_z(velocity[2], z),
        ahead_y(along_x) + ahead_x(along_y),
        ahead_z(velocity[0], z) + ahead_x(along_z),
        ahead_z(velocity[1], z) + ahead_y(along_z),
    )


def new_stress(stress, strains, lame_lambda, shear_modulus, z):
    dilated = lame_lambda[z] * (strains[0] + strains[1] + strains[2])
    shear = shear_modulus[z]
    normal = [stress[n][z] + STEP * (dilated + 2.0 * shear * strains[n]) for n in range(3)]
    return normal + [stress[n][z] + STEP * shear * strains[n] for n in range(3, 6)]


def advance(state, medium, emit, target):
    velocity, stress = state[:3], state[3:]
    lame_lambda, shear_modulus, buoyancy = medium
    depth = len(buoyancy)
    wide = target is not None and target is not state
    for z in range(depth):
        scale = STEP * buoyancy[z]
        accel = (
            ahead_x(stress[0][z]) + behind_y(stress[3][z]) + behind_z(stress[4], z),
            behind_x(stress[3][z]) + ahead_y(stress[1][z]) + behind_z(stress[5], z),
            behind_x(stress[4][z]) + behind_y(stress[5][z]) + ahead_z(stress[2], z),
        )
        for number in range(3):
            moved = velocity[number][z] + scale * accel[number]
            velocity[number][z] = moved
            if wide:
                target[number][z] = narrowed(moved)
    for z in range(depth):
        strains = strain_rates(velocity, z)
        emit(z, strains)
        if target is not None:
            for number, plane in enumerate(new_stress(stress, strains, lame_lambda, shear_modulus, z)):
                target[3 + number][z] = narrowed(plane) if wide else plane


def pack_body(*refs):
    inputs, (fields_ref, out_ref, side_ref, cells_ref, wavelet_ref, arrived) = refs[:6], refs[6:]
    targets, at = [], 0
    for source in inputs[:4]:
        targets.append(fields_ref.at[at : at + source.shape[0]])
        at = at + source.shape[0]
    copies = [
        pltpu.make_async_copy(source, target, arrived.at[number])
        for number, (source, target) in enumerate(zip(inputs, targets + [cells_ref, wavelet_ref]))
    ]
    for copy in copies:
        copy.start()
    copies[4].wait()
    copies[5].wait()
    cells_row = inputs[1].shape[0]
    cells = cells_ref[...]
    count = cells.shape[1]
    at_lane = iota((LANES, count), 0) == (cells & (LANES - 1))
    at_row = iota((cells_row, count), 0) == (cells >> (LANES.bit_length() - 1))
    stack = [
        jnp.where(at_row, third[step : step + 1, :], 0.0) for third in pieces(wavelet_ref[...]) for step in range(3)
    ]
    maps = sum_thirds(
        times_turned(jnp.concatenate(stack, axis=0).astype(BF16), jnp.where(at_lane, 1.0, 0.0).astype(BF16))
    )
    for copy in copies[:4]:
        copy.wait()
    fields_ref[at:, :] = maps[cells_row:]
    for number in range(3, 6):
        rows = slice(number * cells_row, (number + 1) * cells_row)
        fields_ref[rows, :] = fields_ref[rows, :] + maps[:cells_row]
    rows = fields_ref[...]
    spare = 2 * LANES - rows.shape[0]
    edge_columns(jnp.concatenate([rows, jnp.zeros((spare, LANES), F32)], axis=0), side_ref)
    send_sides(side_ref, out_ref, [(dx, dy) for dx, dy in NEAR if dy])


def slots_body(capacity, devices, cols_y, owner_ref, start_ref, slot_ref, row_ref, cover_ref, place_ref, rank_ref):
    blocks = owner_ref.shape[0]
    group = 32
    before = jnp.where(iota((LANES, 2 * LANES), 0) < iota((LANES, 2 * LANES), 1), 1.0, 0.0).astype(BF16)
    rank_ref[...] = jnp.zeros_like(rank_ref)

    def count_group(number, carry):
        names = iota((group, LANES), 0) + number * group
        hot = [names == owner_ref[b : b + 1, :] for b in range(blocks)]
        marks = jnp.concatenate([jnp.where(h, 1.0, 0.0) for h in hot], axis=0).astype(BF16)
        counts = times(marks, before)
        total = jnp.zeros((group, LANES), F32)
        for b in range(blocks):
            part = counts[b * group : (b + 1) * group]
            rank_ref[b : b + 1, :] = rank_ref[b : b + 1, :] + jnp.sum(
                jnp.where(hot[b], part[:, :LANES] + total, 0.0), axis=0, keepdims=True
            )
            total = total + part[:, LANES:]
        return carry

    if devices == group:
        count_group(0, 0)
    else:
        lax.fori_loop(0, devices // group, count_group, 0)
    slot = owner_ref[...] * capacity + rank_ref[...].astype(I32)
    slot_ref[...] = slot >> 7
    low = slot & (LANES - 1)
    span = cols_y - GAUGE + 1
    start = start_ref[...]
    row = ((start.astype(F32) + 0.5) * (1.0 / span)).astype(I32)
    row_ref[...] = row
    first = start - row * span
    down = iota((LANES, LANES), 0)
    for b in range(blocks):
        lanes = slice(b * LANES, (b + 1) * LANES)
        offset = down - first[b : b + 1, :]
        cover_ref[:, lanes] = jnp.where((offset >= 0) & (offset < GAUGE), 1.0, 0.0).astype(BF16)
        place_ref[:, lanes] = jnp.where(down == low[b : b + 1, :], 1.0, 0.0).astype(BF16)


def forward_body(
    fields_ref,
    higher_ref,
    lower_ref,
    recv_ref,
    slot_ref,
    row_ref,
    weight_ref,
    channel_ref,
    cover_ref,
    place_ref,
    out_ref,
    strain_ref,
    medium_ref,
    wide_ref,
    source_ref,
    state_ref,
    near_ref,
    turn_ref,
    spread_ref,
):
    depth = medium_ref.shape[0] // 3
    cells_row = depth * TILE_X
    turn_ref[...] = jnp.zeros_like(turn_ref)
    rims = [rim_rows(recv_ref, dx, turn_ref) for dx in (0, 1, -1)]
    lay_planes(wide_ref, source_ref, 0, fields_ref, higher_ref, lower_ref)
    lay_planes(wide_ref, source_ref, LANES, *rims)
    first = 9 * depth
    medium_ref[...] = wide_ref[first:]
    for plane in range(3 * depth):
        near_ref[plane] = narrowed(wide_ref[first + plane])
    state, near = fields_of(state_ref, 9, depth), fields_of(near_ref, 3, depth)
    for step in range(3):

        def emit(z, strains, step=step):
            for number, strain in enumerate(strains):
                base = ((step * 6 + number) * depth + z) * TILE_X
                strain_ref[base : base + TILE_X, :] = strain[0:TILE_X, 0:LANES]

        if step == 0:
            advance(fields_of(wide_ref, 9, depth), fields_of(wide_ref, 3, depth, 9), emit, state)
            continue
        for z in range(depth):
            load = source_ref[(step - 1) * depth + z]
            for number in range(3, 6):
                state[number][z] = state[number][z] + load
        advance(state, near, emit, state if step == 1 else None)
    axial = jnp.concatenate(
        [strain_ref[step * 6 * cells_row : (step * 6 + 2) * cells_row, :] for step in range(3)], axis=0
    )
    axial = jnp.concatenate(pieces(axial), axis=0).astype(BF16)
    rows_down = iota((cells_row, LANES), 0)
    slots_down = iota((LANES, LANES), 0) >> 2
    for block in range(slot_ref.shape[0]):
        lanes = slice(block * LANES, (block + 1) * LANES)
        if block % 2 == 0:
            both = sum_thirds(times(axial, cover_ref[:, block * LANES : (block + 2) * LANES]))
        windows = both[:, :LANES] if block % 2 == 0 else both[:, LANES:]
        at_row = rows_down == row_ref[block : block + 1, :]
        weight_x, weight_y = weight_ref[0:1, lanes], weight_ref[1:2, lanes]
        sums = []
        for step in range(3):
            base = 2 * step * cells_row
            axial_sum = (
                weight_x * windows[base : base + cells_row]
                + weight_y * windows[base + cells_row : base + 2 * cells_row]
            )
            sums.append(jnp.sum(jnp.where(at_row, axial_sum, 0.0), axis=0, keepdims=True))
        sums.append(channel_ref[block : block + 1, :].astype(F32))
        values = jnp.concatenate(sums + sums, axis=0)
        in_slot = slots_down == slot_ref[block : block + 1, :]
        for third, piece in enumerate(pieces(values)):
            spread_ref[third * LANES : (third + 1) * LANES, lanes] = jnp.where(
                in_slot, jnp.concatenate([piece] * (LANES // 8), axis=0), 0.0
            ).astype(BF16)
    out_ref[...] = sum_thirds(times_turned(spread_ref[...], place_ref[...]))


def owner_body(arrived_ref, observed_ref, residual_ref, reply_ref, values_ref, place_ref, held_ref):
    groups = arrived_ref.shape[0] // 4
    parts = observed_ref.shape[1] // LANES
    down = iota((LANES, LANES), 0)
    part_down = iota((parts, LANES), 0)
    nothing = jnp.zeros((parts, LANES), F32)
    numbers = [arrived_ref[4 * s + 3 : 4 * s + 4, :].astype(I32) for s in range(groups)]
    for s in range(groups):
        lanes = slice(s * LANES, (s + 1) * LANES)
        place_ref[:, lanes] = jnp.where(down == (numbers[s] & (LANES - 1)), 1.0, 0.0).astype(BF16)
        at_part = part_down == (numbers[s] >> 7)
        thirds = pieces(arrived_ref[4 * s : 4 * s + 3, :])
        stack = []
        for third in thirds:
            for step in range(3):
                stack.append(jnp.where(at_part, third[step : step + 1, :], 0.0))
            stack.append(nothing)
        values_ref[:, lanes] = jnp.concatenate(stack, axis=0).astype(BF16)
    sums = sum_thirds(times_turned(values_ref[...], place_ref[...]))
    for step in range(3):
        for part in range(parts):
            at = step * parts + part
            held_ref[at : at + 1, :] = observed_ref[step : step + 1, part * LANES : (part + 1) * LANES]
    held_ref[3 * parts :, :] = nothing
    held_ref[...] = sums - held_ref[...]
    for step in range(3):
        for part in range(parts):
            at = step * parts + part
            residual_ref[step : step + 1, part * LANES : (part + 1) * LANES] = held_ref[at : at + 1, :]
    residual = jnp.concatenate(two_pieces(held_ref[...]), axis=0).astype(BF16)
    for s in range(groups):
        if s % 2 == 0:
            both = sum_halves(times(residual, place_ref[:, s * LANES : (s + 2) * LANES]))
        found = both[:, :LANES] if s % 2 == 0 else both[:, LANES:]
        at_part = part_down == (numbers[s] >> 7)
        for step in range(3):
            reply_ref[4 * s + step : 4 * s + step + 1, :] = jnp.sum(
                jnp.where(at_part, found[step * parts : (step + 1) * parts], 0.0), axis=0, keepdims=True
            )
        reply_ref[4 * s + 3 : 4 * s + 4, :] = jnp.zeros((1, LANES), F32)


def load_body(
    arrived_ref,
    slot_ref,
    row_ref,
    weight_ref,
    cover_ref,
    place_ref,
    load_ref,
    out_ref,
    spread_ref,
    side_ref,
):
    cells_row = load_ref.shape[0] // 6
    stack_rows = load_ref.shape[0]
    arrived = jnp.concatenate(two_pieces(arrived_ref[...]), axis=0).astype(BF16)
    slots_down = iota((LANES, LANES), 0) >> 2
    rows_down = iota((cells_row, LANES), 0)
    for block in range(slot_ref.shape[0]):
        lanes = slice(block * LANES, (block + 1) * LANES)
        if block % 2 == 0:
            both = sum_halves(times(arrived, place_ref[:, block * LANES : (block + 2) * LANES]))
        found = both[:, :LANES] if block % 2 == 0 else both[:, LANES:]
        found = jnp.where(slots_down == slot_ref[block : block + 1, :], found, 0.0)
        folded = found[0:8]
        for part in range(1, LANES // 8):
            folded = folded + found[8 * part : 8 * part + 8]
        folded = folded + pltpu.roll(folded, 4, 0)
        at_row = rows_down == row_ref[block : block + 1, :]
        for turn in range(3):
            back = folded[2 - turn : 3 - turn, :]
            for part in range(2):
                for half, piece in enumerate(two_pieces(weight_ref[part : part + 1, lanes] * back)):
                    base = half * stack_rows + (2 * turn + part) * cells_row
                    spread_ref[base : base + cells_row, lanes] = jnp.where(at_row, piece, 0.0).astype(BF16)
    load = sum_halves(times_turned(spread_ref[...], cover_ref[...]))
    load_ref[...] = load
    spare = LANES - stack_rows
    edge_columns(jnp.concatenate([load, jnp.zeros((spare, LANES), F32)], axis=0), side_ref)
    send_sides(side_ref, out_ref, [(dx, dy) for dx, dy in NEAR if dy])


def adjoint_body(
    load_ref,
    higher_ref,
    lower_ref,
    recv_ref,
    strain_ref,
    medium_ref,
    gradient_ref,
    first_ref,
    later_ref,
    velocity_ref,
    state_ref,
    near_ref,
    turn_ref,
):
    depth = medium_ref.shape[0] // 3
    turn_ref[...] = jnp.zeros_like(turn_ref)
    rims = [rim_rows(recv_ref, dx, turn_ref) for dx in (0, 1, -1)]
    lay_planes(first_ref, later_ref, 0, load_ref, higher_ref, lower_ref)
    lay_planes(first_ref, later_ref, LANES, *rims)
    for plane in range(3 * depth):
        near_ref[plane] = narrowed(medium_ref[plane])
    gradient_ref[...] = jnp.zeros_like(gradient_ref)
    state, near, medium = (
        fields_of(state_ref, 9, depth),
        fields_of(near_ref, 3, depth),
        fields_of(medium_ref, 3, depth),
    )

    def add_terms(turn, z, strains):
        dilation, dilation_back, doubled, product = None, None, None, None
        for number, strain in enumerate(strains):
            base = (((2 - turn) * 6 + number) * depth + z) * TILE_X
            forward = strain_ref[base : base + TILE_X, :]
            if number < 3:
                dilation = forward if dilation is None else dilation + forward
            if strain is None:
                continue
            back = strain[0:TILE_X, 0:LANES]
            term = forward * back
            if number < 3:
                dilation_back = back if dilation_back is None else dilation_back + back
                doubled = term if doubled is None else doubled + term
            else:
                product = term if product is None else product + term
        for part, term in enumerate((dilation * dilation_back, 2.0 * doubled + product)):
            base = (part * depth + z) * TILE_X
            gradient_ref[base : base + TILE_X, :] = gradient_ref[base : base + TILE_X, :] + term

    loads, velocity = fields_of(first_ref, 2, depth), fields_of(velocity_ref, 2, depth)
    for z in range(depth):
        scale = STEP * medium[2][z]
        velocity[0][z] = scale * ahead_x(loads[0][z])
        velocity[1][z] = scale * ahead_y(loads[1][z])
        state[0][z] = narrowed(velocity[0][z])
        state[1][z] = narrowed(velocity[1][z])
        state[2][z] = jnp.zeros((SPAN_NEAR, SPAN_Y), F32)
    for z in range(depth):
        along_x, along_y = velocity[0][z], velocity[1][z]
        strain_x, strain_y = behind_x(along_x), behind_y(along_y)
        sheared = (
            ahead_y(along_x) + ahead_x(along_y),
            ahead_z(velocity[0], z),
            ahead_z(velocity[1], z),
        )
        add_terms(0, z, (strain_x, strain_y, None) + sheared)
        dilated = medium[0][z] * (strain_x + strain_y)
        shear = medium[1][z]
        state[3][z] = narrowed(loads[0][z] + STEP * (dilated + 2.0 * shear * strain_x))
        state[4][z] = narrowed(loads[1][z] + STEP * (dilated + 2.0 * shear * strain_y))
        state[5][z] = narrowed(STEP * dilated)
        for number, strain in enumerate(sheared):
            state[6 + number][z] = narrowed(STEP * shear * strain)
    for turn in (1, 2):
        for part in range(2):
            for z in range(depth):
                load = later_ref[(2 * (turn - 1) + part) * depth + z]
                state[3 + part][z] = state[3 + part][z] + load
        advance(state, near, functools.partial(add_terms, turn), state if turn == 1 else None)


def shards(
    initial_state,
    lame_lambda,
    shear_modulus,
    buoyancy,
    source_cells,
    source_wavelet,
    segment_start,
    segment_weight,
    partial_owner,
    partial_channel,
    observed_data,
):
    depth, rows_x, cols_y = lame_lambda.shape
    part_count = segment_start.shape[0]
    count_x, count_y = lax.axis_size("gx"), lax.axis_size("gy")
    devices = count_x * count_y
    capacity = max(2, 2 * part_count // devices)
    slot_groups = devices * capacity // LANES
    blocks = part_count // LANES
    per_group = LANES // capacity
    cells_row = depth * rows_x
    both = ("gx", "gy")
    up = [(i, i + 1) for i in range(count_x - 1)]
    down = [(j, i) for i, j in up]
    shape = jax.ShapeDtypeStruct

    def exchange(chunks):
        return lax.all_to_all(chunks, both, split_axis=0, concat_axis=0, tiled=True)

    def to_owners(rows):
        chunks = rows.reshape(slot_groups, 4, per_group, capacity).transpose(0, 2, 1, 3)
        back = exchange(chunks.reshape(devices, 4, capacity)).reshape(slot_groups, per_group, 4, capacity)
        return back.transpose(0, 2, 1, 3).reshape(slot_groups * 4, LANES)

    fields, edges = call_kernel(
        pack_body,
        "pack_edges",
        [shape((14 * cells_row, cols_y), F32), shape((devices, 1, 2 * RIM * LANES), F32)],
        [
            pltpu.VMEM((2, 1, 2 * RIM * LANES), F32),
            pltpu.VMEM((1, source_cells.shape[0]), I32),
            pltpu.VMEM(source_wavelet.shape, F32),
            pltpu.SemaphoreType.DMA((6,)),
        ],
        *[values.reshape(-1, cols_y) for values in (initial_state, lame_lambda, shear_modulus, buoyancy)],
        source_cells.reshape(1, -1),
        source_wavelet,
        place=pl.ANY,
        room=60 * 1024 * 1024,
    )
    lower = lax.ppermute(fields, "gx", up)
    higher = lax.ppermute(fields, "gx", down)
    rims = exchange(edges)
    channels = partial_channel.reshape(blocks, LANES)
    slot, row, cover, place = call_kernel(
        functools.partial(slots_body, capacity, devices, cols_y),
        "segment_slots",
        [
            shape((blocks, LANES), I32),
            shape((blocks, LANES), I32),
            shape((cols_y, part_count), BF16),
            shape((LANES, part_count), BF16),
        ],
        [pltpu.VMEM((blocks, LANES), F32)],
        partial_owner.reshape(blocks, LANES),
        segment_start.reshape(blocks, LANES),
    )
    partials, strains, medium = call_kernel(
        forward_body,
        "forward_run",
        [
            shape((slot_groups * 4, LANES), F32),
            shape((18 * cells_row, cols_y), F32),
            shape((3 * depth, SPAN_X, SPAN_Y), F32),
        ],
        [
            pltpu.VMEM((12 * depth, SPAN_X, SPAN_Y), F32),
            pltpu.VMEM((2 * depth, SPAN_NEAR, SPAN_Y), F32),
            pltpu.VMEM((9 * depth, SPAN_NEAR, SPAN_Y), F32),
            pltpu.VMEM((3 * depth, SPAN_NEAR, SPAN_Y), F32),
            pltpu.VMEM((LANES, 2 * LANES), F32),
            pltpu.VMEM((3 * LANES, part_count), BF16),
        ],
        fields,
        higher,
        lower,
        rims,
        slot,
        row,
        segment_weight,
        channels,
        cover,
        place,
    )
    parts = observed_data.shape[1] // LANES
    residuals, reply = call_kernel(
        owner_body,
        "channel_sums",
        [shape(observed_data.shape, F32), shape((slot_groups * 4, LANES), F32)],
        [
            pltpu.VMEM((12 * parts, slot_groups * LANES), BF16),
            pltpu.VMEM((LANES, slot_groups * LANES), BF16),
            pltpu.VMEM((4 * parts, LANES), F32),
        ],
        to_owners(partials),
        observed_data,
    )
    loads, load_edges = call_kernel(
        load_body,
        "segment_loads",
        [shape((6 * cells_row, cols_y), F32), shape((devices, 1, RIM * LANES), F32)],
        [pltpu.VMEM((12 * cells_row, part_count), BF16), pltpu.VMEM((2, 1, RIM * LANES), F32)],
        to_owners(reply),
        slot,
        row,
        segment_weight,
        cover,
        place,
    )
    load_lower = lax.ppermute(loads, "gx", up)
    load_higher = lax.ppermute(loads, "gx", down)
    load_rims = exchange(load_edges)
    (gradients,) = call_kernel(
        adjoint_body,
        "adjoint_run",
        [shape((2 * cells_row, cols_y), F32)],
        [
            pltpu.VMEM((2 * depth, SPAN_X, SPAN_Y), F32),
            pltpu.VMEM((4 * depth, SPAN_NEAR, SPAN_Y), F32),
            pltpu.VMEM((2 * depth, SPAN_X, SPAN_Y), F32),
            pltpu.VMEM((9 * depth, SPAN_NEAR, SPAN_Y), F32),
            pltpu.VMEM((3 * depth, SPAN_NEAR, SPAN_Y), F32),
            pltpu.VMEM((LANES, LANES), F32),
        ],
        loads,
        load_higher,
        load_lower,
        load_rims,
        strains,
        medium,
    )
    return (residuals, gradients.reshape(2, depth, rows_x, cols_y))


def solution(mesh):
    in_specs = (
        P(None, None, "gx", "gy"),
        P(None, "gx", "gy"),
        P(None, "gx", "gy"),
        P(None, "gx", "gy"),
        P(("gx", "gy")),
        P(None, ("gx", "gy")),
        P(("gx", "gy")),
        P(None, ("gx", "gy")),
        P(("gx", "gy"), None),
        P(("gx", "gy")),
        P(None, ("gx", "gy")),
    )
    out_specs = (P(None, ("gx", "gy")), P(None, None, "gx", "gy"))
    return jax.shard_map(shards, mesh=mesh, in_specs=in_specs, out_specs=out_specs, check_vma=False)
```

time: 63.2 us -> 60 us (0.949)
  local copies, waits for them, and re-layouts: 3.67 us -> 0.04 us
    unnamed x22 -> x12, local copies, waits for them, and re-layouts: 3.67 us -> 0.04 us
where the time goes in v5:
time: 60 us; the launch traced here: 59.5 us
  blocking collectives  20.9 us (35%)
  starting transfers between devices  19.7 us (33%)
  waiting for transfers between devices  9.52 us (16%)
  Pallas kernels  8.52 us (14%)
  between operations  0.78 us (1%)
    all_to_all x2, blocking collectives, exchange(): return lax.all_to_all(chunks, both, split_axis=0, concat_axis=0, tiled=True)  20.9 us
    all_to_all x2, starting transfers between devices, exchange(): return lax.all_to_all(chunks, both, split_axis=0, concat_axis=0, tiled=True)  9.86 us
    pallas_call x6, Pallas kernels, call_kernel(): pl.pallas_call(body, name=name, out_shape=outs, in_specs=[pl.BlockSpec(me...  8.52 us
    ppermute x1, waiting for transfers between devices, shards(): load_higher = lax.ppermute(loads, 'gx', down)  4.25 us
    ppermute x1, waiting for transfers between devices, shards(): higher = lax.ppermute(fields, 'gx', down)  4.12 us
    ppermute x1, starting transfers between devices, shards(): lower = lax.ppermute(fields, 'gx', up)  3.68 us
    ppermute x1, starting transfers between devices, shards(): load_lower = lax.ppermute(loads, 'gx', up)  3.59 us
    ppermute x1, starting transfers between devices, shards(): higher = lax.ppermute(fields, 'gx', down)  1.29 us
  transfers between devices with their start and end apart: 6, of which 4 were waited for; matrix products, arithmetic and copies ran while one was open for 0% of the time, Pallas kernels for 1%

profile of v5, /device:TPU:0, one launch (start us, length us, event | category | flops | bytes accessed | tf_op | source)
XLA Modules:
  0.0 59.5 jit_solution(5950933791655052996)
XLA Ops:
  0.6 1.8 %pack_edges.1 = (f32[224,128]{1,0:T(8,128)}, f32[32,1,768]{2,1,0:T(1,128)}) custom-call(f32[144,128]{1,0:T(8,128)} %bitcast.20, f32[16,128]{1,0:T(8,128)} %bitcast.22, f32[16,128]{1,0:T(8,128)} %bitcast.23, f32[16,128]{1,0:T(8,128)} %bitcast.24, s32[1,64]{1,0:T(1,128)} %bitcast.25, f32[3,64]{1,0:T(4,128)} %refs_5_.1), custom_call_target="tpu_custom_call" | custom-call | tf_op jit(solution)/shard_map/pack_edges/pallas_call | solution.py:24
  2.5 0.0 copy-start.4
  2.5 0.0 copy-start.5
  2.5 7.3 %all-to-all-start = ((f32[32,1,768]{2,1,0:T(1,128)}), f32[32,1,768]{2,1,0:T(1,128)S(1)}, u32[]{:S(2)}, u32[]{:S(2)}) async-start(f32[32,1,768]{2,1,0:T(1,128)} %get-tuple-element.16), calls=%async_computation | async-start | bytes 196608 | tf_op jit(solution)/shard_map/all_to_all | solution.py:564
  9.8 0.0 copy-start.1
  9.8 3.7 %collective-permute-start.1 = (f32[224,128]{1,0:T(8,128)S(1)}, f32[224,128]{1,0:T(8,128)S(1)}, u32[]{:S(2)}, u32[]{:S(2)}) collective-permute-start(f32[224,128]{1,0:T(8,128)S(1)} %copy-done), channel_id=1, source_target_pairs={{0,8},{8,16},{16,24},{1,9},{9,17},{17,25},{2,10},{10,18},{18,26},{... | collective-permute-start | bytes 344072 | tf_op jit(solution)/shard_map/ppermute | solution.py:587
  13.5 1.3 %collective-permute-start = (f32[224,128]{1,0:T(8,128)S(1)}, f32[224,128]{1,0:T(8,128)S(1)}, u32[]{:S(2)}, u32[]{:S(2)}) collective-permute-start(f32[224,128]{1,0:T(8,128)S(1)} %copy-done), channel_id=1, source_target_pairs={{8,0},{16,8},{24,16},{9,1},{17,9},{25,17},{10,2},{18,10},{26,18},{... | collective-permute-start | bytes 344072 | tf_op jit(solution)/shard_map/ppermute | solution.py:588
  14.8 0.6 %segment_slots.1 = (s32[16,128]{1,0:T(8,128)S(1)}, s32[16,128]{1,0:T(8,128)S(1)}, bf16[128,2048]{1,0:T(8,128)(2,1)S(1)}, bf16[128,2048]{1,0:T(8,128)(2,1)S(1)}) custom-call(s32[16,128]{1,0:T(8,128)S(1)} %bitcast.18, s32[16,128]{1,0:T(8,128)S(1)} %bitcast.19), custom_call_target="tpu_custom_call" | custom-call | tf_op jit(solution)/shard_map/segment_slots/pallas_call | solution.py:24
  15.5 0.0 copy-start.3
  15.5 0.7 %collective-permute-done.1.lower_ref = f32[224,128]{1,0:T(8,128)S(1)} collective-permute-done((f32[224,128]{1,0:T(8,128)S(1)}, f32[224,128]{1,0:T(8,128)S(1)}, u32[]{:S(2)}, u32[]{:S(2)}) %collective-permute-start.1) | collective-permute-done | bytes 114720 | tf_op jit(solution)/shard_map/ppermute | solution.py:587
  16.2 4.1 %collective-permute-done.higher_ref = f32[224,128]{1,0:T(8,128)S(1)} collective-permute-done((f32[224,128]{1,0:T(8,128)S(1)}, f32[224,128]{1,0:T(8,128)S(1)}, u32[]{:S(2)}, u32[]{:S(2)}) %collective-permute-start) | collective-permute-done | bytes 114720 | tf_op jit(solution)/shard_map/ppermute | solution.py:588
  20.3 0.0 all-to-all-done.recv_ref
  20.4 1.7 %forward_run.1 = (f32[128,128]{1,0:T(8,128)S(1)}, f32[288,128]{1,0:T(8,128)S(1)}, f32[12,16,256]{2,1,0:T(8,128)S(1)}) custom-call(f32[224,128]{1,0:T(8,128)S(1)} %copy-done, f32[224,128]{1,0:T(8,128)S(1)} %collective-permute-done.higher_ref, f32[224,128]{1,0:T(8,128)S(1)} %collective-permute-done.1.lower_ref, f32[32,1,768]{2,1,0:T(1,128)S(1)} %all-to-all-done.recv_ref, ...), custom_call_target="tpu_custom_call" | custom-call | tf_op jit(solution)/shard_map/forward_run/pallas_call | solution.py:24
  22.0 0.0 copy-start.2
  22.0 11.8 %all_to_all.20 = f32[32,4,128]{2,1,0:T(4,128)S(1)} all-to-all(f32[32,4,128]{2,1,0:T(4,128)S(1)} %bitcast.15), channel_id=1, replica_groups=mesh['gx'=4,'gy'=8] {'gx','gy'}, dimensions={0} | all-to-all | bytes 131072 | tf_op jit(solution)/shard_map/all_to_all | solution.py:564
  33.9 1.5 %channel_sums.1 = (f32[3,1024]{1,0:T(4,128)}, f32[128,128]{1,0:T(8,128)S(1)}) custom-call(f32[128,128]{1,0:T(8,128)S(1)} %bitcast.14, f32[3,1024]{1,0:T(4,128)S(1)} %copy-done.2), custom_call_target="tpu_custom_call" | custom-call | tf_op jit(solution)/shard_map/channel_sums/pallas_call | solution.py:24
  35.4 9.1 %all_to_all.21 = f32[32,4,128]{2,1,0:T(4,128)S(1)} all-to-all(f32[32,4,128]{2,1,0:T(4,128)S(1)} %bitcast.16), channel_id=1, replica_groups=mesh['gx'=4,'gy'=8] {'gx','gy'}, dimensions={0} | all-to-all | bytes 131072 | tf_op jit(solution)/shard_map/all_to_all | solution.py:564
  44.4 1.7 %segment_loads.1 = (f32[96,128]{1,0:T(8,128)S(1)}, f32[32,1,384]{2,1,0:T(1,128)}) custom-call(f32[128,128]{1,0:T(8,128)S(1)} %bitcast.13, s32[16,128]{1,0:T(8,128)S(1)} %get-tuple-element.17.slot_ref, s32[16,128]{1,0:T(8,128)S(1)} %get-tuple-element.18.row_ref, f32[2,2048]{1,0:T(2,128)S(1)} %copy-done.1, bf16[128,2048]{1,0:T(8,128)(2,1)S(1)} %get-tuple-element.19.cover_ref, ...), custom_call_target="tpu_custom_call" | custom-call | tf_op jit(solution)/shard_map/segment_loads/pallas_call | solution.py:24
  46.1 2.6 %all-to-all-start.3 = ((f32[32,1,384]{2,1,0:T(1,128)}), f32[32,1,384]{2,1,0:T(1,128)S(1)}, u32[]{:S(2)}, u32[]{:S(2)}) async-start(f32[32,1,384]{2,1,0:T(1,128)} %get-tuple-element.25), calls=%async_computation.3 | async-start | bytes 98304 | tf_op jit(solution)/shard_map/all_to_all | solution.py:564
  48.7 3.6 %collective-permute-start.3 = (f32[96,128]{1,0:T(8,128)S(1)}, f32[96,128]{1,0:T(8,128)S(1)}, u32[]{:S(2)}, u32[]{:S(2)}) collective-permute-start(f32[96,128]{1,0:T(8,128)S(1)} %get-tuple-element.24.load_ref), channel_id=1, source_target_pairs={{0,8},{8,16},{16,24},{1,9},{9,17},{17,25},{2,10},{10,18},{18,26},{... | collective-permute-start | bytes 147464 | tf_op jit(solution)/shard_map/ppermute | solution.py:656
  52.3 1.3 %collective-permute-start.2 = (f32[96,128]{1,0:T(8,128)S(1)}, f32[96,128]{1,0:T(8,128)S(1)}, u32[]{:S(2)}, u32[]{:S(2)}) collective-permute-start(f32[96,128]{1,0:T(8,128)S(1)} %get-tuple-element.24.load_ref), channel_id=1, source_target_pairs={{8,0},{16,8},{24,16},{9,1},{17,9},{25,17},{10,2},{18,10},{26,18},{... | collective-permute-start | bytes 147464 | tf_op jit(solution)/shard_map/ppermute | solution.py:657
  53.6 0.4 collective-permute-done.3.lower_ref
  54.0 4.3 %collective-permute-done.2.higher_ref = f32[96,128]{1,0:T(8,128)S(1)} collective-permute-done((f32[96,128]{1,0:T(8,128)S(1)}, f32[96,128]{1,0:T(8,128)S(1)}, u32[]{:S(2)}, u32[]{:S(2)}) %collective-permute-start.2) | collective-permute-done | bytes 49184 | tf_op jit(solution)/shard_map/ppermute | solution.py:657
  58.3 1.2 %adjoint_run.1 = f32[32,128]{1,0:T(8,128)} custom-call(f32[96,128]{1,0:T(8,128)S(1)} %get-tuple-element.24.load_ref, f32[96,128]{1,0:T(8,128)S(1)} %collective-permute-done.2.higher_ref, f32[96,128]{1,0:T(8,128)S(1)} %collective-permute-done.3.lower_ref, f32[32,1,384]{2,1,0:T(1,128)S(1)} %all-to-all-done.3.recv_ref, ...), custom_call_target="tpu_custom_call" | custom-call | tf_op jit(solution)/shard_map/adjoint_run/pallas_call | solution.py:24
  (8 shorter events, 0.0 us)
Async XLA Ops:
  2.5 7.4 %copy-start = (f32[224,128]{1,0:T(8,128)S(1)}, f32[224,128]{1,0:T(8,128)}, u32[]{:S(2)}) copy-start(f32[224,128]{1,0:T(8,128)} %get-tuple-element.15.fields_ref) | copy-start | bytes 344068
  2.5 12.3 %copy-start.4 = (s32[2048,1]{0,1:T(1,128)S(1)}, s32[2048,1]{0,1:T(1,128)}, u32[]{:S(2)}) copy-start(s32[2048,1]{0,1:T(1,128)} %param.19) | copy-start | bytes 24580
  2.5 12.3 %copy-start.5 = (s32[2048]{0:T(1024)S(1)}, s32[2048]{0:T(1024)}, u32[]{:S(2)}) copy-start(s32[2048]{0:T(1024)} %param.17) | copy-start | bytes 24580
  2.5 17.8 %all-to-all-start = ((f32[32,1,768]{2,1,0:T(1,128)}), f32[32,1,768]{2,1,0:T(1,128)S(1)}, u32[]{:S(2)}, u32[]{:S(2)}) async-start(f32[32,1,768]{2,1,0:T(1,128)} %get-tuple-element.16), calls=%async_computation | async-start | bytes 196608 | tf_op jit(solution)/shard_map/all_to_all | solution.py:564
  9.8 10.5 %copy-start.1 = (f32[2,2048]{1,0:T(2,128)S(1)}, f32[2,2048]{1,0:T(2,128)}, u32[]{:S(2)}) copy-start(f32[2,2048]{1,0:T(2,128)} %weight_ref.3) | copy-start | bytes 49156
  9.8 6.4 %collective-permute-start.1 = (f32[224,128]{1,0:T(8,128)S(1)}, f32[224,128]{1,0:T(8,128)S(1)}, u32[]{:S(2)}, u32[]{:S(2)}) collective-permute-start(f32[224,128]{1,0:T(8,128)S(1)} %copy-done), channel_id=1, source_target_pairs={{0,8},{8,16},{16,24},{1,9},{9,17},{17,25},{2,10},{10,18},{18,26},{... | collective-permute-start | bytes 344072 | tf_op jit(solution)/shard_map/ppermute | solution.py:587
  13.5 6.8 %collective-permute-start = (f32[224,128]{1,0:T(8,128)S(1)}, f32[224,128]{1,0:T(8,128)S(1)}, u32[]{:S(2)}, u32[]{:S(2)}) collective-permute-start(f32[224,128]{1,0:T(8,128)S(1)} %copy-done), channel_id=1, source_target_pairs={{8,0},{16,8},{24,16},{9,1},{17,9},{25,17},{10,2},{18,10},{26,18},{... | collective-permute-start | bytes 344072 | tf_op jit(solution)/shard_map/ppermute | solution.py:588
  15.5 4.9 %copy-start.3 = (s32[2048]{0:T(1024)S(1)}, s32[2048]{0:T(1024)}, u32[]{:S(2)}) copy-start(s32[2048]{0:T(1024)} %param.20) | copy-start | bytes 24580
  22.0 11.9 %copy-start.2 = (f32[3,1024]{1,0:T(4,128)S(1)}, f32[3,1024]{1,0:T(4,128)}, u32[]{:S(2)}) copy-start(f32[3,1024]{1,0:T(4,128)} %observed_ref.1) | copy-start | bytes 36868
  46.1 12.2 %all-to-all-start.3 = ((f32[32,1,384]{2,1,0:T(1,128)}), f32[32,1,384]{2,1,0:T(1,128)S(1)}, u32[]{:S(2)}, u32[]{:S(2)}) async-start(f32[32,1,384]{2,1,0:T(1,128)} %get-tuple-element.25), calls=%async_computation.3 | async-start | bytes 98304 | tf_op jit(solution)/shard_map/all_to_all | solution.py:564
  48.7 5.3 %collective-permute-start.3 = (f32[96,128]{1,0:T(8,128)S(1)}, f32[96,128]{1,0:T(8,128)S(1)}, u32[]{:S(2)}, u32[]{:S(2)}) collective-permute-start(f32[96,128]{1,0:T(8,128)S(1)} %get-tuple-element.24.load_ref), channel_id=1, source_target_pairs={{0,8},{8,16},{16,24},{1,9},{9,17},{17,25},{2,10},{10,18},{18,26},{... | collective-permute-start | bytes 147464 | tf_op jit(solution)/shard_map/ppermute | solution.py:656
  52.3 6.0 %collective-permute-start.2 = (f32[96,128]{1,0:T(8,128)S(1)}, f32[96,128]{1,0:T(8,128)S(1)}, u32[]{:S(2)}, u32[]{:S(2)}) collective-permute-start(f32[96,128]{1,0:T(8,128)S(1)} %get-tuple-element.24.load_ref), channel_id=1, source_target_pairs={{8,0},{16,8},{24,16},{9,1},{17,9},{25,17},{10,2},{18,10},{26,18},{... | collective-permute-start | bytes 147464 | tf_op jit(solution)/shard_map/ppermute | solution.py:657

commit v6 on v5

--- a/solution.py
+++ b/solution.py
@@ -19,14 +19,15 @@
 NEAR = tuple((dx, dy) for dx in (-1, 0, 1) for dy in (-1, 0, 1))
 
 
-def call_kernel(body, name, outs, scratch, *args, place=pltpu.VMEM, room=24 * 1024 * 1024):
-    whole = pl.BlockSpec(memory_space=pltpu.VMEM)
+def call_kernel(
+    body, name, outs, scratch, *args, place=pltpu.VMEM, place_out=pltpu.VMEM, room=24 * 1024 * 1024
+):
     return pl.pallas_call(
         body,
         name=name,
         out_shape=outs,
         in_specs=[pl.BlockSpec(memory_space=place)] * len(args),
-        out_specs=[whole] * len(outs),
+        out_specs=[pl.BlockSpec(memory_space=place_out)] * len(outs),
         scratch_shapes=scratch,
         compiler_params=pltpu.CompilerParams(vmem_limit_bytes=room),
     )(*args)
@@ -49,6 +50,15 @@
 
 def times_turned(left, right):
     return lax.dot_general(left, right, (((1,), (1,)), ((), ())), preferred_element_type=F32)
+
+
+def packed_rows(row, height):
+    tile = jnp.broadcast_to(row.astype(F32), (16, row.shape[1])).astype(BF16)
+    return jnp.concatenate([tile] * (height // 16), axis=0) if height > 16 else tile
+
+
+def packed_iota(height, shift=0):
+    return (iota((height, LANES), 0) >> shift).astype(F32).astype(BF16)
 
 
 def two_pieces(values):
@@ -215,7 +225,8 @@
 
 
 def pack_body(*refs):
-    inputs, (fields_ref, out_ref, side_ref, cells_ref, wavelet_ref, arrived) = refs[:6], refs[6:]
+    inputs, outputs, scratch = refs[:6], refs[6:10], refs[10:]
+    fields_ref, low_ref, high_ref, side_ref, cells_ref, wavelet_ref, arrived, sent, sent_sides = scratch
     targets, at = [], 0
     for source in inputs[:4]:
         targets.append(fields_ref.at[at : at + source.shape[0]])
@@ -245,10 +256,34 @@
     for number in range(3, 6):
         rows = slice(number * cells_row, (number + 1) * cells_row)
         fields_ref[rows, :] = fields_ref[rows, :] + maps[:cells_row]
+    height = fields_ref.shape[0] // TILE_X
+    for x in range(TILE_X):
+        slab = fields_ref[pl.ds(x, height, stride=TILE_X), :]
+        if x < RIM:
+            low_ref[x * height : (x + 1) * height, :] = slab
+        if x >= TILE_X - RIM:
+            at = x - TILE_X + RIM
+            high_ref[at * height : (at + 1) * height, :] = slab
+    writes = [
+        pltpu.make_async_copy(source, target, sent.at[number])
+        for number, (source, target) in enumerate(zip((fields_ref, low_ref, high_ref), outputs))
+    ]
+    for copy in writes:
+        copy.start()
     rows = fields_ref[...]
     spare = 2 * LANES - rows.shape[0]
     edge_columns(jnp.concatenate([rows, jnp.zeros((spare, LANES), F32)], axis=0), side_ref)
-    send_sides(side_ref, out_ref, [(dx, dy) for dx, dy in NEAR if dy])
+    sides = []
+    for number, (dx, dy) in enumerate((dx, dy) for dx, dy in NEAR if dy):
+        index, inside = neighbour(dx, dy)
+        source, target = side_ref.at[1 if dy > 0 else 0], outputs[3].at[index]
+        sides.append((inside, pltpu.make_async_copy(source, target, sent_sides.at[number])))
+    for inside, copy in sides:
+        pl.when(inside)(copy.start)
+    for copy in writes:
+        copy.wait()
+    for inside, copy in sides:
+        pl.when(inside)(copy.wait)
 
 
 def slots_body(capacity, devices, cols_y, owner_ref, start_ref, slot_ref, row_ref, cover_ref, place_ref, rank_ref):
@@ -310,13 +345,20 @@
     state_ref,
     near_ref,
     turn_ref,
+    sides_ref,
     spread_ref,
 ):
     depth = medium_ref.shape[0] // 3
     cells_row = depth * TILE_X
     turn_ref[...] = jnp.zeros_like(turn_ref)
     rims = [rim_rows(recv_ref, dx, turn_ref) for dx in (0, 1, -1)]
-    lay_planes(wide_ref, source_ref, 0, fields_ref, higher_ref, lower_ref)
+    height = fields_ref.shape[0] // TILE_X
+    sides_ref[...] = jnp.zeros_like(sides_ref)
+    for x in range(RIM):
+        slab = slice(x * height, (x + 1) * height)
+        sides_ref[0, pl.ds(x, height, stride=TILE_X), :] = higher_ref[slab, :]
+        sides_ref[1, pl.ds(x + TILE_X - RIM, height, stride=TILE_X), :] = lower_ref[slab, :]
+    lay_planes(wide_ref, source_ref, 0, fields_ref, sides_ref.at[0], sides_ref.at[1])
     lay_planes(wide_ref, source_ref, LANES, *rims)
     first = 9 * depth
     medium_ref[...] = wide_ref[first:]
@@ -343,7 +385,7 @@
     )
     axial = jnp.concatenate(pieces(axial), axis=0).astype(BF16)
     rows_down = iota((cells_row, LANES), 0)
-    slots_down = iota((LANES, LANES), 0) >> 2
+    slots_down = packed_iota(LANES, 2)
     for block in range(slot_ref.shape[0]):
         lanes = slice(block * LANES, (block + 1) * LANES)
         if block % 2 == 0:
@@ -361,24 +403,27 @@
             sums.append(jnp.sum(jnp.where(at_row, axial_sum, 0.0), axis=0, keepdims=True))
         sums.append(channel_ref[block : block + 1, :].astype(F32))
         values = jnp.concatenate(sums + sums, axis=0)
-        in_slot = slots_down == slot_ref[block : block + 1, :]
+        in_slot = slots_down == packed_rows(slot_ref[block : block + 1, :], LANES)
         for third, piece in enumerate(pieces(values)):
+            tile = jnp.concatenate([piece, piece], axis=0).astype(BF16)
             spread_ref[third * LANES : (third + 1) * LANES, lanes] = jnp.where(
-                in_slot, jnp.concatenate([piece] * (LANES // 8), axis=0), 0.0
-            ).astype(BF16)
+                in_slot, jnp.concatenate([tile] * (LANES // 16), axis=0), jnp.zeros((), BF16)
+            )
     out_ref[...] = sum_thirds(times_turned(spread_ref[...], place_ref[...]))
 
 
 def owner_body(arrived_ref, observed_ref, residual_ref, reply_ref, values_ref, place_ref, held_ref):
     groups = arrived_ref.shape[0] // 4
     parts = observed_ref.shape[1] // LANES
-    down = iota((LANES, LANES), 0)
+    down = packed_iota(LANES)
     part_down = iota((parts, LANES), 0)
     nothing = jnp.zeros((parts, LANES), F32)
     numbers = [arrived_ref[4 * s + 3 : 4 * s + 4, :].astype(I32) for s in range(groups)]
     for s in range(groups):
         lanes = slice(s * LANES, (s + 1) * LANES)
-        place_ref[:, lanes] = jnp.where(down == (numbers[s] & (LANES - 1)), 1.0, 0.0).astype(BF16)
+        place_ref[:, lanes] = jnp.where(
+            down == packed_rows(numbers[s] & (LANES - 1), LANES), jnp.ones((), BF16), jnp.zeros((), BF16)
+        )
         at_part = part_down == (numbers[s] >> 7)
         thirds = pieces(arrived_ref[4 * s : 4 * s + 3, :])
         stack = []
@@ -427,7 +472,7 @@
     stack_rows = load_ref.shape[0]
     arrived = jnp.concatenate(two_pieces(arrived_ref[...]), axis=0).astype(BF16)
     slots_down = iota((LANES, LANES), 0) >> 2
-    rows_down = iota((cells_row, LANES), 0)
+    rows_down = packed_iota(cells_row)
     for block in range(slot_ref.shape[0]):
         lanes = slice(block * LANES, (block + 1) * LANES)
         if block % 2 == 0:
@@ -438,13 +483,15 @@
         for part in range(1, LANES // 8):
             folded = folded + found[8 * part : 8 * part + 8]
         folded = folded + pltpu.roll(folded, 4, 0)
-        at_row = rows_down == row_ref[block : block + 1, :]
+        at_row = rows_down == packed_rows(row_ref[block : block + 1, :], cells_row)
         for turn in range(3):
             back = folded[2 - turn : 3 - turn, :]
             for part in range(2):
                 for half, piece in enumerate(two_pieces(weight_ref[part : part + 1, lanes] * back)):
                     base = half * stack_rows + (2 * turn + part) * cells_row
-                    spread_ref[base : base + cells_row, lanes] = jnp.where(at_row, piece, 0.0).astype(BF16)
+                    spread_ref[base : base + cells_row, lanes] = jnp.where(
+                        at_row, packed_rows(piece, cells_row), jnp.zeros((), BF16)
+                    )
     load = sum_halves(times_turned(spread_ref[...], cover_ref[...]))
     load_ref[...] = load
     spare = LANES - stack_rows
@@ -568,24 +615,31 @@
         back = exchange(chunks.reshape(devices, 4, capacity)).reshape(slot_groups, per_group, 4, capacity)
         return back.transpose(0, 2, 1, 3).reshape(slot_groups * 4, LANES)
 
-    fields, edges = call_kernel(
+    trimmed = shape((14 * depth * RIM, cols_y), F32)
+    fields, low, high, edges = call_kernel(
         pack_body,
         "pack_edges",
-        [shape((14 * cells_row, cols_y), F32), shape((devices, 1, 2 * RIM * LANES), F32)],
+        [shape((14 * cells_row, cols_y), F32), trimmed, trimmed, shape((devices, 1, 2 * RIM * LANES), F32)],
         [
+            pltpu.VMEM((14 * cells_row, cols_y), F32),
+            pltpu.VMEM(trimmed.shape, F32),
+            pltpu.VMEM(trimmed.shape, F32),
             pltpu.VMEM((2, 1, 2 * RIM * LANES), F32),
             pltpu.VMEM((1, source_cells.shape[0]), I32),
             pltpu.VMEM(source_wavelet.shape, F32),
+            pltpu.SemaphoreType.DMA((6,)),
+            pltpu.SemaphoreType.DMA((3,)),
             pltpu.SemaphoreType.DMA((6,)),
         ],
         *[values.reshape(-1, cols_y) for values in (initial_state, lame_lambda, shear_modulus, buoyancy)],
         source_cells.reshape(1, -1),
         source_wavelet,
         place=pl.ANY,
+        place_out=pl.ANY,
         room=60 * 1024 * 1024,
     )
-    lower = lax.ppermute(fields, "gx", up)
-    higher = lax.ppermute(fields, "gx", down)
+    lower = lax.ppermute(high, "gx", up)
+    higher = lax.ppermute(low, "gx", down)
     rims = exchange(edges)
     channels = partial_channel.reshape(blocks, LANES)
     slot, row, cover, place = call_kernel(
@@ -615,6 +669,7 @@
             pltpu.VMEM((9 * depth, SPAN_NEAR, SPAN_Y), F32),
             pltpu.VMEM((3 * depth, SPAN_NEAR, SPAN_Y), F32),
             pltpu.VMEM((LANES, 2 * LANES), F32),
+            pltpu.VMEM((2, 14 * cells_row, cols_y), F32),
             pltpu.VMEM((3 * LANES, part_count), BF16),
         ],
         fields,

time: 60 us -> 59.5 us (level)
  waiting for transfers between devices: 9.52 us -> 6.4 us
  blocking collectives: 20.9 us -> 22.9 us
  starting transfers between devices: 19.7 us -> 20.6 us
    ppermute x2, waiting for transfers between devices: 4.83 us -> 1.71 us  [the longest x1 1.02 us: shards(): lower = lax.ppermute(high, 'gx', up)]
    all_to_all x2, blocking collectives: 20.9 us -> 22.9 us  [exchange(): return lax.all_to_all(chunks, both, split_axis=0, concat_axis=0, tiled=True)]
    ppermute x2, starting transfers between devices: 4.97 us -> 5.84 us  [the longest x1 4.55 us: shards(): lower = lax.ppermute(high, 'gx', up)]
where the time goes in v6:
time: 59.5 us; the launch traced here: 59.1 us
  blocking collectives  22.9 us (38%)
  starting transfers between devices  20.6 us (35%)
  Pallas kernels  8.37 us (14%)
  waiting for transfers between devices  6.4 us (11%)
  between operations  0.78 us (1%)
    all_to_all x2, blocking collectives, exchange(): return lax.all_to_all(chunks, both, split_axis=0, concat_axis=0, tiled=True)  22.9 us
    all_to_all x2, starting transfers between devices, exchange(): return lax.all_to_all(chunks, both, split_axis=0, concat_axis=0, tiled=True)  9.87 us
    pallas_call x6, Pallas kernels, call_kernel(): pl.pallas_call(body, name=name, out_shape=outs, in_specs=[pl.BlockSpec(me...  8.37 us
    ppermute x1, starting transfers between devices, shards(): lower = lax.ppermute(high, 'gx', up)  4.55 us
    ppermute x1, waiting for transfers between devices, shards(): load_higher = lax.ppermute(loads, 'gx', down)  4.25 us
    ppermute x1, starting transfers between devices, shards(): load_lower = lax.ppermute(loads, 'gx', up)  3.59 us
    ppermute x1, starting transfers between devices, shards(): higher = lax.ppermute(low, 'gx', down)  1.29 us
    ppermute x1, starting transfers between devices, shards(): load_higher = lax.ppermute(loads, 'gx', down)  1.29 us
  transfers between devices with their start and end apart: 6, of which 4 were waited for; matrix products, arithmetic and copies ran while one was open for 0% of the time, Pallas kernels for 1%

profile of v6, /device:TPU:0, one launch (start us, length us, event | category | flops | bytes accessed | tf_op | source)
XLA Modules:
  0.0 59.1 jit_solution(1431101294864229676)
XLA Ops:
  0.6 1.8 %pack_edges.1 = (f32[224,128]{1,0:T(8,128)}, f32[168,128]{1,0:T(8,128)}, f32[168,128]{1,0:T(8,128)}, f32[32,1,768]{2,1,0:T(1,128)}) custom-call(f32[144,128]{1,0:T(8,128)} %bitcast.20, f32[16,128]{1,0:T(8,128)} %bitcast.22, f32[16,128]{1,0:T(8,128)} %bitcast.23, f32[16,128]{1,0:T(8,128)} %bitcast.24, s32[1,64]{1,0:T(1,128)} %bitcast.25, f32[3,64]{1,0:T(4,128)} %refs_5_.1), custom_call_target="tpu_custom_call" | custom-call | tf_op jit(solution)/shard_map/pack_edges/pallas_call | solution.py:25
  2.5 0.0 copy-start.4
  2.5 0.0 copy-start.5
  2.5 7.3 %all-to-all-start = ((f32[32,1,768]{2,1,0:T(1,128)}), f32[32,1,768]{2,1,0:T(1,128)S(1)}, u32[]{:S(2)}, u32[]{:S(2)}) async-start(f32[32,1,768]{2,1,0:T(1,128)} %get-tuple-element.20), calls=%async_computation | async-start | bytes 196608 | tf_op jit(solution)/shard_map/all_to_all | solution.py:611
  9.8 1.3 %collective-permute-start = (f32[168,128]{1,0:T(8,128)}, f32[168,128]{1,0:T(8,128)S(1)}, u32[]{:S(2)}, u32[]{:S(2)}) collective-permute-start(f32[168,128]{1,0:T(8,128)} %get-tuple-element.18), channel_id=1, source_target_pairs={{8,0},{16,8},{24,16},{9,1},{17,9},{25,17},{10,2},{18,10},{26,18},{... | collective-permute-start | bytes 258056 | tf_op jit(solution)/shard_map/ppermute | solution.py:642
  11.1 0.0 copy-start.1
  11.1 4.5 %collective-permute-start.1 = (f32[168,128]{1,0:T(8,128)}, f32[168,128]{1,0:T(8,128)S(1)}, u32[]{:S(2)}, u32[]{:S(2)}) collective-permute-start(f32[168,128]{1,0:T(8,128)} %get-tuple-element.19), channel_id=1, source_target_pairs={{0,8},{8,16},{16,24},{1,9},{9,17},{17,25},{2,10},{10,18},{18,26},{... | collective-permute-start | bytes 258056 | tf_op jit(solution)/shard_map/ppermute | solution.py:641
  15.7 0.6 %segment_slots.1 = (s32[16,128]{1,0:T(8,128)S(1)}, s32[16,128]{1,0:T(8,128)S(1)}, bf16[128,2048]{1,0:T(8,128)(2,1)S(1)}, bf16[128,2048]{1,0:T(8,128)(2,1)S(1)}) custom-call(s32[16,128]{1,0:T(8,128)S(1)} %bitcast.18, s32[16,128]{1,0:T(8,128)S(1)} %bitcast.19), custom_call_target="tpu_custom_call" | custom-call | tf_op jit(solution)/shard_map/segment_slots/pallas_call | solution.py:25
  16.3 0.0 copy-start.3
  16.4 0.7 %collective-permute-done.higher_ref = f32[168,128]{1,0:T(8,128)S(1)} collective-permute-done((f32[168,128]{1,0:T(8,128)}, f32[168,128]{1,0:T(8,128)S(1)}, u32[]{:S(2)}, u32[]{:S(2)}) %collective-permute-start) | collective-permute-done | bytes 86048 | tf_op jit(solution)/shard_map/ppermute | solution.py:642
  17.0 1.0 %collective-permute-done.1.lower_ref = f32[168,128]{1,0:T(8,128)S(1)} collective-permute-done((f32[168,128]{1,0:T(8,128)}, f32[168,128]{1,0:T(8,128)S(1)}, u32[]{:S(2)}, u32[]{:S(2)}) %collective-permute-start.1) | collective-permute-done | bytes 86048 | tf_op jit(solution)/shard_map/ppermute | solution.py:641
  18.1 1.7 %forward_run.1 = (f32[128,128]{1,0:T(8,128)S(1)}, f32[288,128]{1,0:T(8,128)S(1)}, f32[12,16,256]{2,1,0:T(8,128)S(1)}) custom-call(f32[224,128]{1,0:T(8,128)S(1)} %copy-done, f32[168,128]{1,0:T(8,128)S(1)} %collective-permute-done.higher_ref, f32[168,128]{1,0:T(8,128)S(1)} %collective-permute-done.1.lower_ref, f32[32,1,768]{2,1,0:T(1,128)S(1)} %all-to-all-done.recv_ref, ...), custom_call_target="tpu_custom_call" | custom-call | tf_op jit(solution)/shard_map/forward_run/pallas_call | solution.py:25
  19.7 0.0 copy-start.2
  19.8 13.8 %all_to_all.20 = f32[32,4,128]{2,1,0:T(4,128)S(1)} all-to-all(f32[32,4,128]{2,1,0:T(4,128)S(1)} %bitcast.15), channel_id=1, replica_groups=mesh['gx'=4,'gy'=8] {'gx','gy'}, dimensions={0} | all-to-all | bytes 131072 | tf_op jit(solution)/shard_map/all_to_all | solution.py:611
  33.6 1.3 %channel_sums.1 = (f32[3,1024]{1,0:T(4,128)}, f32[128,128]{1,0:T(8,128)S(1)}) custom-call(f32[128,128]{1,0:T(8,128)S(1)} %bitcast.14, f32[3,1024]{1,0:T(4,128)S(1)} %copy-done.2), custom_call_target="tpu_custom_call" | custom-call | tf_op jit(solution)/shard_map/channel_sums/pallas_call | solution.py:25
  34.9 9.1 %all_to_all.21 = f32[32,4,128]{2,1,0:T(4,128)S(1)} all-to-all(f32[32,4,128]{2,1,0:T(4,128)S(1)} %bitcast.16), channel_id=1, replica_groups=mesh['gx'=4,'gy'=8] {'gx','gy'}, dimensions={0} | all-to-all | bytes 131072 | tf_op jit(solution)/shard_map/all_to_all | solution.py:611
  44.0 1.7 %segment_loads.1 = (f32[96,128]{1,0:T(8,128)S(1)}, f32[32,1,384]{2,1,0:T(1,128)}) custom-call(f32[128,128]{1,0:T(8,128)S(1)} %bitcast.13, s32[16,128]{1,0:T(8,128)S(1)} %get-tuple-element.21.slot_ref, s32[16,128]{1,0:T(8,128)S(1)} %get-tuple-element.22.row_ref, f32[2,2048]{1,0:T(2,128)S(1)} %copy-done.1, bf16[128,2048]{1,0:T(8,128)(2,1)S(1)} %get-tuple-element.23.cover_ref, ...), custom_call_target="tpu_custom_call" | custom-call | tf_op jit(solution)/shard_map/segment_loads/pallas_call | solution.py:25
  45.7 2.6 %all-to-all-start.3 = ((f32[32,1,384]{2,1,0:T(1,128)}), f32[32,1,384]{2,1,0:T(1,128)S(1)}, u32[]{:S(2)}, u32[]{:S(2)}) async-start(f32[32,1,384]{2,1,0:T(1,128)} %get-tuple-element.29), calls=%async_computation.3 | async-start | bytes 98304 | tf_op jit(solution)/shard_map/all_to_all | solution.py:611
  48.2 3.6 %collective-permute-start.3 = (f32[96,128]{1,0:T(8,128)S(1)}, f32[96,128]{1,0:T(8,128)S(1)}, u32[]{:S(2)}, u32[]{:S(2)}) collective-permute-start(f32[96,128]{1,0:T(8,128)S(1)} %get-tuple-element.28.load_ref), channel_id=1, source_target_pairs={{0,8},{8,16},{16,24},{1,9},{9,17},{17,25},{2,10},{10,18},{18,26},{... | collective-permute-start | bytes 147464 | tf_op jit(solution)/shard_map/ppermute | solution.py:711
  51.8 1.3 %collective-permute-start.2 = (f32[96,128]{1,0:T(8,128)S(1)}, f32[96,128]{1,0:T(8,128)S(1)}, u32[]{:S(2)}, u32[]{:S(2)}) collective-permute-start(f32[96,128]{1,0:T(8,128)S(1)} %get-tuple-element.28.load_ref), channel_id=1, source_target_pairs={{8,0},{16,8},{24,16},{9,1},{17,9},{25,17},{10,2},{18,10},{26,18},{... | collective-permute-start | bytes 147464 | tf_op jit(solution)/shard_map/ppermute | solution.py:712
  53.1 0.4 collective-permute-done.3.lower_ref
  53.6 4.3 %collective-permute-done.2.higher_ref = f32[96,128]{1,0:T(8,128)S(1)} collective-permute-done((f32[96,128]{1,0:T(8,128)S(1)}, f32[96,128]{1,0:T(8,128)S(1)}, u32[]{:S(2)}, u32[]{:S(2)}) %collective-permute-start.2) | collective-permute-done | bytes 49184 | tf_op jit(solution)/shard_map/ppermute | solution.py:712
  57.8 0.0 all-to-all-done.3.recv_ref
  57.8 1.2 %adjoint_run.1 = f32[32,128]{1,0:T(8,128)} custom-call(f32[96,128]{1,0:T(8,128)S(1)} %get-tuple-element.28.load_ref, f32[96,128]{1,0:T(8,128)S(1)} %collective-permute-done.2.higher_ref, f32[96,128]{1,0:T(8,128)S(1)} %collective-permute-done.3.lower_ref, f32[32,1,384]{2,1,0:T(1,128)S(1)} %all-to-all-done.3.recv_ref, ...), custom_call_target="tpu_custom_call" | custom-call | tf_op jit(solution)/shard_map/adjoint_run/pallas_call | solution.py:25
  (8 shorter events, 0.0 us)
Async XLA Ops:
  2.5 13.2 %copy-start.4 = (s32[2048,1]{0,1:T(1,128)S(1)}, s32[2048,1]{0,1:T(1,128)}, u32[]{:S(2)}) copy-start(s32[2048,1]{0,1:T(1,128)} %param.19) | copy-start | bytes 24580
  2.5 13.2 %copy-start.5 = (s32[2048]{0:T(1024)S(1)}, s32[2048]{0:T(1024)}, u32[]{:S(2)}) copy-start(s32[2048]{0:T(1024)} %param.17) | copy-start | bytes 24580
  2.5 15.6 %copy-start = (f32[224,128]{1,0:T(8,128)S(1)}, f32[224,128]{1,0:T(8,128)}, u32[]{:S(2)}) copy-start(f32[224,128]{1,0:T(8,128)} %get-tuple-element.17.fields_ref) | copy-start | bytes 344068
  2.5 15.6 %all-to-all-start = ((f32[32,1,768]{2,1,0:T(1,128)}), f32[32,1,768]{2,1,0:T(1,128)S(1)}, u32[]{:S(2)}, u32[]{:S(2)}) async-start(f32[32,1,768]{2,1,0:T(1,128)} %get-tuple-element.20), calls=%async_computation | async-start | bytes 196608 | tf_op jit(solution)/shard_map/all_to_all | solution.py:611
  9.8 7.2 %collective-permute-start = (f32[168,128]{1,0:T(8,128)}, f32[168,128]{1,0:T(8,128)S(1)}, u32[]{:S(2)}, u32[]{:S(2)}) collective-permute-start(f32[168,128]{1,0:T(8,128)} %get-tuple-element.18), channel_id=1, source_target_pairs={{8,0},{16,8},{24,16},{9,1},{17,9},{25,17},{10,2},{18,10},{26,18},{... | collective-permute-start | bytes 258056 | tf_op jit(solution)/shard_map/ppermute | solution.py:642
  11.1 7.0 %copy-start.1 = (f32[2,2048]{1,0:T(2,128)S(1)}, f32[2,2048]{1,0:T(2,128)}, u32[]{:S(2)}) copy-start(f32[2,2048]{1,0:T(2,128)} %weight_ref.3) | copy-start | bytes 49156
  11.1 6.9 %collective-permute-start.1 = (f32[168,128]{1,0:T(8,128)}, f32[168,128]{1,0:T(8,128)S(1)}, u32[]{:S(2)}, u32[]{:S(2)}) collective-permute-start(f32[168,128]{1,0:T(8,128)} %get-tuple-element.19), channel_id=1, source_target_pairs={{0,8},{8,16},{16,24},{1,9},{9,17},{17,25},{2,10},{10,18},{18,26},{... | collective-permute-start | bytes 258056 | tf_op jit(solution)/shard_map/ppermute | solution.py:641
  16.3 1.7 %copy-start.3 = (s32[2048]{0:T(1024)S(1)}, s32[2048]{0:T(1024)}, u32[]{:S(2)}) copy-start(s32[2048]{0:T(1024)} %param.20) | copy-start | bytes 24580
  19.7 13.8 %copy-start.2 = (f32[3,1024]{1,0:T(4,128)S(1)}, f32[3,1024]{1,0:T(4,128)}, u32[]{:S(2)}) copy-start(f32[3,1024]{1,0:T(4,128)} %observed_ref.1) | copy-start | bytes 36868
  45.7 12.2 %all-to-all-start.3 = ((f32[32,1,384]{2,1,0:T(1,128)}), f32[32,1,384]{2,1,0:T(1,128)S(1)}, u32[]{:S(2)}, u32[]{:S(2)}) async-start(f32[32,1,384]{2,1,0:T(1,128)} %get-tuple-element.29), calls=%async_computation.3 | async-start | bytes 98304 | tf_op jit(solution)/shard_map/all_to_all | solution.py:611
  48.2 5.3 %collective-permute-start.3 = (f32[96,128]{1,0:T(8,128)S(1)}, f32[96,128]{1,0:T(8,128)S(1)}, u32[]{:S(2)}, u32[]{:S(2)}) collective-permute-start(f32[96,128]{1,0:T(8,128)S(1)} %get-tuple-element.28.load_ref), channel_id=1, source_target_pairs={{0,8},{8,16},{16,24},{1,9},{9,17},{17,25},{2,10},{10,18},{18,26},{... | collective-permute-start | bytes 147464 | tf_op jit(solution)/shard_map/ppermute | solution.py:711
  51.8 6.0 %collective-permute-start.2 = (f32[96,128]{1,0:T(8,128)S(1)}, f32[96,128]{1,0:T(8,128)S(1)}, u32[]{:S(2)}, u32[]{:S(2)}) collective-permute-start(f32[96,128]{1,0:T(8,128)S(1)} %get-tuple-element.28.load_ref), channel_id=1, source_target_pairs={{8,0},{16,8},{24,16},{9,1},{17,9},{25,17},{10,2},{18,10},{26,18},{... | collective-permute-start | bytes 147464 | tf_op jit(solution)/shard_map/ppermute | solution.py:712

commit v7 on v6

--- a/solution.py
+++ b/solution.py
@@ -22,12 +22,13 @@
 def call_kernel(
     body, name, outs, scratch, *args, place=pltpu.VMEM, place_out=pltpu.VMEM, room=24 * 1024 * 1024
 ):
+    spaces = place_out if isinstance(place_out, tuple) else (place_out,) * len(outs)
     return pl.pallas_call(
         body,
         name=name,
         out_shape=outs,
         in_specs=[pl.BlockSpec(memory_space=place)] * len(args),
-        out_specs=[pl.BlockSpec(memory_space=place_out)] * len(outs),
+        out_specs=[pl.BlockSpec(memory_space=space) for space in spaces],
         scratch_shapes=scratch,
         compiler_params=pltpu.CompilerParams(vmem_limit_bytes=room),
     )(*args)
@@ -91,13 +92,20 @@
             side_ref[side, 0:1, column * width : (column + 1) * width] = turned[base + column : base + column + 1, :]
 
 
-def send_sides(side_ref, out_ref, places):
-    for dx, dy in places:
+def start_sides(side_ref, out_ref, sent):
+    sides = []
+    for number, (dx, dy) in enumerate((dx, dy) for dx, dy in NEAR if dy):
         index, inside = neighbour(dx, dy)
-
-        @pl.when(inside)
-        def _(index=index, dy=dy):
-            out_ref[index] = side_ref[1 if dy > 0 else 0]
+        source, target = side_ref.at[1 if dy > 0 else 0], out_ref.at[index]
+        sides.append((inside, pltpu.make_async_copy(source, target, sent.at[number])))
+    for inside, copy in sides:
+        pl.when(inside)(copy.start)
+    return sides
+
+
+def wait_sides(sides):
+    for inside, copy in sides:
+        pl.when(inside)(copy.wait)
 
 
 def arrived_chunk(recv_ref, dx, dy):
@@ -226,7 +234,7 @@
 
 def pack_body(*refs):
     inputs, outputs, scratch = refs[:6], refs[6:10], refs[10:]
-    fields_ref, low_ref, high_ref, side_ref, cells_ref, wavelet_ref, arrived, sent, sent_sides = scratch
+    fields_ref, high_ref, low_ref, side_ref, cells_ref, wavelet_ref, arrived, sent, sent_sides = scratch
     targets, at = [], 0
     for source in inputs[:4]:
         targets.append(fields_ref.at[at : at + source.shape[0]])
@@ -266,24 +274,17 @@
             high_ref[at * height : (at + 1) * height, :] = slab
     writes = [
         pltpu.make_async_copy(source, target, sent.at[number])
-        for number, (source, target) in enumerate(zip((fields_ref, low_ref, high_ref), outputs))
+        for number, (source, target) in enumerate(zip((fields_ref, high_ref, low_ref), outputs))
     ]
     for copy in writes:
         copy.start()
     rows = fields_ref[...]
     spare = 2 * LANES - rows.shape[0]
     edge_columns(jnp.concatenate([rows, jnp.zeros((spare, LANES), F32)], axis=0), side_ref)
-    sides = []
-    for number, (dx, dy) in enumerate((dx, dy) for dx, dy in NEAR if dy):
-        index, inside = neighbour(dx, dy)
-        source, target = side_ref.at[1 if dy > 0 else 0], outputs[3].at[index]
-        sides.append((inside, pltpu.make_async_copy(source, target, sent_sides.at[number])))
-    for inside, copy in sides:
-        pl.when(inside)(copy.start)
+    sides = start_sides(side_ref, outputs[3], sent_sides)
     for copy in writes:
         copy.wait()
-    for inside, copy in sides:
-        pl.when(inside)(copy.wait)
+    wait_sides(sides)
 
 
 def slots_body(capacity, devices, cols_y, owner_ref, start_ref, slot_ref, row_ref, cover_ref, place_ref, rank_ref):
@@ -328,8 +329,8 @@
 
 def forward_body(
     fields_ref,
+    lower_ref,
     higher_ref,
-    lower_ref,
     recv_ref,
     slot_ref,
     row_ref,
@@ -467,6 +468,7 @@
     out_ref,
     spread_ref,
     side_ref,
+    sent_sides,
 ):
     cells_row = load_ref.shape[0] // 6
     stack_rows = load_ref.shape[0]
@@ -492,11 +494,16 @@
                     spread_ref[base : base + cells_row, lanes] = jnp.where(
                         at_row, packed_rows(piece, cells_row), jnp.zeros((), BF16)
                     )
-    load = sum_halves(times_turned(spread_ref[...], cover_ref[...]))
-    load_ref[...] = load
-    spare = LANES - stack_rows
-    edge_columns(jnp.concatenate([load, jnp.zeros((spare, LANES), F32)], axis=0), side_ref)
-    send_sides(side_ref, out_ref, [(dx, dy) for dx, dy in NEAR if dy])
+    cover = jnp.concatenate([cover_ref[0:16, :], cover_ref[LANES - 16 :, :]], axis=0)
+    edges = times_turned(cover, spread_ref[0:stack_rows, :]) + times_turned(cover, spread_ref[stack_rows:, :])
+    side_ref[...] = jnp.zeros_like(side_ref)
+    for side, base in ((0, 0), (1, 32 - RIM)):
+        for column in range(RIM):
+            lanes = slice(column * LANES, column * LANES + stack_rows)
+            side_ref[side, 0:1, lanes] = edges[base + column : base + column + 1, :]
+    sides = start_sides(side_ref, out_ref, sent_sides)
+    load_ref[...] = sum_halves(times_turned(spread_ref[...], cover_ref[...]))
+    wait_sides(sides)
 
 
 def adjoint_body(
@@ -616,7 +623,7 @@
         return back.transpose(0, 2, 1, 3).reshape(slot_groups * 4, LANES)
 
     trimmed = shape((14 * depth * RIM, cols_y), F32)
-    fields, low, high, edges = call_kernel(
+    fields, high, low, edges = call_kernel(
         pack_body,
         "pack_edges",
         [shape((14 * cells_row, cols_y), F32), trimmed, trimmed, shape((devices, 1, 2 * RIM * LANES), F32)],
@@ -673,8 +680,8 @@
             pltpu.VMEM((3 * LANES, part_count), BF16),
         ],
         fields,
+        lower,
         higher,
-        lower,
         rims,
         slot,
         row,
@@ -700,13 +707,18 @@
         load_body,
         "segment_loads",
         [shape((6 * cells_row, cols_y), F32), shape((devices, 1, RIM * LANES), F32)],
-        [pltpu.VMEM((12 * cells_row, part_count), BF16), pltpu.VMEM((2, 1, RIM * LANES), F32)],
+        [
+            pltpu.VMEM((12 * cells_row, part_count), BF16),
+            pltpu.VMEM((2, 1, RIM * LANES), F32),
+            pltpu.SemaphoreType.DMA((6,)),
+        ],
         to_owners(reply),
         slot,
         row,
         segment_weight,
         cover,
         place,
+        place_out=(pltpu.VMEM, pl.ANY),
     )
     load_lower = lax.ppermute(loads, "gx", up)
     load_higher = lax.ppermute(loads, "gx", down)

time: 59.5 us -> 59.6 us (level)
  waiting for transfers between devices: 6.4 us -> 9.29 us
  blocking collectives: 22.9 us -> 20.9 us
  starting transfers between devices: 20.6 us -> 19.7 us
    ppermute x1, waiting for transfers between devices: 0.69 us -> 4.2 us  [shards(): higher = lax.ppermute(low, 'gx', down)]
    all_to_all x2, blocking collectives: 22.9 us -> 20.9 us  [exchange(): return lax.all_to_all(chunks, both, split_axis=0, concat_axis=0, tiled=True)]
    ppermute x1, starting transfers between devices: 4.55 us -> 3.68 us  [shards(): lower = lax.ppermute(high, 'gx', up)]
    ppermute x1, waiting for transfers between devices: 1.02 us -> 0.4 us  [shards(): lower = lax.ppermute(high, 'gx', up)]
where the time goes in v7:
time: 59.6 us; the launch traced here: 59.1 us
  blocking collectives  20.9 us (35%)
  starting transfers between devices  19.7 us (33%)
  waiting for transfers between devices  9.29 us (16%)
  Pallas kernels  8.35 us (14%)
  between operations  0.79 us (1%)
    all_to_all x2, blocking collectives, exchange(): return lax.all_to_all(chunks, both, split_axis=0, concat_axis=0, tiled=True)  20.9 us
    all_to_all x2, starting transfers between devices, exchange(): return lax.all_to_all(chunks, both, split_axis=0, concat_axis=0, tiled=True)  9.89 us
    pallas_call x6, Pallas kernels, call_kernel(): pl.pallas_call(body, name=name, out_shape=outs, in_specs=[pl.BlockSpec(me...  8.35 us
    ppermute x1, waiting for transfers between devices, shards(): load_higher = lax.ppermute(loads, 'gx', down)  4.25 us
    ppermute x1, waiting for transfers between devices, shards(): higher = lax.ppermute(low, 'gx', down)  4.2 us
    ppermute x1, starting transfers between devices, shards(): lower = lax.ppermute(high, 'gx', up)  3.68 us
    ppermute x1, starting transfers between devices, shards(): load_lower = lax.ppermute(loads, 'gx', up)  3.59 us
    ppermute x1, starting transfers between devices, shards(): higher = lax.ppermute(low, 'gx', down)  1.29 us
  transfers between devices with their start and end apart: 6, of which 4 were waited for; matrix products, arithmetic and copies ran while one was open for 0% of the time, Pallas kernels for 1%

profile of v7, /device:TPU:0, one launch (start us, length us, event | category | flops | bytes accessed | tf_op | source)
XLA Modules:
  0.0 59.1 jit_solution(12092514525822269714)
XLA Ops:
  0.6 1.8 %pack_edges.1 = (f32[224,128]{1,0:T(8,128)}, f32[168,128]{1,0:T(8,128)}, f32[168,128]{1,0:T(8,128)}, f32[32,1,768]{2,1,0:T(1,128)}) custom-call(f32[144,128]{1,0:T(8,128)} %bitcast.20, f32[16,128]{1,0:T(8,128)} %bitcast.22, f32[16,128]{1,0:T(8,128)} %bitcast.23, f32[16,128]{1,0:T(8,128)} %bitcast.24, s32[1,64]{1,0:T(1,128)} %bitcast.25, f32[3,64]{1,0:T(4,128)} %refs_5_.1), custom_call_target="tpu_custom_call" | custom-call | tf_op jit(solution)/shard_map/pack_edges/pallas_call | solution.py:26
  2.5 0.0 copy-start.4
  2.5 0.0 copy-start.5
  2.5 7.3 %all-to-all-start = ((f32[32,1,768]{2,1,0:T(1,128)}), f32[32,1,768]{2,1,0:T(1,128)S(1)}, u32[]{:S(2)}, u32[]{:S(2)}) async-start(f32[32,1,768]{2,1,0:T(1,128)} %get-tuple-element.20), calls=%async_computation | async-start | bytes 196608 | tf_op jit(solution)/shard_map/all_to_all | solution.py:618
  9.8 3.7 %collective-permute-start = (f32[168,128]{1,0:T(8,128)}, f32[168,128]{1,0:T(8,128)S(1)}, u32[]{:S(2)}, u32[]{:S(2)}) collective-permute-start(f32[168,128]{1,0:T(8,128)} %get-tuple-element.18), channel_id=1, source_target_pairs={{0,8},{8,16},{16,24},{1,9},{9,17},{17,25},{2,10},{10,18},{18,26},{... | collective-permute-start | bytes 258056 | tf_op jit(solution)/shard_map/ppermute | solution.py:648
  13.5 0.0 copy-start.1
  13.5 1.3 %collective-permute-start.1 = (f32[168,128]{1,0:T(8,128)}, f32[168,128]{1,0:T(8,128)S(1)}, u32[]{:S(2)}, u32[]{:S(2)}) collective-permute-start(f32[168,128]{1,0:T(8,128)} %get-tuple-element.19), channel_id=1, source_target_pairs={{8,0},{16,8},{24,16},{9,1},{17,9},{25,17},{10,2},{18,10},{26,18},{... | collective-permute-start | bytes 258056 | tf_op jit(solution)/shard_map/ppermute | solution.py:649
  14.8 0.6 %segment_slots.1 = (s32[16,128]{1,0:T(8,128)S(1)}, s32[16,128]{1,0:T(8,128)S(1)}, bf16[128,2048]{1,0:T(8,128)(2,1)S(1)}, bf16[128,2048]{1,0:T(8,128)(2,1)S(1)}) custom-call(s32[16,128]{1,0:T(8,128)S(1)} %bitcast.18, s32[16,128]{1,0:T(8,128)S(1)} %bitcast.19), custom_call_target="tpu_custom_call" | custom-call | tf_op jit(solution)/shard_map/segment_slots/pallas_call | solution.py:26
  15.5 0.0 copy-start.3
  15.5 0.4 collective-permute-done.lower_ref
  15.9 4.2 %collective-permute-done.1.higher_ref = f32[168,128]{1,0:T(8,128)S(1)} collective-permute-done((f32[168,128]{1,0:T(8,128)}, f32[168,128]{1,0:T(8,128)S(1)}, u32[]{:S(2)}, u32[]{:S(2)}) %collective-permute-start.1) | collective-permute-done | bytes 86048 | tf_op jit(solution)/shard_map/ppermute | solution.py:649
  20.1 0.0 all-to-all-done.recv_ref
  20.1 1.6 %forward_run.1 = (f32[128,128]{1,0:T(8,128)S(1)}, f32[288,128]{1,0:T(8,128)S(1)}, f32[12,16,256]{2,1,0:T(8,128)S(1)}) custom-call(f32[224,128]{1,0:T(8,128)S(1)} %copy-done, f32[168,128]{1,0:T(8,128)S(1)} %collective-permute-done.lower_ref, f32[168,128]{1,0:T(8,128)S(1)} %collective-permute-done.1.higher_ref, f32[32,1,768]{2,1,0:T(1,128)S(1)} %all-to-all-done.recv_ref, ...), custom_call_target="tpu_custom_call" | custom-call | tf_op jit(solution)/shard_map/forward_run/pallas_call | solution.py:26
  21.8 0.0 copy-start.2
  21.8 11.8 %all_to_all.20 = f32[32,4,128]{2,1,0:T(4,128)S(1)} all-to-all(f32[32,4,128]{2,1,0:T(4,128)S(1)} %bitcast.15), channel_id=1, replica_groups=mesh['gx'=4,'gy'=8] {'gx','gy'}, dimensions={0} | all-to-all | bytes 131072 | tf_op jit(solution)/shard_map/all_to_all | solution.py:618
  33.6 1.3 %channel_sums.1 = (f32[3,1024]{1,0:T(4,128)}, f32[128,128]{1,0:T(8,128)S(1)}) custom-call(f32[128,128]{1,0:T(8,128)S(1)} %bitcast.14, f32[3,1024]{1,0:T(4,128)S(1)} %copy-done.2), custom_call_target="tpu_custom_call" | custom-call | tf_op jit(solution)/shard_map/channel_sums/pallas_call | solution.py:26
  35.0 9.1 %all_to_all.21 = f32[32,4,128]{2,1,0:T(4,128)S(1)} all-to-all(f32[32,4,128]{2,1,0:T(4,128)S(1)} %bitcast.16), channel_id=1, replica_groups=mesh['gx'=4,'gy'=8] {'gx','gy'}, dimensions={0} | all-to-all | bytes 131072 | tf_op jit(solution)/shard_map/all_to_all | solution.py:618
  44.0 1.7 %segment_loads.1 = (f32[96,128]{1,0:T(8,128)S(1)}, f32[32,1,384]{2,1,0:T(1,128)}) custom-call(f32[128,128]{1,0:T(8,128)S(1)} %bitcast.13, s32[16,128]{1,0:T(8,128)S(1)} %get-tuple-element.21.slot_ref, s32[16,128]{1,0:T(8,128)S(1)} %get-tuple-element.22.row_ref, f32[2,2048]{1,0:T(2,128)S(1)} %copy-done.1, bf16[128,2048]{1,0:T(8,128)(2,1)S(1)} %get-tuple-element.23.cover_ref, ...), custom_call_target="tpu_custom_call" | custom-call | tf_op jit(solution)/shard_map/segment_loads/pallas_call | solution.py:26
  45.7 2.6 %all-to-all-start.3 = ((f32[32,1,384]{2,1,0:T(1,128)}), f32[32,1,384]{2,1,0:T(1,128)S(1)}, u32[]{:S(2)}, u32[]{:S(2)}) async-start(f32[32,1,384]{2,1,0:T(1,128)} %get-tuple-element.29), calls=%async_computation.3 | async-start | bytes 98304 | tf_op jit(solution)/shard_map/all_to_all | solution.py:618
  48.3 3.6 %collective-permute-start.3 = (f32[96,128]{1,0:T(8,128)S(1)}, f32[96,128]{1,0:T(8,128)S(1)}, u32[]{:S(2)}, u32[]{:S(2)}) collective-permute-start(f32[96,128]{1,0:T(8,128)S(1)} %get-tuple-element.28.load_ref), channel_id=1, source_target_pairs={{0,8},{8,16},{16,24},{1,9},{9,17},{17,25},{2,10},{10,18},{18,26},{... | collective-permute-start | bytes 147464 | tf_op jit(solution)/shard_map/ppermute | solution.py:723
  51.9 1.3 %collective-permute-start.2 = (f32[96,128]{1,0:T(8,128)S(1)}, f32[96,128]{1,0:T(8,128)S(1)}, u32[]{:S(2)}, u32[]{:S(2)}) collective-permute-start(f32[96,128]{1,0:T(8,128)S(1)} %get-tuple-element.28.load_ref), channel_id=1, source_target_pairs={{8,0},{16,8},{24,16},{9,1},{17,9},{25,17},{10,2},{18,10},{26,18},{... | collective-permute-start | bytes 147464 | tf_op jit(solution)/shard_map/ppermute | solution.py:724
  53.2 0.4 collective-permute-done.3.lower_ref
  53.6 4.3 %collective-permute-done.2.higher_ref = f32[96,128]{1,0:T(8,128)S(1)} collective-permute-done((f32[96,128]{1,0:T(8,128)S(1)}, f32[96,128]{1,0:T(8,128)S(1)}, u32[]{:S(2)}, u32[]{:S(2)}) %collective-permute-start.2) | collective-permute-done | bytes 49184 | tf_op jit(solution)/shard_map/ppermute | solution.py:724
  57.9 1.2 %adjoint_run.1 = f32[32,128]{1,0:T(8,128)} custom-call(f32[96,128]{1,0:T(8,128)S(1)} %get-tuple-element.28.load_ref, f32[96,128]{1,0:T(8,128)S(1)} %collective-permute-done.2.higher_ref, f32[96,128]{1,0:T(8,128)S(1)} %collective-permute-done.3.lower_ref, f32[32,1,384]{2,1,0:T(1,128)S(1)} %all-to-all-done.3.recv_ref, ...), custom_call_target="tpu_custom_call" | custom-call | tf_op jit(solution)/shard_map/adjoint_run/pallas_call | solution.py:26
  (8 shorter events, 0.0 us)
Async XLA Ops:
  2.5 12.3 %copy-start.4 = (s32[2048,1]{0,1:T(1,128)S(1)}, s32[2048,1]{0,1:T(1,128)}, u32[]{:S(2)}) copy-start(s32[2048,1]{0,1:T(1,128)} %param.19) | copy-start | bytes 24580
  2.5 12.3 %copy-start.5 = (s32[2048]{0:T(1024)S(1)}, s32[2048]{0:T(1024)}, u32[]{:S(2)}) copy-start(s32[2048]{0:T(1024)} %param.17) | copy-start | bytes 24580
  2.5 17.6 %copy-start = (f32[224,128]{1,0:T(8,128)S(1)}, f32[224,128]{1,0:T(8,128)}, u32[]{:S(2)}) copy-start(f32[224,128]{1,0:T(8,128)} %get-tuple-element.17.fields_ref) | copy-start | bytes 344068
  2.5 17.6 %all-to-all-start = ((f32[32,1,768]{2,1,0:T(1,128)}), f32[32,1,768]{2,1,0:T(1,128)S(1)}, u32[]{:S(2)}, u32[]{:S(2)}) async-start(f32[32,1,768]{2,1,0:T(1,128)} %get-tuple-element.20), calls=%async_computation | async-start | bytes 196608 | tf_op jit(solution)/shard_map/all_to_all | solution.py:618
  9.8 6.1 %collective-permute-start = (f32[168,128]{1,0:T(8,128)}, f32[168,128]{1,0:T(8,128)S(1)}, u32[]{:S(2)}, u32[]{:S(2)}) collective-permute-start(f32[168,128]{1,0:T(8,128)} %get-tuple-element.18), channel_id=1, source_target_pairs={{0,8},{8,16},{16,24},{1,9},{9,17},{17,25},{2,10},{10,18},{18,26},{... | collective-permute-start | bytes 258056 | tf_op jit(solution)/shard_map/ppermute | solution.py:648
  13.5 6.6 %copy-start.1 = (f32[2,2048]{1,0:T(2,128)S(1)}, f32[2,2048]{1,0:T(2,128)}, u32[]{:S(2)}) copy-start(f32[2,2048]{1,0:T(2,128)} %weight_ref.3) | copy-start | bytes 49156
  13.5 6.6 %collective-permute-start.1 = (f32[168,128]{1,0:T(8,128)}, f32[168,128]{1,0:T(8,128)S(1)}, u32[]{:S(2)}, u32[]{:S(2)}) collective-permute-start(f32[168,128]{1,0:T(8,128)} %get-tuple-element.19), channel_id=1, source_target_pairs={{8,0},{16,8},{24,16},{9,1},{17,9},{25,17},{10,2},{18,10},{26,18},{... | collective-permute-start | bytes 258056 | tf_op jit(solution)/shard_map/ppermute | solution.py:649
  15.5 4.6 %copy-start.3 = (s32[2048]{0:T(1024)S(1)}, s32[2048]{0:T(1024)}, u32[]{:S(2)}) copy-start(s32[2048]{0:T(1024)} %param.20) | copy-start | bytes 24580
  21.8 11.9 %copy-start.2 = (f32[3,1024]{1,0:T(4,128)S(1)}, f32[3,1024]{1,0:T(4,128)}, u32[]{:S(2)}) copy-start(f32[3,1024]{1,0:T(4,128)} %observed_ref.1) | copy-start | bytes 36868
  45.7 12.2 %all-to-all-start.3 = ((f32[32,1,384]{2,1,0:T(1,128)}), f32[32,1,384]{2,1,0:T(1,128)S(1)}, u32[]{:S(2)}, u32[]{:S(2)}) async-start(f32[32,1,384]{2,1,0:T(1,128)} %get-tuple-element.29), calls=%async_computation.3 | async-start | bytes 98304 | tf_op jit(solution)/shard_map/all_to_all | solution.py:618
  48.3 5.3 %collective-permute-start.3 = (f32[96,128]{1,0:T(8,128)S(1)}, f32[96,128]{1,0:T(8,128)S(1)}, u32[]{:S(2)}, u32[]{:S(2)}) collective-permute-start(f32[96,128]{1,0:T(8,128)S(1)} %get-tuple-element.28.load_ref), channel_id=1, source_target_pairs={{0,8},{8,16},{16,24},{1,9},{9,17},{17,25},{2,10},{10,18},{18,26},{... | collective-permute-start | bytes 147464 | tf_op jit(solution)/shard_map/ppermute | solution.py:723
  51.9 6.0 %collective-permute-start.2 = (f32[96,128]{1,0:T(8,128)S(1)}, f32[96,128]{1,0:T(8,128)S(1)}, u32[]{:S(2)}, u32[]{:S(2)}) collective-permute-start(f32[96,128]{1,0:T(8,128)S(1)} %get-tuple-element.28.load_ref), channel_id=1, source_target_pairs={{8,0},{16,8},{24,16},{9,1},{17,9},{25,17},{10,2},{18,10},{26,18},{... | collective-permute-start | bytes 147464 | tf_op jit(solution)/shard_map/ppermute | solution.py:724

commit v8 on v7

--- a/solution.py
+++ b/solution.py
@@ -465,10 +465,8 @@
     cover_ref,
     place_ref,
     load_ref,
-    out_ref,
+    side_ref,
     spread_ref,
-    side_ref,
-    sent_sides,
 ):
     cells_row = load_ref.shape[0] // 6
     stack_rows = load_ref.shape[0]
@@ -501,8 +499,12 @@
         for column in range(RIM):
             lanes = slice(column * LANES, column * LANES + stack_rows)
             side_ref[side, 0:1, lanes] = edges[base + column : base + column + 1, :]
+    load_ref[...] = sum_halves(times_turned(spread_ref[...], cover_ref[...]))
+
+
+def rims_body(load_ref, side_ref, copy_ref, out_ref, sent_sides):
     sides = start_sides(side_ref, out_ref, sent_sides)
-    load_ref[...] = sum_halves(times_turned(spread_ref[...], cover_ref[...]))
+    copy_ref[...] = load_ref[...]
     wait_sides(sides)
 
 
@@ -703,25 +705,30 @@
         to_owners(partials),
         observed_data,
     )
-    loads, load_edges = call_kernel(
+    load_rows, load_sides = shape((6 * cells_row, cols_y), F32), shape((2, 1, RIM * LANES), F32)
+    loads, sides = call_kernel(
         load_body,
         "segment_loads",
-        [shape((6 * cells_row, cols_y), F32), shape((devices, 1, RIM * LANES), F32)],
-        [
-            pltpu.VMEM((12 * cells_row, part_count), BF16),
-            pltpu.VMEM((2, 1, RIM * LANES), F32),
-            pltpu.SemaphoreType.DMA((6,)),
-        ],
+        [load_rows, load_sides],
+        [pltpu.VMEM((12 * cells_row, part_count), BF16)],
         to_owners(reply),
         slot,
         row,
         segment_weight,
         cover,
         place,
+    )
+    load_lower = lax.ppermute(loads, "gx", up)
+    loads_again, load_edges = call_kernel(
+        rims_body,
+        "load_rims",
+        [load_rows, shape((devices, 1, RIM * LANES), F32)],
+        [pltpu.SemaphoreType.DMA((6,))],
+        loads,
+        sides,
         place_out=(pltpu.VMEM, pl.ANY),
     )
-    load_lower = lax.ppermute(loads, "gx", up)
-    load_higher = lax.ppermute(loads, "gx", down)
+    load_higher = lax.ppermute(loads_again, "gx", down)
     load_rims = exchange(load_edges)
     (gradients,) = call_kernel(
         adjoint_body,

time: 59.6 us -> 59.6 us (level)
    pallas_call x6 -> x7, Pallas kernels: 8.35 us -> 8.38 us  [call_kernel(): pl.pallas_call(body, name=name, out_shape=outs, in_specs=[pl.BlockSpec(me...]
where the time goes in v8:
time: 59.6 us; the launch traced here: 59.2 us
  blocking collectives  20.9 us (35%)
  starting transfers between devices  19.7 us (33%)
  waiting for transfers between devices  9.3 us (16%)
  Pallas kernels  8.38 us (14%)
  between operations  0.79 us (1%)
    all_to_all x2, blocking collectives, exchange(): return lax.all_to_all(chunks, both, split_axis=0, concat_axis=0, tiled=True)  20.9 us
    all_to_all x2, starting transfers between devices, exchange(): return lax.all_to_all(chunks, both, split_axis=0, concat_axis=0, tiled=True)  9.88 us
    pallas_call x7, Pallas kernels, call_kernel(): pl.pallas_call(body, name=name, out_shape=outs, in_specs=[pl.BlockSpec(me...  8.38 us
    ppermute x1, waiting for transfers between devices, shards(): load_higher = lax.ppermute(loads_again, 'gx', down)  4.25 us
    ppermute x1, waiting for transfers between devices, shards(): higher = lax.ppermute(low, 'gx', down)  4.2 us
    ppermute x1, starting transfers between devices, shards(): lower = lax.ppermute(high, 'gx', up)  3.68 us
    ppermute x1, starting transfers between devices, shards(): load_lower = lax.ppermute(loads, 'gx', up)  3.59 us
    ppermute x1, starting transfers between devices, shards(): higher = lax.ppermute(low, 'gx', down)  1.29 us
  transfers between devices with their start and end apart: 6, of which 4 were waited for; matrix products, arithmetic and copies ran while one was open for 0% of the time, Pallas kernels for 1%

profile of v8, /device:TPU:0, one launch (start us, length us, event | category | flops | bytes accessed | tf_op | source)
XLA Modules:
  0.0 59.2 jit_solution(17376075870811516580)
XLA Ops:
  0.6 1.8 %pack_edges.1 = (f32[224,128]{1,0:T(8,128)}, f32[168,128]{1,0:T(8,128)}, f32[168,128]{1,0:T(8,128)}, f32[32,1,768]{2,1,0:T(1,128)}) custom-call(f32[144,128]{1,0:T(8,128)} %bitcast.20, f32[16,128]{1,0:T(8,128)} %bitcast.22, f32[16,128]{1,0:T(8,128)} %bitcast.23, f32[16,128]{1,0:T(8,128)} %bitcast.24, s32[1,64]{1,0:T(1,128)} %bitcast.25, f32[3,64]{1,0:T(4,128)} %refs_5_.1), custom_call_target="tpu_custom_call" | custom-call | tf_op jit(solution)/shard_map/pack_edges/pallas_call | solution.py:26
  2.5 0.0 copy-start.4
  2.5 0.0 copy-start.5
  2.5 7.3 %all-to-all-start = ((f32[32,1,768]{2,1,0:T(1,128)}), f32[32,1,768]{2,1,0:T(1,128)S(1)}, u32[]{:S(2)}, u32[]{:S(2)}) async-start(f32[32,1,768]{2,1,0:T(1,128)} %get-tuple-element.22), calls=%async_computation | async-start | bytes 196608 | tf_op jit(solution)/shard_map/all_to_all | solution.py:620
  9.8 3.7 %collective-permute-start = (f32[168,128]{1,0:T(8,128)}, f32[168,128]{1,0:T(8,128)S(1)}, u32[]{:S(2)}, u32[]{:S(2)}) collective-permute-start(f32[168,128]{1,0:T(8,128)} %get-tuple-element.20), channel_id=1, source_target_pairs={{0,8},{8,16},{16,24},{1,9},{9,17},{17,25},{2,10},{10,18},{18,26},{... | collective-permute-start | bytes 258056 | tf_op jit(solution)/shard_map/ppermute | solution.py:650
  13.5 0.0 copy-start.1
  13.5 1.3 %collective-permute-start.1 = (f32[168,128]{1,0:T(8,128)}, f32[168,128]{1,0:T(8,128)S(1)}, u32[]{:S(2)}, u32[]{:S(2)}) collective-permute-start(f32[168,128]{1,0:T(8,128)} %get-tuple-element.21), channel_id=1, source_target_pairs={{8,0},{16,8},{24,16},{9,1},{17,9},{25,17},{10,2},{18,10},{26,18},{... | collective-permute-start | bytes 258056 | tf_op jit(solution)/shard_map/ppermute | solution.py:651
  14.8 0.6 %segment_slots.1 = (s32[16,128]{1,0:T(8,128)S(1)}, s32[16,128]{1,0:T(8,128)S(1)}, bf16[128,2048]{1,0:T(8,128)(2,1)S(1)}, bf16[128,2048]{1,0:T(8,128)(2,1)S(1)}) custom-call(s32[16,128]{1,0:T(8,128)S(1)} %bitcast.18, s32[16,128]{1,0:T(8,128)S(1)} %bitcast.19), custom_call_target="tpu_custom_call" | custom-call | tf_op jit(solution)/shard_map/segment_slots/pallas_call | solution.py:26
  15.5 0.0 copy-start.3
  15.5 0.4 collective-permute-done.lower_ref
  15.9 4.2 %collective-permute-done.1.higher_ref = f32[168,128]{1,0:T(8,128)S(1)} collective-permute-done((f32[168,128]{1,0:T(8,128)}, f32[168,128]{1,0:T(8,128)S(1)}, u32[]{:S(2)}, u32[]{:S(2)}) %collective-permute-start.1) | collective-permute-done | bytes 86048 | tf_op jit(solution)/shard_map/ppermute | solution.py:651
  20.1 1.7 %forward_run.1 = (f32[128,128]{1,0:T(8,128)S(1)}, f32[288,128]{1,0:T(8,128)S(1)}, f32[12,16,256]{2,1,0:T(8,128)S(1)}) custom-call(f32[224,128]{1,0:T(8,128)S(1)} %copy-done, f32[168,128]{1,0:T(8,128)S(1)} %collective-permute-done.lower_ref, f32[168,128]{1,0:T(8,128)S(1)} %collective-permute-done.1.higher_ref, f32[32,1,768]{2,1,0:T(1,128)S(1)} %all-to-all-done.recv_ref, ...), custom_call_target="tpu_custom_call" | custom-call | tf_op jit(solution)/shard_map/forward_run/pallas_call | solution.py:26
  21.8 0.0 copy-start.2
  21.8 11.8 %all_to_all.20 = f32[32,4,128]{2,1,0:T(4,128)S(1)} all-to-all(f32[32,4,128]{2,1,0:T(4,128)S(1)} %bitcast.15), channel_id=1, replica_groups=mesh['gx'=4,'gy'=8] {'gx','gy'}, dimensions={0} | all-to-all | bytes 131072 | tf_op jit(solution)/shard_map/all_to_all | solution.py:620
  33.6 1.3 %channel_sums.1 = (f32[3,1024]{1,0:T(4,128)}, f32[128,128]{1,0:T(8,128)S(1)}) custom-call(f32[128,128]{1,0:T(8,128)S(1)} %bitcast.14, f32[3,1024]{1,0:T(4,128)S(1)} %copy-done.2), custom_call_target="tpu_custom_call" | custom-call | tf_op jit(solution)/shard_map/channel_sums/pallas_call | solution.py:26
  35.0 9.1 %all_to_all.21 = f32[32,4,128]{2,1,0:T(4,128)S(1)} all-to-all(f32[32,4,128]{2,1,0:T(4,128)S(1)} %bitcast.16), channel_id=1, replica_groups=mesh['gx'=4,'gy'=8] {'gx','gy'}, dimensions={0} | all-to-all | bytes 131072 | tf_op jit(solution)/shard_map/all_to_all | solution.py:620
  44.0 1.0 %segment_loads.1 = (f32[96,128]{1,0:T(8,128)S(1)}, f32[2,1,384]{2,1,0:T(1,128)S(1)}) custom-call(f32[128,128]{1,0:T(8,128)S(1)} %bitcast.13, s32[16,128]{1,0:T(8,128)S(1)} %get-tuple-element.23.slot_ref, s32[16,128]{1,0:T(8,128)S(1)} %get-tuple-element.24.row_ref, f32[2,2048]{1,0:T(2,128)S(1)} %copy-done.1, ...), custom_call_target="tpu_custom_call" | custom-call | tf_op jit(solution)/shard_map/segment_loads/pallas_call | solution.py:26
  45.1 0.7 %load_rims.1 = (f32[96,128]{1,0:T(8,128)S(1)}, f32[32,1,384]{2,1,0:T(1,128)}) custom-call(f32[96,128]{1,0:T(8,128)S(1)} %get-tuple-element.30.load_ref, f32[2,1,384]{2,1,0:T(1,128)S(1)} %get-tuple-element.31.side_ref), custom_call_target="tpu_custom_call" | custom-call | tf_op jit(solution)/shard_map/load_rims/pallas_call | solution.py:26
  45.8 2.6 %all-to-all-start.3 = ((f32[32,1,384]{2,1,0:T(1,128)}), f32[32,1,384]{2,1,0:T(1,128)S(1)}, u32[]{:S(2)}, u32[]{:S(2)}) async-start(f32[32,1,384]{2,1,0:T(1,128)} %get-tuple-element.33), calls=%async_computation.3 | async-start | bytes 98304 | tf_op jit(solution)/shard_map/all_to_all | solution.py:620
  48.3 3.6 %collective-permute-start.3 = (f32[96,128]{1,0:T(8,128)S(1)}, f32[96,128]{1,0:T(8,128)S(1)}, u32[]{:S(2)}, u32[]{:S(2)}) collective-permute-start(f32[96,128]{1,0:T(8,128)S(1)} %get-tuple-element.30.load_ref), channel_id=1, source_target_pairs={{0,8},{8,16},{16,24},{1,9},{9,17},{17,25},{2,10},{10,18},{18,26},{... | collective-permute-start | bytes 147464 | tf_op jit(solution)/shard_map/ppermute | solution.py:721
  51.9 1.3 %collective-permute-start.2 = (f32[96,128]{1,0:T(8,128)S(1)}, f32[96,128]{1,0:T(8,128)S(1)}, u32[]{:S(2)}, u32[]{:S(2)}) collective-permute-start(f32[96,128]{1,0:T(8,128)S(1)} %get-tuple-element.32), channel_id=1, source_target_pairs={{8,0},{16,8},{24,16},{9,1},{17,9},{25,17},{10,2},{18,10},{26,18},{... | collective-permute-start | bytes 147464 | tf_op jit(solution)/shard_map/ppermute | solution.py:731
  53.2 0.4 collective-permute-done.3.lower_ref
  53.7 4.3 %collective-permute-done.2.higher_ref = f32[96,128]{1,0:T(8,128)S(1)} collective-permute-done((f32[96,128]{1,0:T(8,128)S(1)}, f32[96,128]{1,0:T(8,128)S(1)}, u32[]{:S(2)}, u32[]{:S(2)}) %collective-permute-start.2) | collective-permute-done | bytes 49184 | tf_op jit(solution)/shard_map/ppermute | solution.py:731
  57.9 1.2 %adjoint_run.1 = f32[32,128]{1,0:T(8,128)} custom-call(f32[96,128]{1,0:T(8,128)S(1)} %get-tuple-element.30.load_ref, f32[96,128]{1,0:T(8,128)S(1)} %collective-permute-done.2.higher_ref, f32[96,128]{1,0:T(8,128)S(1)} %collective-permute-done.3.lower_ref, f32[32,1,384]{2,1,0:T(1,128)S(1)} %all-to-all-done.3.recv_ref, ...), custom_call_target="tpu_custom_call" | custom-call | tf_op jit(solution)/shard_map/adjoint_run/pallas_call | solution.py:26
  (9 shorter events, 0.0 us)
Async XLA Ops:
  2.5 12.3 %copy-start.4 = (s32[2048,1]{0,1:T(1,128)S(1)}, s32[2048,1]{0,1:T(1,128)}, u32[]{:S(2)}) copy-start(s32[2048,1]{0,1:T(1,128)} %param.19) | copy-start | bytes 24580
  2.5 12.3 %copy-start.5 = (s32[2048]{0:T(1024)S(1)}, s32[2048]{0:T(1024)}, u32[]{:S(2)}) copy-start(s32[2048]{0:T(1024)} %param.17) | copy-start | bytes 24580
  2.5 17.6 %copy-start = (f32[224,128]{1,0:T(8,128)S(1)}, f32[224,128]{1,0:T(8,128)}, u32[]{:S(2)}) copy-start(f32[224,128]{1,0:T(8,128)} %get-tuple-element.19.fields_ref) | copy-start | bytes 344068
  2.5 17.6 %all-to-all-start = ((f32[32,1,768]{2,1,0:T(1,128)}), f32[32,1,768]{2,1,0:T(1,128)S(1)}, u32[]{:S(2)}, u32[]{:S(2)}) async-start(f32[32,1,768]{2,1,0:T(1,128)} %get-tuple-element.22), calls=%async_computation | async-start | bytes 196608 | tf_op jit(solution)/shard_map/all_to_all | solution.py:620
  9.8 6.1 %collective-permute-start = (f32[168,128]{1,0:T(8,128)}, f32[168,128]{1,0:T(8,128)S(1)}, u32[]{:S(2)}, u32[]{:S(2)}) collective-permute-start(f32[168,128]{1,0:T(8,128)} %get-tuple-element.20), channel_id=1, source_target_pairs={{0,8},{8,16},{16,24},{1,9},{9,17},{17,25},{2,10},{10,18},{18,26},{... | collective-permute-start | bytes 258056 | tf_op jit(solution)/shard_map/ppermute | solution.py:650
  13.5 6.6 %copy-start.1 = (f32[2,2048]{1,0:T(2,128)S(1)}, f32[2,2048]{1,0:T(2,128)}, u32[]{:S(2)}) copy-start(f32[2,2048]{1,0:T(2,128)} %weight_ref.3) | copy-start | bytes 49156
  13.5 6.6 %collective-permute-start.1 = (f32[168,128]{1,0:T(8,128)}, f32[168,128]{1,0:T(8,128)S(1)}, u32[]{:S(2)}, u32[]{:S(2)}) collective-permute-start(f32[168,128]{1,0:T(8,128)} %get-tuple-element.21), channel_id=1, source_target_pairs={{8,0},{16,8},{24,16},{9,1},{17,9},{25,17},{10,2},{18,10},{26,18},{... | collective-permute-start | bytes 258056 | tf_op jit(solution)/shard_map/ppermute | solution.py:651
  15.5 4.6 %copy-start.3 = (s32[2048]{0:T(1024)S(1)}, s32[2048]{0:T(1024)}, u32[]{:S(2)}) copy-start(s32[2048]{0:T(1024)} %param.20) | copy-start | bytes 24580
  21.8 11.9 %copy-start.2 = (f32[3,1024]{1,0:T(4,128)S(1)}, f32[3,1024]{1,0:T(4,128)}, u32[]{:S(2)}) copy-start(f32[3,1024]{1,0:T(4,128)} %observed_ref.1) | copy-start | bytes 36868
  45.8 12.2 %all-to-all-start.3 = ((f32[32,1,384]{2,1,0:T(1,128)}), f32[32,1,384]{2,1,0:T(1,128)S(1)}, u32[]{:S(2)}, u32[]{:S(2)}) async-start(f32[32,1,384]{2,1,0:T(1,128)} %get-tuple-element.33), calls=%async_computation.3 | async-start | bytes 98304 | tf_op jit(solution)/shard_map/all_to_all | solution.py:620
  48.3 5.3 %collective-permute-start.3 = (f32[96,128]{1,0:T(8,128)S(1)}, f32[96,128]{1,0:T(8,128)S(1)}, u32[]{:S(2)}, u32[]{:S(2)}) collective-permute-start(f32[96,128]{1,0:T(8,128)S(1)} %get-tuple-element.30.load_ref), channel_id=1, source_target_pairs={{0,8},{8,16},{16,24},{1,9},{9,17},{17,25},{2,10},{10,18},{18,26},{... | collective-permute-start | bytes 147464 | tf_op jit(solution)/shard_map/ppermute | solution.py:721
  51.9 6.0 %collective-permute-start.2 = (f32[96,128]{1,0:T(8,128)S(1)}, f32[96,128]{1,0:T(8,128)S(1)}, u32[]{:S(2)}, u32[]{:S(2)}) collective-permute-start(f32[96,128]{1,0:T(8,128)S(1)} %get-tuple-element.32), channel_id=1, source_target_pairs={{8,0},{16,8},{24,16},{9,1},{17,9},{25,17},{10,2},{18,10},{26,18},{... | collective-permute-start | bytes 147464 | tf_op jit(solution)/shard_map/ppermute | solution.py:731

commit v9 on v8

--- a/solution.py
+++ b/solution.py
@@ -508,28 +508,45 @@
     wait_sides(sides)
 
 
+def adjoint_planes_body(load_ref, lower_ref, medium_ref, first_ref, later_ref, near_ref):
+    lay_planes(first_ref, later_ref, 0, load_ref, jnp.zeros_like(load_ref), lower_ref)
+    for plane in range(medium_ref.shape[0]):
+        near_ref[plane] = narrowed(medium_ref[plane])
+
+
 def adjoint_body(
-    load_ref,
+    first_laid_ref,
+    later_laid_ref,
     higher_ref,
-    lower_ref,
     recv_ref,
     strain_ref,
     medium_ref,
+    near_ref,
     gradient_ref,
     first_ref,
     later_ref,
     velocity_ref,
     state_ref,
-    near_ref,
     turn_ref,
 ):
     depth = medium_ref.shape[0] // 3
     turn_ref[...] = jnp.zeros_like(turn_ref)
     rims = [rim_rows(recv_ref, dx, turn_ref) for dx in (0, 1, -1)]
-    lay_planes(first_ref, later_ref, 0, load_ref, higher_ref, lower_ref)
     lay_planes(first_ref, later_ref, LANES, *rims)
-    for plane in range(3 * depth):
-        near_ref[plane] = narrowed(medium_ref[plane])
+    row = iota((8, LANES), 0)
+    wide = first_ref.shape[0]
+    for plane in range(wide + later_ref.shape[0]):
+        high = higher_ref[8 * (plane // 2) : 8 * (plane // 2) + 8, :]
+        if plane % 2 == 0:
+            high = pltpu.roll(high, TILE_X, 0)
+        if plane < wide:
+            first_ref[plane, 0:8, 0:LANES] = jnp.where(row < TILE_X, first_laid_ref[plane, 0:8, 0:LANES], high)
+            first_ref[plane, 8:16, 0:LANES] = first_laid_ref[plane, 8:16, 0:LANES]
+        else:
+            laid = later_laid_ref[plane - wide, :, 0:LANES]
+            later_ref[plane - wide, :, 0:LANES] = jnp.where(
+                (row >= TILE_X) & (row < SPAN_NEAR - 2), high, laid
+            )
     gradient_ref[...] = jnp.zeros_like(gradient_ref)
     state, near, medium = (
         fields_of(state_ref, 9, depth),
@@ -730,6 +747,19 @@
     )
     load_higher = lax.ppermute(loads_again, "gx", down)
     load_rims = exchange(load_edges)
+    first_laid, later_laid, near = call_kernel(
+        adjoint_planes_body,
+        "adjoint_planes",
+        [
+            shape((2 * depth, SPAN_X, LANES), F32),
+            shape((4 * depth, SPAN_NEAR, LANES), F32),
+            shape((3 * depth, SPAN_NEAR, SPAN_Y), F32),
+        ],
+        [],
+        loads,
+        load_lower,
+        medium,
+    )
     (gradients,) = call_kernel(
         adjoint_body,
         "adjoint_run",
@@ -739,15 +769,15 @@
             pltpu.VMEM((4 * depth, SPAN_NEAR, SPAN_Y), F32),
             pltpu.VMEM((2 * depth, SPAN_X, SPAN_Y), F32),
             pltpu.VMEM((9 * depth, SPAN_NEAR, SPAN_Y), F32),
-            pltpu.VMEM((3 * depth, SPAN_NEAR, SPAN_Y), F32),
             pltpu.VMEM((LANES, LANES), F32),
         ],
-        loads,
+        first_laid,
+        later_laid,
         load_higher,
-        load_lower,
         load_rims,
         strains,
         medium,
+        near,
     )
     return (residuals, gradients.reshape(2, depth, rows_x, cols_y))
 

time: 59.6 us -> 59.6 us (level)
    pallas_call x7 -> x8, Pallas kernels: 8.38 us -> 8.37 us  [call_kernel(): pl.pallas_call(body, name=name, out_shape=outs, in_specs=[pl.BlockSpec(me...]
where the time goes in v9:
time: 59.6 us; the launch traced here: 59.1 us
  blocking collectives  20.9 us (35%)
  starting transfers between devices  19.7 us (33%)
  waiting for transfers between devices  9.27 us (16%)
  Pallas kernels  8.37 us (14%)
  between operations  0.8 us (1%)
    all_to_all x2, blocking collectives, exchange(): return lax.all_to_all(chunks, both, split_axis=0, concat_axis=0, tiled=True)  20.9 us
    all_to_all x2, starting transfers between devices, exchange(): return lax.all_to_all(chunks, both, split_axis=0, concat_axis=0, tiled=True)  9.89 us
    pallas_call x8, Pallas kernels, call_kernel(): pl.pallas_call(body, name=name, out_shape=outs, in_specs=[pl.BlockSpec(me...  8.37 us
    ppermute x1, waiting for transfers between devices, shards(): load_higher = lax.ppermute(loads_again, 'gx', down)  4.23 us
    ppermute x1, waiting for transfers between devices, shards(): higher = lax.ppermute(low, 'gx', down)  4.2 us
    ppermute x1, starting transfers between devices, shards(): lower = lax.ppermute(high, 'gx', up)  3.68 us
    ppermute x1, starting transfers between devices, shards(): load_lower = lax.ppermute(loads, 'gx', up)  3.59 us
    ppermute x1, starting transfers between devices, shards(): higher = lax.ppermute(low, 'gx', down)  1.29 us
  transfers between devices with their start and end apart: 6, of which 4 were waited for; matrix products, arithmetic and copies ran while one was open for 0% of the time, Pallas kernels for 1%

profile of v9, /device:TPU:0, one launch (start us, length us, event | category | flops | bytes accessed | tf_op | source)
XLA Modules:
  0.0 59.1 jit_solution(13826781514778774709)
XLA Ops:
  0.6 1.8 %pack_edges.1 = (f32[224,128]{1,0:T(8,128)}, f32[168,128]{1,0:T(8,128)}, f32[168,128]{1,0:T(8,128)}, f32[32,1,768]{2,1,0:T(1,128)}) custom-call(f32[144,128]{1,0:T(8,128)} %bitcast.20, f32[16,128]{1,0:T(8,128)} %bitcast.22, f32[16,128]{1,0:T(8,128)} %bitcast.23, f32[16,128]{1,0:T(8,128)} %bitcast.24, s32[1,64]{1,0:T(1,128)} %bitcast.25, f32[3,64]{1,0:T(4,128)} %refs_5_.1), custom_call_target="tpu_custom_call" | custom-call | tf_op jit(solution)/shard_map/pack_edges/pallas_call | solution.py:26
  2.4 0.0 copy-start.4
  2.5 0.0 copy-start.5
  2.5 7.3 %all-to-all-start = ((f32[32,1,768]{2,1,0:T(1,128)}), f32[32,1,768]{2,1,0:T(1,128)S(1)}, u32[]{:S(2)}, u32[]{:S(2)}) async-start(f32[32,1,768]{2,1,0:T(1,128)} %get-tuple-element.25), calls=%async_computation | async-start | bytes 196608 | tf_op jit(solution)/shard_map/all_to_all | solution.py:637
  9.8 3.7 %collective-permute-start = (f32[168,128]{1,0:T(8,128)}, f32[168,128]{1,0:T(8,128)S(1)}, u32[]{:S(2)}, u32[]{:S(2)}) collective-permute-start(f32[168,128]{1,0:T(8,128)} %get-tuple-element.23), channel_id=1, source_target_pairs={{0,8},{8,16},{16,24},{1,9},{9,17},{17,25},{2,10},{10,18},{18,26},{... | collective-permute-start | bytes 258056 | tf_op jit(solution)/shard_map/ppermute | solution.py:667
  13.5 0.0 copy-start.1
  13.5 1.3 %collective-permute-start.1 = (f32[168,128]{1,0:T(8,128)}, f32[168,128]{1,0:T(8,128)S(1)}, u32[]{:S(2)}, u32[]{:S(2)}) collective-permute-start(f32[168,128]{1,0:T(8,128)} %get-tuple-element.24), channel_id=1, source_target_pairs={{8,0},{16,8},{24,16},{9,1},{17,9},{25,17},{10,2},{18,10},{26,18},{... | collective-permute-start | bytes 258056 | tf_op jit(solution)/shard_map/ppermute | solution.py:668
  14.8 0.6 %segment_slots.1 = (s32[16,128]{1,0:T(8,128)S(1)}, s32[16,128]{1,0:T(8,128)S(1)}, bf16[128,2048]{1,0:T(8,128)(2,1)S(1)}, bf16[128,2048]{1,0:T(8,128)(2,1)S(1)}) custom-call(s32[16,128]{1,0:T(8,128)S(1)} %bitcast.18, s32[16,128]{1,0:T(8,128)S(1)} %bitcast.19), custom_call_target="tpu_custom_call" | custom-call | tf_op jit(solution)/shard_map/segment_slots/pallas_call | solution.py:26
  15.5 0.0 copy-start.3
  15.5 0.4 collective-permute-done.lower_ref
  15.9 4.2 %collective-permute-done.1.higher_ref = f32[168,128]{1,0:T(8,128)S(1)} collective-permute-done((f32[168,128]{1,0:T(8,128)}, f32[168,128]{1,0:T(8,128)S(1)}, u32[]{:S(2)}, u32[]{:S(2)}) %collective-permute-start.1) | collective-permute-done | bytes 86048 | tf_op jit(solution)/shard_map/ppermute | solution.py:668
  20.1 1.7 %forward_run.1 = (f32[128,128]{1,0:T(8,128)S(1)}, f32[288,128]{1,0:T(8,128)S(1)}, f32[12,16,256]{2,1,0:T(8,128)S(1)}) custom-call(f32[224,128]{1,0:T(8,128)S(1)} %copy-done, f32[168,128]{1,0:T(8,128)S(1)} %collective-permute-done.lower_ref, f32[168,128]{1,0:T(8,128)S(1)} %collective-permute-done.1.higher_ref, f32[32,1,768]{2,1,0:T(1,128)S(1)} %all-to-all-done.recv_ref, ...), custom_call_target="tpu_custom_call" | custom-call | tf_op jit(solution)/shard_map/forward_run/pallas_call | solution.py:26
  21.8 0.0 copy-start.2
  21.8 11.8 %all_to_all.20 = f32[32,4,128]{2,1,0:T(4,128)S(1)} all-to-all(f32[32,4,128]{2,1,0:T(4,128)S(1)} %bitcast.15), channel_id=1, replica_groups=mesh['gx'=4,'gy'=8] {'gx','gy'}, dimensions={0} | all-to-all | bytes 131072 | tf_op jit(solution)/shard_map/all_to_all | solution.py:637
  33.6 1.3 %channel_sums.1 = (f32[3,1024]{1,0:T(4,128)}, f32[128,128]{1,0:T(8,128)S(1)}) custom-call(f32[128,128]{1,0:T(8,128)S(1)} %bitcast.14, f32[3,1024]{1,0:T(4,128)S(1)} %copy-done.2), custom_call_target="tpu_custom_call" | custom-call | tf_op jit(solution)/shard_map/channel_sums/pallas_call | solution.py:26
  34.9 9.1 %all_to_all.21 = f32[32,4,128]{2,1,0:T(4,128)S(1)} all-to-all(f32[32,4,128]{2,1,0:T(4,128)S(1)} %bitcast.16), channel_id=1, replica_groups=mesh['gx'=4,'gy'=8] {'gx','gy'}, dimensions={0} | all-to-all | bytes 131072 | tf_op jit(solution)/shard_map/all_to_all | solution.py:637
  44.0 1.0 %segment_loads.1 = (f32[96,128]{1,0:T(8,128)S(1)}, f32[2,1,384]{2,1,0:T(1,128)S(1)}) custom-call(f32[128,128]{1,0:T(8,128)S(1)} %bitcast.13, s32[16,128]{1,0:T(8,128)S(1)} %get-tuple-element.26.slot_ref, s32[16,128]{1,0:T(8,128)S(1)} %get-tuple-element.27.row_ref, f32[2,2048]{1,0:T(2,128)S(1)} %copy-done.1, ...), custom_call_target="tpu_custom_call" | custom-call | tf_op jit(solution)/shard_map/segment_loads/pallas_call | solution.py:26
  45.1 0.7 %load_rims.1 = (f32[96,128]{1,0:T(8,128)S(1)}, f32[32,1,384]{2,1,0:T(1,128)}) custom-call(f32[96,128]{1,0:T(8,128)S(1)} %get-tuple-element.33.load_ref, f32[2,1,384]{2,1,0:T(1,128)S(1)} %get-tuple-element.37.side_ref), custom_call_target="tpu_custom_call" | custom-call | tf_op jit(solution)/shard_map/load_rims/pallas_call | solution.py:26
  45.7 2.6 %all-to-all-start.3 = ((f32[32,1,384]{2,1,0:T(1,128)}), f32[32,1,384]{2,1,0:T(1,128)S(1)}, u32[]{:S(2)}, u32[]{:S(2)}) async-start(f32[32,1,384]{2,1,0:T(1,128)} %get-tuple-element.39), calls=%async_computation.3 | async-start | bytes 98304 | tf_op jit(solution)/shard_map/all_to_all | solution.py:637
  48.3 3.6 %collective-permute-start.2 = (f32[96,128]{1,0:T(8,128)S(1)}, f32[96,128]{1,0:T(8,128)S(1)}, u32[]{:S(2)}, u32[]{:S(2)}) collective-permute-start(f32[96,128]{1,0:T(8,128)S(1)} %get-tuple-element.33.load_ref), channel_id=1, source_target_pairs={{0,8},{8,16},{16,24},{1,9},{9,17},{17,25},{2,10},{10,18},{18,26},{... | collective-permute-start | bytes 147464 | tf_op jit(solution)/shard_map/ppermute | solution.py:738
  51.9 1.3 %collective-permute-start.3 = (f32[96,128]{1,0:T(8,128)S(1)}, f32[96,128]{1,0:T(8,128)S(1)}, u32[]{:S(2)}, u32[]{:S(2)}) collective-permute-start(f32[96,128]{1,0:T(8,128)S(1)} %get-tuple-element.38), channel_id=1, source_target_pairs={{8,0},{16,8},{24,16},{9,1},{17,9},{25,17},{10,2},{18,10},{26,18},{... | collective-permute-start | bytes 147464 | tf_op jit(solution)/shard_map/ppermute | solution.py:748
  53.2 0.4 collective-permute-done.2.lower_ref
  53.7 4.2 %collective-permute-done.3.higher_ref = f32[96,128]{1,0:T(8,128)S(1)} collective-permute-done((f32[96,128]{1,0:T(8,128)S(1)}, f32[96,128]{1,0:T(8,128)S(1)}, u32[]{:S(2)}, u32[]{:S(2)}) %collective-permute-start.3) | collective-permute-done | bytes 49184 | tf_op jit(solution)/shard_map/ppermute | solution.py:748
  57.9 1.2 %adjoint_run.1 = f32[32,128]{1,0:T(8,128)} custom-call(f32[8,16,128]{2,1,0:T(8,128)S(1)} %get-tuple-element.35.first_laid_ref, f32[16,8,128]{2,1,0:T(8,128)S(1)} %get-tuple-element.36.later_laid_ref, f32[96,128]{1,0:T(8,128)S(1)} %collective-permute-done.3.higher_ref, f32[32,1,384]{2,1,0:T(1,128)S(1)} %all-to-all-done.3.recv_ref, ...), custom_call_target="tpu_custom_call" | custom-call | tf_op jit(solution)/shard_map/adjoint_run/pallas_call | solution.py:26
  (10 shorter events, 0.0 us)
Async XLA Ops:
  2.4 12.4 %copy-start.4 = (s32[2048,1]{0,1:T(1,128)S(1)}, s32[2048,1]{0,1:T(1,128)}, u32[]{:S(2)}) copy-start(s32[2048,1]{0,1:T(1,128)} %param.19) | copy-start | bytes 24580
  2.5 12.3 %copy-start.5 = (s32[2048]{0:T(1024)S(1)}, s32[2048]{0:T(1024)}, u32[]{:S(2)}) copy-start(s32[2048]{0:T(1024)} %param.17) | copy-start | bytes 24580
  2.5 17.6 %copy-start = (f32[224,128]{1,0:T(8,128)S(1)}, f32[224,128]{1,0:T(8,128)}, u32[]{:S(2)}) copy-start(f32[224,128]{1,0:T(8,128)} %get-tuple-element.22.fields_ref) | copy-start | bytes 344068
  2.5 17.6 %all-to-all-start = ((f32[32,1,768]{2,1,0:T(1,128)}), f32[32,1,768]{2,1,0:T(1,128)S(1)}, u32[]{:S(2)}, u32[]{:S(2)}) async-start(f32[32,1,768]{2,1,0:T(1,128)} %get-tuple-element.25), calls=%async_computation | async-start | bytes 196608 | tf_op jit(solution)/shard_map/all_to_all | solution.py:637
  9.8 6.1 %collective-permute-start = (f32[168,128]{1,0:T(8,128)}, f32[168,128]{1,0:T(8,128)S(1)}, u32[]{:S(2)}, u32[]{:S(2)}) collective-permute-start(f32[168,128]{1,0:T(8,128)} %get-tuple-element.23), channel_id=1, source_target_pairs={{0,8},{8,16},{16,24},{1,9},{9,17},{17,25},{2,10},{10,18},{18,26},{... | collective-permute-start | bytes 258056 | tf_op jit(solution)/shard_map/ppermute | solution.py:667
  13.5 6.6 %copy-start.1 = (f32[2,2048]{1,0:T(2,128)S(1)}, f32[2,2048]{1,0:T(2,128)}, u32[]{:S(2)}) copy-start(f32[2,2048]{1,0:T(2,128)} %weight_ref.3) | copy-start | bytes 49156
  13.5 6.6 %collective-permute-start.1 = (f32[168,128]{1,0:T(8,128)}, f32[168,128]{1,0:T(8,128)S(1)}, u32[]{:S(2)}, u32[]{:S(2)}) collective-permute-start(f32[168,128]{1,0:T(8,128)} %get-tuple-element.24), channel_id=1, source_target_pairs={{8,0},{16,8},{24,16},{9,1},{17,9},{25,17},{10,2},{18,10},{26,18},{... | collective-permute-start | bytes 258056 | tf_op jit(solution)/shard_map/ppermute | solution.py:668
  15.5 4.6 %copy-start.3 = (s32[2048]{0:T(1024)S(1)}, s32[2048]{0:T(1024)}, u32[]{:S(2)}) copy-start(s32[2048]{0:T(1024)} %param.20) | copy-start | bytes 24580
  21.8 11.9 %copy-start.2 = (f32[3,1024]{1,0:T(4,128)S(1)}, f32[3,1024]{1,0:T(4,128)}, u32[]{:S(2)}) copy-start(f32[3,1024]{1,0:T(4,128)} %observed_ref.1) | copy-start | bytes 36868
  45.7 12.2 %all-to-all-start.3 = ((f32[32,1,384]{2,1,0:T(1,128)}), f32[32,1,384]{2,1,0:T(1,128)S(1)}, u32[]{:S(2)}, u32[]{:S(2)}) async-start(f32[32,1,384]{2,1,0:T(1,128)} %get-tuple-element.39), calls=%async_computation.3 | async-start | bytes 98304 | tf_op jit(solution)/shard_map/all_to_all | solution.py:637
  48.3 5.3 %collective-permute-start.2 = (f32[96,128]{1,0:T(8,128)S(1)}, f32[96,128]{1,0:T(8,128)S(1)}, u32[]{:S(2)}, u32[]{:S(2)}) collective-permute-start(f32[96,128]{1,0:T(8,128)S(1)} %get-tuple-element.33.load_ref), channel_id=1, source_target_pairs={{0,8},{8,16},{16,24},{1,9},{9,17},{17,25},{2,10},{10,18},{18,26},{... | collective-permute-start | bytes 147464 | tf_op jit(solution)/shard_map/ppermute | solution.py:738
  51.9 6.0 %collective-permute-start.3 = (f32[96,128]{1,0:T(8,128)S(1)}, f32[96,128]{1,0:T(8,128)S(1)}, u32[]{:S(2)}, u32[]{:S(2)}) collective-permute-start(f32[96,128]{1,0:T(8,128)S(1)} %get-tuple-element.38), channel_id=1, source_target_pairs={{8,0},{16,8},{24,16},{9,1},{17,9},{25,17},{10,2},{18,10},{26,18},{... | collective-permute-start | bytes 147464 | tf_op jit(solution)/shard_map/ppermute | solution.py:748

commit v10 on v7

--- a/solution.py
+++ b/solution.py
@@ -113,13 +113,17 @@
     return jnp.where(inside, recv_ref[index], 0.0)
 
 
-def rim_rows(recv_ref, dx, turn_ref):
+def rim_rows(recv_ref, turn_ref):
     width = turn_ref.shape[1]
-    for dy, base in ((1, 0), (-1, LANES - RIM)):
-        chunk = arrived_chunk(recv_ref, dx, dy)
-        for column in range(RIM):
-            turn_ref[base + column : base + column + 1, :] = chunk[:, column * width : (column + 1) * width]
-    return turn_ref[...].T
+    turn_ref[...] = jnp.zeros_like(turn_ref)
+    blocks = ((0, 0), (1, 40), (-1, 80))
+    for dx, base in blocks:
+        for dy, first in ((1, base), (-1, (base - RIM) % LANES)):
+            chunk = arrived_chunk(recv_ref, dx, dy)
+            for column in range(RIM):
+                turn_ref[first + column : first + column + 1, :] = chunk[:, column * width : (column + 1) * width]
+    turned = turn_ref[...].T
+    return [pltpu.roll(turned, LANES - base, 1) if base else turned for _, base in blocks]
 
 
 def lay_planes(wide_ref, narrow_ref, lane, centre, higher, lower):
@@ -351,8 +355,7 @@
 ):
     depth = medium_ref.shape[0] // 3
     cells_row = depth * TILE_X
-    turn_ref[...] = jnp.zeros_like(turn_ref)
-    rims = [rim_rows(recv_ref, dx, turn_ref) for dx in (0, 1, -1)]
+    rims = rim_rows(recv_ref, turn_ref)
     height = fields_ref.shape[0] // TILE_X
     sides_ref[...] = jnp.zeros_like(sides_ref)
     for x in range(RIM):
@@ -513,7 +516,9 @@
     recv_ref,
     strain_ref,
     medium_ref,
+    residual_ref,
     gradient_ref,
+    residual_out_ref,
     first_ref,
     later_ref,
     velocity_ref,
@@ -522,13 +527,13 @@
     turn_ref,
 ):
     depth = medium_ref.shape[0] // 3
-    turn_ref[...] = jnp.zeros_like(turn_ref)
-    rims = [rim_rows(recv_ref, dx, turn_ref) for dx in (0, 1, -1)]
+    rims = rim_rows(recv_ref, turn_ref)
     lay_planes(first_ref, later_ref, 0, load_ref, higher_ref, lower_ref)
     lay_planes(first_ref, later_ref, LANES, *rims)
     for plane in range(3 * depth):
         near_ref[plane] = narrowed(medium_ref[plane])
     gradient_ref[...] = jnp.zeros_like(gradient_ref)
+    residual_out_ref[...] = residual_ref[...]
     state, near, medium = (
         fields_of(state_ref, 9, depth),
         fields_of(near_ref, 3, depth),
@@ -723,10 +728,10 @@
     load_lower = lax.ppermute(loads, "gx", up)
     load_higher = lax.ppermute(loads, "gx", down)
     load_rims = exchange(load_edges)
-    (gradients,) = call_kernel(
+    gradients, residuals = call_kernel(
         adjoint_body,
         "adjoint_run",
-        [shape((2 * cells_row, cols_y), F32)],
+        [shape((2 * cells_row, cols_y), F32), shape(observed_data.shape, F32)],
         [
             pltpu.VMEM((2 * depth, SPAN_X, SPAN_Y), F32),
             pltpu.VMEM((4 * depth, SPAN_NEAR, SPAN_Y), F32),
@@ -741,6 +746,7 @@
         load_rims,
         strains,
         medium,
+        residuals,
     )
     return (residuals, gradients.reshape(2, depth, rows_x, cols_y))
 

time: 59.6 us -> 59.5 us (level)
  no operation moved by 1% of the time
where the time goes in v10:
time: 59.5 us; the launch traced here: 59 us
  blocking collectives  20.9 us (35%)
  starting transfers between devices  19.7 us (33%)
  waiting for transfers between devices  9.3 us (16%)
  Pallas kernels  8.22 us (14%)
  between operations  0.8 us (1%)
    all_to_all x2, blocking collectives, exchange(): return lax.all_to_all(chunks, both, split_axis=0, concat_axis=0, tiled=True)  20.9 us
    all_to_all x2, starting transfers between devices, exchange(): return lax.all_to_all(chunks, both, split_axis=0, concat_axis=0, tiled=True)  9.88 us
    pallas_call x6, Pallas kernels, call_kernel(): pl.pallas_call(body, name=name, out_shape=outs, in_specs=[pl.BlockSpec(me...  8.22 us
    ppermute x1, waiting for transfers between devices, shards(): load_higher = lax.ppermute(loads, 'gx', down)  4.25 us
    ppermute x1, waiting for transfers between devices, shards(): higher = lax.ppermute(low, 'gx', down)  4.2 us
    ppermute x1, starting transfers between devices, shards(): lower = lax.ppermute(high, 'gx', up)  3.68 us
    ppermute x1, starting transfers between devices, shards(): load_lower = lax.ppermute(loads, 'gx', up)  3.59 us
    ppermute x1, starting transfers between devices, shards(): load_higher = lax.ppermute(loads, 'gx', down)  1.29 us
  transfers between devices with their start and end apart: 6, of which 4 were waited for; matrix products, arithmetic and copies ran while one was open for 0% of the time, Pallas kernels for 1%

profile of v10, /device:TPU:0, one launch (start us, length us, event | category | flops | bytes accessed | tf_op | source)
XLA Modules:
  0.0 59.0 jit_solution(7630974755997726352)
XLA Ops:
  0.6 1.8 %pack_edges.1 = (f32[224,128]{1,0:T(8,128)}, f32[168,128]{1,0:T(8,128)}, f32[168,128]{1,0:T(8,128)}, f32[32,1,768]{2,1,0:T(1,128)}) custom-call(f32[144,128]{1,0:T(8,128)} %bitcast.20, f32[16,128]{1,0:T(8,128)} %bitcast.21, f32[16,128]{1,0:T(8,128)} %bitcast.22, f32[16,128]{1,0:T(8,128)} %bitcast.23, s32[1,64]{1,0:T(1,128)} %bitcast.24, f32[3,64]{1,0:T(4,128)} %refs_5_.1), custom_call_target="tpu_custom_call" | custom-call | tf_op jit(solution)/shard_map/pack_edges/pallas_call | solution.py:26
  2.5 0.0 copy-start.4
  2.5 0.0 copy-start.5
  2.5 7.3 %all-to-all-start = ((f32[32,1,768]{2,1,0:T(1,128)}), f32[32,1,768]{2,1,0:T(1,128)S(1)}, u32[]{:S(2)}, u32[]{:S(2)}) async-start(f32[32,1,768]{2,1,0:T(1,128)} %get-tuple-element.22), calls=%async_computation | async-start | bytes 196608 | tf_op jit(solution)/shard_map/all_to_all | solution.py:623
  9.8 3.7 %collective-permute-start = (f32[168,128]{1,0:T(8,128)}, f32[168,128]{1,0:T(8,128)S(1)}, u32[]{:S(2)}, u32[]{:S(2)}) collective-permute-start(f32[168,128]{1,0:T(8,128)} %get-tuple-element.20), channel_id=1, source_target_pairs={{0,8},{8,16},{16,24},{1,9},{9,17},{17,25},{2,10},{10,18},{18,26},{... | collective-permute-start | bytes 258056 | tf_op jit(solution)/shard_map/ppermute | solution.py:653
  13.5 0.0 copy-start.1
  13.5 1.3 %collective-permute-start.1 = (f32[168,128]{1,0:T(8,128)}, f32[168,128]{1,0:T(8,128)S(1)}, u32[]{:S(2)}, u32[]{:S(2)}) collective-permute-start(f32[168,128]{1,0:T(8,128)} %get-tuple-element.21), channel_id=1, source_target_pairs={{8,0},{16,8},{24,16},{9,1},{17,9},{25,17},{10,2},{18,10},{26,18},{... | collective-permute-start | bytes 258056 | tf_op jit(solution)/shard_map/ppermute | solution.py:654
  14.8 0.6 %segment_slots.1 = (s32[16,128]{1,0:T(8,128)S(1)}, s32[16,128]{1,0:T(8,128)S(1)}, bf16[128,2048]{1,0:T(8,128)(2,1)S(1)}, bf16[128,2048]{1,0:T(8,128)(2,1)S(1)}) custom-call(s32[16,128]{1,0:T(8,128)S(1)} %bitcast.18, s32[16,128]{1,0:T(8,128)S(1)} %bitcast.19), custom_call_target="tpu_custom_call" | custom-call | tf_op jit(solution)/shard_map/segment_slots/pallas_call | solution.py:26
  15.5 0.0 copy-start.3
  15.5 0.4 collective-permute-done.lower_ref
  15.9 4.2 %collective-permute-done.1.higher_ref = f32[168,128]{1,0:T(8,128)S(1)} collective-permute-done((f32[168,128]{1,0:T(8,128)}, f32[168,128]{1,0:T(8,128)S(1)}, u32[]{:S(2)}, u32[]{:S(2)}) %collective-permute-start.1) | collective-permute-done | bytes 86048 | tf_op jit(solution)/shard_map/ppermute | solution.py:654
  20.1 0.0 all-to-all-done.recv_ref
  20.1 1.7 %forward_run.1 = (f32[128,128]{1,0:T(8,128)S(1)}, f32[288,128]{1,0:T(8,128)S(1)}, f32[12,16,256]{2,1,0:T(8,128)S(1)}) custom-call(f32[224,128]{1,0:T(8,128)S(1)} %copy-done, f32[168,128]{1,0:T(8,128)S(1)} %collective-permute-done.lower_ref, f32[168,128]{1,0:T(8,128)S(1)} %collective-permute-done.1.higher_ref, f32[32,1,768]{2,1,0:T(1,128)S(1)} %all-to-all-done.recv_ref, ...), custom_call_target="tpu_custom_call" | custom-call | tf_op jit(solution)/shard_map/forward_run/pallas_call | solution.py:26
  21.8 0.0 copy-start.2
  21.8 11.8 %all_to_all.20 = f32[32,4,128]{2,1,0:T(4,128)S(1)} all-to-all(f32[32,4,128]{2,1,0:T(4,128)S(1)} %bitcast.15), channel_id=1, replica_groups=mesh['gx'=4,'gy'=8] {'gx','gy'}, dimensions={0} | all-to-all | bytes 131072 | tf_op jit(solution)/shard_map/all_to_all | solution.py:623
  33.6 1.1 %channel_sums.1 = (f32[3,1024]{1,0:T(4,128)S(1)}, f32[128,128]{1,0:T(8,128)S(1)}) custom-call(f32[128,128]{1,0:T(8,128)S(1)} %bitcast.14, f32[3,1024]{1,0:T(4,128)S(1)} %copy-done.2), custom_call_target="tpu_custom_call" | custom-call | tf_op jit(solution)/shard_map/channel_sums/pallas_call | solution.py:26
  34.8 9.1 %all_to_all.21 = f32[32,4,128]{2,1,0:T(4,128)S(1)} all-to-all(f32[32,4,128]{2,1,0:T(4,128)S(1)} %bitcast.16), channel_id=1, replica_groups=mesh['gx'=4,'gy'=8] {'gx','gy'}, dimensions={0} | all-to-all | bytes 131072 | tf_op jit(solution)/shard_map/all_to_all | solution.py:623
  43.9 1.7 %segment_loads.1 = (f32[96,128]{1,0:T(8,128)S(1)}, f32[32,1,384]{2,1,0:T(1,128)}) custom-call(f32[128,128]{1,0:T(8,128)S(1)} %bitcast.13, s32[16,128]{1,0:T(8,128)S(1)} %get-tuple-element.23.slot_ref, s32[16,128]{1,0:T(8,128)S(1)} %get-tuple-element.24.row_ref, f32[2,2048]{1,0:T(2,128)S(1)} %copy-done.1, bf16[128,2048]{1,0:T(8,128)(2,1)S(1)} %get-tuple-element.25.cover_ref, ...), custom_call_target="tpu_custom_call" | custom-call | tf_op jit(solution)/shard_map/segment_loads/pallas_call | solution.py:26
  45.5 2.6 %all-to-all-start.3 = ((f32[32,1,384]{2,1,0:T(1,128)}), f32[32,1,384]{2,1,0:T(1,128)S(1)}, u32[]{:S(2)}, u32[]{:S(2)}) async-start(f32[32,1,384]{2,1,0:T(1,128)} %get-tuple-element.30), calls=%async_computation.3 | async-start | bytes 98304 | tf_op jit(solution)/shard_map/all_to_all | solution.py:623
  48.1 3.6 %collective-permute-start.3 = (f32[96,128]{1,0:T(8,128)S(1)}, f32[96,128]{1,0:T(8,128)S(1)}, u32[]{:S(2)}, u32[]{:S(2)}) collective-permute-start(f32[96,128]{1,0:T(8,128)S(1)} %get-tuple-element.29.load_ref), channel_id=1, source_target_pairs={{0,8},{8,16},{16,24},{1,9},{9,17},{17,25},{2,10},{10,18},{18,26},{... | collective-permute-start | bytes 147464 | tf_op jit(solution)/shard_map/ppermute | solution.py:728
  51.7 1.3 %collective-permute-start.2 = (f32[96,128]{1,0:T(8,128)S(1)}, f32[96,128]{1,0:T(8,128)S(1)}, u32[]{:S(2)}, u32[]{:S(2)}) collective-permute-start(f32[96,128]{1,0:T(8,128)S(1)} %get-tuple-element.29.load_ref), channel_id=1, source_target_pairs={{8,0},{16,8},{24,16},{9,1},{17,9},{25,17},{10,2},{18,10},{26,18},{... | collective-permute-start | bytes 147464 | tf_op jit(solution)/shard_map/ppermute | solution.py:729
  53.0 0.4 collective-permute-done.3.lower_ref
  53.5 4.3 %collective-permute-done.2.higher_ref = f32[96,128]{1,0:T(8,128)S(1)} collective-permute-done((f32[96,128]{1,0:T(8,128)S(1)}, f32[96,128]{1,0:T(8,128)S(1)}, u32[]{:S(2)}, u32[]{:S(2)}) %collective-permute-start.2) | collective-permute-done | bytes 49184 | tf_op jit(solution)/shard_map/ppermute | solution.py:729
  57.7 1.3 %adjoint_run.1 = (f32[32,128]{1,0:T(8,128)}, f32[3,1024]{1,0:T(4,128)}) custom-call(f32[96,128]{1,0:T(8,128)S(1)} %get-tuple-element.29.load_ref, f32[96,128]{1,0:T(8,128)S(1)} %collective-permute-done.2.higher_ref, f32[96,128]{1,0:T(8,128)S(1)} %collective-permute-done.3.lower_ref, f32[32,1,384]{2,1,0:T(1,128)S(1)} %all-to-all-done.3.recv_ref, ...), custom_call_target="tpu_custom_call" | custom-call | tf_op jit(solution)/shard_map/adjoint_run/pallas_call | solution.py:26
  (8 shorter events, 0.0 us)
Async XLA Ops:
  2.5 12.3 %copy-start.4 = (s32[2048,1]{0,1:T(1,128)S(1)}, s32[2048,1]{0,1:T(1,128)}, u32[]{:S(2)}) copy-start(s32[2048,1]{0,1:T(1,128)} %param.19) | copy-start | bytes 24580
  2.5 12.3 %copy-start.5 = (s32[2048]{0:T(1024)S(1)}, s32[2048]{0:T(1024)}, u32[]{:S(2)}) copy-start(s32[2048]{0:T(1024)} %param.17) | copy-start | bytes 24580
  2.5 17.6 %copy-start = (f32[224,128]{1,0:T(8,128)S(1)}, f32[224,128]{1,0:T(8,128)}, u32[]{:S(2)}) copy-start(f32[224,128]{1,0:T(8,128)} %get-tuple-element.19.fields_ref) | copy-start | bytes 344068
  2.5 17.6 %all-to-all-start = ((f32[32,1,768]{2,1,0:T(1,128)}), f32[32,1,768]{2,1,0:T(1,128)S(1)}, u32[]{:S(2)}, u32[]{:S(2)}) async-start(f32[32,1,768]{2,1,0:T(1,128)} %get-tuple-element.22), calls=%async_computation | async-start | bytes 196608 | tf_op jit(solution)/shard_map/all_to_all | solution.py:623
  9.8 6.1 %collective-permute-start = (f32[168,128]{1,0:T(8,128)}, f32[168,128]{1,0:T(8,128)S(1)}, u32[]{:S(2)}, u32[]{:S(2)}) collective-permute-start(f32[168,128]{1,0:T(8,128)} %get-tuple-element.20), channel_id=1, source_target_pairs={{0,8},{8,16},{16,24},{1,9},{9,17},{17,25},{2,10},{10,18},{18,26},{... | collective-permute-start | bytes 258056 | tf_op jit(solution)/shard_map/ppermute | solution.py:653
  13.5 6.6 %copy-start.1 = (f32[2,2048]{1,0:T(2,128)S(1)}, f32[2,2048]{1,0:T(2,128)}, u32[]{:S(2)}) copy-start(f32[2,2048]{1,0:T(2,128)} %weight_ref.3) | copy-start | bytes 49156
  13.5 6.6 %collective-permute-start.1 = (f32[168,128]{1,0:T(8,128)}, f32[168,128]{1,0:T(8,128)S(1)}, u32[]{:S(2)}, u32[]{:S(2)}) collective-permute-start(f32[168,128]{1,0:T(8,128)} %get-tuple-element.21), channel_id=1, source_target_pairs={{8,0},{16,8},{24,16},{9,1},{17,9},{25,17},{10,2},{18,10},{26,18},{... | collective-permute-start | bytes 258056 | tf_op jit(solution)/shard_map/ppermute | solution.py:654
  15.5 4.6 %copy-start.3 = (s32[2048]{0:T(1024)S(1)}, s32[2048]{0:T(1024)}, u32[]{:S(2)}) copy-start(s32[2048]{0:T(1024)} %param.20) | copy-start | bytes 24580
  21.8 11.9 %copy-start.2 = (f32[3,1024]{1,0:T(4,128)S(1)}, f32[3,1024]{1,0:T(4,128)}, u32[]{:S(2)}) copy-start(f32[3,1024]{1,0:T(4,128)} %observed_ref.1) | copy-start | bytes 36868
  45.5 12.2 %all-to-all-start.3 = ((f32[32,1,384]{2,1,0:T(1,128)}), f32[32,1,384]{2,1,0:T(1,128)S(1)}, u32[]{:S(2)}, u32[]{:S(2)}) async-start(f32[32,1,384]{2,1,0:T(1,128)} %get-tuple-element.30), calls=%async_computation.3 | async-start | bytes 98304 | tf_op jit(solution)/shard_map/all_to_all | solution.py:623
  48.1 5.3 %collective-permute-start.3 = (f32[96,128]{1,0:T(8,128)S(1)}, f32[96,128]{1,0:T(8,128)S(1)}, u32[]{:S(2)}, u32[]{:S(2)}) collective-permute-start(f32[96,128]{1,0:T(8,128)S(1)} %get-tuple-element.29.load_ref), channel_id=1, source_target_pairs={{0,8},{8,16},{16,24},{1,9},{9,17},{17,25},{2,10},{10,18},{18,26},{... | collective-permute-start | bytes 147464 | tf_op jit(solution)/shard_map/ppermute | solution.py:728
  51.7 6.0 %collective-permute-start.2 = (f32[96,128]{1,0:T(8,128)S(1)}, f32[96,128]{1,0:T(8,128)S(1)}, u32[]{:S(2)}, u32[]{:S(2)}) collective-permute-start(f32[96,128]{1,0:T(8,128)S(1)} %get-tuple-element.29.load_ref), channel_id=1, source_target_pairs={{8,0},{16,8},{24,16},{9,1},{17,9},{25,17},{10,2},{18,10},{26,18},{... | collective-permute-start | bytes 147464 | tf_op jit(solution)/shard_map/ppermute | solution.py:729

commit v11 on v8

--- a/solution.py
+++ b/solution.py
@@ -464,12 +464,14 @@
     weight_ref,
     cover_ref,
     place_ref,
+    strain_ref,
     load_ref,
     side_ref,
     spread_ref,
 ):
-    cells_row = load_ref.shape[0] // 6
-    stack_rows = load_ref.shape[0]
+    stack_rows = load_ref.shape[0] - strain_ref.shape[0]
+    cells_row = stack_rows // 6
+    load_ref[stack_rows:, :] = strain_ref[...]
     arrived = jnp.concatenate(two_pieces(arrived_ref[...]), axis=0).astype(BF16)
     slots_down = iota((LANES, LANES), 0) >> 2
     rows_down = packed_iota(cells_row)
@@ -499,12 +501,12 @@
         for column in range(RIM):
             lanes = slice(column * LANES, column * LANES + stack_rows)
             side_ref[side, 0:1, lanes] = edges[base + column : base + column + 1, :]
-    load_ref[...] = sum_halves(times_turned(spread_ref[...], cover_ref[...]))
+    load_ref[0:stack_rows, :] = sum_halves(times_turned(spread_ref[...], cover_ref[...]))
 
 
 def rims_body(load_ref, side_ref, copy_ref, out_ref, sent_sides):
     sides = start_sides(side_ref, out_ref, sent_sides)
-    copy_ref[...] = load_ref[...]
+    copy_ref[...] = load_ref[0 : copy_ref.shape[0], :]
     wait_sides(sides)
 
 
@@ -515,7 +517,9 @@
     recv_ref,
     strain_ref,
     medium_ref,
+    residual_ref,
     gradient_ref,
+    residual_out_ref,
     first_ref,
     later_ref,
     velocity_ref,
@@ -531,6 +535,7 @@
     for plane in range(3 * depth):
         near_ref[plane] = narrowed(medium_ref[plane])
     gradient_ref[...] = jnp.zeros_like(gradient_ref)
+    residual_out_ref[...] = residual_ref[...]
     state, near, medium = (
         fields_of(state_ref, 9, depth),
         fields_of(near_ref, 3, depth),
@@ -709,7 +714,7 @@
     loads, sides = call_kernel(
         load_body,
         "segment_loads",
-        [load_rows, load_sides],
+        [shape((24 * cells_row, cols_y), F32), load_sides],
         [pltpu.VMEM((12 * cells_row, part_count), BF16)],
         to_owners(reply),
         slot,
@@ -717,6 +722,7 @@
         segment_weight,
         cover,
         place,
+        strains,
     )
     load_lower = lax.ppermute(loads, "gx", up)
     loads_again, load_edges = call_kernel(
@@ -730,10 +736,10 @@
     )
     load_higher = lax.ppermute(loads_again, "gx", down)
     load_rims = exchange(load_edges)
-    (gradients,) = call_kernel(
+    gradients, residuals = call_kernel(
         adjoint_body,
         "adjoint_run",
-        [shape((2 * cells_row, cols_y), F32)],
+        [shape((2 * cells_row, cols_y), F32), shape(observed_data.shape, F32)],
         [
             pltpu.VMEM((2 * depth, SPAN_X, SPAN_Y), F32),
             pltpu.VMEM((4 * depth, SPAN_NEAR, SPAN_Y), F32),
@@ -748,6 +754,7 @@
         load_rims,
         strains,
         medium,
+        residuals,
     )
     return (residuals, gradients.reshape(2, depth, rows_x, cols_y))
 

time: 59.6 us -> 59.7 us (level)
  waiting for transfers between devices: 9.3 us -> 10.6 us
  starting transfers between devices: 19.7 us -> 18.7 us
    all_to_all x2, waiting for transfers between devices: 0.01 us -> 1.29 us  [exchange(): return lax.all_to_all(chunks, both, split_axis=0, concat_axis=0, tiled=True)]
    ppermute x1, starting transfers between devices: 3.59 us -> 2.52 us  [shards(): load_lower = lax.ppermute(loads, 'gx', up)]
  transfers between devices with their start and end apart: 6 -> 6, of which waited for: 4 -> 4; matrix products, arithmetic and copies ran while one was open for 0% -> 0% of each run, Pallas kernels for 1% -> 2%
where the time goes in v11:
time: 59.7 us; the launch traced here: 59.2 us
  blocking collectives  20.9 us (35%)
  starting transfers between devices  18.7 us (31%)
  waiting for transfers between devices  10.6 us (18%)
  Pallas kernels  8.14 us (14%)
  between operations  0.8 us (1%)
    all_to_all x2, blocking collectives, exchange(): return lax.all_to_all(chunks, both, split_axis=0, concat_axis=0, tiled=True)  20.9 us
    all_to_all x2, starting transfers between devices, exchange(): return lax.all_to_all(chunks, both, split_axis=0, concat_axis=0, tiled=True)  9.89 us
    pallas_call x7, Pallas kernels, call_kernel(): pl.pallas_call(body, name=name, out_shape=outs, in_specs=[pl.BlockSpec(me...  8.14 us
    ppermute x1, waiting for transfers between devices, shards(): load_higher = lax.ppermute(loads_again, 'gx', down)  4.75 us
    ppermute x1, waiting for transfers between devices, shards(): higher = lax.ppermute(low, 'gx', down)  4.2 us
    ppermute x1, starting transfers between devices, shards(): lower = lax.ppermute(high, 'gx', up)  3.68 us
    ppermute x1, starting transfers between devices, shards(): load_lower = lax.ppermute(loads, 'gx', up)  2.52 us
    ppermute x1, starting transfers between devices, shards(): higher = lax.ppermute(low, 'gx', down)  1.29 us
  transfers between devices with their start and end apart: 6, of which 4 were waited for; matrix products, arithmetic and copies ran while one was open for 0% of the time, Pallas kernels for 2%

profile of v11, /device:TPU:0, one launch (start us, length us, event | category | flops | bytes accessed | tf_op | source)
XLA Modules:
  0.0 59.2 jit_solution(18067359484081809552)
XLA Ops:
  0.6 1.8 %pack_edges.1 = (f32[224,128]{1,0:T(8,128)}, f32[168,128]{1,0:T(8,128)}, f32[168,128]{1,0:T(8,128)}, f32[32,1,768]{2,1,0:T(1,128)}) custom-call(f32[144,128]{1,0:T(8,128)} %bitcast.20, f32[16,128]{1,0:T(8,128)} %bitcast.21, f32[16,128]{1,0:T(8,128)} %bitcast.22, f32[16,128]{1,0:T(8,128)} %bitcast.23, s32[1,64]{1,0:T(1,128)} %bitcast.24, f32[3,64]{1,0:T(4,128)} %refs_5_.1), custom_call_target="tpu_custom_call" | custom-call | tf_op jit(solution)/shard_map/pack_edges/pallas_call | solution.py:26
  2.4 0.0 copy-start.4
  2.5 0.0 copy-start.5
  2.5 7.3 %all-to-all-start = ((f32[32,1,768]{2,1,0:T(1,128)}), f32[32,1,768]{2,1,0:T(1,128)S(1)}, u32[]{:S(2)}, u32[]{:S(2)}) async-start(f32[32,1,768]{2,1,0:T(1,128)} %get-tuple-element.24), calls=%async_computation | async-start | bytes 196608 | tf_op jit(solution)/shard_map/all_to_all | solution.py:625
  9.8 3.7 %collective-permute-start = (f32[168,128]{1,0:T(8,128)}, f32[168,128]{1,0:T(8,128)S(1)}, u32[]{:S(2)}, u32[]{:S(2)}) collective-permute-start(f32[168,128]{1,0:T(8,128)} %get-tuple-element.22), channel_id=1, source_target_pairs={{0,8},{8,16},{16,24},{1,9},{9,17},{17,25},{2,10},{10,18},{18,26},{... | collective-permute-start | bytes 258056 | tf_op jit(solution)/shard_map/ppermute | solution.py:655
  13.5 0.0 copy-start.1
  13.5 1.3 %collective-permute-start.1 = (f32[168,128]{1,0:T(8,128)}, f32[168,128]{1,0:T(8,128)S(1)}, u32[]{:S(2)}, u32[]{:S(2)}) collective-permute-start(f32[168,128]{1,0:T(8,128)} %get-tuple-element.23), channel_id=1, source_target_pairs={{8,0},{16,8},{24,16},{9,1},{17,9},{25,17},{10,2},{18,10},{26,18},{... | collective-permute-start | bytes 258056 | tf_op jit(solution)/shard_map/ppermute | solution.py:656
  14.8 0.6 %segment_slots.1 = (s32[16,128]{1,0:T(8,128)S(1)}, s32[16,128]{1,0:T(8,128)S(1)}, bf16[128,2048]{1,0:T(8,128)(2,1)S(1)}, bf16[128,2048]{1,0:T(8,128)(2,1)S(1)}) custom-call(s32[16,128]{1,0:T(8,128)S(1)} %bitcast.18, s32[16,128]{1,0:T(8,128)S(1)} %bitcast.19), custom_call_target="tpu_custom_call" | custom-call | tf_op jit(solution)/shard_map/segment_slots/pallas_call | solution.py:26
  15.5 0.0 copy-start.3
  15.5 0.4 collective-permute-done.lower_ref
  15.9 4.2 %collective-permute-done.1.higher_ref = f32[168,128]{1,0:T(8,128)S(1)} collective-permute-done((f32[168,128]{1,0:T(8,128)}, f32[168,128]{1,0:T(8,128)S(1)}, u32[]{:S(2)}, u32[]{:S(2)}) %collective-permute-start.1) | collective-permute-done | bytes 86048 | tf_op jit(solution)/shard_map/ppermute | solution.py:656
  20.1 1.7 %forward_run.1 = (f32[128,128]{1,0:T(8,128)S(1)}, f32[288,128]{1,0:T(8,128)S(1)}, f32[12,16,256]{2,1,0:T(8,128)S(1)}) custom-call(f32[224,128]{1,0:T(8,128)S(1)} %copy-done, f32[168,128]{1,0:T(8,128)S(1)} %collective-permute-done.lower_ref, f32[168,128]{1,0:T(8,128)S(1)} %collective-permute-done.1.higher_ref, f32[32,1,768]{2,1,0:T(1,128)S(1)} %all-to-all-done.recv_ref, ...), custom_call_target="tpu_custom_call" | custom-call | tf_op jit(solution)/shard_map/forward_run/pallas_call | solution.py:26
  21.8 0.0 copy-start.2
  21.8 11.8 %all_to_all.20 = f32[32,4,128]{2,1,0:T(4,128)S(1)} all-to-all(f32[32,4,128]{2,1,0:T(4,128)S(1)} %bitcast.15), channel_id=1, replica_groups=mesh['gx'=4,'gy'=8] {'gx','gy'}, dimensions={0} | all-to-all | bytes 131072 | tf_op jit(solution)/shard_map/all_to_all | solution.py:625
  33.6 1.1 %channel_sums.1 = (f32[3,1024]{1,0:T(4,128)S(1)}, f32[128,128]{1,0:T(8,128)S(1)}) custom-call(f32[128,128]{1,0:T(8,128)S(1)} %bitcast.14, f32[3,1024]{1,0:T(4,128)S(1)} %copy-done.2), custom_call_target="tpu_custom_call" | custom-call | tf_op jit(solution)/shard_map/channel_sums/pallas_call | solution.py:26
  34.7 9.1 %all_to_all.21 = f32[32,4,128]{2,1,0:T(4,128)S(1)} all-to-all(f32[32,4,128]{2,1,0:T(4,128)S(1)} %bitcast.16), channel_id=1, replica_groups=mesh['gx'=4,'gy'=8] {'gx','gy'}, dimensions={0} | all-to-all | bytes 131072 | tf_op jit(solution)/shard_map/all_to_all | solution.py:625
  43.8 1.0 %segment_loads.1 = (f32[384,128]{1,0:T(8,128)S(1)}, f32[2,1,384]{2,1,0:T(1,128)S(1)}) custom-call(f32[128,128]{1,0:T(8,128)S(1)} %bitcast.13, s32[16,128]{1,0:T(8,128)S(1)} %get-tuple-element.25.slot_ref, s32[16,128]{1,0:T(8,128)S(1)} %get-tuple-element.26.row_ref, f32[2,2048]{1,0:T(2,128)S(1)} %copy-done.1, ...), custom_call_target="tpu_custom_call" | custom-call | tf_op jit(solution)/shard_map/segment_loads/pallas_call | solution.py:26
  44.9 2.5 %collective-permute-start.3 = (f32[384,128]{1,0:T(8,128)S(1)}, f32[384,128]{1,0:T(8,128)S(1)}, u32[]{:S(2)}, u32[]{:S(2)}) collective-permute-start(f32[384,128]{1,0:T(8,128)S(1)} %get-tuple-element.32.load_ref), channel_id=1, source_target_pairs={{0,8},{8,16},{16,24},{1,9},{9,17},{17,25},{2,10},{10,18},{18,26},{... | collective-permute-start | bytes 589832 | tf_op jit(solution)/shard_map/ppermute | solution.py:727
  47.4 0.7 %load_rims.1 = (f32[96,128]{1,0:T(8,128)S(1)}, f32[32,1,384]{2,1,0:T(1,128)}) custom-call(f32[384,128]{1,0:T(8,128)S(1)} %get-tuple-element.32.load_ref, f32[2,1,384]{2,1,0:T(1,128)S(1)} %get-tuple-element.33.side_ref), custom_call_target="tpu_custom_call" | custom-call | tf_op jit(solution)/shard_map/load_rims/pallas_call | solution.py:26
  48.1 2.6 %all-to-all-start.3 = ((f32[32,1,384]{2,1,0:T(1,128)}), f32[32,1,384]{2,1,0:T(1,128)S(1)}, u32[]{:S(2)}, u32[]{:S(2)}) async-start(f32[32,1,384]{2,1,0:T(1,128)} %get-tuple-element.35), calls=%async_computation.3 | async-start | bytes 98304 | tf_op jit(solution)/shard_map/all_to_all | solution.py:625
  50.7 1.3 %collective-permute-start.2 = (f32[96,128]{1,0:T(8,128)S(1)}, f32[96,128]{1,0:T(8,128)S(1)}, u32[]{:S(2)}, u32[]{:S(2)}) collective-permute-start(f32[96,128]{1,0:T(8,128)S(1)} %get-tuple-element.34), channel_id=1, source_target_pairs={{8,0},{16,8},{24,16},{9,1},{17,9},{25,17},{10,2},{18,10},{26,18},{... | collective-permute-start | bytes 147464 | tf_op jit(solution)/shard_map/ppermute | solution.py:737
  52.0 4.7 %collective-permute-done.2.higher_ref = f32[96,128]{1,0:T(8,128)S(1)} collective-permute-done((f32[96,128]{1,0:T(8,128)S(1)}, f32[96,128]{1,0:T(8,128)S(1)}, u32[]{:S(2)}, u32[]{:S(2)}) %collective-permute-start.2) | collective-permute-done | bytes 49184 | tf_op jit(solution)/shard_map/ppermute | solution.py:737
  56.7 1.3 %all-to-all-done.3.recv_ref = f32[32,1,384]{2,1,0:T(1,128)S(1)} async-done(((f32[32,1,384]{2,1,0:T(1,128)}), f32[32,1,384]{2,1,0:T(1,128)S(1)}, u32[]{:S(2)}, u32[]{:S(2)}) %all-to-all-start.3) | async-done | bytes 49184 | tf_op jit(solution)/shard_map/all_to_all | solution.py:625
  58.0 1.2 %adjoint_run.1 = (f32[32,128]{1,0:T(8,128)}, f32[3,1024]{1,0:T(4,128)}) custom-call(f32[384,128]{1,0:T(8,128)S(1)} %get-tuple-element.32.load_ref, f32[96,128]{1,0:T(8,128)S(1)} %collective-permute-done.2.higher_ref, f32[384,128]{1,0:T(8,128)S(1)} %collective-permute-done.3.lower_ref, f32[32,1,384]{2,1,0:T(1,128)S(1)} %all-to-all-done.3.recv_ref, ...), custom_call_target="tpu_custom_call" | custom-call | tf_op jit(solution)/shard_map/adjoint_run/pallas_call | solution.py:26
  (9 shorter events, 0.0 us)
Async XLA Ops:
  2.4 12.4 %copy-start.4 = (s32[2048,1]{0,1:T(1,128)S(1)}, s32[2048,1]{0,1:T(1,128)}, u32[]{:S(2)}) copy-start(s32[2048,1]{0,1:T(1,128)} %param.19) | copy-start | bytes 24580
  2.5 12.3 %copy-start.5 = (s32[2048]{0:T(1024)S(1)}, s32[2048]{0:T(1024)}, u32[]{:S(2)}) copy-start(s32[2048]{0:T(1024)} %param.17) | copy-start | bytes 24580
  2.5 17.6 %copy-start = (f32[224,128]{1,0:T(8,128)S(1)}, f32[224,128]{1,0:T(8,128)}, u32[]{:S(2)}) copy-start(f32[224,128]{1,0:T(8,128)} %get-tuple-element.21.fields_ref) | copy-start | bytes 344068
  2.5 17.6 %all-to-all-start = ((f32[32,1,768]{2,1,0:T(1,128)}), f32[32,1,768]{2,1,0:T(1,128)S(1)}, u32[]{:S(2)}, u32[]{:S(2)}) async-start(f32[32,1,768]{2,1,0:T(1,128)} %get-tuple-element.24), calls=%async_computation | async-start | bytes 196608 | tf_op jit(solution)/shard_map/all_to_all | solution.py:625
  9.8 6.1 %collective-permute-start = (f32[168,128]{1,0:T(8,128)}, f32[168,128]{1,0:T(8,128)S(1)}, u32[]{:S(2)}, u32[]{:S(2)}) collective-permute-start(f32[168,128]{1,0:T(8,128)} %get-tuple-element.22), channel_id=1, source_target_pairs={{0,8},{8,16},{16,24},{1,9},{9,17},{17,25},{2,10},{10,18},{18,26},{... | collective-permute-start | bytes 258056 | tf_op jit(solution)/shard_map/ppermute | solution.py:655
  13.5 6.6 %copy-start.1 = (f32[2,2048]{1,0:T(2,128)S(1)}, f32[2,2048]{1,0:T(2,128)}, u32[]{:S(2)}) copy-start(f32[2,2048]{1,0:T(2,128)} %weight_ref.3) | copy-start | bytes 49156
  13.5 6.6 %collective-permute-start.1 = (f32[168,128]{1,0:T(8,128)}, f32[168,128]{1,0:T(8,128)S(1)}, u32[]{:S(2)}, u32[]{:S(2)}) collective-permute-start(f32[168,128]{1,0:T(8,128)} %get-tuple-element.23), channel_id=1, source_target_pairs={{8,0},{16,8},{24,16},{9,1},{17,9},{25,17},{10,2},{18,10},{26,18},{... | collective-permute-start | bytes 258056 | tf_op jit(solution)/shard_map/ppermute | solution.py:656
  15.5 4.6 %copy-start.3 = (s32[2048]{0:T(1024)S(1)}, s32[2048]{0:T(1024)}, u32[]{:S(2)}) copy-start(s32[2048]{0:T(1024)} %param.20) | copy-start | bytes 24580
  21.8 11.9 %copy-start.2 = (f32[3,1024]{1,0:T(4,128)S(1)}, f32[3,1024]{1,0:T(4,128)}, u32[]{:S(2)}) copy-start(f32[3,1024]{1,0:T(4,128)} %observed_ref.1) | copy-start | bytes 36868
  44.9 13.1 %collective-permute-start.3 = (f32[384,128]{1,0:T(8,128)S(1)}, f32[384,128]{1,0:T(8,128)S(1)}, u32[]{:S(2)}, u32[]{:S(2)}) collective-permute-start(f32[384,128]{1,0:T(8,128)S(1)} %get-tuple-element.32.load_ref), channel_id=1, source_target_pairs={{0,8},{8,16},{16,24},{1,9},{9,17},{17,25},{2,10},{10,18},{18,26},{... | collective-permute-start | bytes 589832 | tf_op jit(solution)/shard_map/ppermute | solution.py:727
  48.1 9.9 %all-to-all-start.3 = ((f32[32,1,384]{2,1,0:T(1,128)}), f32[32,1,384]{2,1,0:T(1,128)S(1)}, u32[]{:S(2)}, u32[]{:S(2)}) async-start(f32[32,1,384]{2,1,0:T(1,128)} %get-tuple-element.35), calls=%async_computation.3 | async-start | bytes 98304 | tf_op jit(solution)/shard_map/all_to_all | solution.py:625
  50.7 6.0 %collective-permute-start.2 = (f32[96,128]{1,0:T(8,128)S(1)}, f32[96,128]{1,0:T(8,128)S(1)}, u32[]{:S(2)}, u32[]{:S(2)}) collective-permute-start(f32[96,128]{1,0:T(8,128)S(1)} %get-tuple-element.34), channel_id=1, source_target_pairs={{8,0},{16,8},{24,16},{9,1},{17,9},{25,17},{10,2},{18,10},{26,18},{... | collective-permute-start | bytes 147464 | tf_op jit(solution)/shard_map/ppermute | solution.py:737

commit v12 on v10

--- a/solution.py
+++ b/solution.py
@@ -114,16 +114,16 @@
 
 
 def rim_rows(recv_ref, turn_ref):
-    width = turn_ref.shape[1]
+    width = turn_ref.shape[2]
     turn_ref[...] = jnp.zeros_like(turn_ref)
-    blocks = ((0, 0), (1, 40), (-1, 80))
-    for dx, base in blocks:
-        for dy, first in ((1, base), (-1, (base - RIM) % LANES)):
+    for block, dx in enumerate((0, 1, -1)):
+        for dy, first in ((1, 0), (-1, LANES - RIM)):
             chunk = arrived_chunk(recv_ref, dx, dy)
             for column in range(RIM):
-                turn_ref[first + column : first + column + 1, :] = chunk[:, column * width : (column + 1) * width]
-    turned = turn_ref[...].T
-    return [pltpu.roll(turned, LANES - base, 1) if base else turned for _, base in blocks]
+                turn_ref[block, first + column : first + column + 1, :] = chunk[
+                    :, column * width : (column + 1) * width
+                ]
+    return [turn_ref[block].T for block in range(3)]
 
 
 def lay_planes(wide_ref, narrow_ref, lane, centre, higher, lower):
@@ -247,7 +247,7 @@
         pltpu.make_async_copy(source, target, arrived.at[number])
         for number, (source, target) in enumerate(zip(inputs, targets + [cells_ref, wavelet_ref]))
     ]
-    for copy in copies:
+    for copy in copies[4:] + copies[:4]:
         copy.start()
     copies[4].wait()
     copies[5].wait()
@@ -268,6 +268,10 @@
     for number in range(3, 6):
         rows = slice(number * cells_row, (number + 1) * cells_row)
         fields_ref[rows, :] = fields_ref[rows, :] + maps[:cells_row]
+    rows = fields_ref[...]
+    spare = 2 * LANES - rows.shape[0]
+    edge_columns(jnp.concatenate([rows, jnp.zeros((spare, LANES), F32)], axis=0), side_ref)
+    sides = start_sides(side_ref, outputs[3], sent_sides)
     height = fields_ref.shape[0] // TILE_X
     for x in range(TILE_X):
         slab = fields_ref[pl.ds(x, height, stride=TILE_X), :]
@@ -282,10 +286,6 @@
     ]
     for copy in writes:
         copy.start()
-    rows = fields_ref[...]
-    spare = 2 * LANES - rows.shape[0]
-    edge_columns(jnp.concatenate([rows, jnp.zeros((spare, LANES), F32)], axis=0), side_ref)
-    sides = start_sides(side_ref, outputs[3], sent_sides)
     for copy in writes:
         copy.wait()
     wait_sides(sides)
@@ -434,15 +434,16 @@
         for third in thirds:
             for step in range(3):
                 stack.append(jnp.where(at_part, third[step : step + 1, :], 0.0))
-            stack.append(nothing)
+        stack.append(nothing)
         values_ref[:, lanes] = jnp.concatenate(stack, axis=0).astype(BF16)
-    sums = sum_thirds(times_turned(values_ref[...], place_ref[...]))
+    rows = 3 * parts
+    sums = sum_thirds(times_turned(values_ref[...], place_ref[...])[: 3 * rows])
     for step in range(3):
         for part in range(parts):
             at = step * parts + part
             held_ref[at : at + 1, :] = observed_ref[step : step + 1, part * LANES : (part + 1) * LANES]
-    held_ref[3 * parts :, :] = nothing
-    held_ref[...] = sums - held_ref[...]
+    held_ref[rows:, :] = nothing
+    held_ref[0:rows, :] = sums - held_ref[0:rows, :]
     for step in range(3):
         for part in range(parts):
             at = step * parts + part
@@ -680,7 +681,7 @@
             pltpu.VMEM((2 * depth, SPAN_NEAR, SPAN_Y), F32),
             pltpu.VMEM((9 * depth, SPAN_NEAR, SPAN_Y), F32),
             pltpu.VMEM((3 * depth, SPAN_NEAR, SPAN_Y), F32),
-            pltpu.VMEM((LANES, 2 * LANES), F32),
+            pltpu.VMEM((3, LANES, 2 * LANES), F32),
             pltpu.VMEM((2, 14 * cells_row, cols_y), F32),
             pltpu.VMEM((3 * LANES, part_count), BF16),
         ],
@@ -701,7 +702,7 @@
         "channel_sums",
         [shape(observed_data.shape, F32), shape((slot_groups * 4, LANES), F32)],
         [
-            pltpu.VMEM((12 * parts, slot_groups * LANES), BF16),
+            pltpu.VMEM((10 * parts, slot_groups * LANES), BF16),
             pltpu.VMEM((LANES, slot_groups * LANES), BF16),
             pltpu.VMEM((4 * parts, LANES), F32),
         ],
@@ -738,7 +739,7 @@
             pltpu.VMEM((2 * depth, SPAN_X, SPAN_Y), F32),
             pltpu.VMEM((9 * depth, SPAN_NEAR, SPAN_Y), F32),
             pltpu.VMEM((3 * depth, SPAN_NEAR, SPAN_Y), F32),
-            pltpu.VMEM((LANES, LANES), F32),
+            pltpu.VMEM((3, LANES, LANES), F32),
         ],
         loads,
         load_higher,

time: 59.5 us -> 59.4 us (level)
  no operation moved by 1% of the time
where the time goes in v12:
time: 59.4 us; the launch traced here: 58.9 us
  blocking collectives  20.9 us (35%)
  starting transfers between devices  19.7 us (33%)
  waiting for transfers between devices  9.3 us (16%)
  Pallas kernels  8.09 us (14%)
  between operations  0.8 us (1%)
    all_to_all x2, blocking collectives, exchange(): return lax.all_to_all(chunks, both, split_axis=0, concat_axis=0, tiled=True)  20.9 us
    all_to_all x2, starting transfers between devices, exchange(): return lax.all_to_all(chunks, both, split_axis=0, concat_axis=0, tiled=True)  9.89 us
    pallas_call x6, Pallas kernels, call_kernel(): pl.pallas_call(body, name=name, out_shape=outs, in_specs=[pl.BlockSpec(me...  8.09 us
    ppermute x1, waiting for transfers between devices, shards(): load_higher = lax.ppermute(loads, 'gx', down)  4.25 us
    ppermute x1, waiting for transfers between devices, shards(): higher = lax.ppermute(low, 'gx', down)  4.2 us
    ppermute x1, starting transfers between devices, shards(): lower = lax.ppermute(high, 'gx', up)  3.68 us
    ppermute x1, starting transfers between devices, shards(): load_lower = lax.ppermute(loads, 'gx', up)  3.59 us
    ppermute x1, starting transfers between devices, shards(): higher = lax.ppermute(low, 'gx', down)  1.29 us
  transfers between devices with their start and end apart: 6, of which 4 were waited for; matrix products, arithmetic and copies ran while one was open for 0% of the time, Pallas kernels for 1%

profile of v12, /device:TPU:0, one launch (start us, length us, event | category | flops | bytes accessed | tf_op | source)
XLA Modules:
  0.0 58.9 jit_solution(13244281517484660975)
XLA Ops:
  0.6 1.8 %pack_edges.1 = (f32[224,128]{1,0:T(8,128)}, f32[168,128]{1,0:T(8,128)}, f32[168,128]{1,0:T(8,128)}, f32[32,1,768]{2,1,0:T(1,128)}) custom-call(f32[144,128]{1,0:T(8,128)} %bitcast.20, f32[16,128]{1,0:T(8,128)} %bitcast.21, f32[16,128]{1,0:T(8,128)} %bitcast.22, f32[16,128]{1,0:T(8,128)} %bitcast.23, s32[1,64]{1,0:T(1,128)} %bitcast.24, f32[3,64]{1,0:T(4,128)} %refs_5_.1), custom_call_target="tpu_custom_call" | custom-call | tf_op jit(solution)/shard_map/pack_edges/pallas_call | solution.py:26
  2.4 0.0 copy-start.4
  2.4 0.0 copy-start.5
  2.4 7.3 %all-to-all-start = ((f32[32,1,768]{2,1,0:T(1,128)}), f32[32,1,768]{2,1,0:T(1,128)S(1)}, u32[]{:S(2)}, u32[]{:S(2)}) async-start(f32[32,1,768]{2,1,0:T(1,128)} %get-tuple-element.22), calls=%async_computation | async-start | bytes 196608 | tf_op jit(solution)/shard_map/all_to_all | solution.py:624
  9.8 3.7 %collective-permute-start = (f32[168,128]{1,0:T(8,128)}, f32[168,128]{1,0:T(8,128)S(1)}, u32[]{:S(2)}, u32[]{:S(2)}) collective-permute-start(f32[168,128]{1,0:T(8,128)} %get-tuple-element.20), channel_id=1, source_target_pairs={{0,8},{8,16},{16,24},{1,9},{9,17},{17,25},{2,10},{10,18},{18,26},{... | collective-permute-start | bytes 258056 | tf_op jit(solution)/shard_map/ppermute | solution.py:654
  13.4 0.0 copy-start.1
  13.5 1.3 %collective-permute-start.1 = (f32[168,128]{1,0:T(8,128)}, f32[168,128]{1,0:T(8,128)S(1)}, u32[]{:S(2)}, u32[]{:S(2)}) collective-permute-start(f32[168,128]{1,0:T(8,128)} %get-tuple-element.21), channel_id=1, source_target_pairs={{8,0},{16,8},{24,16},{9,1},{17,9},{25,17},{10,2},{18,10},{26,18},{... | collective-permute-start | bytes 258056 | tf_op jit(solution)/shard_map/ppermute | solution.py:655
  14.8 0.6 %segment_slots.1 = (s32[16,128]{1,0:T(8,128)S(1)}, s32[16,128]{1,0:T(8,128)S(1)}, bf16[128,2048]{1,0:T(8,128)(2,1)S(1)}, bf16[128,2048]{1,0:T(8,128)(2,1)S(1)}) custom-call(s32[16,128]{1,0:T(8,128)S(1)} %bitcast.18, s32[16,128]{1,0:T(8,128)S(1)} %bitcast.19), custom_call_target="tpu_custom_call" | custom-call | tf_op jit(solution)/shard_map/segment_slots/pallas_call | solution.py:26
  15.4 0.0 copy-start.3
  15.4 0.4 collective-permute-done.lower_ref
  15.8 4.2 %collective-permute-done.1.higher_ref = f32[168,128]{1,0:T(8,128)S(1)} collective-permute-done((f32[168,128]{1,0:T(8,128)}, f32[168,128]{1,0:T(8,128)S(1)}, u32[]{:S(2)}, u32[]{:S(2)}) %collective-permute-start.1) | collective-permute-done | bytes 86048 | tf_op jit(solution)/shard_map/ppermute | solution.py:655
  20.1 0.0 all-to-all-done.recv_ref
  20.1 1.7 %forward_run.1 = (f32[128,128]{1,0:T(8,128)S(1)}, f32[288,128]{1,0:T(8,128)S(1)}, f32[12,16,256]{2,1,0:T(8,128)S(1)}) custom-call(f32[224,128]{1,0:T(8,128)S(1)} %copy-done, f32[168,128]{1,0:T(8,128)S(1)} %collective-permute-done.lower_ref, f32[168,128]{1,0:T(8,128)S(1)} %collective-permute-done.1.higher_ref, f32[32,1,768]{2,1,0:T(1,128)S(1)} %all-to-all-done.recv_ref, ...), custom_call_target="tpu_custom_call" | custom-call | tf_op jit(solution)/shard_map/forward_run/pallas_call | solution.py:26
  21.7 0.0 copy-start.2
  21.8 11.8 %all_to_all.20 = f32[32,4,128]{2,1,0:T(4,128)S(1)} all-to-all(f32[32,4,128]{2,1,0:T(4,128)S(1)} %bitcast.15), channel_id=1, replica_groups=mesh['gx'=4,'gy'=8] {'gx','gy'}, dimensions={0} | all-to-all | bytes 131072 | tf_op jit(solution)/shard_map/all_to_all | solution.py:624
  33.6 1.1 %channel_sums.1 = (f32[3,1024]{1,0:T(4,128)S(1)}, f32[128,128]{1,0:T(8,128)S(1)}) custom-call(f32[128,128]{1,0:T(8,128)S(1)} %bitcast.14, f32[3,1024]{1,0:T(4,128)S(1)} %copy-done.2), custom_call_target="tpu_custom_call" | custom-call | tf_op jit(solution)/shard_map/channel_sums/pallas_call | solution.py:26
  34.7 9.1 %all_to_all.21 = f32[32,4,128]{2,1,0:T(4,128)S(1)} all-to-all(f32[32,4,128]{2,1,0:T(4,128)S(1)} %bitcast.16), channel_id=1, replica_groups=mesh['gx'=4,'gy'=8] {'gx','gy'}, dimensions={0} | all-to-all | bytes 131072 | tf_op jit(solution)/shard_map/all_to_all | solution.py:624
  43.8 1.7 %segment_loads.1 = (f32[96,128]{1,0:T(8,128)S(1)}, f32[32,1,384]{2,1,0:T(1,128)}) custom-call(f32[128,128]{1,0:T(8,128)S(1)} %bitcast.13, s32[16,128]{1,0:T(8,128)S(1)} %get-tuple-element.23.slot_ref, s32[16,128]{1,0:T(8,128)S(1)} %get-tuple-element.24.row_ref, f32[2,2048]{1,0:T(2,128)S(1)} %copy-done.1, bf16[128,2048]{1,0:T(8,128)(2,1)S(1)} %get-tuple-element.25.cover_ref, ...), custom_call_target="tpu_custom_call" | custom-call | tf_op jit(solution)/shard_map/segment_loads/pallas_call | solution.py:26
  45.5 2.6 %all-to-all-start.3 = ((f32[32,1,384]{2,1,0:T(1,128)}), f32[32,1,384]{2,1,0:T(1,128)S(1)}, u32[]{:S(2)}, u32[]{:S(2)}) async-start(f32[32,1,384]{2,1,0:T(1,128)} %get-tuple-element.30), calls=%async_computation.3 | async-start | bytes 98304 | tf_op jit(solution)/shard_map/all_to_all | solution.py:624
  48.1 3.6 %collective-permute-start.3 = (f32[96,128]{1,0:T(8,128)S(1)}, f32[96,128]{1,0:T(8,128)S(1)}, u32[]{:S(2)}, u32[]{:S(2)}) collective-permute-start(f32[96,128]{1,0:T(8,128)S(1)} %get-tuple-element.29.load_ref), channel_id=1, source_target_pairs={{0,8},{8,16},{16,24},{1,9},{9,17},{17,25},{2,10},{10,18},{18,26},{... | collective-permute-start | bytes 147464 | tf_op jit(solution)/shard_map/ppermute | solution.py:729
  51.7 1.3 %collective-permute-start.2 = (f32[96,128]{1,0:T(8,128)S(1)}, f32[96,128]{1,0:T(8,128)S(1)}, u32[]{:S(2)}, u32[]{:S(2)}) collective-permute-start(f32[96,128]{1,0:T(8,128)S(1)} %get-tuple-element.29.load_ref), channel_id=1, source_target_pairs={{8,0},{16,8},{24,16},{9,1},{17,9},{25,17},{10,2},{18,10},{26,18},{... | collective-permute-start | bytes 147464 | tf_op jit(solution)/shard_map/ppermute | solution.py:730
  53.0 0.4 collective-permute-done.3.lower_ref
  53.4 4.3 %collective-permute-done.2.higher_ref = f32[96,128]{1,0:T(8,128)S(1)} collective-permute-done((f32[96,128]{1,0:T(8,128)S(1)}, f32[96,128]{1,0:T(8,128)S(1)}, u32[]{:S(2)}, u32[]{:S(2)}) %collective-permute-start.2) | collective-permute-done | bytes 49184 | tf_op jit(solution)/shard_map/ppermute | solution.py:730
  57.6 1.3 %adjoint_run.1 = (f32[32,128]{1,0:T(8,128)}, f32[3,1024]{1,0:T(4,128)}) custom-call(f32[96,128]{1,0:T(8,128)S(1)} %get-tuple-element.29.load_ref, f32[96,128]{1,0:T(8,128)S(1)} %collective-permute-done.2.higher_ref, f32[96,128]{1,0:T(8,128)S(1)} %collective-permute-done.3.lower_ref, f32[32,1,384]{2,1,0:T(1,128)S(1)} %all-to-all-done.3.recv_ref, ...), custom_call_target="tpu_custom_call" | custom-call | tf_op jit(solution)/shard_map/adjoint_run/pallas_call | solution.py:26
  (8 shorter events, 0.0 us)
Async XLA Ops:
  2.4 12.4 %copy-start.4 = (s32[2048,1]{0,1:T(1,128)S(1)}, s32[2048,1]{0,1:T(1,128)}, u32[]{:S(2)}) copy-start(s32[2048,1]{0,1:T(1,128)} %param.19) | copy-start | bytes 24580
  2.4 12.3 %copy-start.5 = (s32[2048]{0:T(1024)S(1)}, s32[2048]{0:T(1024)}, u32[]{:S(2)}) copy-start(s32[2048]{0:T(1024)} %param.17) | copy-start | bytes 24580
  2.4 17.6 %copy-start = (f32[224,128]{1,0:T(8,128)S(1)}, f32[224,128]{1,0:T(8,128)}, u32[]{:S(2)}) copy-start(f32[224,128]{1,0:T(8,128)} %get-tuple-element.19.fields_ref) | copy-start | bytes 344068
  2.4 17.6 %all-to-all-start = ((f32[32,1,768]{2,1,0:T(1,128)}), f32[32,1,768]{2,1,0:T(1,128)S(1)}, u32[]{:S(2)}, u32[]{:S(2)}) async-start(f32[32,1,768]{2,1,0:T(1,128)} %get-tuple-element.22), calls=%async_computation | async-start | bytes 196608 | tf_op jit(solution)/shard_map/all_to_all | solution.py:624
  9.8 6.1 %collective-permute-start = (f32[168,128]{1,0:T(8,128)}, f32[168,128]{1,0:T(8,128)S(1)}, u32[]{:S(2)}, u32[]{:S(2)}) collective-permute-start(f32[168,128]{1,0:T(8,128)} %get-tuple-element.20), channel_id=1, source_target_pairs={{0,8},{8,16},{16,24},{1,9},{9,17},{17,25},{2,10},{10,18},{18,26},{... | collective-permute-start | bytes 258056 | tf_op jit(solution)/shard_map/ppermute | solution.py:654
  13.4 6.6 %copy-start.1 = (f32[2,2048]{1,0:T(2,128)S(1)}, f32[2,2048]{1,0:T(2,128)}, u32[]{:S(2)}) copy-start(f32[2,2048]{1,0:T(2,128)} %weight_ref.3) | copy-start | bytes 49156
  13.5 6.6 %collective-permute-start.1 = (f32[168,128]{1,0:T(8,128)}, f32[168,128]{1,0:T(8,128)S(1)}, u32[]{:S(2)}, u32[]{:S(2)}) collective-permute-start(f32[168,128]{1,0:T(8,128)} %get-tuple-element.21), channel_id=1, source_target_pairs={{8,0},{16,8},{24,16},{9,1},{17,9},{25,17},{10,2},{18,10},{26,18},{... | collective-permute-start | bytes 258056 | tf_op jit(solution)/shard_map/ppermute | solution.py:655
  15.4 4.6 %copy-start.3 = (s32[2048]{0:T(1024)S(1)}, s32[2048]{0:T(1024)}, u32[]{:S(2)}) copy-start(s32[2048]{0:T(1024)} %param.20) | copy-start | bytes 24580
  21.7 11.9 %copy-start.2 = (f32[3,1024]{1,0:T(4,128)S(1)}, f32[3,1024]{1,0:T(4,128)}, u32[]{:S(2)}) copy-start(f32[3,1024]{1,0:T(4,128)} %observed_ref.1) | copy-start | bytes 36868
  45.5 12.2 %all-to-all-start.3 = ((f32[32,1,384]{2,1,0:T(1,128)}), f32[32,1,384]{2,1,0:T(1,128)S(1)}, u32[]{:S(2)}, u32[]{:S(2)}) async-start(f32[32,1,384]{2,1,0:T(1,128)} %get-tuple-element.30), calls=%async_computation.3 | async-start | bytes 98304 | tf_op jit(solution)/shard_map/all_to_all | solution.py:624
  48.1 5.3 %collective-permute-start.3 = (f32[96,128]{1,0:T(8,128)S(1)}, f32[96,128]{1,0:T(8,128)S(1)}, u32[]{:S(2)}, u32[]{:S(2)}) collective-permute-start(f32[96,128]{1,0:T(8,128)S(1)} %get-tuple-element.29.load_ref), channel_id=1, source_target_pairs={{0,8},{8,16},{16,24},{1,9},{9,17},{17,25},{2,10},{10,18},{18,26},{... | collective-permute-start | bytes 147464 | tf_op jit(solution)/shard_map/ppermute | solution.py:729
  51.7 6.0 %collective-permute-start.2 = (f32[96,128]{1,0:T(8,128)S(1)}, f32[96,128]{1,0:T(8,128)S(1)}, u32[]{:S(2)}, u32[]{:S(2)}) collective-permute-start(f32[96,128]{1,0:T(8,128)S(1)} %get-tuple-element.29.load_ref), channel_id=1, source_target_pairs={{8,0},{16,8},{24,16},{9,1},{17,9},{25,17},{10,2},{18,10},{26,18},{... | collective-permute-start | bytes 147464 | tf_op jit(solution)/shard_map/ppermute | solution.py:730

commit v13 on v12

--- a/solution.py
+++ b/solution.py
@@ -5,7 +5,7 @@
 from jax import lax
 from jax.experimental import pallas as pl
 from jax.experimental.pallas import tpu as pltpu
-from jax.sharding import PartitionSpec as P
+from jax.sharding import Mesh, PartitionSpec as P
 
 GAUGE = 8
 STEP = 0.25
@@ -78,8 +78,9 @@
 
 
 def neighbour(dx, dy):
-    count_x, count_y = lax.axis_size("gx"), lax.axis_size("gy")
-    at_x, at_y = lax.axis_index("gx") + dx, lax.axis_index("gy") + dy
+    count_x, count_y = lax.axis_size("gx"), lax.axis_size("gz") * lax.axis_size("core")
+    at_x = lax.axis_index("gx") + dx
+    at_y = lax.axis_index("gz") * lax.axis_size("core") + lax.axis_index("core") + dy
     inside = (at_x >= 0) & (at_x < count_x) & (at_y >= 0) & (at_y < count_y)
     return jnp.where(inside, at_x * count_y + at_y, 0), inside
 
@@ -416,19 +417,21 @@
     out_ref[...] = sum_thirds(times_turned(spread_ref[...], place_ref[...]))
 
 
-def owner_body(arrived_ref, observed_ref, residual_ref, reply_ref, values_ref, place_ref, held_ref):
+def sums_body(arrived_ref, observed_ref, message_ref, place_ref, values_ref, held_ref):
     groups = arrived_ref.shape[0] // 4
     parts = observed_ref.shape[1] // LANES
+    rows = 3 * parts
     down = packed_iota(LANES)
     part_down = iota((parts, LANES), 0)
     nothing = jnp.zeros((parts, LANES), F32)
-    numbers = [arrived_ref[4 * s + 3 : 4 * s + 4, :].astype(I32) for s in range(groups)]
     for s in range(groups):
-        lanes = slice(s * LANES, (s + 1) * LANES)
+        block = s % 2 * (groups // 2) + s // 2
+        lanes = slice(block * LANES, (block + 1) * LANES)
+        number = arrived_ref[4 * s + 3 : 4 * s + 4, :].astype(I32)
         place_ref[:, lanes] = jnp.where(
-            down == packed_rows(numbers[s] & (LANES - 1), LANES), jnp.ones((), BF16), jnp.zeros((), BF16)
+            down == packed_rows(number & (LANES - 1), LANES), jnp.ones((), BF16), jnp.zeros((), BF16)
         )
-        at_part = part_down == (numbers[s] >> 7)
+        at_part = part_down == (number >> 7)
         thirds = pieces(arrived_ref[4 * s : 4 * s + 3, :])
         stack = []
         for third in thirds:
@@ -436,29 +439,51 @@
                 stack.append(jnp.where(at_part, third[step : step + 1, :], 0.0))
         stack.append(nothing)
         values_ref[:, lanes] = jnp.concatenate(stack, axis=0).astype(BF16)
-    rows = 3 * parts
-    sums = sum_thirds(times_turned(values_ref[...], place_ref[...])[: 3 * rows])
     for step in range(3):
         for part in range(parts):
             at = step * parts + part
             held_ref[at : at + 1, :] = observed_ref[step : step + 1, part * LANES : (part + 1) * LANES]
-    held_ref[rows:, :] = nothing
-    held_ref[0:rows, :] = sums - held_ref[0:rows, :]
+    half = groups // 2 * LANES
+    sums = [
+        sum_thirds(
+            times_turned(values_ref[:, core * half : (core + 1) * half], place_ref[:, core * half : (core + 1) * half])[
+                : 3 * rows
+            ]
+        )
+        for core in range(2)
+    ]
+    first = lax.axis_index("core") == 0
+    message_ref[0:rows, :] = jnp.where(first, sums[1], sums[0])
+    message_ref[rows:, :] = jnp.where(first, sums[0], sums[1]) - held_ref[...]
+
+
+def reply_body(arrived_ref, place_ref, message_ref, swapped_ref, residual_ref, reply_ref, held_ref):
+    groups = arrived_ref.shape[0] // 4
+    rows = message_ref.shape[0] // 2
+    parts = rows // 3
+    part_down = iota((parts, LANES), 0)
+    own = message_ref[rows:, :] + swapped_ref[0:rows, :]
+    other = message_ref[0:rows, :] + swapped_ref[rows:, :]
+    held_ref[...] = own
     for step in range(3):
         for part in range(parts):
             at = step * parts + part
             residual_ref[step : step + 1, part * LANES : (part + 1) * LANES] = held_ref[at : at + 1, :]
-    residual = jnp.concatenate(two_pieces(held_ref[...]), axis=0).astype(BF16)
-    for s in range(groups):
-        if s % 2 == 0:
-            both = sum_halves(times(residual, place_ref[:, s * LANES : (s + 2) * LANES]))
-        found = both[:, :LANES] if s % 2 == 0 else both[:, LANES:]
-        at_part = part_down == (numbers[s] >> 7)
-        for step in range(3):
-            reply_ref[4 * s + step : 4 * s + step + 1, :] = jnp.sum(
-                jnp.where(at_part, found[step * parts : (step + 1) * parts], 0.0), axis=0, keepdims=True
-            )
-        reply_ref[4 * s + 3 : 4 * s + 4, :] = jnp.zeros((1, LANES), F32)
+    first = lax.axis_index("core") == 0
+    for core, residual in enumerate((jnp.where(first, own, other), jnp.where(first, other, own))):
+        halves = jnp.concatenate(two_pieces(residual), axis=0).astype(BF16)
+        for k in range(groups // 2):
+            block = core * (groups // 2) + k
+            if k % 2 == 0:
+                both = sum_halves(times(halves, place_ref[:, block * LANES : (block + 2) * LANES]))
+            found = both[:, :LANES] if k % 2 == 0 else both[:, LANES:]
+            base = 4 * (2 * k + core)
+            at_part = part_down == (arrived_ref[base + 3 : base + 4, :].astype(I32) >> 7)
+            for step in range(3):
+                reply_ref[base + step : base + step + 1, :] = jnp.sum(
+                    jnp.where(at_part, found[step * parts : (step + 1) * parts], 0.0), axis=0, keepdims=True
+                )
+            reply_ref[base + 3 : base + 4, :] = jnp.zeros((1, LANES), F32)
 
 
 def load_body(
@@ -608,24 +633,28 @@
 ):
     depth, rows_x, cols_y = lame_lambda.shape
     part_count = segment_start.shape[0]
-    count_x, count_y = lax.axis_size("gx"), lax.axis_size("gy")
-    devices = count_x * count_y
+    count_x, pairs = lax.axis_size("gx"), lax.axis_size("gx") * lax.axis_size("gz")
+    devices = pairs * lax.axis_size("core")
     capacity = max(2, 2 * part_count // devices)
     slot_groups = devices * capacity // LANES
     blocks = part_count // LANES
     per_group = LANES // capacity
     cells_row = depth * rows_x
-    both = ("gx", "gy")
     up = [(i, i + 1) for i in range(count_x - 1)]
     down = [(j, i) for i, j in up]
     shape = jax.ShapeDtypeStruct
 
-    def exchange(chunks):
-        return lax.all_to_all(chunks, both, split_axis=0, concat_axis=0, tiled=True)
+    def exchange(chunks, axes=("gx", "gz", "core")):
+        return lax.all_to_all(chunks, axes, split_axis=0, concat_axis=0, tiled=True)
 
     def to_owners(rows):
-        chunks = rows.reshape(slot_groups, 4, per_group, capacity).transpose(0, 2, 1, 3)
-        back = exchange(chunks.reshape(devices, 4, capacity)).reshape(slot_groups, per_group, 4, capacity)
+        chunks = rows.reshape(slot_groups, 4, per_group, capacity).transpose(0, 2, 1, 3).reshape(pairs, 8, capacity)
+        back = exchange(chunks, ("gx", "gz")).reshape(-1, per_group, 2, 4, capacity)
+        return back.transpose(0, 2, 3, 1, 4).reshape(slot_groups * 4, LANES)
+
+    def from_owners(rows):
+        chunks = rows.reshape(-1, 2, 4, per_group, capacity).transpose(0, 3, 1, 2, 4).reshape(pairs, 8, capacity)
+        back = exchange(chunks, ("gx", "gz")).reshape(slot_groups, per_group, 4, capacity)
         return back.transpose(0, 2, 1, 3).reshape(slot_groups * 4, LANES)
 
     trimmed = shape((14 * depth * RIM, cols_y), F32)
@@ -697,17 +726,24 @@
         place,
     )
     parts = observed_data.shape[1] // LANES
+    arrived = to_owners(partials)
+    message, channel_place = call_kernel(
+        sums_body,
+        "channel_sums",
+        [shape((6 * parts, LANES), F32), shape((LANES, slot_groups * LANES), BF16)],
+        [pltpu.VMEM((10 * parts, slot_groups * LANES), BF16), pltpu.VMEM((3 * parts, LANES), F32)],
+        arrived,
+        observed_data,
+    )
     residuals, reply = call_kernel(
-        owner_body,
-        "channel_sums",
+        reply_body,
+        "channel_replies",
         [shape(observed_data.shape, F32), shape((slot_groups * 4, LANES), F32)],
-        [
-            pltpu.VMEM((10 * parts, slot_groups * LANES), BF16),
-            pltpu.VMEM((LANES, slot_groups * LANES), BF16),
-            pltpu.VMEM((4 * parts, LANES), F32),
-        ],
-        to_owners(partials),
-        observed_data,
+        [pltpu.VMEM((3 * parts, LANES), F32)],
+        arrived,
+        channel_place,
+        message,
+        lax.ppermute(message, "core", [(0, 1), (1, 0)]),
     )
     loads, load_edges = call_kernel(
         load_body,
@@ -718,7 +754,7 @@
             pltpu.VMEM((2, 1, RIM * LANES), F32),
             pltpu.SemaphoreType.DMA((6,)),
         ],
-        to_owners(reply),
+        from_owners(reply),
         slot,
         row,
         segment_weight,
@@ -753,18 +789,21 @@
 
 
 def solution(mesh):
+    rows_gx, cols_gy = mesh.devices.shape
+    split = Mesh(mesh.devices.reshape(rows_gx, cols_gy // 2, 2), ("gx", "gz", "core"))
+    column, tile = ("gz", "core"), ("gx", "gz", "core")
     in_specs = (
-        P(None, None, "gx", "gy"),
-        P(None, "gx", "gy"),
-        P(None, "gx", "gy"),
-        P(None, "gx", "gy"),
-        P(("gx", "gy")),
-        P(None, ("gx", "gy")),
-        P(("gx", "gy")),
-        P(None, ("gx", "gy")),
-        P(("gx", "gy"), None),
-        P(("gx", "gy")),
-        P(None, ("gx", "gy")),
-    )
-    out_specs = (P(None, ("gx", "gy")), P(None, None, "gx", "gy"))
-    return jax.shard_map(shards, mesh=mesh, in_specs=in_specs, out_specs=out_specs, check_vma=False)
+        P(None, None, "gx", column),
+        P(None, "gx", column),
+        P(None, "gx", column),
+        P(None, "gx", column),
+        P(tile),
+        P(None, tile),
+        P(tile),
+        P(None, tile),
+        P(tile, None),
+        P(tile),
+        P(None, tile),
+    )
+    out_specs = (P(None, tile), P(None, None, "gx", column))
+    return jax.shard_map(shards, mesh=split, in_specs=in_specs, out_specs=out_specs, check_vma=False)

time: 59.4 us -> 62.7 us (1.056)
  blocking collectives: 20.9 us -> 23.1 us
  waiting for transfers between devices: 9.3 us -> 10.5 us
    all_to_all x2, blocking collectives: 20.9 us -> 23.1 us  [exchange(): return lax.all_to_all(chunks, axes, split_axis=0, concat_axis=0, tiled=True)]
    ppermute x0 -> x1, waiting for transfers between devices: none -> 1.18 us  [shards(): lax.ppermute(message, 'core', [(0, 1), (1, 0)])]
    pallas_call x6 -> x7, Pallas kernels: 8.09 us -> 7.98 us  [call_kernel(): pl.pallas_call(body, name=name, out_shape=outs, in_specs=[pl.BlockSpec(me...]
  transfers between devices with their start and end apart: 6 -> 7, of which waited for: 4 -> 5; matrix products, arithmetic and copies ran while one was open for 0% -> 0% of each run, Pallas kernels for 1% -> 1%
where the time goes in v13:
time: 62.7 us; the launch traced here: 62.2 us
  blocking collectives  23.1 us (37%)
  starting transfers between devices  19.8 us (32%)
  waiting for transfers between devices  10.5 us (17%)
  Pallas kernels  7.98 us (13%)
  between operations  0.81 us (1%)
    all_to_all x2, blocking collectives, exchange(): return lax.all_to_all(chunks, axes, split_axis=0, concat_axis=0, tiled=True)  23.1 us
    all_to_all x2, starting transfers between devices, exchange(): return lax.all_to_all(chunks, axes, split_axis=0, concat_axis=0, tiled=True)  9.87 us
    pallas_call x7, Pallas kernels, call_kernel(): pl.pallas_call(body, name=name, out_shape=outs, in_specs=[pl.BlockSpec(me...  7.98 us
    ppermute x1, waiting for transfers between devices, shards(): load_higher = lax.ppermute(loads, 'gx', down)  4.25 us
    ppermute x1, waiting for transfers between devices, shards(): higher = lax.ppermute(low, 'gx', down)  4.2 us
    ppermute x1, starting transfers between devices, shards(): lower = lax.ppermute(high, 'gx', up)  3.68 us
    ppermute x1, starting transfers between devices, shards(): load_lower = lax.ppermute(loads, 'gx', up)  3.59 us
    ppermute x1, starting transfers between devices, shards(): higher = lax.ppermute(low, 'gx', down)  1.29 us
  transfers between devices with their start and end apart: 7, of which 5 were waited for; matrix products, arithmetic and copies ran while one was open for 0% of the time, Pallas kernels for 1%

profile of v13, /device:TPU:0, one launch (start us, length us, event | category | flops | bytes accessed | tf_op | source)
XLA Modules:
  0.0 62.2 jit_solution(12586511084433283330)
XLA Ops:
  0.6 1.8 %pack_edges.1 = (f32[224,128]{1,0:T(8,128)}, f32[168,128]{1,0:T(8,128)}, f32[168,128]{1,0:T(8,128)}, f32[32,1,768]{2,1,0:T(1,128)}) custom-call(f32[144,128]{1,0:T(8,128)} %bitcast.21, f32[16,128]{1,0:T(8,128)} %bitcast.22, f32[16,128]{1,0:T(8,128)} %bitcast.23, f32[16,128]{1,0:T(8,128)} %bitcast.24, s32[1,64]{1,0:T(1,128)} %bitcast.25, f32[3,64]{1,0:T(4,128)} %refs_5_.1), custom_call_target="tpu_custom_call" | custom-call | tf_op jit(solution)/shard_map/pack_edges/pallas_call | solution.py:26
  2.4 0.0 copy-start.5
  2.4 7.3 %all-to-all-start = ((f32[32,1,768]{2,1,0:T(1,128)}), f32[32,1,768]{2,1,0:T(1,128)S(1)}, u32[]{:S(2)}, u32[]{:S(2)}) async-start(f32[32,1,768]{2,1,0:T(1,128)} %get-tuple-element.24), calls=%async_computation | async-start | bytes 196608 | tf_op jit(solution)/shard_map/all_to_all | solution.py:648
  9.8 3.7 %collective-permute-start = (f32[168,128]{1,0:T(8,128)}, f32[168,128]{1,0:T(8,128)S(1)}, u32[]{:S(2)}, u32[]{:S(2)}) collective-permute-start(f32[168,128]{1,0:T(8,128)} %get-tuple-element.22), channel_id=1, source_target_pairs={{0,8},{8,16},{16,24},{1,9},{9,17},{17,25},{2,10},{10,18},{18,26},{... | collective-permute-start | bytes 258056 | tf_op jit(solution)/shard_map/ppermute | solution.py:683
  13.4 0.0 copy-start.1
  13.5 1.3 %collective-permute-start.1 = (f32[168,128]{1,0:T(8,128)}, f32[168,128]{1,0:T(8,128)S(1)}, u32[]{:S(2)}, u32[]{:S(2)}) collective-permute-start(f32[168,128]{1,0:T(8,128)} %get-tuple-element.23), channel_id=1, source_target_pairs={{8,0},{16,8},{24,16},{9,1},{17,9},{25,17},{10,2},{18,10},{26,18},{... | collective-permute-start | bytes 258056 | tf_op jit(solution)/shard_map/ppermute | solution.py:684
  14.8 0.6 %segment_slots.1 = (s32[16,128]{1,0:T(8,128)S(1)}, s32[16,128]{1,0:T(8,128)S(1)}, bf16[128,2048]{1,0:T(8,128)(2,1)S(1)}, bf16[128,2048]{1,0:T(8,128)(2,1)S(1)}) custom-call(s32[16,128]{1,0:T(8,128)S(1)} %bitcast.19, s32[16,128]{1,0:T(8,128)S(1)} %bitcast.20), custom_call_target="tpu_custom_call" | custom-call | tf_op jit(solution)/shard_map/segment_slots/pallas_call | solution.py:26
  15.4 0.0 copy-start.3
  15.4 0.4 collective-permute-done.lower_ref
  15.8 4.2 %collective-permute-done.1.higher_ref = f32[168,128]{1,0:T(8,128)S(1)} collective-permute-done((f32[168,128]{1,0:T(8,128)}, f32[168,128]{1,0:T(8,128)S(1)}, u32[]{:S(2)}, u32[]{:S(2)}) %collective-permute-start.1) | collective-permute-done | bytes 86048 | tf_op jit(solution)/shard_map/ppermute | solution.py:684
  20.1 1.7 %forward_run.1 = (f32[128,128]{1,0:T(8,128)S(1)}, f32[288,128]{1,0:T(8,128)S(1)}, f32[12,16,256]{2,1,0:T(8,128)S(1)}) custom-call(f32[224,128]{1,0:T(8,128)S(1)} %copy-done, f32[168,128]{1,0:T(8,128)S(1)} %collective-permute-done.lower_ref, f32[168,128]{1,0:T(8,128)S(1)} %collective-permute-done.1.higher_ref, f32[32,1,768]{2,1,0:T(1,128)S(1)} %all-to-all-done.recv_ref, ...), custom_call_target="tpu_custom_call" | custom-call | tf_op jit(solution)/shard_map/forward_run/pallas_call | solution.py:26
  21.7 13.0 %all_to_all.20 = f32[16,8,128]{2,1,0:T(8,128)S(1)} all-to-all(f32[16,8,128]{2,1,0:T(8,128)S(1)} %bitcast.16), channel_id=1, replica_groups=mesh['gx'=4,'gz'=4,'core'=2] {'gx','gz'}, dimensions={0} | all-to-all | bytes 131072 | tf_op jit(solution)/shard_map/all_to_all | solution.py:648
  34.7 0.7 %channel_sums.1 = (f32[48,128]{1,0:T(8,128)S(1)}, bf16[128,4096]{1,0:T(8,128)(2,1)S(1)}) custom-call(f32[128,128]{1,0:T(8,128)S(1)} %bitcast.13, f32[3,1024]{1,0:T(4,128)S(1)} %copy-done.2), custom_call_target="tpu_custom_call" | custom-call | tf_op jit(solution)/shard_map/channel_sums/pallas_call | solution.py:26
  35.4 0.1 collective-permute-start.2
  35.5 1.2 %collective-permute-done.2.swapped_ref = f32[48,128]{1,0:T(8,128)S(1)} collective-permute-done((f32[48,128]{1,0:T(8,128)S(1)}, f32[48,128]{1,0:T(8,128)S(1)}, u32[]{:S(2)}, u32[]{:S(2)}) %collective-permute-start.2) | collective-permute-done | bytes 24608 | tf_op jit(solution)/shard_map/ppermute | solution.py:746
  36.7 0.3 channel_replies.1
  37.0 10.1 %all_to_all.21 = f32[16,8,128]{2,1,0:T(8,128)S(1)} all-to-all(f32[16,8,128]{2,1,0:T(8,128)S(1)} %bitcast.17), channel_id=1, replica_groups=mesh['gx'=4,'gz'=4,'core'=2] {'gx','gz'}, dimensions={0} | all-to-all | bytes 131072 | tf_op jit(solution)/shard_map/all_to_all | solution.py:648
  47.1 1.7 %segment_loads.1 = (f32[96,128]{1,0:T(8,128)S(1)}, f32[32,1,384]{2,1,0:T(1,128)}) custom-call(f32[128,128]{1,0:T(8,128)S(1)} %bitcast.15, s32[16,128]{1,0:T(8,128)S(1)} %get-tuple-element.25.slot_ref, s32[16,128]{1,0:T(8,128)S(1)} %get-tuple-element.26.row_ref, f32[2,2048]{1,0:T(2,128)S(1)} %copy-done.1, bf16[128,2048]{1,0:T(8,128)(2,1)S(1)} %get-tuple-element.27.cover_ref, ...), custom_call_target="tpu_custom_call" | custom-call | tf_op jit(solution)/shard_map/segment_loads/pallas_call | solution.py:26
  48.8 2.6 %all-to-all-start.3 = ((f32[32,1,384]{2,1,0:T(1,128)}), f32[32,1,384]{2,1,0:T(1,128)S(1)}, u32[]{:S(2)}, u32[]{:S(2)}) async-start(f32[32,1,384]{2,1,0:T(1,128)} %get-tuple-element.34), calls=%async_computation.3 | async-start | bytes 98304 | tf_op jit(solution)/shard_map/all_to_all | solution.py:648
  51.3 3.6 %collective-permute-start.4 = (f32[96,128]{1,0:T(8,128)S(1)}, f32[96,128]{1,0:T(8,128)S(1)}, u32[]{:S(2)}, u32[]{:S(2)}) collective-permute-start(f32[96,128]{1,0:T(8,128)S(1)} %get-tuple-element.33.load_ref), channel_id=1, source_target_pairs={{0,8},{8,16},{16,24},{1,9},{9,17},{17,25},{2,10},{10,18},{18,26},{... | collective-permute-start | bytes 147464 | tf_op jit(solution)/shard_map/ppermute | solution.py:765
  54.9 1.3 %collective-permute-start.3 = (f32[96,128]{1,0:T(8,128)S(1)}, f32[96,128]{1,0:T(8,128)S(1)}, u32[]{:S(2)}, u32[]{:S(2)}) collective-permute-start(f32[96,128]{1,0:T(8,128)S(1)} %get-tuple-element.33.load_ref), channel_id=1, source_target_pairs={{8,0},{16,8},{24,16},{9,1},{17,9},{25,17},{10,2},{18,10},{26,18},{... | collective-permute-start | bytes 147464 | tf_op jit(solution)/shard_map/ppermute | solution.py:766
  56.2 0.4 collective-permute-done.4.lower_ref
  56.7 4.3 %collective-permute-done.3.higher_ref = f32[96,128]{1,0:T(8,128)S(1)} collective-permute-done((f32[96,128]{1,0:T(8,128)S(1)}, f32[96,128]{1,0:T(8,128)S(1)}, u32[]{:S(2)}, u32[]{:S(2)}) %collective-permute-start.3) | collective-permute-done | bytes 49184 | tf_op jit(solution)/shard_map/ppermute | solution.py:766
  60.9 1.3 %adjoint_run.1 = (f32[32,128]{1,0:T(8,128)}, f32[3,1024]{1,0:T(4,128)}) custom-call(f32[96,128]{1,0:T(8,128)S(1)} %get-tuple-element.33.load_ref, f32[96,128]{1,0:T(8,128)S(1)} %collective-permute-done.3.higher_ref, f32[96,128]{1,0:T(8,128)S(1)} %collective-permute-done.4.lower_ref, f32[32,1,384]{2,1,0:T(1,128)S(1)} %all-to-all-done.3.recv_ref, ...), custom_call_target="tpu_custom_call" | custom-call | tf_op jit(solution)/shard_map/adjoint_run/pallas_call | solution.py:26
  (11 shorter events, 0.0 us)
Async XLA Ops:
  2.4 12.4 %copy-start.4 = (s32[2048,1]{0,1:T(1,128)S(1)}, s32[2048,1]{0,1:T(1,128)}, u32[]{:S(2)}) copy-start(s32[2048,1]{0,1:T(1,128)} %param.19) | copy-start | bytes 24580
  2.4 12.3 %copy-start.5 = (s32[2048]{0:T(1024)S(1)}, s32[2048]{0:T(1024)}, u32[]{:S(2)}) copy-start(s32[2048]{0:T(1024)} %param.17) | copy-start | bytes 24580
  2.4 17.6 %copy-start = (f32[224,128]{1,0:T(8,128)S(1)}, f32[224,128]{1,0:T(8,128)}, u32[]{:S(2)}) copy-start(f32[224,128]{1,0:T(8,128)} %get-tuple-element.21.fields_ref) | copy-start | bytes 344068
  2.4 17.6 %all-to-all-start = ((f32[32,1,768]{2,1,0:T(1,128)}), f32[32,1,768]{2,1,0:T(1,128)S(1)}, u32[]{:S(2)}, u32[]{:S(2)}) async-start(f32[32,1,768]{2,1,0:T(1,128)} %get-tuple-element.24), calls=%async_computation | async-start | bytes 196608 | tf_op jit(solution)/shard_map/all_to_all | solution.py:648
  9.8 6.1 %collective-permute-start = (f32[168,128]{1,0:T(8,128)}, f32[168,128]{1,0:T(8,128)S(1)}, u32[]{:S(2)}, u32[]{:S(2)}) collective-permute-start(f32[168,128]{1,0:T(8,128)} %get-tuple-element.22), channel_id=1, source_target_pairs={{0,8},{8,16},{16,24},{1,9},{9,17},{17,25},{2,10},{10,18},{18,26},{... | collective-permute-start | bytes 258056 | tf_op jit(solution)/shard_map/ppermute | solution.py:683
  13.4 6.6 %copy-start.1 = (f32[2,2048]{1,0:T(2,128)S(1)}, f32[2,2048]{1,0:T(2,128)}, u32[]{:S(2)}) copy-start(f32[2,2048]{1,0:T(2,128)} %weight_ref.3) | copy-start | bytes 49156
  13.5 6.6 %collective-permute-start.1 = (f32[168,128]{1,0:T(8,128)}, f32[168,128]{1,0:T(8,128)S(1)}, u32[]{:S(2)}, u32[]{:S(2)}) collective-permute-start(f32[168,128]{1,0:T(8,128)} %get-tuple-element.23), channel_id=1, source_target_pairs={{8,0},{16,8},{24,16},{9,1},{17,9},{25,17},{10,2},{18,10},{26,18},{... | collective-permute-start | bytes 258056 | tf_op jit(solution)/shard_map/ppermute | solution.py:684
  15.4 4.6 %copy-start.3 = (s32[2048]{0:T(1024)S(1)}, s32[2048]{0:T(1024)}, u32[]{:S(2)}) copy-start(s32[2048]{0:T(1024)} %param.20) | copy-start | bytes 24580
  21.7 13.0 %copy-start.2 = (f32[3,1024]{1,0:T(4,128)S(1)}, f32[3,1024]{1,0:T(4,128)}, u32[]{:S(2)}) copy-start(f32[3,1024]{1,0:T(4,128)} %observed_ref.1) | copy-start | bytes 36868
  35.4 1.3 %collective-permute-start.2 = (f32[48,128]{1,0:T(8,128)S(1)}, f32[48,128]{1,0:T(8,128)S(1)}, u32[]{:S(2)}, u32[]{:S(2)}) collective-permute-start(f32[48,128]{1,0:T(8,128)S(1)} %get-tuple-element.31.message_ref), channel_id=1, source_target_pairs={{0,1},{1,0},{2,3},{3,2},{4,5},{5,4},{6,7},{7,6},{8,9},{9,8},{10,11... | collective-permute-start | bytes 73736 | tf_op jit(solution)/shard_map/ppermute | solution.py:746
  48.8 12.2 %all-to-all-start.3 = ((f32[32,1,384]{2,1,0:T(1,128)}), f32[32,1,384]{2,1,0:T(1,128)S(1)}, u32[]{:S(2)}, u32[]{:S(2)}) async-start(f32[32,1,384]{2,1,0:T(1,128)} %get-tuple-element.34), calls=%async_computation.3 | async-start | bytes 98304 | tf_op jit(solution)/shard_map/all_to_all | solution.py:648
  51.3 5.3 %collective-permute-start.4 = (f32[96,128]{1,0:T(8,128)S(1)}, f32[96,128]{1,0:T(8,128)S(1)}, u32[]{:S(2)}, u32[]{:S(2)}) collective-permute-start(f32[96,128]{1,0:T(8,128)S(1)} %get-tuple-element.33.load_ref), channel_id=1, source_target_pairs={{0,8},{8,16},{16,24},{1,9},{9,17},{17,25},{2,10},{10,18},{18,26},{... | collective-permute-start | bytes 147464 | tf_op jit(solution)/shard_map/ppermute | solution.py:765
  54.9 6.0 %collective-permute-start.3 = (f32[96,128]{1,0:T(8,128)S(1)}, f32[96,128]{1,0:T(8,128)S(1)}, u32[]{:S(2)}, u32[]{:S(2)}) collective-permute-start(f32[96,128]{1,0:T(8,128)S(1)} %get-tuple-element.33.load_ref), channel_id=1, source_target_pairs={{8,0},{16,8},{24,16},{9,1},{17,9},{25,17},{10,2},{18,10},{26,18},{... | collective-permute-start | bytes 147464 | tf_op jit(solution)/shard_map/ppermute | solution.py:766

commit v14 on v12

--- a/solution.py
+++ b/solution.py
@@ -461,6 +461,10 @@
         reply_ref[4 * s + 3 : 4 * s + 4, :] = jnp.zeros((1, LANES), F32)
 
 
+def reached():
+    return [(turn, distance) for turn in range(3) for distance in range(RIM - turn)]
+
+
 def load_body(
     arrived_ref,
     slot_ref,
@@ -469,6 +473,8 @@
     cover_ref,
     place_ref,
     load_ref,
+    high_ref,
+    low_ref,
     out_ref,
     spread_ref,
     side_ref,
@@ -507,13 +513,19 @@
             side_ref[side, 0:1, lanes] = edges[base + column : base + column + 1, :]
     sides = start_sides(side_ref, out_ref, sent_sides)
     load_ref[...] = sum_halves(times_turned(spread_ref[...], cover_ref[...]))
+    count = stack_rows // (3 * TILE_X)
+    for at, (turn, distance) in enumerate(reached()):
+        rows = slice(at * count, (at + 1) * count)
+        first = turn * count * TILE_X
+        low_ref[rows, :] = load_ref[pl.ds(first + distance, count, stride=TILE_X), :]
+        high_ref[rows, :] = load_ref[pl.ds(first + TILE_X - 1 - distance, count, stride=TILE_X), :]
     wait_sides(sides)
 
 
 def adjoint_body(
     load_ref,
+    lower_ref,
     higher_ref,
-    lower_ref,
     recv_ref,
     strain_ref,
     medium_ref,
@@ -526,10 +538,18 @@
     state_ref,
     near_ref,
     turn_ref,
+    sides_ref,
 ):
     depth = medium_ref.shape[0] // 3
     rims = rim_rows(recv_ref, turn_ref)
-    lay_planes(first_ref, later_ref, 0, load_ref, higher_ref, lower_ref)
+    sides_ref[...] = jnp.zeros_like(sides_ref)
+    count = load_ref.shape[0] // (3 * TILE_X)
+    for at, (turn, distance) in enumerate(reached()):
+        rows = slice(at * count, (at + 1) * count)
+        first = turn * count * TILE_X
+        sides_ref[0, pl.ds(first + distance, count, stride=TILE_X), :] = higher_ref[rows, :]
+        sides_ref[1, pl.ds(first + TILE_X - 1 - distance, count, stride=TILE_X), :] = lower_ref[rows, :]
+    lay_planes(first_ref, later_ref, 0, load_ref, sides_ref.at[0], sides_ref.at[1])
     lay_planes(first_ref, later_ref, LANES, *rims)
     for plane in range(3 * depth):
         near_ref[plane] = narrowed(medium_ref[plane])
@@ -709,10 +729,11 @@
         to_owners(partials),
         observed_data,
     )
-    loads, load_edges = call_kernel(
+    reach = shape((len(reached()) * 2 * depth, cols_y), F32)
+    loads, load_high, load_low, load_edges = call_kernel(
         load_body,
         "segment_loads",
-        [shape((6 * cells_row, cols_y), F32), shape((devices, 1, RIM * LANES), F32)],
+        [shape((6 * cells_row, cols_y), F32), reach, reach, shape((devices, 1, RIM * LANES), F32)],
         [
             pltpu.VMEM((12 * cells_row, part_count), BF16),
             pltpu.VMEM((2, 1, RIM * LANES), F32),
@@ -724,10 +745,10 @@
         segment_weight,
         cover,
         place,
-        place_out=(pltpu.VMEM, pl.ANY),
-    )
-    load_lower = lax.ppermute(loads, "gx", up)
-    load_higher = lax.ppermute(loads, "gx", down)
+        place_out=(pltpu.VMEM, pltpu.VMEM, pltpu.VMEM, pl.ANY),
+    )
+    load_lower = lax.ppermute(load_high, "gx", up)
+    load_higher = lax.ppermute(load_low, "gx", down)
     load_rims = exchange(load_edges)
     gradients, residuals = call_kernel(
         adjoint_body,
@@ -740,10 +761,11 @@
             pltpu.VMEM((9 * depth, SPAN_NEAR, SPAN_Y), F32),
             pltpu.VMEM((3 * depth, SPAN_NEAR, SPAN_Y), F32),
             pltpu.VMEM((3, LANES, LANES), F32),
+            pltpu.VMEM((2, 6 * cells_row, cols_y), F32),
         ],
         loads,
+        load_lower,
         load_higher,
-        load_lower,
         load_rims,
         strains,
         medium,

time: 59.4 us -> 59.1 us (level)
  no operation moved by 1% of the time
where the time goes in v14:
time: 59.1 us; the launch traced here: 58.7 us
  blocking collectives  20.9 us (35%)
  starting transfers between devices  19.7 us (33%)
  waiting for transfers between devices  9.03 us (15%)
  Pallas kernels  8.11 us (14%)
  between operations  0.8 us (1%)
    all_to_all x2, blocking collectives, exchange(): return lax.all_to_all(chunks, both, split_axis=0, concat_axis=0, tiled=True)  20.9 us
    all_to_all x2, starting transfers between devices, exchange(): return lax.all_to_all(chunks, both, split_axis=0, concat_axis=0, tiled=True)  9.89 us
    pallas_call x6, Pallas kernels, call_kernel(): pl.pallas_call(body, name=name, out_shape=outs, in_specs=[pl.BlockSpec(me...  8.11 us
    ppermute x1, waiting for transfers between devices, shards(): load_higher = lax.ppermute(load_low, 'gx', down)  4.22 us
    ppermute x1, waiting for transfers between devices, shards(): higher = lax.ppermute(low, 'gx', down)  4.2 us
    ppermute x1, starting transfers between devices, shards(): lower = lax.ppermute(high, 'gx', up)  3.68 us
    ppermute x1, starting transfers between devices, shards(): load_lower = lax.ppermute(load_high, 'gx', up)  3.59 us
    ppermute x1, starting transfers between devices, shards(): load_higher = lax.ppermute(load_low, 'gx', down)  1.29 us
  transfers between devices with their start and end apart: 6, of which 4 were waited for; matrix products, arithmetic and copies ran while one was open for 0% of the time, Pallas kernels for 1%

profile of v14, /device:TPU:0, one launch (start us, length us, event | category | flops | bytes accessed | tf_op | source)
XLA Modules:
  0.0 58.7 jit_solution(2497379048785865287)
XLA Ops:
  0.6 1.8 %pack_edges.1 = (f32[224,128]{1,0:T(8,128)}, f32[168,128]{1,0:T(8,128)}, f32[168,128]{1,0:T(8,128)}, f32[32,1,768]{2,1,0:T(1,128)}) custom-call(f32[144,128]{1,0:T(8,128)} %bitcast.20, f32[16,128]{1,0:T(8,128)} %bitcast.21, f32[16,128]{1,0:T(8,128)} %bitcast.22, f32[16,128]{1,0:T(8,128)} %bitcast.23, s32[1,64]{1,0:T(1,128)} %bitcast.24, f32[3,64]{1,0:T(4,128)} %refs_5_.1), custom_call_target="tpu_custom_call" | custom-call | tf_op jit(solution)/shard_map/pack_edges/pallas_call | solution.py:26
  2.4 0.0 copy-start.4
  2.4 0.0 copy-start.5
  2.4 7.3 %all-to-all-start = ((f32[32,1,768]{2,1,0:T(1,128)}), f32[32,1,768]{2,1,0:T(1,128)S(1)}, u32[]{:S(2)}, u32[]{:S(2)}) async-start(f32[32,1,768]{2,1,0:T(1,128)} %get-tuple-element.24), calls=%async_computation | async-start | bytes 196608 | tf_op jit(solution)/shard_map/all_to_all | solution.py:644
  9.8 3.7 %collective-permute-start = (f32[168,128]{1,0:T(8,128)}, f32[168,128]{1,0:T(8,128)S(1)}, u32[]{:S(2)}, u32[]{:S(2)}) collective-permute-start(f32[168,128]{1,0:T(8,128)} %get-tuple-element.22), channel_id=1, source_target_pairs={{0,8},{8,16},{16,24},{1,9},{9,17},{17,25},{2,10},{10,18},{18,26},{... | collective-permute-start | bytes 258056 | tf_op jit(solution)/shard_map/ppermute | solution.py:674
  13.4 0.0 copy-start.1
  13.5 1.3 %collective-permute-start.1 = (f32[168,128]{1,0:T(8,128)}, f32[168,128]{1,0:T(8,128)S(1)}, u32[]{:S(2)}, u32[]{:S(2)}) collective-permute-start(f32[168,128]{1,0:T(8,128)} %get-tuple-element.23), channel_id=1, source_target_pairs={{8,0},{16,8},{24,16},{9,1},{17,9},{25,17},{10,2},{18,10},{26,18},{... | collective-permute-start | bytes 258056 | tf_op jit(solution)/shard_map/ppermute | solution.py:675
  14.8 0.6 %segment_slots.1 = (s32[16,128]{1,0:T(8,128)S(1)}, s32[16,128]{1,0:T(8,128)S(1)}, bf16[128,2048]{1,0:T(8,128)(2,1)S(1)}, bf16[128,2048]{1,0:T(8,128)(2,1)S(1)}) custom-call(s32[16,128]{1,0:T(8,128)S(1)} %bitcast.18, s32[16,128]{1,0:T(8,128)S(1)} %bitcast.19), custom_call_target="tpu_custom_call" | custom-call | tf_op jit(solution)/shard_map/segment_slots/pallas_call | solution.py:26
  15.4 0.0 copy-start.3
  15.4 0.4 collective-permute-done.lower_ref
  15.8 4.2 %collective-permute-done.1.higher_ref = f32[168,128]{1,0:T(8,128)S(1)} collective-permute-done((f32[168,128]{1,0:T(8,128)}, f32[168,128]{1,0:T(8,128)S(1)}, u32[]{:S(2)}, u32[]{:S(2)}) %collective-permute-start.1) | collective-permute-done | bytes 86048 | tf_op jit(solution)/shard_map/ppermute | solution.py:675
  20.1 0.0 all-to-all-done.recv_ref
  20.1 1.7 %forward_run.1 = (f32[128,128]{1,0:T(8,128)S(1)}, f32[288,128]{1,0:T(8,128)S(1)}, f32[12,16,256]{2,1,0:T(8,128)S(1)}) custom-call(f32[224,128]{1,0:T(8,128)S(1)} %copy-done, f32[168,128]{1,0:T(8,128)S(1)} %collective-permute-done.lower_ref, f32[168,128]{1,0:T(8,128)S(1)} %collective-permute-done.1.higher_ref, f32[32,1,768]{2,1,0:T(1,128)S(1)} %all-to-all-done.recv_ref, ...), custom_call_target="tpu_custom_call" | custom-call | tf_op jit(solution)/shard_map/forward_run/pallas_call | solution.py:26
  21.7 0.0 copy-start.2
  21.8 11.8 %all_to_all.20 = f32[32,4,128]{2,1,0:T(4,128)S(1)} all-to-all(f32[32,4,128]{2,1,0:T(4,128)S(1)} %bitcast.15), channel_id=1, replica_groups=mesh['gx'=4,'gy'=8] {'gx','gy'}, dimensions={0} | all-to-all | bytes 131072 | tf_op jit(solution)/shard_map/all_to_all | solution.py:644
  33.6 1.1 %channel_sums.1 = (f32[3,1024]{1,0:T(4,128)S(1)}, f32[128,128]{1,0:T(8,128)S(1)}) custom-call(f32[128,128]{1,0:T(8,128)S(1)} %bitcast.14, f32[3,1024]{1,0:T(4,128)S(1)} %copy-done.2), custom_call_target="tpu_custom_call" | custom-call | tf_op jit(solution)/shard_map/channel_sums/pallas_call | solution.py:26
  34.7 9.1 %all_to_all.21 = f32[32,4,128]{2,1,0:T(4,128)S(1)} all-to-all(f32[32,4,128]{2,1,0:T(4,128)S(1)} %bitcast.16), channel_id=1, replica_groups=mesh['gx'=4,'gy'=8] {'gx','gy'}, dimensions={0} | all-to-all | bytes 131072 | tf_op jit(solution)/shard_map/all_to_all | solution.py:644
  43.8 1.7 %segment_loads.1 = (f32[96,128]{1,0:T(8,128)S(1)}, f32[48,128]{1,0:T(8,128)S(1)}, f32[48,128]{1,0:T(8,128)S(1)}, f32[32,1,384]{2,1,0:T(1,128)}) custom-call(f32[128,128]{1,0:T(8,128)S(1)} %bitcast.13, s32[16,128]{1,0:T(8,128)S(1)} %get-tuple-element.25.slot_ref, s32[16,128]{1,0:T(8,128)S(1)} %get-tuple-element.26.row_ref, f32[2,2048]{1,0:T(2,128)S(1)} %copy-done.1, ...), custom_call_target="tpu_custom_call" | custom-call | tf_op jit(solution)/shard_map/segment_loads/pallas_call | solution.py:26
  45.5 2.6 %all-to-all-start.3 = ((f32[32,1,384]{2,1,0:T(1,128)}), f32[32,1,384]{2,1,0:T(1,128)S(1)}, u32[]{:S(2)}, u32[]{:S(2)}) async-start(f32[32,1,384]{2,1,0:T(1,128)} %get-tuple-element.34), calls=%async_computation.3 | async-start | bytes 98304 | tf_op jit(solution)/shard_map/all_to_all | solution.py:644
  48.1 3.6 %collective-permute-start.2 = (f32[48,128]{1,0:T(8,128)S(1)}, f32[48,128]{1,0:T(8,128)S(1)}, u32[]{:S(2)}, u32[]{:S(2)}) collective-permute-start(f32[48,128]{1,0:T(8,128)S(1)} %get-tuple-element.32), channel_id=1, source_target_pairs={{0,8},{8,16},{16,24},{1,9},{9,17},{17,25},{2,10},{10,18},{18,26},{... | collective-permute-start | bytes 73736 | tf_op jit(solution)/shard_map/ppermute | solution.py:750
  51.7 1.3 %collective-permute-start.3 = (f32[48,128]{1,0:T(8,128)S(1)}, f32[48,128]{1,0:T(8,128)S(1)}, u32[]{:S(2)}, u32[]{:S(2)}) collective-permute-start(f32[48,128]{1,0:T(8,128)S(1)} %get-tuple-element.33), channel_id=1, source_target_pairs={{8,0},{16,8},{24,16},{9,1},{17,9},{25,17},{10,2},{18,10},{26,18},{... | collective-permute-start | bytes 73736 | tf_op jit(solution)/shard_map/ppermute | solution.py:751
  53.0 0.2 collective-permute-done.2.lower_ref
  53.2 4.2 %collective-permute-done.3.higher_ref = f32[48,128]{1,0:T(8,128)S(1)} collective-permute-done((f32[48,128]{1,0:T(8,128)S(1)}, f32[48,128]{1,0:T(8,128)S(1)}, u32[]{:S(2)}, u32[]{:S(2)}) %collective-permute-start.3) | collective-permute-done | bytes 24608 | tf_op jit(solution)/shard_map/ppermute | solution.py:751
  57.4 1.3 %adjoint_run.1 = (f32[32,128]{1,0:T(8,128)}, f32[3,1024]{1,0:T(4,128)}) custom-call(f32[96,128]{1,0:T(8,128)S(1)} %get-tuple-element.31.load_ref, f32[48,128]{1,0:T(8,128)S(1)} %collective-permute-done.2.lower_ref, f32[48,128]{1,0:T(8,128)S(1)} %collective-permute-done.3.higher_ref, f32[32,1,384]{2,1,0:T(1,128)S(1)} %all-to-all-done.3.recv_ref, ...), custom_call_target="tpu_custom_call" | custom-call | tf_op jit(solution)/shard_map/adjoint_run/pallas_call | solution.py:26
  (8 shorter events, 0.0 us)
Async XLA Ops:
  2.4 12.4 %copy-start.4 = (s32[2048,1]{0,1:T(1,128)S(1)}, s32[2048,1]{0,1:T(1,128)}, u32[]{:S(2)}) copy-start(s32[2048,1]{0,1:T(1,128)} %param.19) | copy-start | bytes 24580
  2.4 12.3 %copy-start.5 = (s32[2048]{0:T(1024)S(1)}, s32[2048]{0:T(1024)}, u32[]{:S(2)}) copy-start(s32[2048]{0:T(1024)} %param.17) | copy-start | bytes 24580
  2.4 17.6 %copy-start = (f32[224,128]{1,0:T(8,128)S(1)}, f32[224,128]{1,0:T(8,128)}, u32[]{:S(2)}) copy-start(f32[224,128]{1,0:T(8,128)} %get-tuple-element.21.fields_ref) | copy-start | bytes 344068
  2.4 17.6 %all-to-all-start = ((f32[32,1,768]{2,1,0:T(1,128)}), f32[32,1,768]{2,1,0:T(1,128)S(1)}, u32[]{:S(2)}, u32[]{:S(2)}) async-start(f32[32,1,768]{2,1,0:T(1,128)} %get-tuple-element.24), calls=%async_computation | async-start | bytes 196608 | tf_op jit(solution)/shard_map/all_to_all | solution.py:644
  9.8 6.1 %collective-permute-start = (f32[168,128]{1,0:T(8,128)}, f32[168,128]{1,0:T(8,128)S(1)}, u32[]{:S(2)}, u32[]{:S(2)}) collective-permute-start(f32[168,128]{1,0:T(8,128)} %get-tuple-element.22), channel_id=1, source_target_pairs={{0,8},{8,16},{16,24},{1,9},{9,17},{17,25},{2,10},{10,18},{18,26},{... | collective-permute-start | bytes 258056 | tf_op jit(solution)/shard_map/ppermute | solution.py:674
  13.4 6.6 %copy-start.1 = (f32[2,2048]{1,0:T(2,128)S(1)}, f32[2,2048]{1,0:T(2,128)}, u32[]{:S(2)}) copy-start(f32[2,2048]{1,0:T(2,128)} %weight_ref.3) | copy-start | bytes 49156
  13.5 6.6 %collective-permute-start.1 = (f32[168,128]{1,0:T(8,128)}, f32[168,128]{1,0:T(8,128)S(1)}, u32[]{:S(2)}, u32[]{:S(2)}) collective-permute-start(f32[168,128]{1,0:T(8,128)} %get-tuple-element.23), channel_id=1, source_target_pairs={{8,0},{16,8},{24,16},{9,1},{17,9},{25,17},{10,2},{18,10},{26,18},{... | collective-permute-start | bytes 258056 | tf_op jit(solution)/shard_map/ppermute | solution.py:675
  15.4 4.6 %copy-start.3 = (s32[2048]{0:T(1024)S(1)}, s32[2048]{0:T(1024)}, u32[]{:S(2)}) copy-start(s32[2048]{0:T(1024)} %param.20) | copy-start | bytes 24580
  21.7 11.9 %copy-start.2 = (f32[3,1024]{1,0:T(4,128)S(1)}, f32[3,1024]{1,0:T(4,128)}, u32[]{:S(2)}) copy-start(f32[3,1024]{1,0:T(4,128)} %observed_ref.1) | copy-start | bytes 36868
  45.5 11.9 %all-to-all-start.3 = ((f32[32,1,384]{2,1,0:T(1,128)}), f32[32,1,384]{2,1,0:T(1,128)S(1)}, u32[]{:S(2)}, u32[]{:S(2)}) async-start(f32[32,1,384]{2,1,0:T(1,128)} %get-tuple-element.34), calls=%async_computation.3 | async-start | bytes 98304 | tf_op jit(solution)/shard_map/all_to_all | solution.py:644
  48.1 5.1 %collective-permute-start.2 = (f32[48,128]{1,0:T(8,128)S(1)}, f32[48,128]{1,0:T(8,128)S(1)}, u32[]{:S(2)}, u32[]{:S(2)}) collective-permute-start(f32[48,128]{1,0:T(8,128)S(1)} %get-tuple-element.32), channel_id=1, source_target_pairs={{0,8},{8,16},{16,24},{1,9},{9,17},{17,25},{2,10},{10,18},{18,26},{... | collective-permute-start | bytes 73736 | tf_op jit(solution)/shard_map/ppermute | solution.py:750
  51.7 5.7 %collective-permute-start.3 = (f32[48,128]{1,0:T(8,128)S(1)}, f32[48,128]{1,0:T(8,128)S(1)}, u32[]{:S(2)}, u32[]{:S(2)}) collective-permute-start(f32[48,128]{1,0:T(8,128)S(1)} %get-tuple-element.33), channel_id=1, source_target_pairs={{8,0},{16,8},{24,16},{9,1},{17,9},{25,17},{10,2},{18,10},{26,18},{... | collective-permute-start | bytes 73736 | tf_op jit(solution)/shard_map/ppermute | solution.py:751

commit v15 on v14

--- a/solution.py
+++ b/solution.py
@@ -524,8 +524,8 @@
 
 def adjoint_body(
     load_ref,
+    higher_ref,
     lower_ref,
-    higher_ref,
     recv_ref,
     strain_ref,
     medium_ref,
@@ -764,8 +764,8 @@
             pltpu.VMEM((2, 6 * cells_row, cols_y), F32),
         ],
         loads,
+        load_higher,
         load_lower,
-        load_higher,
         load_rims,
         strains,
         medium,

time: 59.1 us -> 57.2 us (0.968)
  waiting for transfers between devices: 9.03 us -> 6.11 us
  starting transfers between devices: 19.7 us -> 20.7 us
    ppermute x1, waiting for transfers between devices: 4.22 us -> 0.01 us  [shards(): load_higher = lax.ppermute(load_low, 'gx', down)]
    ppermute x1, waiting for transfers between devices: 0.2 us -> 1.49 us  [shards(): load_lower = lax.ppermute(load_high, 'gx', up)]
    ppermute x1, starting transfers between devices: 3.59 us -> 4.55 us  [shards(): load_lower = lax.ppermute(load_high, 'gx', up)]
  transfers between devices with their start and end apart: 6 -> 6, of which waited for: 4 -> 3; matrix products, arithmetic and copies ran while one was open for 0% -> 0% of each run, Pallas kernels for 1% -> 1%
where the time goes in v15:
time: 57.2 us; the launch traced here: 56.7 us
  blocking collectives  20.9 us (37%)
  starting transfers between devices  20.7 us (36%)
  Pallas kernels  8.11 us (14%)
  waiting for transfers between devices  6.11 us (11%)
  between operations  0.8 us (1%)
    all_to_all x2, blocking collectives, exchange(): return lax.all_to_all(chunks, both, split_axis=0, concat_axis=0, tiled=True)  20.9 us
    all_to_all x2, starting transfers between devices, exchange(): return lax.all_to_all(chunks, both, split_axis=0, concat_axis=0, tiled=True)  9.89 us
    pallas_call x6, Pallas kernels, call_kernel(): pl.pallas_call(body, name=name, out_shape=outs, in_specs=[pl.BlockSpec(me...  8.11 us
    ppermute x1, starting transfers between devices, shards(): load_lower = lax.ppermute(load_high, 'gx', up)  4.55 us
    ppermute x1, waiting for transfers between devices, shards(): higher = lax.ppermute(low, 'gx', down)  4.2 us
    ppermute x1, starting transfers between devices, shards(): lower = lax.ppermute(high, 'gx', up)  3.68 us
    ppermute x1, waiting for transfers between devices, shards(): load_lower = lax.ppermute(load_high, 'gx', up)  1.49 us
    ppermute x1, starting transfers between devices, shards(): higher = lax.ppermute(low, 'gx', down)  1.29 us
  transfers between devices with their start and end apart: 6, of which 3 were waited for; matrix products, arithmetic and copies ran while one was open for 0% of the time, Pallas kernels for 1%

profile of v15, /device:TPU:0, one launch (start us, length us, event | category | flops | bytes accessed | tf_op | source)
XLA Modules:
  0.0 56.7 jit_solution(9431830745833524882)
XLA Ops:
  0.6 1.8 %pack_edges.1 = (f32[224,128]{1,0:T(8,128)}, f32[168,128]{1,0:T(8,128)}, f32[168,128]{1,0:T(8,128)}, f32[32,1,768]{2,1,0:T(1,128)}) custom-call(f32[144,128]{1,0:T(8,128)} %bitcast.20, f32[16,128]{1,0:T(8,128)} %bitcast.21, f32[16,128]{1,0:T(8,128)} %bitcast.22, f32[16,128]{1,0:T(8,128)} %bitcast.23, s32[1,64]{1,0:T(1,128)} %bitcast.24, f32[3,64]{1,0:T(4,128)} %refs_5_.1), custom_call_target="tpu_custom_call" | custom-call | tf_op jit(solution)/shard_map/pack_edges/pallas_call | solution.py:26
  2.4 0.0 copy-start.4
  2.4 0.0 copy-start.5
  2.4 7.3 %all-to-all-start = ((f32[32,1,768]{2,1,0:T(1,128)}), f32[32,1,768]{2,1,0:T(1,128)S(1)}, u32[]{:S(2)}, u32[]{:S(2)}) async-start(f32[32,1,768]{2,1,0:T(1,128)} %get-tuple-element.24), calls=%async_computation | async-start | bytes 196608 | tf_op jit(solution)/shard_map/all_to_all | solution.py:644
  9.8 3.7 %collective-permute-start = (f32[168,128]{1,0:T(8,128)}, f32[168,128]{1,0:T(8,128)S(1)}, u32[]{:S(2)}, u32[]{:S(2)}) collective-permute-start(f32[168,128]{1,0:T(8,128)} %get-tuple-element.22), channel_id=1, source_target_pairs={{0,8},{8,16},{16,24},{1,9},{9,17},{17,25},{2,10},{10,18},{18,26},{... | collective-permute-start | bytes 258056 | tf_op jit(solution)/shard_map/ppermute | solution.py:674
  13.4 0.0 copy-start.1
  13.5 1.3 %collective-permute-start.1 = (f32[168,128]{1,0:T(8,128)}, f32[168,128]{1,0:T(8,128)S(1)}, u32[]{:S(2)}, u32[]{:S(2)}) collective-permute-start(f32[168,128]{1,0:T(8,128)} %get-tuple-element.23), channel_id=1, source_target_pairs={{8,0},{16,8},{24,16},{9,1},{17,9},{25,17},{10,2},{18,10},{26,18},{... | collective-permute-start | bytes 258056 | tf_op jit(solution)/shard_map/ppermute | solution.py:675
  14.8 0.6 %segment_slots.1 = (s32[16,128]{1,0:T(8,128)S(1)}, s32[16,128]{1,0:T(8,128)S(1)}, bf16[128,2048]{1,0:T(8,128)(2,1)S(1)}, bf16[128,2048]{1,0:T(8,128)(2,1)S(1)}) custom-call(s32[16,128]{1,0:T(8,128)S(1)} %bitcast.18, s32[16,128]{1,0:T(8,128)S(1)} %bitcast.19), custom_call_target="tpu_custom_call" | custom-call | tf_op jit(solution)/shard_map/segment_slots/pallas_call | solution.py:26
  15.4 0.0 copy-start.3
  15.4 0.4 collective-permute-done.lower_ref
  15.8 4.2 %collective-permute-done.1.higher_ref = f32[168,128]{1,0:T(8,128)S(1)} collective-permute-done((f32[168,128]{1,0:T(8,128)}, f32[168,128]{1,0:T(8,128)S(1)}, u32[]{:S(2)}, u32[]{:S(2)}) %collective-permute-start.1) | collective-permute-done | bytes 86048 | tf_op jit(solution)/shard_map/ppermute | solution.py:675
  20.1 0.0 all-to-all-done.recv_ref
  20.1 1.7 %forward_run.1 = (f32[128,128]{1,0:T(8,128)S(1)}, f32[288,128]{1,0:T(8,128)S(1)}, f32[12,16,256]{2,1,0:T(8,128)S(1)}) custom-call(f32[224,128]{1,0:T(8,128)S(1)} %copy-done, f32[168,128]{1,0:T(8,128)S(1)} %collective-permute-done.lower_ref, f32[168,128]{1,0:T(8,128)S(1)} %collective-permute-done.1.higher_ref, f32[32,1,768]{2,1,0:T(1,128)S(1)} %all-to-all-done.recv_ref, ...), custom_call_target="tpu_custom_call" | custom-call | tf_op jit(solution)/shard_map/forward_run/pallas_call | solution.py:26
  21.7 0.0 copy-start.2
  21.8 11.8 %all_to_all.20 = f32[32,4,128]{2,1,0:T(4,128)S(1)} all-to-all(f32[32,4,128]{2,1,0:T(4,128)S(1)} %bitcast.15), channel_id=1, replica_groups=mesh['gx'=4,'gy'=8] {'gx','gy'}, dimensions={0} | all-to-all | bytes 131072 | tf_op jit(solution)/shard_map/all_to_all | solution.py:644
  33.6 1.1 %channel_sums.1 = (f32[3,1024]{1,0:T(4,128)S(1)}, f32[128,128]{1,0:T(8,128)S(1)}) custom-call(f32[128,128]{1,0:T(8,128)S(1)} %bitcast.14, f32[3,1024]{1,0:T(4,128)S(1)} %copy-done.2), custom_call_target="tpu_custom_call" | custom-call | tf_op jit(solution)/shard_map/channel_sums/pallas_call | solution.py:26
  34.7 9.1 %all_to_all.21 = f32[32,4,128]{2,1,0:T(4,128)S(1)} all-to-all(f32[32,4,128]{2,1,0:T(4,128)S(1)} %bitcast.16), channel_id=1, replica_groups=mesh['gx'=4,'gy'=8] {'gx','gy'}, dimensions={0} | all-to-all | bytes 131072 | tf_op jit(solution)/shard_map/all_to_all | solution.py:644
  43.8 1.7 %segment_loads.1 = (f32[96,128]{1,0:T(8,128)S(1)}, f32[48,128]{1,0:T(8,128)S(1)}, f32[48,128]{1,0:T(8,128)S(1)}, f32[32,1,384]{2,1,0:T(1,128)}) custom-call(f32[128,128]{1,0:T(8,128)S(1)} %bitcast.13, s32[16,128]{1,0:T(8,128)S(1)} %get-tuple-element.25.slot_ref, s32[16,128]{1,0:T(8,128)S(1)} %get-tuple-element.26.row_ref, f32[2,2048]{1,0:T(2,128)S(1)} %copy-done.1, ...), custom_call_target="tpu_custom_call" | custom-call | tf_op jit(solution)/shard_map/segment_loads/pallas_call | solution.py:26
  45.5 2.6 %all-to-all-start.3 = ((f32[32,1,384]{2,1,0:T(1,128)}), f32[32,1,384]{2,1,0:T(1,128)S(1)}, u32[]{:S(2)}, u32[]{:S(2)}) async-start(f32[32,1,384]{2,1,0:T(1,128)} %get-tuple-element.34), calls=%async_computation.3 | async-start | bytes 98304 | tf_op jit(solution)/shard_map/all_to_all | solution.py:644
  48.1 1.3 %collective-permute-start.2 = (f32[48,128]{1,0:T(8,128)S(1)}, f32[48,128]{1,0:T(8,128)S(1)}, u32[]{:S(2)}, u32[]{:S(2)}) collective-permute-start(f32[48,128]{1,0:T(8,128)S(1)} %get-tuple-element.32), channel_id=1, source_target_pairs={{8,0},{16,8},{24,16},{9,1},{17,9},{25,17},{10,2},{18,10},{26,18},{... | collective-permute-start | bytes 73736 | tf_op jit(solution)/shard_map/ppermute | solution.py:751
  49.4 4.5 %collective-permute-start.3 = (f32[48,128]{1,0:T(8,128)S(1)}, f32[48,128]{1,0:T(8,128)S(1)}, u32[]{:S(2)}, u32[]{:S(2)}) collective-permute-start(f32[48,128]{1,0:T(8,128)S(1)} %get-tuple-element.33), channel_id=1, source_target_pairs={{0,8},{8,16},{16,24},{1,9},{9,17},{17,25},{2,10},{10,18},{18,26},{... | collective-permute-start | bytes 73736 | tf_op jit(solution)/shard_map/ppermute | solution.py:750
  53.9 1.5 %collective-permute-done.3.lower_ref = f32[48,128]{1,0:T(8,128)S(1)} collective-permute-done((f32[48,128]{1,0:T(8,128)S(1)}, f32[48,128]{1,0:T(8,128)S(1)}, u32[]{:S(2)}, u32[]{:S(2)}) %collective-permute-start.3) | collective-permute-done | bytes 24608 | tf_op jit(solution)/shard_map/ppermute | solution.py:750
  55.4 0.0 all-to-all-done.3.recv_ref
  55.4 1.3 %adjoint_run.1 = (f32[32,128]{1,0:T(8,128)}, f32[3,1024]{1,0:T(4,128)}) custom-call(f32[96,128]{1,0:T(8,128)S(1)} %get-tuple-element.31.load_ref, f32[48,128]{1,0:T(8,128)S(1)} %collective-permute-done.2.higher_ref, f32[48,128]{1,0:T(8,128)S(1)} %collective-permute-done.3.lower_ref, f32[32,1,384]{2,1,0:T(1,128)S(1)} %all-to-all-done.3.recv_ref, ...), custom_call_target="tpu_custom_call" | custom-call | tf_op jit(solution)/shard_map/adjoint_run/pallas_call | solution.py:26
  (8 shorter events, 0.0 us)
Async XLA Ops:
  2.4 12.4 %copy-start.4 = (s32[2048,1]{0,1:T(1,128)S(1)}, s32[2048,1]{0,1:T(1,128)}, u32[]{:S(2)}) copy-start(s32[2048,1]{0,1:T(1,128)} %param.19) | copy-start | bytes 24580
  2.4 12.3 %copy-start.5 = (s32[2048]{0:T(1024)S(1)}, s32[2048]{0:T(1024)}, u32[]{:S(2)}) copy-start(s32[2048]{0:T(1024)} %param.17) | copy-start | bytes 24580
  2.4 17.6 %copy-start = (f32[224,128]{1,0:T(8,128)S(1)}, f32[224,128]{1,0:T(8,128)}, u32[]{:S(2)}) copy-start(f32[224,128]{1,0:T(8,128)} %get-tuple-element.21.fields_ref) | copy-start | bytes 344068
  2.4 17.6 %all-to-all-start = ((f32[32,1,768]{2,1,0:T(1,128)}), f32[32,1,768]{2,1,0:T(1,128)S(1)}, u32[]{:S(2)}, u32[]{:S(2)}) async-start(f32[32,1,768]{2,1,0:T(1,128)} %get-tuple-element.24), calls=%async_computation | async-start | bytes 196608 | tf_op jit(solution)/shard_map/all_to_all | solution.py:644
  9.8 6.1 %collective-permute-start = (f32[168,128]{1,0:T(8,128)}, f32[168,128]{1,0:T(8,128)S(1)}, u32[]{:S(2)}, u32[]{:S(2)}) collective-permute-start(f32[168,128]{1,0:T(8,128)} %get-tuple-element.22), channel_id=1, source_target_pairs={{0,8},{8,16},{16,24},{1,9},{9,17},{17,25},{2,10},{10,18},{18,26},{... | collective-permute-start | bytes 258056 | tf_op jit(solution)/shard_map/ppermute | solution.py:674
  13.4 6.6 %copy-start.1 = (f32[2,2048]{1,0:T(2,128)S(1)}, f32[2,2048]{1,0:T(2,128)}, u32[]{:S(2)}) copy-start(f32[2,2048]{1,0:T(2,128)} %weight_ref.3) | copy-start | bytes 49156
  13.5 6.6 %collective-permute-start.1 = (f32[168,128]{1,0:T(8,128)}, f32[168,128]{1,0:T(8,128)S(1)}, u32[]{:S(2)}, u32[]{:S(2)}) collective-permute-start(f32[168,128]{1,0:T(8,128)} %get-tuple-element.23), channel_id=1, source_target_pairs={{8,0},{16,8},{24,16},{9,1},{17,9},{25,17},{10,2},{18,10},{26,18},{... | collective-permute-start | bytes 258056 | tf_op jit(solution)/shard_map/ppermute | solution.py:675
  15.4 4.6 %copy-start.3 = (s32[2048]{0:T(1024)S(1)}, s32[2048]{0:T(1024)}, u32[]{:S(2)}) copy-start(s32[2048]{0:T(1024)} %param.20) | copy-start | bytes 24580
  21.7 11.9 %copy-start.2 = (f32[3,1024]{1,0:T(4,128)S(1)}, f32[3,1024]{1,0:T(4,128)}, u32[]{:S(2)}) copy-start(f32[3,1024]{1,0:T(4,128)} %observed_ref.1) | copy-start | bytes 36868
  45.5 9.9 %all-to-all-start.3 = ((f32[32,1,384]{2,1,0:T(1,128)}), f32[32,1,384]{2,1,0:T(1,128)S(1)}, u32[]{:S(2)}, u32[]{:S(2)}) async-start(f32[32,1,384]{2,1,0:T(1,128)} %get-tuple-element.34), calls=%async_computation.3 | async-start | bytes 98304 | tf_op jit(solution)/shard_map/all_to_all | solution.py:644
  48.1 5.9 %collective-permute-start.2 = (f32[48,128]{1,0:T(8,128)S(1)}, f32[48,128]{1,0:T(8,128)S(1)}, u32[]{:S(2)}, u32[]{:S(2)}) collective-permute-start(f32[48,128]{1,0:T(8,128)S(1)} %get-tuple-element.32), channel_id=1, source_target_pairs={{8,0},{16,8},{24,16},{9,1},{17,9},{25,17},{10,2},{18,10},{26,18},{... | collective-permute-start | bytes 73736 | tf_op jit(solution)/shard_map/ppermute | solution.py:751
  49.4 6.1 %collective-permute-start.3 = (f32[48,128]{1,0:T(8,128)S(1)}, f32[48,128]{1,0:T(8,128)S(1)}, u32[]{:S(2)}, u32[]{:S(2)}) collective-permute-start(f32[48,128]{1,0:T(8,128)S(1)} %get-tuple-element.33), channel_id=1, source_target_pairs={{0,8},{8,16},{16,24},{1,9},{9,17},{17,25},{2,10},{10,18},{18,26},{... | collective-permute-start | bytes 73736 | tf_op jit(solution)/shard_map/ppermute | solution.py:750

commit v16 on v15

--- a/solution.py
+++ b/solution.py
@@ -236,21 +236,31 @@
                 target[3 + number][z] = narrowed(plane) if wide else plane
 
 
+def slabs_of(depth):
+    whole, inner, first = 14 * depth, 10 * depth, 2 * depth
+    low = ((0, 0, whole), (1, 0, whole), (2, first, inner))
+    high = ((1, first, inner), (2, 0, whole), (3, 0, whole))
+    return low, high
+
+
 def pack_body(*refs):
     inputs, outputs, scratch = refs[:6], refs[6:10], refs[10:]
     fields_ref, high_ref, low_ref, side_ref, cells_ref, wavelet_ref, arrived, sent, sent_sides = scratch
-    targets, at = [], 0
-    for source in inputs[:4]:
-        targets.append(fields_ref.at[at : at + source.shape[0]])
+    state, lame_lambda, shear_modulus, buoyancy, cells, wavelet = inputs
+    third = state.shape[0] // 3
+    sources, at = [lame_lambda, shear_modulus], 0
+    sources += [state.at[part * third : (part + 1) * third] for part in range(3)] + [buoyancy]
+    copies = [(cells, cells_ref), (wavelet, wavelet_ref)]
+    for source in sources:
+        copies.append((source, fields_ref.at[at : at + source.shape[0]]))
         at = at + source.shape[0]
     copies = [
-        pltpu.make_async_copy(source, target, arrived.at[number])
-        for number, (source, target) in enumerate(zip(inputs, targets + [cells_ref, wavelet_ref]))
+        pltpu.make_async_copy(source, target, arrived.at[number]) for number, (source, target) in enumerate(copies)
     ]
-    for copy in copies[4:] + copies[:4]:
+    for copy in copies:
         copy.start()
-    copies[4].wait()
-    copies[5].wait()
+    copies[0].wait()
+    copies[1].wait()
     cells_row = inputs[1].shape[0]
     cells = cells_ref[...]
     count = cells.shape[1]
@@ -262,24 +272,21 @@
     maps = sum_thirds(
         times_turned(jnp.concatenate(stack, axis=0).astype(BF16), jnp.where(at_lane, 1.0, 0.0).astype(BF16))
     )
-    for copy in copies[:4]:
+    for copy in copies[2:]:
         copy.wait()
     fields_ref[at:, :] = maps[cells_row:]
-    for number in range(3, 6):
+    for number in range(5, 8):
         rows = slice(number * cells_row, (number + 1) * cells_row)
         fields_ref[rows, :] = fields_ref[rows, :] + maps[:cells_row]
     rows = fields_ref[...]
     spare = 2 * LANES - rows.shape[0]
     edge_columns(jnp.concatenate([rows, jnp.zeros((spare, LANES), F32)], axis=0), side_ref)
     sides = start_sides(side_ref, outputs[3], sent_sides)
-    height = fields_ref.shape[0] // TILE_X
-    for x in range(TILE_X):
-        slab = fields_ref[pl.ds(x, height, stride=TILE_X), :]
-        if x < RIM:
-            low_ref[x * height : (x + 1) * height, :] = slab
-        if x >= TILE_X - RIM:
-            at = x - TILE_X + RIM
-            high_ref[at * height : (at + 1) * height, :] = slab
+    for target, slabs in zip((low_ref, high_ref), slabs_of(cells_row // TILE_X)):
+        at = 0
+        for x, first, count in slabs:
+            target[at : at + count, :] = fields_ref[pl.ds(first * TILE_X + x, count, stride=TILE_X), :]
+            at = at + count
     writes = [
         pltpu.make_async_copy(source, target, sent.at[number])
         for number, (source, target) in enumerate(zip((fields_ref, high_ref, low_ref), outputs))
@@ -356,18 +363,18 @@
     depth = medium_ref.shape[0] // 3
     cells_row = depth * TILE_X
     rims = rim_rows(recv_ref, turn_ref)
-    height = fields_ref.shape[0] // TILE_X
     sides_ref[...] = jnp.zeros_like(sides_ref)
-    for x in range(RIM):
-        slab = slice(x * height, (x + 1) * height)
-        sides_ref[0, pl.ds(x, height, stride=TILE_X), :] = higher_ref[slab, :]
-        sides_ref[1, pl.ds(x + TILE_X - RIM, height, stride=TILE_X), :] = lower_ref[slab, :]
+    for side, (source, slabs) in enumerate(zip((higher_ref, lower_ref), slabs_of(depth))):
+        at = 0
+        for x, first, count in slabs:
+            sides_ref[side, pl.ds(first * TILE_X + x, count, stride=TILE_X), :] = source[at : at + count, :]
+            at = at + count
     lay_planes(wide_ref, source_ref, 0, fields_ref, sides_ref.at[0], sides_ref.at[1])
     lay_planes(wide_ref, source_ref, LANES, *rims)
-    first = 9 * depth
-    medium_ref[...] = wide_ref[first:]
+    medium_ref[0 : 2 * depth] = wide_ref[0 : 2 * depth]
+    medium_ref[2 * depth :] = wide_ref[11 * depth :]
     for plane in range(3 * depth):
-        near_ref[plane] = narrowed(wide_ref[first + plane])
+        near_ref[plane] = narrowed(medium_ref[plane])
     state, near = fields_of(state_ref, 9, depth), fields_of(near_ref, 3, depth)
     for step in range(3):
 
@@ -377,7 +384,7 @@
                 strain_ref[base : base + TILE_X, :] = strain[0:TILE_X, 0:LANES]
 
         if step == 0:
-            advance(fields_of(wide_ref, 9, depth), fields_of(wide_ref, 3, depth, 9), emit, state)
+            advance(fields_of(wide_ref, 9, depth, 2), fields_of(medium_ref, 3, depth), emit, state)
             continue
         for z in range(depth):
             load = source_ref[(step - 1) * depth + z]
@@ -648,7 +655,7 @@
         back = exchange(chunks.reshape(devices, 4, capacity)).reshape(slot_groups, per_group, 4, capacity)
         return back.transpose(0, 2, 1, 3).reshape(slot_groups * 4, LANES)
 
-    trimmed = shape((14 * depth * RIM, cols_y), F32)
+    trimmed = shape((sum(count for _, _, count in slabs_of(depth)[0]), cols_y), F32)
     fields, high, low, edges = call_kernel(
         pack_body,
         "pack_edges",
@@ -660,7 +667,7 @@
             pltpu.VMEM((2, 1, 2 * RIM * LANES), F32),
             pltpu.VMEM((1, source_cells.shape[0]), I32),
             pltpu.VMEM(source_wavelet.shape, F32),
-            pltpu.SemaphoreType.DMA((6,)),
+            pltpu.SemaphoreType.DMA((8,)),
             pltpu.SemaphoreType.DMA((3,)),
             pltpu.SemaphoreType.DMA((6,)),
         ],

time: 57.2 us -> 57.1 us (level)
  no operation moved by 1% of the time
where the time goes in v16:
time: 57.1 us; the launch traced here: 56.6 us
  blocking collectives  20.9 us (37%)
  starting transfers between devices  20.7 us (36%)
  Pallas kernels  8.13 us (14%)
  waiting for transfers between devices  6.02 us (11%)
  between operations  0.8 us (1%)
    all_to_all x2, blocking collectives, exchange(): return lax.all_to_all(chunks, both, split_axis=0, concat_axis=0, tiled=True)  20.9 us
    all_to_all x2, starting transfers between devices, exchange(): return lax.all_to_all(chunks, both, split_axis=0, concat_axis=0, tiled=True)  9.88 us
    pallas_call x6, Pallas kernels, call_kernel(): pl.pallas_call(body, name=name, out_shape=outs, in_specs=[pl.BlockSpec(me...  8.13 us
    ppermute x1, starting transfers between devices, shards(): load_lower = lax.ppermute(load_high, 'gx', up)  4.55 us
    ppermute x1, waiting for transfers between devices, shards(): higher = lax.ppermute(low, 'gx', down)  4.2 us
    ppermute x1, starting transfers between devices, shards(): lower = lax.ppermute(high, 'gx', up)  3.68 us
    ppermute x1, waiting for transfers between devices, shards(): load_lower = lax.ppermute(load_high, 'gx', up)  1.49 us
    ppermute x1, starting transfers between devices, shards(): load_higher = lax.ppermute(load_low, 'gx', down)  1.29 us
  transfers between devices with their start and end apart: 6, of which 3 were waited for; matrix products, arithmetic and copies ran while one was open for 0% of the time, Pallas kernels for 1%

profile of v16, /device:TPU:0, one launch (start us, length us, event | category | flops | bytes accessed | tf_op | source)
XLA Modules:
  0.0 56.6 jit_solution(6869061249252056162)
XLA Ops:
  0.6 1.8 %pack_edges.1 = (f32[224,128]{1,0:T(8,128)}, f32[152,128]{1,0:T(8,128)}, f32[152,128]{1,0:T(8,128)}, f32[32,1,768]{2,1,0:T(1,128)}) custom-call(f32[144,128]{1,0:T(8,128)} %bitcast.20, f32[16,128]{1,0:T(8,128)} %bitcast.21, f32[16,128]{1,0:T(8,128)} %bitcast.22, f32[16,128]{1,0:T(8,128)} %bitcast.23, s32[1,64]{1,0:T(1,128)} %bitcast.24, f32[3,64]{1,0:T(4,128)} %refs_5_.1), custom_call_target="tpu_custom_call" | custom-call | tf_op jit(solution)/shard_map/pack_edges/pallas_call | solution.py:26
  2.4 0.0 copy-start.4
  2.4 0.0 copy-start.5
  2.4 7.3 %all-to-all-start = ((f32[32,1,768]{2,1,0:T(1,128)}), f32[32,1,768]{2,1,0:T(1,128)S(1)}, u32[]{:S(2)}, u32[]{:S(2)}) async-start(f32[32,1,768]{2,1,0:T(1,128)} %get-tuple-element.24), calls=%async_computation | async-start | bytes 196608 | tf_op jit(solution)/shard_map/all_to_all | solution.py:651
  9.7 3.7 %collective-permute-start = (f32[152,128]{1,0:T(8,128)}, f32[152,128]{1,0:T(8,128)S(1)}, u32[]{:S(2)}, u32[]{:S(2)}) collective-permute-start(f32[152,128]{1,0:T(8,128)} %get-tuple-element.22), channel_id=1, source_target_pairs={{0,8},{8,16},{16,24},{1,9},{9,17},{17,25},{2,10},{10,18},{18,26},{... | collective-permute-start | bytes 233480 | tf_op jit(solution)/shard_map/ppermute | solution.py:681
  13.4 0.0 copy-start.1
  13.4 1.3 %collective-permute-start.1 = (f32[152,128]{1,0:T(8,128)}, f32[152,128]{1,0:T(8,128)S(1)}, u32[]{:S(2)}, u32[]{:S(2)}) collective-permute-start(f32[152,128]{1,0:T(8,128)} %get-tuple-element.23), channel_id=1, source_target_pairs={{8,0},{16,8},{24,16},{9,1},{17,9},{25,17},{10,2},{18,10},{26,18},{... | collective-permute-start | bytes 233480 | tf_op jit(solution)/shard_map/ppermute | solution.py:682
  14.8 0.6 %segment_slots.1 = (s32[16,128]{1,0:T(8,128)S(1)}, s32[16,128]{1,0:T(8,128)S(1)}, bf16[128,2048]{1,0:T(8,128)(2,1)S(1)}, bf16[128,2048]{1,0:T(8,128)(2,1)S(1)}) custom-call(s32[16,128]{1,0:T(8,128)S(1)} %bitcast.18, s32[16,128]{1,0:T(8,128)S(1)} %bitcast.19), custom_call_target="tpu_custom_call" | custom-call | tf_op jit(solution)/shard_map/segment_slots/pallas_call | solution.py:26
  15.4 0.0 copy-start.3
  15.4 0.3 collective-permute-done.lower_ref
  15.7 4.2 %collective-permute-done.1.higher_ref = f32[152,128]{1,0:T(8,128)S(1)} collective-permute-done((f32[152,128]{1,0:T(8,128)}, f32[152,128]{1,0:T(8,128)S(1)}, u32[]{:S(2)}, u32[]{:S(2)}) %collective-permute-start.1) | collective-permute-done | bytes 77856 | tf_op jit(solution)/shard_map/ppermute | solution.py:682
  19.9 0.0 all-to-all-done.recv_ref
  20.0 1.7 %forward_run.1 = (f32[128,128]{1,0:T(8,128)S(1)}, f32[288,128]{1,0:T(8,128)S(1)}, f32[12,16,256]{2,1,0:T(8,128)S(1)}) custom-call(f32[224,128]{1,0:T(8,128)S(1)} %copy-done, f32[152,128]{1,0:T(8,128)S(1)} %collective-permute-done.lower_ref, f32[152,128]{1,0:T(8,128)S(1)} %collective-permute-done.1.higher_ref, f32[32,1,768]{2,1,0:T(1,128)S(1)} %all-to-all-done.recv_ref, ...), custom_call_target="tpu_custom_call" | custom-call | tf_op jit(solution)/shard_map/forward_run/pallas_call | solution.py:26
  21.7 0.0 copy-start.2
  21.7 11.8 %all_to_all.20 = f32[32,4,128]{2,1,0:T(4,128)S(1)} all-to-all(f32[32,4,128]{2,1,0:T(4,128)S(1)} %bitcast.15), channel_id=1, replica_groups=mesh['gx'=4,'gy'=8] {'gx','gy'}, dimensions={0} | all-to-all | bytes 131072 | tf_op jit(solution)/shard_map/all_to_all | solution.py:651
  33.5 1.1 %channel_sums.1 = (f32[3,1024]{1,0:T(4,128)S(1)}, f32[128,128]{1,0:T(8,128)S(1)}) custom-call(f32[128,128]{1,0:T(8,128)S(1)} %bitcast.14, f32[3,1024]{1,0:T(4,128)S(1)} %copy-done.2), custom_call_target="tpu_custom_call" | custom-call | tf_op jit(solution)/shard_map/channel_sums/pallas_call | solution.py:26
  34.6 9.1 %all_to_all.21 = f32[32,4,128]{2,1,0:T(4,128)S(1)} all-to-all(f32[32,4,128]{2,1,0:T(4,128)S(1)} %bitcast.16), channel_id=1, replica_groups=mesh['gx'=4,'gy'=8] {'gx','gy'}, dimensions={0} | all-to-all | bytes 131072 | tf_op jit(solution)/shard_map/all_to_all | solution.py:651
  43.7 1.7 %segment_loads.1 = (f32[96,128]{1,0:T(8,128)S(1)}, f32[48,128]{1,0:T(8,128)S(1)}, f32[48,128]{1,0:T(8,128)S(1)}, f32[32,1,384]{2,1,0:T(1,128)}) custom-call(f32[128,128]{1,0:T(8,128)S(1)} %bitcast.13, s32[16,128]{1,0:T(8,128)S(1)} %get-tuple-element.25.slot_ref, s32[16,128]{1,0:T(8,128)S(1)} %get-tuple-element.26.row_ref, f32[2,2048]{1,0:T(2,128)S(1)} %copy-done.1, ...), custom_call_target="tpu_custom_call" | custom-call | tf_op jit(solution)/shard_map/segment_loads/pallas_call | solution.py:26
  45.4 2.6 %all-to-all-start.3 = ((f32[32,1,384]{2,1,0:T(1,128)}), f32[32,1,384]{2,1,0:T(1,128)S(1)}, u32[]{:S(2)}, u32[]{:S(2)}) async-start(f32[32,1,384]{2,1,0:T(1,128)} %get-tuple-element.34), calls=%async_computation.3 | async-start | bytes 98304 | tf_op jit(solution)/shard_map/all_to_all | solution.py:651
  48.0 1.3 %collective-permute-start.2 = (f32[48,128]{1,0:T(8,128)S(1)}, f32[48,128]{1,0:T(8,128)S(1)}, u32[]{:S(2)}, u32[]{:S(2)}) collective-permute-start(f32[48,128]{1,0:T(8,128)S(1)} %get-tuple-element.32), channel_id=1, source_target_pairs={{8,0},{16,8},{24,16},{9,1},{17,9},{25,17},{10,2},{18,10},{26,18},{... | collective-permute-start | bytes 73736 | tf_op jit(solution)/shard_map/ppermute | solution.py:758
  49.3 4.5 %collective-permute-start.3 = (f32[48,128]{1,0:T(8,128)S(1)}, f32[48,128]{1,0:T(8,128)S(1)}, u32[]{:S(2)}, u32[]{:S(2)}) collective-permute-start(f32[48,128]{1,0:T(8,128)S(1)} %get-tuple-element.33), channel_id=1, source_target_pairs={{0,8},{8,16},{16,24},{1,9},{9,17},{17,25},{2,10},{10,18},{18,26},{... | collective-permute-start | bytes 73736 | tf_op jit(solution)/shard_map/ppermute | solution.py:757
  53.9 0.0 collective-permute-done.2.higher_ref
  53.9 1.5 %collective-permute-done.3.lower_ref = f32[48,128]{1,0:T(8,128)S(1)} collective-permute-done((f32[48,128]{1,0:T(8,128)S(1)}, f32[48,128]{1,0:T(8,128)S(1)}, u32[]{:S(2)}, u32[]{:S(2)}) %collective-permute-start.3) | collective-permute-done | bytes 24608 | tf_op jit(solution)/shard_map/ppermute | solution.py:757
  55.4 1.3 %adjoint_run.1 = (f32[32,128]{1,0:T(8,128)}, f32[3,1024]{1,0:T(4,128)}) custom-call(f32[96,128]{1,0:T(8,128)S(1)} %get-tuple-element.31.load_ref, f32[48,128]{1,0:T(8,128)S(1)} %collective-permute-done.2.higher_ref, f32[48,128]{1,0:T(8,128)S(1)} %collective-permute-done.3.lower_ref, f32[32,1,384]{2,1,0:T(1,128)S(1)} %all-to-all-done.3.recv_ref, ...), custom_call_target="tpu_custom_call" | custom-call | tf_op jit(solution)/shard_map/adjoint_run/pallas_call | solution.py:26
  (8 shorter events, 0.0 us)
Async XLA Ops:
  2.4 12.3 %copy-start.4 = (s32[2048,1]{0,1:T(1,128)S(1)}, s32[2048,1]{0,1:T(1,128)}, u32[]{:S(2)}) copy-start(s32[2048,1]{0,1:T(1,128)} %param.19) | copy-start | bytes 24580
  2.4 12.3 %copy-start.5 = (s32[2048]{0:T(1024)S(1)}, s32[2048]{0:T(1024)}, u32[]{:S(2)}) copy-start(s32[2048]{0:T(1024)} %param.17) | copy-start | bytes 24580
  2.4 17.5 %copy-start = (f32[224,128]{1,0:T(8,128)S(1)}, f32[224,128]{1,0:T(8,128)}, u32[]{:S(2)}) copy-start(f32[224,128]{1,0:T(8,128)} %get-tuple-element.21.fields_ref) | copy-start | bytes 344068
  2.4 17.5 %all-to-all-start = ((f32[32,1,768]{2,1,0:T(1,128)}), f32[32,1,768]{2,1,0:T(1,128)S(1)}, u32[]{:S(2)}, u32[]{:S(2)}) async-start(f32[32,1,768]{2,1,0:T(1,128)} %get-tuple-element.24), calls=%async_computation | async-start | bytes 196608 | tf_op jit(solution)/shard_map/all_to_all | solution.py:651
  9.7 6.0 %collective-permute-start = (f32[152,128]{1,0:T(8,128)}, f32[152,128]{1,0:T(8,128)S(1)}, u32[]{:S(2)}, u32[]{:S(2)}) collective-permute-start(f32[152,128]{1,0:T(8,128)} %get-tuple-element.22), channel_id=1, source_target_pairs={{0,8},{8,16},{16,24},{1,9},{9,17},{17,25},{2,10},{10,18},{18,26},{... | collective-permute-start | bytes 233480 | tf_op jit(solution)/shard_map/ppermute | solution.py:681
  13.4 6.5 %copy-start.1 = (f32[2,2048]{1,0:T(2,128)S(1)}, f32[2,2048]{1,0:T(2,128)}, u32[]{:S(2)}) copy-start(f32[2,2048]{1,0:T(2,128)} %weight_ref.3) | copy-start | bytes 49156
  13.4 6.5 %collective-permute-start.1 = (f32[152,128]{1,0:T(8,128)}, f32[152,128]{1,0:T(8,128)S(1)}, u32[]{:S(2)}, u32[]{:S(2)}) collective-permute-start(f32[152,128]{1,0:T(8,128)} %get-tuple-element.23), channel_id=1, source_target_pairs={{8,0},{16,8},{24,16},{9,1},{17,9},{25,17},{10,2},{18,10},{26,18},{... | collective-permute-start | bytes 233480 | tf_op jit(solution)/shard_map/ppermute | solution.py:682
  15.4 4.5 %copy-start.3 = (s32[2048]{0:T(1024)S(1)}, s32[2048]{0:T(1024)}, u32[]{:S(2)}) copy-start(s32[2048]{0:T(1024)} %param.20) | copy-start | bytes 24580
  21.7 11.9 %copy-start.2 = (f32[3,1024]{1,0:T(4,128)S(1)}, f32[3,1024]{1,0:T(4,128)}, u32[]{:S(2)}) copy-start(f32[3,1024]{1,0:T(4,128)} %observed_ref.1) | copy-start | bytes 36868
  45.4 9.9 %all-to-all-start.3 = ((f32[32,1,384]{2,1,0:T(1,128)}), f32[32,1,384]{2,1,0:T(1,128)S(1)}, u32[]{:S(2)}, u32[]{:S(2)}) async-start(f32[32,1,384]{2,1,0:T(1,128)} %get-tuple-element.34), calls=%async_computation.3 | async-start | bytes 98304 | tf_op jit(solution)/shard_map/all_to_all | solution.py:651
  48.0 5.9 %collective-permute-start.2 = (f32[48,128]{1,0:T(8,128)S(1)}, f32[48,128]{1,0:T(8,128)S(1)}, u32[]{:S(2)}, u32[]{:S(2)}) collective-permute-start(f32[48,128]{1,0:T(8,128)S(1)} %get-tuple-element.32), channel_id=1, source_target_pairs={{8,0},{16,8},{24,16},{9,1},{17,9},{25,17},{10,2},{18,10},{26,18},{... | collective-permute-start | bytes 73736 | tf_op jit(solution)/shard_map/ppermute | solution.py:758
  49.3 6.1 %collective-permute-start.3 = (f32[48,128]{1,0:T(8,128)S(1)}, f32[48,128]{1,0:T(8,128)S(1)}, u32[]{:S(2)}, u32[]{:S(2)}) collective-permute-start(f32[48,128]{1,0:T(8,128)S(1)} %get-tuple-element.33), channel_id=1, source_target_pairs={{0,8},{8,16},{16,24},{1,9},{9,17},{17,25},{2,10},{10,18},{18,26},{... | collective-permute-start | bytes 73736 | tf_op jit(solution)/shard_map/ppermute | solution.py:757

commit v17 on v15

--- a/solution.py
+++ b/solution.py
@@ -12,6 +12,7 @@
 RIM = 3
 LANES = 128
 TILE_X = 4
+SPARE = 8
 SPAN_X = 16
 SPAN_NEAR = 8
 SPAN_Y = 256
@@ -264,15 +265,16 @@
     )
     for copy in copies[:4]:
         copy.wait()
-    fields_ref[at:, :] = maps[cells_row:]
+    total = at + 2 * cells_row
+    fields_ref[at:total, :] = maps[cells_row:]
     for number in range(3, 6):
         rows = slice(number * cells_row, (number + 1) * cells_row)
         fields_ref[rows, :] = fields_ref[rows, :] + maps[:cells_row]
-    rows = fields_ref[...]
-    spare = 2 * LANES - rows.shape[0]
+    rows = fields_ref[0:total, :]
+    spare = 2 * LANES - total
     edge_columns(jnp.concatenate([rows, jnp.zeros((spare, LANES), F32)], axis=0), side_ref)
     sides = start_sides(side_ref, outputs[3], sent_sides)
-    height = fields_ref.shape[0] // TILE_X
+    height = total // TILE_X
     for x in range(TILE_X):
         slab = fields_ref[pl.ds(x, height, stride=TILE_X), :]
         if x < RIM:
@@ -282,7 +284,7 @@
             high_ref[at * height : (at + 1) * height, :] = slab
     writes = [
         pltpu.make_async_copy(source, target, sent.at[number])
-        for number, (source, target) in enumerate(zip((fields_ref, high_ref, low_ref), outputs))
+        for number, (source, target) in enumerate(zip((fields_ref.at[0:total], high_ref, low_ref), outputs))
     ]
     for copy in writes:
         copy.start()
@@ -478,6 +480,7 @@
     out_ref,
     spread_ref,
     side_ref,
+    held_ref,
     sent_sides,
 ):
     cells_row = load_ref.shape[0] // 6
@@ -512,13 +515,15 @@
             lanes = slice(column * LANES, column * LANES + stack_rows)
             side_ref[side, 0:1, lanes] = edges[base + column : base + column + 1, :]
     sides = start_sides(side_ref, out_ref, sent_sides)
-    load_ref[...] = sum_halves(times_turned(spread_ref[...], cover_ref[...]))
+    load = sum_halves(times_turned(spread_ref[...], cover_ref[...]))
+    load_ref[...] = load
+    held_ref[0:stack_rows, :] = load
     count = stack_rows // (3 * TILE_X)
     for at, (turn, distance) in enumerate(reached()):
         rows = slice(at * count, (at + 1) * count)
         first = turn * count * TILE_X
-        low_ref[rows, :] = load_ref[pl.ds(first + distance, count, stride=TILE_X), :]
-        high_ref[rows, :] = load_ref[pl.ds(first + TILE_X - 1 - distance, count, stride=TILE_X), :]
+        low_ref[rows, :] = held_ref[pl.ds(first + distance, count, stride=TILE_X), :]
+        high_ref[rows, :] = held_ref[pl.ds(first + TILE_X - 1 - distance, count, stride=TILE_X), :]
     wait_sides(sides)
 
 
@@ -654,7 +659,7 @@
         "pack_edges",
         [shape((14 * cells_row, cols_y), F32), trimmed, trimmed, shape((devices, 1, 2 * RIM * LANES), F32)],
         [
-            pltpu.VMEM((14 * cells_row, cols_y), F32),
+            pltpu.VMEM((14 * cells_row + SPARE, cols_y), F32),
             pltpu.VMEM(trimmed.shape, F32),
             pltpu.VMEM(trimmed.shape, F32),
             pltpu.VMEM((2, 1, 2 * RIM * LANES), F32),
@@ -702,7 +707,7 @@
             pltpu.VMEM((9 * depth, SPAN_NEAR, SPAN_Y), F32),
             pltpu.VMEM((3 * depth, SPAN_NEAR, SPAN_Y), F32),
             pltpu.VMEM((3, LANES, 2 * LANES), F32),
-            pltpu.VMEM((2, 14 * cells_row, cols_y), F32),
+            pltpu.VMEM((2, 14 * cells_row + SPARE, cols_y), F32),
             pltpu.VMEM((3 * LANES, part_count), BF16),
         ],
         fields,
@@ -737,6 +742,7 @@
         [
             pltpu.VMEM((12 * cells_row, part_count), BF16),
             pltpu.VMEM((2, 1, RIM * LANES), F32),
+            pltpu.VMEM((6 * cells_row + SPARE, cols_y), F32),
             pltpu.SemaphoreType.DMA((6,)),
         ],
         to_owners(reply),
@@ -761,7 +767,7 @@
             pltpu.VMEM((9 * depth, SPAN_NEAR, SPAN_Y), F32),
             pltpu.VMEM((3 * depth, SPAN_NEAR, SPAN_Y), F32),
             pltpu.VMEM((3, LANES, LANES), F32),
-            pltpu.VMEM((2, 6 * cells_row, cols_y), F32),
+            pltpu.VMEM((2, 6 * cells_row + SPARE, cols_y), F32),
         ],
         loads,
         load_higher,

time: 57.2 us -> 57.1 us (level)
  no operation moved by 1% of the time
where the time goes in v17:
time: 57.1 us; the launch traced here: 56.7 us
  blocking collectives  20.9 us (37%)
  starting transfers between devices  20.7 us (36%)
  Pallas kernels  8.11 us (14%)
  waiting for transfers between devices  6.11 us (11%)
  between operations  0.8 us (1%)
    all_to_all x2, blocking collectives, exchange(): return lax.all_to_all(chunks, both, split_axis=0, concat_axis=0, tiled=True)  20.9 us
    all_to_all x2, starting transfers between devices, exchange(): return lax.all_to_all(chunks, both, split_axis=0, concat_axis=0, tiled=True)  9.89 us
    pallas_call x6, Pallas kernels, call_kernel(): pl.pallas_call(body, name=name, out_shape=outs, in_specs=[pl.BlockSpec(me...  8.11 us
    ppermute x1, starting transfers between devices, shards(): load_lower = lax.ppermute(load_high, 'gx', up)  4.55 us
    ppermute x1, waiting for transfers between devices, shards(): higher = lax.ppermute(low, 'gx', down)  4.2 us
    ppermute x1, starting transfers between devices, shards(): lower = lax.ppermute(high, 'gx', up)  3.68 us
    ppermute x1, waiting for transfers between devices, shards(): load_lower = lax.ppermute(load_high, 'gx', up)  1.49 us
    ppermute x1, starting transfers between devices, shards(): higher = lax.ppermute(low, 'gx', down)  1.29 us
  transfers between devices with their start and end apart: 6, of which 3 were waited for; matrix products, arithmetic and copies ran while one was open for 0% of the time, Pallas kernels for 1%

profile of v17, /device:TPU:0, one launch (start us, length us, event | category | flops | bytes accessed | tf_op | source)
XLA Modules:
  0.0 56.7 jit_solution(13418868768494448528)
XLA Ops:
  0.6 1.8 %pack_edges.1 = (f32[224,128]{1,0:T(8,128)}, f32[168,128]{1,0:T(8,128)}, f32[168,128]{1,0:T(8,128)}, f32[32,1,768]{2,1,0:T(1,128)}) custom-call(f32[144,128]{1,0:T(8,128)} %bitcast.20, f32[16,128]{1,0:T(8,128)} %bitcast.21, f32[16,128]{1,0:T(8,128)} %bitcast.22, f32[16,128]{1,0:T(8,128)} %bitcast.23, s32[1,64]{1,0:T(1,128)} %bitcast.24, f32[3,64]{1,0:T(4,128)} %refs_5_.1), custom_call_target="tpu_custom_call" | custom-call | tf_op jit(solution)/shard_map/pack_edges/pallas_call | solution.py:27
  2.4 0.0 copy-start.4
  2.4 0.0 copy-start.5
  2.4 7.3 %all-to-all-start = ((f32[32,1,768]{2,1,0:T(1,128)}), f32[32,1,768]{2,1,0:T(1,128)S(1)}, u32[]{:S(2)}, u32[]{:S(2)}) async-start(f32[32,1,768]{2,1,0:T(1,128)} %get-tuple-element.24), calls=%async_computation | async-start | bytes 196608 | tf_op jit(solution)/shard_map/all_to_all | solution.py:649
  9.8 3.7 %collective-permute-start = (f32[168,128]{1,0:T(8,128)}, f32[168,128]{1,0:T(8,128)S(1)}, u32[]{:S(2)}, u32[]{:S(2)}) collective-permute-start(f32[168,128]{1,0:T(8,128)} %get-tuple-element.22), channel_id=1, source_target_pairs={{0,8},{8,16},{16,24},{1,9},{9,17},{17,25},{2,10},{10,18},{18,26},{... | collective-permute-start | bytes 258056 | tf_op jit(solution)/shard_map/ppermute | solution.py:679
  13.4 0.0 copy-start.1
  13.5 1.3 %collective-permute-start.1 = (f32[168,128]{1,0:T(8,128)}, f32[168,128]{1,0:T(8,128)S(1)}, u32[]{:S(2)}, u32[]{:S(2)}) collective-permute-start(f32[168,128]{1,0:T(8,128)} %get-tuple-element.23), channel_id=1, source_target_pairs={{8,0},{16,8},{24,16},{9,1},{17,9},{25,17},{10,2},{18,10},{26,18},{... | collective-permute-start | bytes 258056 | tf_op jit(solution)/shard_map/ppermute | solution.py:680
  14.8 0.6 %segment_slots.1 = (s32[16,128]{1,0:T(8,128)S(1)}, s32[16,128]{1,0:T(8,128)S(1)}, bf16[128,2048]{1,0:T(8,128)(2,1)S(1)}, bf16[128,2048]{1,0:T(8,128)(2,1)S(1)}) custom-call(s32[16,128]{1,0:T(8,128)S(1)} %bitcast.18, s32[16,128]{1,0:T(8,128)S(1)} %bitcast.19), custom_call_target="tpu_custom_call" | custom-call | tf_op jit(solution)/shard_map/segment_slots/pallas_call | solution.py:27
  15.4 0.0 copy-start.3
  15.4 0.4 collective-permute-done.lower_ref
  15.8 4.2 %collective-permute-done.1.higher_ref = f32[168,128]{1,0:T(8,128)S(1)} collective-permute-done((f32[168,128]{1,0:T(8,128)}, f32[168,128]{1,0:T(8,128)S(1)}, u32[]{:S(2)}, u32[]{:S(2)}) %collective-permute-start.1) | collective-permute-done | bytes 86048 | tf_op jit(solution)/shard_map/ppermute | solution.py:680
  20.1 0.0 all-to-all-done.recv_ref
  20.1 1.7 %forward_run.1 = (f32[128,128]{1,0:T(8,128)S(1)}, f32[288,128]{1,0:T(8,128)S(1)}, f32[12,16,256]{2,1,0:T(8,128)S(1)}) custom-call(f32[224,128]{1,0:T(8,128)S(1)} %copy-done, f32[168,128]{1,0:T(8,128)S(1)} %collective-permute-done.lower_ref, f32[168,128]{1,0:T(8,128)S(1)} %collective-permute-done.1.higher_ref, f32[32,1,768]{2,1,0:T(1,128)S(1)} %all-to-all-done.recv_ref, ...), custom_call_target="tpu_custom_call" | custom-call | tf_op jit(solution)/shard_map/forward_run/pallas_call | solution.py:27
  21.7 0.0 copy-start.2
  21.8 11.8 %all_to_all.20 = f32[32,4,128]{2,1,0:T(4,128)S(1)} all-to-all(f32[32,4,128]{2,1,0:T(4,128)S(1)} %bitcast.15), channel_id=1, replica_groups=mesh['gx'=4,'gy'=8] {'gx','gy'}, dimensions={0} | all-to-all | bytes 131072 | tf_op jit(solution)/shard_map/all_to_all | solution.py:649
  33.6 1.1 %channel_sums.1 = (f32[3,1024]{1,0:T(4,128)S(1)}, f32[128,128]{1,0:T(8,128)S(1)}) custom-call(f32[128,128]{1,0:T(8,128)S(1)} %bitcast.14, f32[3,1024]{1,0:T(4,128)S(1)} %copy-done.2), custom_call_target="tpu_custom_call" | custom-call | tf_op jit(solution)/shard_map/channel_sums/pallas_call | solution.py:27
  34.7 9.1 %all_to_all.21 = f32[32,4,128]{2,1,0:T(4,128)S(1)} all-to-all(f32[32,4,128]{2,1,0:T(4,128)S(1)} %bitcast.16), channel_id=1, replica_groups=mesh['gx'=4,'gy'=8] {'gx','gy'}, dimensions={0} | all-to-all | bytes 131072 | tf_op jit(solution)/shard_map/all_to_all | solution.py:649
  43.8 1.7 %segment_loads.1 = (f32[96,128]{1,0:T(8,128)S(1)}, f32[48,128]{1,0:T(8,128)S(1)}, f32[48,128]{1,0:T(8,128)S(1)}, f32[32,1,384]{2,1,0:T(1,128)}) custom-call(f32[128,128]{1,0:T(8,128)S(1)} %bitcast.13, s32[16,128]{1,0:T(8,128)S(1)} %get-tuple-element.25.slot_ref, s32[16,128]{1,0:T(8,128)S(1)} %get-tuple-element.26.row_ref, f32[2,2048]{1,0:T(2,128)S(1)} %copy-done.1, ...), custom_call_target="tpu_custom_call" | custom-call | tf_op jit(solution)/shard_map/segment_loads/pallas_call | solution.py:27
  45.5 2.6 %all-to-all-start.3 = ((f32[32,1,384]{2,1,0:T(1,128)}), f32[32,1,384]{2,1,0:T(1,128)S(1)}, u32[]{:S(2)}, u32[]{:S(2)}) async-start(f32[32,1,384]{2,1,0:T(1,128)} %get-tuple-element.34), calls=%async_computation.3 | async-start | bytes 98304 | tf_op jit(solution)/shard_map/all_to_all | solution.py:649
  48.1 1.3 %collective-permute-start.2 = (f32[48,128]{1,0:T(8,128)S(1)}, f32[48,128]{1,0:T(8,128)S(1)}, u32[]{:S(2)}, u32[]{:S(2)}) collective-permute-start(f32[48,128]{1,0:T(8,128)S(1)} %get-tuple-element.32), channel_id=1, source_target_pairs={{8,0},{16,8},{24,16},{9,1},{17,9},{25,17},{10,2},{18,10},{26,18},{... | collective-permute-start | bytes 73736 | tf_op jit(solution)/shard_map/ppermute | solution.py:757
  49.4 4.5 %collective-permute-start.3 = (f32[48,128]{1,0:T(8,128)S(1)}, f32[48,128]{1,0:T(8,128)S(1)}, u32[]{:S(2)}, u32[]{:S(2)}) collective-permute-start(f32[48,128]{1,0:T(8,128)S(1)} %get-tuple-element.33), channel_id=1, source_target_pairs={{0,8},{8,16},{16,24},{1,9},{9,17},{17,25},{2,10},{10,18},{18,26},{... | collective-permute-start | bytes 73736 | tf_op jit(solution)/shard_map/ppermute | solution.py:756
  53.9 1.5 %collective-permute-done.3.lower_ref = f32[48,128]{1,0:T(8,128)S(1)} collective-permute-done((f32[48,128]{1,0:T(8,128)S(1)}, f32[48,128]{1,0:T(8,128)S(1)}, u32[]{:S(2)}, u32[]{:S(2)}) %collective-permute-start.3) | collective-permute-done | bytes 24608 | tf_op jit(solution)/shard_map/ppermute | solution.py:756
  55.4 0.0 all-to-all-done.3.recv_ref
  55.4 1.3 %adjoint_run.1 = (f32[32,128]{1,0:T(8,128)}, f32[3,1024]{1,0:T(4,128)}) custom-call(f32[96,128]{1,0:T(8,128)S(1)} %get-tuple-element.31.load_ref, f32[48,128]{1,0:T(8,128)S(1)} %collective-permute-done.2.higher_ref, f32[48,128]{1,0:T(8,128)S(1)} %collective-permute-done.3.lower_ref, f32[32,1,384]{2,1,0:T(1,128)S(1)} %all-to-all-done.3.recv_ref, ...), custom_call_target="tpu_custom_call" | custom-call | tf_op jit(solution)/shard_map/adjoint_run/pallas_call | solution.py:27
  (8 shorter events, 0.0 us)
Async XLA Ops:
  2.4 12.4 %copy-start.4 = (s32[2048,1]{0,1:T(1,128)S(1)}, s32[2048,1]{0,1:T(1,128)}, u32[]{:S(2)}) copy-start(s32[2048,1]{0,1:T(1,128)} %param.19) | copy-start | bytes 24580
  2.4 12.3 %copy-start.5 = (s32[2048]{0:T(1024)S(1)}, s32[2048]{0:T(1024)}, u32[]{:S(2)}) copy-start(s32[2048]{0:T(1024)} %param.17) | copy-start | bytes 24580
  2.4 17.6 %copy-start = (f32[224,128]{1,0:T(8,128)S(1)}, f32[224,128]{1,0:T(8,128)}, u32[]{:S(2)}) copy-start(f32[224,128]{1,0:T(8,128)} %get-tuple-element.21.fields_ref) | copy-start | bytes 344068
  2.4 17.6 %all-to-all-start = ((f32[32,1,768]{2,1,0:T(1,128)}), f32[32,1,768]{2,1,0:T(1,128)S(1)}, u32[]{:S(2)}, u32[]{:S(2)}) async-start(f32[32,1,768]{2,1,0:T(1,128)} %get-tuple-element.24), calls=%async_computation | async-start | bytes 196608 | tf_op jit(solution)/shard_map/all_to_all | solution.py:649
  9.8 6.1 %collective-permute-start = (f32[168,128]{1,0:T(8,128)}, f32[168,128]{1,0:T(8,128)S(1)}, u32[]{:S(2)}, u32[]{:S(2)}) collective-permute-start(f32[168,128]{1,0:T(8,128)} %get-tuple-element.22), channel_id=1, source_target_pairs={{0,8},{8,16},{16,24},{1,9},{9,17},{17,25},{2,10},{10,18},{18,26},{... | collective-permute-start | bytes 258056 | tf_op jit(solution)/shard_map/ppermute | solution.py:679
  13.4 6.6 %copy-start.1 = (f32[2,2048]{1,0:T(2,128)S(1)}, f32[2,2048]{1,0:T(2,128)}, u32[]{:S(2)}) copy-start(f32[2,2048]{1,0:T(2,128)} %weight_ref.3) | copy-start | bytes 49156
  13.5 6.6 %collective-permute-start.1 = (f32[168,128]{1,0:T(8,128)}, f32[168,128]{1,0:T(8,128)S(1)}, u32[]{:S(2)}, u32[]{:S(2)}) collective-permute-start(f32[168,128]{1,0:T(8,128)} %get-tuple-element.23), channel_id=1, source_target_pairs={{8,0},{16,8},{24,16},{9,1},{17,9},{25,17},{10,2},{18,10},{26,18},{... | collective-permute-start | bytes 258056 | tf_op jit(solution)/shard_map/ppermute | solution.py:680
  15.4 4.6 %copy-start.3 = (s32[2048]{0:T(1024)S(1)}, s32[2048]{0:T(1024)}, u32[]{:S(2)}) copy-start(s32[2048]{0:T(1024)} %param.20) | copy-start | bytes 24580
  21.7 11.9 %copy-start.2 = (f32[3,1024]{1,0:T(4,128)S(1)}, f32[3,1024]{1,0:T(4,128)}, u32[]{:S(2)}) copy-start(f32[3,1024]{1,0:T(4,128)} %observed_ref.1) | copy-start | bytes 36868
  45.5 9.9 %all-to-all-start.3 = ((f32[32,1,384]{2,1,0:T(1,128)}), f32[32,1,384]{2,1,0:T(1,128)S(1)}, u32[]{:S(2)}, u32[]{:S(2)}) async-start(f32[32,1,384]{2,1,0:T(1,128)} %get-tuple-element.34), calls=%async_computation.3 | async-start | bytes 98304 | tf_op jit(solution)/shard_map/all_to_all | solution.py:649
  48.1 5.9 %collective-permute-start.2 = (f32[48,128]{1,0:T(8,128)S(1)}, f32[48,128]{1,0:T(8,128)S(1)}, u32[]{:S(2)}, u32[]{:S(2)}) collective-permute-start(f32[48,128]{1,0:T(8,128)S(1)} %get-tuple-element.32), channel_id=1, source_target_pairs={{8,0},{16,8},{24,16},{9,1},{17,9},{25,17},{10,2},{18,10},{26,18},{... | collective-permute-start | bytes 73736 | tf_op jit(solution)/shard_map/ppermute | solution.py:757
  49.4 6.1 %collective-permute-start.3 = (f32[48,128]{1,0:T(8,128)S(1)}, f32[48,128]{1,0:T(8,128)S(1)}, u32[]{:S(2)}, u32[]{:S(2)}) collective-permute-start(f32[48,128]{1,0:T(8,128)S(1)} %get-tuple-element.33), channel_id=1, source_target_pairs={{0,8},{8,16},{16,24},{1,9},{9,17},{17,25},{2,10},{10,18},{18,26},{... | collective-permute-start | bytes 73736 | tf_op jit(solution)/shard_map/ppermute | solution.py:756

commit v18 on v17

--- a/solution.py
+++ b/solution.py
@@ -83,6 +83,21 @@
     at_x, at_y = lax.axis_index("gx") + dx, lax.axis_index("gy") + dy
     inside = (at_x >= 0) & (at_x < count_x) & (at_y >= 0) & (at_y < count_y)
     return jnp.where(inside, at_x * count_y + at_y, 0), inside
+
+
+def odd_column():
+    return lax.axis_index("gy") % 2 == 1
+
+
+def opposed(rows_up):
+    count_x, count_y = lax.axis_size("gx"), lax.axis_size("gy")
+    pairs = []
+    for x in range(count_x):
+        for y in range(count_y):
+            there = x + 1 if y % 2 == rows_up else x - 1
+            if 0 <= there < count_x:
+                pairs.append((x * count_y + y, there * count_y + y))
+    return pairs
 
 
 def edge_columns(rows, side_ref):
@@ -239,7 +254,7 @@
 
 def pack_body(*refs):
     inputs, outputs, scratch = refs[:6], refs[6:10], refs[10:]
-    fields_ref, high_ref, low_ref, side_ref, cells_ref, wavelet_ref, arrived, sent, sent_sides = scratch
+    fields_ref, first_ref, second_ref, side_ref, cells_ref, wavelet_ref, arrived, sent, sent_sides = scratch
     targets, at = [], 0
     for source in inputs[:4]:
         targets.append(fields_ref.at[at : at + source.shape[0]])
@@ -275,16 +290,16 @@
     edge_columns(jnp.concatenate([rows, jnp.zeros((spare, LANES), F32)], axis=0), side_ref)
     sides = start_sides(side_ref, outputs[3], sent_sides)
     height = total // TILE_X
-    for x in range(TILE_X):
-        slab = fields_ref[pl.ds(x, height, stride=TILE_X), :]
-        if x < RIM:
-            low_ref[x * height : (x + 1) * height, :] = slab
-        if x >= TILE_X - RIM:
-            at = x - TILE_X + RIM
-            high_ref[at * height : (at + 1) * height, :] = slab
+    odd = odd_column()
+    for distance in range(RIM):
+        rows = slice(distance * height, (distance + 1) * height)
+        low = fields_ref[pl.ds(distance, height, stride=TILE_X), :]
+        high = fields_ref[pl.ds(distance + TILE_X - RIM, height, stride=TILE_X), :]
+        first_ref[rows, :] = jnp.where(odd, low, high)
+        second_ref[rows, :] = jnp.where(odd, high, low)
     writes = [
         pltpu.make_async_copy(source, target, sent.at[number])
-        for number, (source, target) in enumerate(zip((fields_ref.at[0:total], high_ref, low_ref), outputs))
+        for number, (source, target) in enumerate(zip((fields_ref.at[0:total], first_ref, second_ref), outputs))
     ]
     for copy in writes:
         copy.start()
@@ -335,8 +350,8 @@
 
 def forward_body(
     fields_ref,
-    lower_ref,
-    higher_ref,
+    first_recv_ref,
+    second_recv_ref,
     recv_ref,
     slot_ref,
     row_ref,
@@ -360,10 +375,12 @@
     rims = rim_rows(recv_ref, turn_ref)
     height = fields_ref.shape[0] // TILE_X
     sides_ref[...] = jnp.zeros_like(sides_ref)
+    odd = odd_column()
     for x in range(RIM):
         slab = slice(x * height, (x + 1) * height)
-        sides_ref[0, pl.ds(x, height, stride=TILE_X), :] = higher_ref[slab, :]
-        sides_ref[1, pl.ds(x + TILE_X - RIM, height, stride=TILE_X), :] = lower_ref[slab, :]
+        one, two = first_recv_ref[slab, :], second_recv_ref[slab, :]
+        sides_ref[0, pl.ds(x, height, stride=TILE_X), :] = jnp.where(odd, one, two)
+        sides_ref[1, pl.ds(x + TILE_X - RIM, height, stride=TILE_X), :] = jnp.where(odd, two, one)
     lay_planes(wide_ref, source_ref, 0, fields_ref, sides_ref.at[0], sides_ref.at[1])
     lay_planes(wide_ref, source_ref, LANES, *rims)
     first = 9 * depth
@@ -475,8 +492,8 @@
     cover_ref,
     place_ref,
     load_ref,
-    high_ref,
-    low_ref,
+    first_ref,
+    second_ref,
     out_ref,
     spread_ref,
     side_ref,
@@ -519,18 +536,21 @@
     load_ref[...] = load
     held_ref[0:stack_rows, :] = load
     count = stack_rows // (3 * TILE_X)
+    odd = odd_column()
     for at, (turn, distance) in enumerate(reached()):
         rows = slice(at * count, (at + 1) * count)
         first = turn * count * TILE_X
-        low_ref[rows, :] = held_ref[pl.ds(first + distance, count, stride=TILE_X), :]
-        high_ref[rows, :] = held_ref[pl.ds(first + TILE_X - 1 - distance, count, stride=TILE_X), :]
+        low = held_ref[pl.ds(first + distance, count, stride=TILE_X), :]
+        high = held_ref[pl.ds(first + TILE_X - 1 - distance, count, stride=TILE_X), :]
+        first_ref[rows, :] = jnp.where(odd, high, low)
+        second_ref[rows, :] = jnp.where(odd, low, high)
     wait_sides(sides)
 
 
 def adjoint_body(
     load_ref,
-    higher_ref,
-    lower_ref,
+    first_recv_ref,
+    second_recv_ref,
     recv_ref,
     strain_ref,
     medium_ref,
@@ -549,11 +569,13 @@
     rims = rim_rows(recv_ref, turn_ref)
     sides_ref[...] = jnp.zeros_like(sides_ref)
     count = load_ref.shape[0] // (3 * TILE_X)
+    odd = odd_column()
     for at, (turn, distance) in enumerate(reached()):
         rows = slice(at * count, (at + 1) * count)
         first = turn * count * TILE_X
-        sides_ref[0, pl.ds(first + distance, count, stride=TILE_X), :] = higher_ref[rows, :]
-        sides_ref[1, pl.ds(first + TILE_X - 1 - distance, count, stride=TILE_X), :] = lower_ref[rows, :]
+        one, two = first_recv_ref[rows, :], second_recv_ref[rows, :]
+        sides_ref[0, pl.ds(first + distance, count, stride=TILE_X), :] = jnp.where(odd, two, one)
+        sides_ref[1, pl.ds(first + TILE_X - 1 - distance, count, stride=TILE_X), :] = jnp.where(odd, one, two)
     lay_planes(first_ref, later_ref, 0, load_ref, sides_ref.at[0], sides_ref.at[1])
     lay_planes(first_ref, later_ref, LANES, *rims)
     for plane in range(3 * depth):
@@ -641,8 +663,6 @@
     per_group = LANES // capacity
     cells_row = depth * rows_x
     both = ("gx", "gy")
-    up = [(i, i + 1) for i in range(count_x - 1)]
-    down = [(j, i) for i, j in up]
     shape = jax.ShapeDtypeStruct
 
     def exchange(chunks):
@@ -654,7 +674,7 @@
         return back.transpose(0, 2, 1, 3).reshape(slot_groups * 4, LANES)
 
     trimmed = shape((14 * depth * RIM, cols_y), F32)
-    fields, high, low, edges = call_kernel(
+    fields, first_slabs, second_slabs, edges = call_kernel(
         pack_body,
         "pack_edges",
         [shape((14 * cells_row, cols_y), F32), trimmed, trimmed, shape((devices, 1, 2 * RIM * LANES), F32)],
@@ -676,8 +696,8 @@
         place_out=pl.ANY,
         room=60 * 1024 * 1024,
     )
-    lower = lax.ppermute(high, "gx", up)
-    higher = lax.ppermute(low, "gx", down)
+    first_fields = lax.ppermute(first_slabs, both, opposed(0))
+    second_fields = lax.ppermute(second_slabs, both, opposed(1))
     rims = exchange(edges)
     channels = partial_channel.reshape(blocks, LANES)
     slot, row, cover, place = call_kernel(
@@ -711,8 +731,8 @@
             pltpu.VMEM((3 * LANES, part_count), BF16),
         ],
         fields,
-        lower,
-        higher,
+        first_fields,
+        second_fields,
         rims,
         slot,
         row,
@@ -735,7 +755,7 @@
         observed_data,
     )
     reach = shape((len(reached()) * 2 * depth, cols_y), F32)
-    loads, load_high, load_low, load_edges = call_kernel(
+    loads, first_loads, second_loads, load_edges = call_kernel(
         load_body,
         "segment_loads",
         [shape((6 * cells_row, cols_y), F32), reach, reach, shape((devices, 1, RIM * LANES), F32)],
@@ -753,8 +773,8 @@
         place,
         place_out=(pltpu.VMEM, pltpu.VMEM, pltpu.VMEM, pl.ANY),
     )
-    load_lower = lax.ppermute(load_high, "gx", up)
-    load_higher = lax.ppermute(load_low, "gx", down)
+    first_arrived = lax.ppermute(first_loads, both, opposed(1))
+    second_arrived = lax.ppermute(second_loads, both, opposed(0))
     load_rims = exchange(load_edges)
     gradients, residuals = call_kernel(
         adjoint_body,
@@ -770,8 +790,8 @@
             pltpu.VMEM((2, 6 * cells_row + SPARE, cols_y), F32),
         ],
         loads,
-        load_higher,
-        load_lower,
+        first_arrived,
+        second_arrived,
         load_rims,
         strains,
         medium,

time: 57.1 us -> 57.4 us (level)
  no operation moved by 1% of the time
where the time goes in v18:
time: 57.4 us; the launch traced here: 56.7 us
  blocking collectives  20.9 us (36%)
  starting transfers between devices  20.7 us (36%)
  Pallas kernels  8.12 us (14%)
  waiting for transfers between devices  6.1 us (11%)
  between operations  0.8 us (1%)
    all_to_all x2, blocking collectives, exchange(): return lax.all_to_all(chunks, both, split_axis=0, concat_axis=0, tiled=True)  20.9 us
    all_to_all x2, starting transfers between devices, exchange(): return lax.all_to_all(chunks, both, split_axis=0, concat_axis=0, tiled=True)  9.89 us
    pallas_call x6, Pallas kernels, call_kernel(): pl.pallas_call(body, name=name, out_shape=outs, in_specs=[pl.BlockSpec(me...  8.12 us
    ppermute x1, starting transfers between devices, shards(): second_arrived = lax.ppermute(second_loads, both, opposed(0))  4.55 us
    ppermute x1, waiting for transfers between devices, shards(): second_fields = lax.ppermute(second_slabs, both, opposed(1))  4.21 us
    ppermute x1, starting transfers between devices, shards(): first_fields = lax.ppermute(first_slabs, both, opposed(0))  3.68 us
    ppermute x1, waiting for transfers between devices, shards(): second_arrived = lax.ppermute(second_loads, both, opposed(0))  1.49 us
    ppermute x1, starting transfers between devices, shards(): second_fields = lax.ppermute(second_slabs, both, opposed(1))  1.29 us
  transfers between devices with their start and end apart: 6, of which 3 were waited for; matrix products, arithmetic and copies ran while one was open for 0% of the time, Pallas kernels for 1%

profile of v18, /device:TPU:0, one launch (start us, length us, event | category | flops | bytes accessed | tf_op | source)
XLA Modules:
  0.0 56.7 jit_solution(2992680910132197663)
XLA Ops:
  0.6 1.8 %pack_edges.1 = (f32[224,128]{1,0:T(8,128)}, f32[168,128]{1,0:T(8,128)}, f32[168,128]{1,0:T(8,128)}, f32[32,1,768]{2,1,0:T(1,128)}) custom-call(f32[144,128]{1,0:T(8,128)} %bitcast.20, f32[16,128]{1,0:T(8,128)} %bitcast.21, f32[16,128]{1,0:T(8,128)} %bitcast.22, f32[16,128]{1,0:T(8,128)} %bitcast.23, s32[1,64]{1,0:T(1,128)} %bitcast.24, f32[3,64]{1,0:T(4,128)} %refs_5_.1), custom_call_target="tpu_custom_call" | custom-call | tf_op jit(solution)/shard_map/pack_edges/pallas_call | solution.py:27
  2.4 0.0 copy-start.4
  2.4 0.0 copy-start.5
  2.5 7.3 %all-to-all-start = ((f32[32,1,768]{2,1,0:T(1,128)}), f32[32,1,768]{2,1,0:T(1,128)S(1)}, u32[]{:S(2)}, u32[]{:S(2)}) async-start(f32[32,1,768]{2,1,0:T(1,128)} %get-tuple-element.24), calls=%async_computation | async-start | bytes 196608 | tf_op jit(solution)/shard_map/all_to_all | solution.py:669
  9.8 3.7 %collective-permute-start = (f32[168,128]{1,0:T(8,128)}, f32[168,128]{1,0:T(8,128)S(1)}, u32[]{:S(2)}, u32[]{:S(2)}) collective-permute-start(f32[168,128]{1,0:T(8,128)} %get-tuple-element.22), channel_id=1, source_target_pairs={{0,8},{2,10},{4,12},{6,14},{8,16},{9,1},{10,18},{11,3},{12,20},{13... | collective-permute-start | bytes 258056 | tf_op jit(solution)/shard_map/ppermute | solution.py:699
  13.5 0.0 copy-start.1
  13.5 1.3 %collective-permute-start.1 = (f32[168,128]{1,0:T(8,128)}, f32[168,128]{1,0:T(8,128)S(1)}, u32[]{:S(2)}, u32[]{:S(2)}) collective-permute-start(f32[168,128]{1,0:T(8,128)} %get-tuple-element.23), channel_id=1, source_target_pairs={{1,9},{3,11},{5,13},{7,15},{8,0},{9,17},{10,2},{11,19},{12,4},{13,... | collective-permute-start | bytes 258056 | tf_op jit(solution)/shard_map/ppermute | solution.py:700
  14.8 0.6 %segment_slots.1 = (s32[16,128]{1,0:T(8,128)S(1)}, s32[16,128]{1,0:T(8,128)S(1)}, bf16[128,2048]{1,0:T(8,128)(2,1)S(1)}, bf16[128,2048]{1,0:T(8,128)(2,1)S(1)}) custom-call(s32[16,128]{1,0:T(8,128)S(1)} %bitcast.18, s32[16,128]{1,0:T(8,128)S(1)} %bitcast.19), custom_call_target="tpu_custom_call" | custom-call | tf_op jit(solution)/shard_map/segment_slots/pallas_call | solution.py:27
  15.4 0.0 copy-start.3
  15.5 0.4 collective-permute-done.first_recv_ref
  15.8 4.2 %collective-permute-done.1.second_recv_ref = f32[168,128]{1,0:T(8,128)S(1)} collective-permute-done((f32[168,128]{1,0:T(8,128)}, f32[168,128]{1,0:T(8,128)S(1)}, u32[]{:S(2)}, u32[]{:S(2)}) %collective-permute-start.1) | collective-permute-done | bytes 86048 | tf_op jit(solution)/shard_map/ppermute | solution.py:700
  20.1 0.0 all-to-all-done.recv_ref
  20.1 1.7 %forward_run.1 = (f32[128,128]{1,0:T(8,128)S(1)}, f32[288,128]{1,0:T(8,128)S(1)}, f32[12,16,256]{2,1,0:T(8,128)S(1)}) custom-call(f32[224,128]{1,0:T(8,128)S(1)} %copy-done, f32[168,128]{1,0:T(8,128)S(1)} %collective-permute-done.first_recv_ref, f32[168,128]{1,0:T(8,128)S(1)} %collective-permute-done.1.second_recv_ref, ...), custom_call_target="tpu_custom_call" | custom-call | tf_op jit(solution)/shard_map/forward_run/pallas_call | solution.py:27
  21.7 0.0 copy-start.2
  21.8 11.8 %all_to_all.20 = f32[32,4,128]{2,1,0:T(4,128)S(1)} all-to-all(f32[32,4,128]{2,1,0:T(4,128)S(1)} %bitcast.15), channel_id=1, replica_groups=mesh['gx'=4,'gy'=8] {'gx','gy'}, dimensions={0} | all-to-all | bytes 131072 | tf_op jit(solution)/shard_map/all_to_all | solution.py:669
  33.6 1.1 %channel_sums.1 = (f32[3,1024]{1,0:T(4,128)S(1)}, f32[128,128]{1,0:T(8,128)S(1)}) custom-call(f32[128,128]{1,0:T(8,128)S(1)} %bitcast.14, f32[3,1024]{1,0:T(4,128)S(1)} %copy-done.2), custom_call_target="tpu_custom_call" | custom-call | tf_op jit(solution)/shard_map/channel_sums/pallas_call | solution.py:27
  34.7 9.1 %all_to_all.21 = f32[32,4,128]{2,1,0:T(4,128)S(1)} all-to-all(f32[32,4,128]{2,1,0:T(4,128)S(1)} %bitcast.16), channel_id=1, replica_groups=mesh['gx'=4,'gy'=8] {'gx','gy'}, dimensions={0} | all-to-all | bytes 131072 | tf_op jit(solution)/shard_map/all_to_all | solution.py:669
  43.8 1.7 %segment_loads.1 = (f32[96,128]{1,0:T(8,128)S(1)}, f32[48,128]{1,0:T(8,128)S(1)}, f32[48,128]{1,0:T(8,128)S(1)}, f32[32,1,384]{2,1,0:T(1,128)}) custom-call(f32[128,128]{1,0:T(8,128)S(1)} %bitcast.13, s32[16,128]{1,0:T(8,128)S(1)} %get-tuple-element.25.slot_ref, s32[16,128]{1,0:T(8,128)S(1)} %get-tuple-element.26.row_ref, f32[2,2048]{1,0:T(2,128)S(1)} %copy-done.1, ...), custom_call_target="tpu_custom_call" | custom-call | tf_op jit(solution)/shard_map/segment_loads/pallas_call | solution.py:27
  45.5 2.6 %all-to-all-start.3 = ((f32[32,1,384]{2,1,0:T(1,128)}), f32[32,1,384]{2,1,0:T(1,128)S(1)}, u32[]{:S(2)}, u32[]{:S(2)}) async-start(f32[32,1,384]{2,1,0:T(1,128)} %get-tuple-element.34), calls=%async_computation.3 | async-start | bytes 98304 | tf_op jit(solution)/shard_map/all_to_all | solution.py:669
  48.1 1.3 %collective-permute-start.2 = (f32[48,128]{1,0:T(8,128)S(1)}, f32[48,128]{1,0:T(8,128)S(1)}, u32[]{:S(2)}, u32[]{:S(2)}) collective-permute-start(f32[48,128]{1,0:T(8,128)S(1)} %get-tuple-element.32), channel_id=1, source_target_pairs={{1,9},{3,11},{5,13},{7,15},{8,0},{9,17},{10,2},{11,19},{12,4},{13,... | collective-permute-start | bytes 73736 | tf_op jit(solution)/shard_map/ppermute | solution.py:776
  49.4 4.5 %collective-permute-start.3 = (f32[48,128]{1,0:T(8,128)S(1)}, f32[48,128]{1,0:T(8,128)S(1)}, u32[]{:S(2)}, u32[]{:S(2)}) collective-permute-start(f32[48,128]{1,0:T(8,128)S(1)} %get-tuple-element.33), channel_id=1, source_target_pairs={{0,8},{2,10},{4,12},{6,14},{8,16},{9,1},{10,18},{11,3},{12,20},{13... | collective-permute-start | bytes 73736 | tf_op jit(solution)/shard_map/ppermute | solution.py:777
  53.9 0.0 collective-permute-done.2.first_recv_ref
  53.9 1.5 %collective-permute-done.3.second_recv_ref = f32[48,128]{1,0:T(8,128)S(1)} collective-permute-done((f32[48,128]{1,0:T(8,128)S(1)}, f32[48,128]{1,0:T(8,128)S(1)}, u32[]{:S(2)}, u32[]{:S(2)}) %collective-permute-start.3) | collective-permute-done | bytes 24608 | tf_op jit(solution)/shard_map/ppermute | solution.py:777
  55.4 1.3 %adjoint_run.1 = (f32[32,128]{1,0:T(8,128)}, f32[3,1024]{1,0:T(4,128)}) custom-call(f32[96,128]{1,0:T(8,128)S(1)} %get-tuple-element.31.load_ref, f32[48,128]{1,0:T(8,128)S(1)} %collective-permute-done.2.first_recv_ref, f32[48,128]{1,0:T(8,128)S(1)} %collective-permute-done.3.second_recv_ref, f32[32,1,384]{2,1,0:T(1,128)S(1)} %all-to-all-done.3.recv_ref, ...), custom_call_target="tpu_custom_call" | custom-call | tf_op jit(solution)/shard_map/adjoint_run/pallas_call | solution.py:27
  (8 shorter events, 0.0 us)
Async XLA Ops:
  2.4 12.4 %copy-start.4 = (s32[2048,1]{0,1:T(1,128)S(1)}, s32[2048,1]{0,1:T(1,128)}, u32[]{:S(2)}) copy-start(s32[2048,1]{0,1:T(1,128)} %param.19) | copy-start | bytes 24580
  2.4 12.3 %copy-start.5 = (s32[2048]{0:T(1024)S(1)}, s32[2048]{0:T(1024)}, u32[]{:S(2)}) copy-start(s32[2048]{0:T(1024)} %param.17) | copy-start | bytes 24580
  2.4 17.6 %copy-start = (f32[224,128]{1,0:T(8,128)S(1)}, f32[224,128]{1,0:T(8,128)}, u32[]{:S(2)}) copy-start(f32[224,128]{1,0:T(8,128)} %get-tuple-element.21.fields_ref) | copy-start | bytes 344068
  2.5 17.6 %all-to-all-start = ((f32[32,1,768]{2,1,0:T(1,128)}), f32[32,1,768]{2,1,0:T(1,128)S(1)}, u32[]{:S(2)}, u32[]{:S(2)}) async-start(f32[32,1,768]{2,1,0:T(1,128)} %get-tuple-element.24), calls=%async_computation | async-start | bytes 196608 | tf_op jit(solution)/shard_map/all_to_all | solution.py:669
  9.8 6.1 %collective-permute-start = (f32[168,128]{1,0:T(8,128)}, f32[168,128]{1,0:T(8,128)S(1)}, u32[]{:S(2)}, u32[]{:S(2)}) collective-permute-start(f32[168,128]{1,0:T(8,128)} %get-tuple-element.22), channel_id=1, source_target_pairs={{0,8},{2,10},{4,12},{6,14},{8,16},{9,1},{10,18},{11,3},{12,20},{13... | collective-permute-start | bytes 258056 | tf_op jit(solution)/shard_map/ppermute | solution.py:699
  13.5 6.6 %copy-start.1 = (f32[2,2048]{1,0:T(2,128)S(1)}, f32[2,2048]{1,0:T(2,128)}, u32[]{:S(2)}) copy-start(f32[2,2048]{1,0:T(2,128)} %weight_ref.3) | copy-start | bytes 49156
  13.5 6.6 %collective-permute-start.1 = (f32[168,128]{1,0:T(8,128)}, f32[168,128]{1,0:T(8,128)S(1)}, u32[]{:S(2)}, u32[]{:S(2)}) collective-permute-start(f32[168,128]{1,0:T(8,128)} %get-tuple-element.23), channel_id=1, source_target_pairs={{1,9},{3,11},{5,13},{7,15},{8,0},{9,17},{10,2},{11,19},{12,4},{13,... | collective-permute-start | bytes 258056 | tf_op jit(solution)/shard_map/ppermute | solution.py:700
  15.4 4.6 %copy-start.3 = (s32[2048]{0:T(1024)S(1)}, s32[2048]{0:T(1024)}, u32[]{:S(2)}) copy-start(s32[2048]{0:T(1024)} %param.20) | copy-start | bytes 24580
  21.7 11.9 %copy-start.2 = (f32[3,1024]{1,0:T(4,128)S(1)}, f32[3,1024]{1,0:T(4,128)}, u32[]{:S(2)}) copy-start(f32[3,1024]{1,0:T(4,128)} %observed_ref.1) | copy-start | bytes 36868
  45.5 9.9 %all-to-all-start.3 = ((f32[32,1,384]{2,1,0:T(1,128)}), f32[32,1,384]{2,1,0:T(1,128)S(1)}, u32[]{:S(2)}, u32[]{:S(2)}) async-start(f32[32,1,384]{2,1,0:T(1,128)} %get-tuple-element.34), calls=%async_computation.3 | async-start | bytes 98304 | tf_op jit(solution)/shard_map/all_to_all | solution.py:669
  48.1 5.9 %collective-permute-start.2 = (f32[48,128]{1,0:T(8,128)S(1)}, f32[48,128]{1,0:T(8,128)S(1)}, u32[]{:S(2)}, u32[]{:S(2)}) collective-permute-start(f32[48,128]{1,0:T(8,128)S(1)} %get-tuple-element.32), channel_id=1, source_target_pairs={{1,9},{3,11},{5,13},{7,15},{8,0},{9,17},{10,2},{11,19},{12,4},{13,... | collective-permute-start | bytes 73736 | tf_op jit(solution)/shard_map/ppermute | solution.py:776
  49.4 6.1 %collective-permute-start.3 = (f32[48,128]{1,0:T(8,128)S(1)}, f32[48,128]{1,0:T(8,128)S(1)}, u32[]{:S(2)}, u32[]{:S(2)}) collective-permute-start(f32[48,128]{1,0:T(8,128)S(1)} %get-tuple-element.33), channel_id=1, source_target_pairs={{0,8},{2,10},{4,12},{6,14},{8,16},{9,1},{10,18},{11,3},{12,20},{13... | collective-permute-start | bytes 73736 | tf_op jit(solution)/shard_map/ppermute | solution.py:777

commit v19 on v17

--- a/solution.py
+++ b/solution.py
@@ -335,8 +335,8 @@
 
 def forward_body(
     fields_ref,
+    higher_ref,
     lower_ref,
-    higher_ref,
     recv_ref,
     slot_ref,
     row_ref,
@@ -711,8 +711,8 @@
             pltpu.VMEM((3 * LANES, part_count), BF16),
         ],
         fields,
+        higher,
         lower,
-        higher,
         rims,
         slot,
         row,

time: 57.1 us -> 57.1 us (level)
  waiting for transfers between devices: 6.11 us -> 3.21 us
  blocking collectives: 20.9 us -> 22.9 us
  starting transfers between devices: 20.7 us -> 21.6 us
    ppermute x1, waiting for transfers between devices: 4.2 us -> 0.68 us  [shards(): higher = lax.ppermute(low, 'gx', down)]
    all_to_all x2, blocking collectives: 20.9 us -> 22.9 us  [exchange(): return lax.all_to_all(chunks, both, split_axis=0, concat_axis=0, tiled=True)]
    ppermute x1, starting transfers between devices: 3.68 us -> 4.55 us  [shards(): lower = lax.ppermute(high, 'gx', up)]
    ppermute x1, waiting for transfers between devices: 0.4 us -> 1.02 us  [shards(): lower = lax.ppermute(high, 'gx', up)]
where the time goes in v19:
time: 57.1 us; the launch traced here: 56.6 us
  blocking collectives  22.9 us (40%)
  starting transfers between devices  21.6 us (38%)
  Pallas kernels  8.11 us (14%)
  waiting for transfers between devices  3.21 us (6%)
  between operations  0.8 us (1%)
    all_to_all x2, blocking collectives, exchange(): return lax.all_to_all(chunks, both, split_axis=0, concat_axis=0, tiled=True)  22.9 us
    all_to_all x2, starting transfers between devices, exchange(): return lax.all_to_all(chunks, both, split_axis=0, concat_axis=0, tiled=True)  9.89 us
    pallas_call x6, Pallas kernels, call_kernel(): pl.pallas_call(body, name=name, out_shape=outs, in_specs=[pl.BlockSpec(me...  8.11 us
    ppermute x1, starting transfers between devices, shards(): lower = lax.ppermute(high, 'gx', up)  4.55 us
    ppermute x1, starting transfers between devices, shards(): load_lower = lax.ppermute(load_high, 'gx', up)  4.55 us
    ppermute x1, waiting for transfers between devices, shards(): load_lower = lax.ppermute(load_high, 'gx', up)  1.49 us
    ppermute x1, starting transfers between devices, shards(): higher = lax.ppermute(low, 'gx', down)  1.29 us
    ppermute x1, starting transfers between devices, shards(): load_higher = lax.ppermute(load_low, 'gx', down)  1.29 us
  transfers between devices with their start and end apart: 6, of which 3 were waited for; matrix products, arithmetic and copies ran while one was open for 0% of the time, Pallas kernels for 1%

profile of v19, /device:TPU:0, one launch (start us, length us, event | category | flops | bytes accessed | tf_op | source)
XLA Modules:
  0.0 56.6 jit_solution(741657033922801800)
XLA Ops:
  0.6 1.8 %pack_edges.1 = (f32[224,128]{1,0:T(8,128)}, f32[168,128]{1,0:T(8,128)}, f32[168,128]{1,0:T(8,128)}, f32[32,1,768]{2,1,0:T(1,128)}) custom-call(f32[144,128]{1,0:T(8,128)} %bitcast.20, f32[16,128]{1,0:T(8,128)} %bitcast.21, f32[16,128]{1,0:T(8,128)} %bitcast.22, f32[16,128]{1,0:T(8,128)} %bitcast.23, s32[1,64]{1,0:T(1,128)} %bitcast.24, f32[3,64]{1,0:T(4,128)} %refs_5_.1), custom_call_target="tpu_custom_call" | custom-call | tf_op jit(solution)/shard_map/pack_edges/pallas_call | solution.py:27
  2.4 0.0 copy-start.4
  2.4 0.0 copy-start.5
  2.4 7.3 %all-to-all-start = ((f32[32,1,768]{2,1,0:T(1,128)}), f32[32,1,768]{2,1,0:T(1,128)S(1)}, u32[]{:S(2)}, u32[]{:S(2)}) async-start(f32[32,1,768]{2,1,0:T(1,128)} %get-tuple-element.24), calls=%async_computation | async-start | bytes 196608 | tf_op jit(solution)/shard_map/all_to_all | solution.py:649
  9.8 1.3 %collective-permute-start = (f32[168,128]{1,0:T(8,128)}, f32[168,128]{1,0:T(8,128)S(1)}, u32[]{:S(2)}, u32[]{:S(2)}) collective-permute-start(f32[168,128]{1,0:T(8,128)} %get-tuple-element.22), channel_id=1, source_target_pairs={{8,0},{16,8},{24,16},{9,1},{17,9},{25,17},{10,2},{18,10},{26,18},{... | collective-permute-start | bytes 258056 | tf_op jit(solution)/shard_map/ppermute | solution.py:680
  11.1 0.0 copy-start.1
  11.1 4.5 %collective-permute-start.1 = (f32[168,128]{1,0:T(8,128)}, f32[168,128]{1,0:T(8,128)S(1)}, u32[]{:S(2)}, u32[]{:S(2)}) collective-permute-start(f32[168,128]{1,0:T(8,128)} %get-tuple-element.23), channel_id=1, source_target_pairs={{0,8},{8,16},{16,24},{1,9},{9,17},{17,25},{2,10},{10,18},{18,26},{... | collective-permute-start | bytes 258056 | tf_op jit(solution)/shard_map/ppermute | solution.py:679
  15.7 0.6 %segment_slots.1 = (s32[16,128]{1,0:T(8,128)S(1)}, s32[16,128]{1,0:T(8,128)S(1)}, bf16[128,2048]{1,0:T(8,128)(2,1)S(1)}, bf16[128,2048]{1,0:T(8,128)(2,1)S(1)}) custom-call(s32[16,128]{1,0:T(8,128)S(1)} %bitcast.18, s32[16,128]{1,0:T(8,128)S(1)} %bitcast.19), custom_call_target="tpu_custom_call" | custom-call | tf_op jit(solution)/shard_map/segment_slots/pallas_call | solution.py:27
  16.3 0.0 copy-start.3
  16.3 0.7 %collective-permute-done.higher_ref = f32[168,128]{1,0:T(8,128)S(1)} collective-permute-done((f32[168,128]{1,0:T(8,128)}, f32[168,128]{1,0:T(8,128)S(1)}, u32[]{:S(2)}, u32[]{:S(2)}) %collective-permute-start) | collective-permute-done | bytes 86048 | tf_op jit(solution)/shard_map/ppermute | solution.py:680
  17.0 1.0 %collective-permute-done.1.lower_ref = f32[168,128]{1,0:T(8,128)S(1)} collective-permute-done((f32[168,128]{1,0:T(8,128)}, f32[168,128]{1,0:T(8,128)S(1)}, u32[]{:S(2)}, u32[]{:S(2)}) %collective-permute-start.1) | collective-permute-done | bytes 86048 | tf_op jit(solution)/shard_map/ppermute | solution.py:679
  18.0 0.0 all-to-all-done.recv_ref
  18.0 1.7 %forward_run.1 = (f32[128,128]{1,0:T(8,128)S(1)}, f32[288,128]{1,0:T(8,128)S(1)}, f32[12,16,256]{2,1,0:T(8,128)S(1)}) custom-call(f32[224,128]{1,0:T(8,128)S(1)} %copy-done, f32[168,128]{1,0:T(8,128)S(1)} %collective-permute-done.higher_ref, f32[168,128]{1,0:T(8,128)S(1)} %collective-permute-done.1.lower_ref, f32[32,1,768]{2,1,0:T(1,128)S(1)} %all-to-all-done.recv_ref, ...), custom_call_target="tpu_custom_call" | custom-call | tf_op jit(solution)/shard_map/forward_run/pallas_call | solution.py:27
  19.7 0.0 copy-start.2
  19.7 13.8 %all_to_all.20 = f32[32,4,128]{2,1,0:T(4,128)S(1)} all-to-all(f32[32,4,128]{2,1,0:T(4,128)S(1)} %bitcast.15), channel_id=1, replica_groups=mesh['gx'=4,'gy'=8] {'gx','gy'}, dimensions={0} | all-to-all | bytes 131072 | tf_op jit(solution)/shard_map/all_to_all | solution.py:649
  33.5 1.1 %channel_sums.1 = (f32[3,1024]{1,0:T(4,128)S(1)}, f32[128,128]{1,0:T(8,128)S(1)}) custom-call(f32[128,128]{1,0:T(8,128)S(1)} %bitcast.14, f32[3,1024]{1,0:T(4,128)S(1)} %copy-done.2), custom_call_target="tpu_custom_call" | custom-call | tf_op jit(solution)/shard_map/channel_sums/pallas_call | solution.py:27
  34.6 9.1 %all_to_all.21 = f32[32,4,128]{2,1,0:T(4,128)S(1)} all-to-all(f32[32,4,128]{2,1,0:T(4,128)S(1)} %bitcast.16), channel_id=1, replica_groups=mesh['gx'=4,'gy'=8] {'gx','gy'}, dimensions={0} | all-to-all | bytes 131072 | tf_op jit(solution)/shard_map/all_to_all | solution.py:649
  43.7 1.7 %segment_loads.1 = (f32[96,128]{1,0:T(8,128)S(1)}, f32[48,128]{1,0:T(8,128)S(1)}, f32[48,128]{1,0:T(8,128)S(1)}, f32[32,1,384]{2,1,0:T(1,128)}) custom-call(f32[128,128]{1,0:T(8,128)S(1)} %bitcast.13, s32[16,128]{1,0:T(8,128)S(1)} %get-tuple-element.25.slot_ref, s32[16,128]{1,0:T(8,128)S(1)} %get-tuple-element.26.row_ref, f32[2,2048]{1,0:T(2,128)S(1)} %copy-done.1, ...), custom_call_target="tpu_custom_call" | custom-call | tf_op jit(solution)/shard_map/segment_loads/pallas_call | solution.py:27
  45.4 2.6 %all-to-all-start.3 = ((f32[32,1,384]{2,1,0:T(1,128)}), f32[32,1,384]{2,1,0:T(1,128)S(1)}, u32[]{:S(2)}, u32[]{:S(2)}) async-start(f32[32,1,384]{2,1,0:T(1,128)} %get-tuple-element.34), calls=%async_computation.3 | async-start | bytes 98304 | tf_op jit(solution)/shard_map/all_to_all | solution.py:649
  48.0 1.3 %collective-permute-start.2 = (f32[48,128]{1,0:T(8,128)S(1)}, f32[48,128]{1,0:T(8,128)S(1)}, u32[]{:S(2)}, u32[]{:S(2)}) collective-permute-start(f32[48,128]{1,0:T(8,128)S(1)} %get-tuple-element.32), channel_id=1, source_target_pairs={{8,0},{16,8},{24,16},{9,1},{17,9},{25,17},{10,2},{18,10},{26,18},{... | collective-permute-start | bytes 73736 | tf_op jit(solution)/shard_map/ppermute | solution.py:757
  49.3 4.5 %collective-permute-start.3 = (f32[48,128]{1,0:T(8,128)S(1)}, f32[48,128]{1,0:T(8,128)S(1)}, u32[]{:S(2)}, u32[]{:S(2)}) collective-permute-start(f32[48,128]{1,0:T(8,128)S(1)} %get-tuple-element.33), channel_id=1, source_target_pairs={{0,8},{8,16},{16,24},{1,9},{9,17},{17,25},{2,10},{10,18},{18,26},{... | collective-permute-start | bytes 73736 | tf_op jit(solution)/shard_map/ppermute | solution.py:756
  53.9 0.0 collective-permute-done.2.higher_ref
  53.9 1.5 %collective-permute-done.3.lower_ref = f32[48,128]{1,0:T(8,128)S(1)} collective-permute-done((f32[48,128]{1,0:T(8,128)S(1)}, f32[48,128]{1,0:T(8,128)S(1)}, u32[]{:S(2)}, u32[]{:S(2)}) %collective-permute-start.3) | collective-permute-done | bytes 24608 | tf_op jit(solution)/shard_map/ppermute | solution.py:756
  55.4 1.3 %adjoint_run.1 = (f32[32,128]{1,0:T(8,128)}, f32[3,1024]{1,0:T(4,128)}) custom-call(f32[96,128]{1,0:T(8,128)S(1)} %get-tuple-element.31.load_ref, f32[48,128]{1,0:T(8,128)S(1)} %collective-permute-done.2.higher_ref, f32[48,128]{1,0:T(8,128)S(1)} %collective-permute-done.3.lower_ref, f32[32,1,384]{2,1,0:T(1,128)S(1)} %all-to-all-done.3.recv_ref, ...), custom_call_target="tpu_custom_call" | custom-call | tf_op jit(solution)/shard_map/adjoint_run/pallas_call | solution.py:27
  (8 shorter events, 0.0 us)
Async XLA Ops:
  2.4 13.2 %copy-start.4 = (s32[2048,1]{0,1:T(1,128)S(1)}, s32[2048,1]{0,1:T(1,128)}, u32[]{:S(2)}) copy-start(s32[2048,1]{0,1:T(1,128)} %param.19) | copy-start | bytes 24580
  2.4 13.2 %copy-start.5 = (s32[2048]{0:T(1024)S(1)}, s32[2048]{0:T(1024)}, u32[]{:S(2)}) copy-start(s32[2048]{0:T(1024)} %param.17) | copy-start | bytes 24580
  2.4 15.6 %copy-start = (f32[224,128]{1,0:T(8,128)S(1)}, f32[224,128]{1,0:T(8,128)}, u32[]{:S(2)}) copy-start(f32[224,128]{1,0:T(8,128)} %get-tuple-element.21.fields_ref) | copy-start | bytes 344068
  2.4 15.6 %all-to-all-start = ((f32[32,1,768]{2,1,0:T(1,128)}), f32[32,1,768]{2,1,0:T(1,128)S(1)}, u32[]{:S(2)}, u32[]{:S(2)}) async-start(f32[32,1,768]{2,1,0:T(1,128)} %get-tuple-element.24), calls=%async_computation | async-start | bytes 196608 | tf_op jit(solution)/shard_map/all_to_all | solution.py:649
  9.8 7.2 %collective-permute-start = (f32[168,128]{1,0:T(8,128)}, f32[168,128]{1,0:T(8,128)S(1)}, u32[]{:S(2)}, u32[]{:S(2)}) collective-permute-start(f32[168,128]{1,0:T(8,128)} %get-tuple-element.22), channel_id=1, source_target_pairs={{8,0},{16,8},{24,16},{9,1},{17,9},{25,17},{10,2},{18,10},{26,18},{... | collective-permute-start | bytes 258056 | tf_op jit(solution)/shard_map/ppermute | solution.py:680
  11.1 7.0 %copy-start.1 = (f32[2,2048]{1,0:T(2,128)S(1)}, f32[2,2048]{1,0:T(2,128)}, u32[]{:S(2)}) copy-start(f32[2,2048]{1,0:T(2,128)} %weight_ref.3) | copy-start | bytes 49156
  11.1 6.9 %collective-permute-start.1 = (f32[168,128]{1,0:T(8,128)}, f32[168,128]{1,0:T(8,128)S(1)}, u32[]{:S(2)}, u32[]{:S(2)}) collective-permute-start(f32[168,128]{1,0:T(8,128)} %get-tuple-element.23), channel_id=1, source_target_pairs={{0,8},{8,16},{16,24},{1,9},{9,17},{17,25},{2,10},{10,18},{18,26},{... | collective-permute-start | bytes 258056 | tf_op jit(solution)/shard_map/ppermute | solution.py:679
  16.3 1.7 %copy-start.3 = (s32[2048]{0:T(1024)S(1)}, s32[2048]{0:T(1024)}, u32[]{:S(2)}) copy-start(s32[2048]{0:T(1024)} %param.20) | copy-start | bytes 24580
  19.7 13.8 %copy-start.2 = (f32[3,1024]{1,0:T(4,128)S(1)}, f32[3,1024]{1,0:T(4,128)}, u32[]{:S(2)}) copy-start(f32[3,1024]{1,0:T(4,128)} %observed_ref.1) | copy-start | bytes 36868
  45.4 9.9 %all-to-all-start.3 = ((f32[32,1,384]{2,1,0:T(1,128)}), f32[32,1,384]{2,1,0:T(1,128)S(1)}, u32[]{:S(2)}, u32[]{:S(2)}) async-start(f32[32,1,384]{2,1,0:T(1,128)} %get-tuple-element.34), calls=%async_computation.3 | async-start | bytes 98304 | tf_op jit(solution)/shard_map/all_to_all | solution.py:649
  48.0 5.9 %collective-permute-start.2 = (f32[48,128]{1,0:T(8,128)S(1)}, f32[48,128]{1,0:T(8,128)S(1)}, u32[]{:S(2)}, u32[]{:S(2)}) collective-permute-start(f32[48,128]{1,0:T(8,128)S(1)} %get-tuple-element.32), channel_id=1, source_target_pairs={{8,0},{16,8},{24,16},{9,1},{17,9},{25,17},{10,2},{18,10},{26,18},{... | collective-permute-start | bytes 73736 | tf_op jit(solution)/shard_map/ppermute | solution.py:757
  49.3 6.1 %collective-permute-start.3 = (f32[48,128]{1,0:T(8,128)S(1)}, f32[48,128]{1,0:T(8,128)S(1)}, u32[]{:S(2)}, u32[]{:S(2)}) collective-permute-start(f32[48,128]{1,0:T(8,128)S(1)} %get-tuple-element.33), channel_id=1, source_target_pairs={{0,8},{8,16},{16,24},{1,9},{9,17},{17,25},{2,10},{10,18},{18,26},{... | collective-permute-start | bytes 73736 | tf_op jit(solution)/shard_map/ppermute | solution.py:756

commit v20 on v19

--- a/solution.py
+++ b/solution.py
@@ -389,13 +389,15 @@
     axial = jnp.concatenate(
         [strain_ref[step * 6 * cells_row : (step * 6 + 2) * cells_row, :] for step in range(3)], axis=0
     )
-    axial = jnp.concatenate(pieces(axial), axis=0).astype(BF16)
+    high, middle, low = [piece.astype(BF16) for piece in pieces(axial)]
+    upper = jnp.concatenate([high, middle], axis=1)
     rows_down = iota((cells_row, LANES), 0)
     slots_down = packed_iota(LANES, 2)
     for block in range(slot_ref.shape[0]):
         lanes = slice(block * LANES, (block + 1) * LANES)
         if block % 2 == 0:
-            both = sum_thirds(times(axial, cover_ref[:, block * LANES : (block + 2) * LANES]))
+            cover = cover_ref[:, block * LANES : (block + 2) * LANES]
+            both = times(upper, jnp.concatenate([cover, cover], axis=0)) + times(low, cover)
         windows = both[:, :LANES] if block % 2 == 0 else both[:, LANES:]
         at_row = rows_down == row_ref[block : block + 1, :]
         weight_x, weight_y = weight_ref[0:1, lanes], weight_ref[1:2, lanes]
@@ -450,10 +452,11 @@
         for part in range(parts):
             at = step * parts + part
             residual_ref[step : step + 1, part * LANES : (part + 1) * LANES] = held_ref[at : at + 1, :]
-    residual = jnp.concatenate(two_pieces(held_ref[...]), axis=0).astype(BF16)
+    residual = jnp.concatenate(two_pieces(held_ref[...]), axis=1).astype(BF16)
     for s in range(groups):
         if s % 2 == 0:
-            both = sum_halves(times(residual, place_ref[:, s * LANES : (s + 2) * LANES]))
+            place = place_ref[:, s * LANES : (s + 2) * LANES]
+            both = times(residual, jnp.concatenate([place, place], axis=0))
         found = both[:, :LANES] if s % 2 == 0 else both[:, LANES:]
         at_part = part_down == (numbers[s] >> 7)
         for step in range(3):
@@ -485,13 +488,14 @@
 ):
     cells_row = load_ref.shape[0] // 6
     stack_rows = load_ref.shape[0]
-    arrived = jnp.concatenate(two_pieces(arrived_ref[...]), axis=0).astype(BF16)
+    arrived = jnp.concatenate(two_pieces(arrived_ref[...]), axis=1).astype(BF16)
     slots_down = iota((LANES, LANES), 0) >> 2
     rows_down = packed_iota(cells_row)
     for block in range(slot_ref.shape[0]):
         lanes = slice(block * LANES, (block + 1) * LANES)
         if block % 2 == 0:
-            both = sum_halves(times(arrived, place_ref[:, block * LANES : (block + 2) * LANES]))
+            place = place_ref[:, block * LANES : (block + 2) * LANES]
+            both = times(arrived, jnp.concatenate([place, place], axis=0))
         found = both[:, :LANES] if block % 2 == 0 else both[:, LANES:]
         found = jnp.where(slots_down == slot_ref[block : block + 1, :], found, 0.0)
         folded = found[0:8]

time: 57.1 us -> 57.3 us (level)
  no operation moved by 1% of the time
where the time goes in v20:
time: 57.3 us; the launch traced here: 56.9 us
  blocking collectives  22.9 us (40%)
  starting transfers between devices  21.6 us (38%)
  Pallas kernels  8.36 us (15%)
  waiting for transfers between devices  3.21 us (6%)
  between operations  0.8 us (1%)
    all_to_all x2, blocking collectives, exchange(): return lax.all_to_all(chunks, both, split_axis=0, concat_axis=0, tiled=True)  22.9 us
    all_to_all x2, starting transfers between devices, exchange(): return lax.all_to_all(chunks, both, split_axis=0, concat_axis=0, tiled=True)  9.89 us
    pallas_call x6, Pallas kernels, call_kernel(): pl.pallas_call(body, name=name, out_shape=outs, in_specs=[pl.BlockSpec(me...  8.36 us
    ppermute x1, starting transfers between devices, shards(): lower = lax.ppermute(high, 'gx', up)  4.55 us
    ppermute x1, starting transfers between devices, shards(): load_lower = lax.ppermute(load_high, 'gx', up)  4.55 us
    ppermute x1, waiting for transfers between devices, shards(): load_lower = lax.ppermute(load_high, 'gx', up)  1.49 us
    ppermute x1, starting transfers between devices, shards(): higher = lax.ppermute(low, 'gx', down)  1.29 us
    ppermute x1, starting transfers between devices, shards(): load_higher = lax.ppermute(load_low, 'gx', down)  1.29 us
  transfers between devices with their start and end apart: 6, of which 3 were waited for; matrix products, arithmetic and copies ran while one was open for 0% of the time, Pallas kernels for 1%

profile of v20, /device:TPU:0, one launch (start us, length us, event | category | flops | bytes accessed | tf_op | source)
XLA Modules:
  0.0 56.9 jit_solution(16021752562175405074)
XLA Ops:
  0.6 1.8 %pack_edges.1 = (f32[224,128]{1,0:T(8,128)}, f32[168,128]{1,0:T(8,128)}, f32[168,128]{1,0:T(8,128)}, f32[32,1,768]{2,1,0:T(1,128)}) custom-call(f32[144,128]{1,0:T(8,128)} %bitcast.20, f32[16,128]{1,0:T(8,128)} %bitcast.21, f32[16,128]{1,0:T(8,128)} %bitcast.22, f32[16,128]{1,0:T(8,128)} %bitcast.23, s32[1,64]{1,0:T(1,128)} %bitcast.24, f32[3,64]{1,0:T(4,128)} %refs_5_.1), custom_call_target="tpu_custom_call" | custom-call | tf_op jit(solution)/shard_map/pack_edges/pallas_call | solution.py:27
  2.4 0.0 copy-start.4
  2.4 0.0 copy-start.5
  2.4 7.3 %all-to-all-start = ((f32[32,1,768]{2,1,0:T(1,128)}), f32[32,1,768]{2,1,0:T(1,128)S(1)}, u32[]{:S(2)}, u32[]{:S(2)}) async-start(f32[32,1,768]{2,1,0:T(1,128)} %get-tuple-element.24), calls=%async_computation | async-start | bytes 196608 | tf_op jit(solution)/shard_map/all_to_all | solution.py:653
  9.8 1.3 %collective-permute-start = (f32[168,128]{1,0:T(8,128)}, f32[168,128]{1,0:T(8,128)S(1)}, u32[]{:S(2)}, u32[]{:S(2)}) collective-permute-start(f32[168,128]{1,0:T(8,128)} %get-tuple-element.22), channel_id=1, source_target_pairs={{8,0},{16,8},{24,16},{9,1},{17,9},{25,17},{10,2},{18,10},{26,18},{... | collective-permute-start | bytes 258056 | tf_op jit(solution)/shard_map/ppermute | solution.py:684
  11.1 0.0 copy-start.1
  11.1 4.5 %collective-permute-start.1 = (f32[168,128]{1,0:T(8,128)}, f32[168,128]{1,0:T(8,128)S(1)}, u32[]{:S(2)}, u32[]{:S(2)}) collective-permute-start(f32[168,128]{1,0:T(8,128)} %get-tuple-element.23), channel_id=1, source_target_pairs={{0,8},{8,16},{16,24},{1,9},{9,17},{17,25},{2,10},{10,18},{18,26},{... | collective-permute-start | bytes 258056 | tf_op jit(solution)/shard_map/ppermute | solution.py:683
  15.7 0.6 %segment_slots.1 = (s32[16,128]{1,0:T(8,128)S(1)}, s32[16,128]{1,0:T(8,128)S(1)}, bf16[128,2048]{1,0:T(8,128)(2,1)S(1)}, bf16[128,2048]{1,0:T(8,128)(2,1)S(1)}) custom-call(s32[16,128]{1,0:T(8,128)S(1)} %bitcast.18, s32[16,128]{1,0:T(8,128)S(1)} %bitcast.19), custom_call_target="tpu_custom_call" | custom-call | tf_op jit(solution)/shard_map/segment_slots/pallas_call | solution.py:27
  16.3 0.0 copy-start.3
  16.3 0.7 %collective-permute-done.higher_ref = f32[168,128]{1,0:T(8,128)S(1)} collective-permute-done((f32[168,128]{1,0:T(8,128)}, f32[168,128]{1,0:T(8,128)S(1)}, u32[]{:S(2)}, u32[]{:S(2)}) %collective-permute-start) | collective-permute-done | bytes 86048 | tf_op jit(solution)/shard_map/ppermute | solution.py:684
  17.0 1.0 %collective-permute-done.1.lower_ref = f32[168,128]{1,0:T(8,128)S(1)} collective-permute-done((f32[168,128]{1,0:T(8,128)}, f32[168,128]{1,0:T(8,128)S(1)}, u32[]{:S(2)}, u32[]{:S(2)}) %collective-permute-start.1) | collective-permute-done | bytes 86048 | tf_op jit(solution)/shard_map/ppermute | solution.py:683
  18.0 1.6 %forward_run.1 = (f32[128,128]{1,0:T(8,128)S(1)}, f32[288,128]{1,0:T(8,128)S(1)}, f32[12,16,256]{2,1,0:T(8,128)S(1)}) custom-call(f32[224,128]{1,0:T(8,128)S(1)} %copy-done, f32[168,128]{1,0:T(8,128)S(1)} %collective-permute-done.higher_ref, f32[168,128]{1,0:T(8,128)S(1)} %collective-permute-done.1.lower_ref, f32[32,1,768]{2,1,0:T(1,128)S(1)} %all-to-all-done.recv_ref, ...), custom_call_target="tpu_custom_call" | custom-call | tf_op jit(solution)/shard_map/forward_run/pallas_call | solution.py:27
  19.7 0.0 copy-start.2
  19.7 13.8 %all_to_all.20 = f32[32,4,128]{2,1,0:T(4,128)S(1)} all-to-all(f32[32,4,128]{2,1,0:T(4,128)S(1)} %bitcast.15), channel_id=1, replica_groups=mesh['gx'=4,'gy'=8] {'gx','gy'}, dimensions={0} | all-to-all | bytes 131072 | tf_op jit(solution)/shard_map/all_to_all | solution.py:653
  33.5 1.4 %channel_sums.1 = (f32[3,1024]{1,0:T(4,128)S(1)}, f32[128,128]{1,0:T(8,128)S(1)}) custom-call(f32[128,128]{1,0:T(8,128)S(1)} %bitcast.14, f32[3,1024]{1,0:T(4,128)S(1)} %copy-done.2), custom_call_target="tpu_custom_call" | custom-call | tf_op jit(solution)/shard_map/channel_sums/pallas_call | solution.py:27
  34.9 9.1 %all_to_all.21 = f32[32,4,128]{2,1,0:T(4,128)S(1)} all-to-all(f32[32,4,128]{2,1,0:T(4,128)S(1)} %bitcast.16), channel_id=1, replica_groups=mesh['gx'=4,'gy'=8] {'gx','gy'}, dimensions={0} | all-to-all | bytes 131072 | tf_op jit(solution)/shard_map/all_to_all | solution.py:653
  44.0 1.7 %segment_loads.1 = (f32[96,128]{1,0:T(8,128)S(1)}, f32[48,128]{1,0:T(8,128)S(1)}, f32[48,128]{1,0:T(8,128)S(1)}, f32[32,1,384]{2,1,0:T(1,128)}) custom-call(f32[128,128]{1,0:T(8,128)S(1)} %bitcast.13, s32[16,128]{1,0:T(8,128)S(1)} %get-tuple-element.25.slot_ref, s32[16,128]{1,0:T(8,128)S(1)} %get-tuple-element.26.row_ref, f32[2,2048]{1,0:T(2,128)S(1)} %copy-done.1, ...), custom_call_target="tpu_custom_call" | custom-call | tf_op jit(solution)/shard_map/segment_loads/pallas_call | solution.py:27
  45.7 2.6 %all-to-all-start.3 = ((f32[32,1,384]{2,1,0:T(1,128)}), f32[32,1,384]{2,1,0:T(1,128)S(1)}, u32[]{:S(2)}, u32[]{:S(2)}) async-start(f32[32,1,384]{2,1,0:T(1,128)} %get-tuple-element.34), calls=%async_computation.3 | async-start | bytes 98304 | tf_op jit(solution)/shard_map/all_to_all | solution.py:653
  48.3 1.3 %collective-permute-start.2 = (f32[48,128]{1,0:T(8,128)S(1)}, f32[48,128]{1,0:T(8,128)S(1)}, u32[]{:S(2)}, u32[]{:S(2)}) collective-permute-start(f32[48,128]{1,0:T(8,128)S(1)} %get-tuple-element.32), channel_id=1, source_target_pairs={{8,0},{16,8},{24,16},{9,1},{17,9},{25,17},{10,2},{18,10},{26,18},{... | collective-permute-start | bytes 73736 | tf_op jit(solution)/shard_map/ppermute | solution.py:761
  49.6 4.5 %collective-permute-start.3 = (f32[48,128]{1,0:T(8,128)S(1)}, f32[48,128]{1,0:T(8,128)S(1)}, u32[]{:S(2)}, u32[]{:S(2)}) collective-permute-start(f32[48,128]{1,0:T(8,128)S(1)} %get-tuple-element.33), channel_id=1, source_target_pairs={{0,8},{8,16},{16,24},{1,9},{9,17},{17,25},{2,10},{10,18},{18,26},{... | collective-permute-start | bytes 73736 | tf_op jit(solution)/shard_map/ppermute | solution.py:760
  54.1 0.0 collective-permute-done.2.higher_ref
  54.1 1.5 %collective-permute-done.3.lower_ref = f32[48,128]{1,0:T(8,128)S(1)} collective-permute-done((f32[48,128]{1,0:T(8,128)S(1)}, f32[48,128]{1,0:T(8,128)S(1)}, u32[]{:S(2)}, u32[]{:S(2)}) %collective-permute-start.3) | collective-permute-done | bytes 24608 | tf_op jit(solution)/shard_map/ppermute | solution.py:760
  55.6 0.0 all-to-all-done.3.recv_ref
  55.6 1.3 %adjoint_run.1 = (f32[32,128]{1,0:T(8,128)}, f32[3,1024]{1,0:T(4,128)}) custom-call(f32[96,128]{1,0:T(8,128)S(1)} %get-tuple-element.31.load_ref, f32[48,128]{1,0:T(8,128)S(1)} %collective-permute-done.2.higher_ref, f32[48,128]{1,0:T(8,128)S(1)} %collective-permute-done.3.lower_ref, f32[32,1,384]{2,1,0:T(1,128)S(1)} %all-to-all-done.3.recv_ref, ...), custom_call_target="tpu_custom_call" | custom-call | tf_op jit(solution)/shard_map/adjoint_run/pallas_call | solution.py:27
  (8 shorter events, 0.0 us)
Async XLA Ops:
  2.4 13.2 %copy-start.4 = (s32[2048,1]{0,1:T(1,128)S(1)}, s32[2048,1]{0,1:T(1,128)}, u32[]{:S(2)}) copy-start(s32[2048,1]{0,1:T(1,128)} %param.19) | copy-start | bytes 24580
  2.4 13.2 %copy-start.5 = (s32[2048]{0:T(1024)S(1)}, s32[2048]{0:T(1024)}, u32[]{:S(2)}) copy-start(s32[2048]{0:T(1024)} %param.17) | copy-start | bytes 24580
  2.4 15.6 %copy-start = (f32[224,128]{1,0:T(8,128)S(1)}, f32[224,128]{1,0:T(8,128)}, u32[]{:S(2)}) copy-start(f32[224,128]{1,0:T(8,128)} %get-tuple-element.21.fields_ref) | copy-start | bytes 344068
  2.4 15.6 %all-to-all-start = ((f32[32,1,768]{2,1,0:T(1,128)}), f32[32,1,768]{2,1,0:T(1,128)S(1)}, u32[]{:S(2)}, u32[]{:S(2)}) async-start(f32[32,1,768]{2,1,0:T(1,128)} %get-tuple-element.24), calls=%async_computation | async-start | bytes 196608 | tf_op jit(solution)/shard_map/all_to_all | solution.py:653
  9.8 7.2 %collective-permute-start = (f32[168,128]{1,0:T(8,128)}, f32[168,128]{1,0:T(8,128)S(1)}, u32[]{:S(2)}, u32[]{:S(2)}) collective-permute-start(f32[168,128]{1,0:T(8,128)} %get-tuple-element.22), channel_id=1, source_target_pairs={{8,0},{16,8},{24,16},{9,1},{17,9},{25,17},{10,2},{18,10},{26,18},{... | collective-permute-start | bytes 258056 | tf_op jit(solution)/shard_map/ppermute | solution.py:684
  11.1 7.0 %copy-start.1 = (f32[2,2048]{1,0:T(2,128)S(1)}, f32[2,2048]{1,0:T(2,128)}, u32[]{:S(2)}) copy-start(f32[2,2048]{1,0:T(2,128)} %weight_ref.3) | copy-start | bytes 49156
  11.1 6.9 %collective-permute-start.1 = (f32[168,128]{1,0:T(8,128)}, f32[168,128]{1,0:T(8,128)S(1)}, u32[]{:S(2)}, u32[]{:S(2)}) collective-permute-start(f32[168,128]{1,0:T(8,128)} %get-tuple-element.23), channel_id=1, source_target_pairs={{0,8},{8,16},{16,24},{1,9},{9,17},{17,25},{2,10},{10,18},{18,26},{... | collective-permute-start | bytes 258056 | tf_op jit(solution)/shard_map/ppermute | solution.py:683
  16.3 1.7 %copy-start.3 = (s32[2048]{0:T(1024)S(1)}, s32[2048]{0:T(1024)}, u32[]{:S(2)}) copy-start(s32[2048]{0:T(1024)} %param.20) | copy-start | bytes 24580
  19.7 13.8 %copy-start.2 = (f32[3,1024]{1,0:T(4,128)S(1)}, f32[3,1024]{1,0:T(4,128)}, u32[]{:S(2)}) copy-start(f32[3,1024]{1,0:T(4,128)} %observed_ref.1) | copy-start | bytes 36868
  45.7 9.9 %all-to-all-start.3 = ((f32[32,1,384]{2,1,0:T(1,128)}), f32[32,1,384]{2,1,0:T(1,128)S(1)}, u32[]{:S(2)}, u32[]{:S(2)}) async-start(f32[32,1,384]{2,1,0:T(1,128)} %get-tuple-element.34), calls=%async_computation.3 | async-start | bytes 98304 | tf_op jit(solution)/shard_map/all_to_all | solution.py:653
  48.3 5.9 %collective-permute-start.2 = (f32[48,128]{1,0:T(8,128)S(1)}, f32[48,128]{1,0:T(8,128)S(1)}, u32[]{:S(2)}, u32[]{:S(2)}) collective-permute-start(f32[48,128]{1,0:T(8,128)S(1)} %get-tuple-element.32), channel_id=1, source_target_pairs={{8,0},{16,8},{24,16},{9,1},{17,9},{25,17},{10,2},{18,10},{26,18},{... | collective-permute-start | bytes 73736 | tf_op jit(solution)/shard_map/ppermute | solution.py:761
  49.6 6.1 %collective-permute-start.3 = (f32[48,128]{1,0:T(8,128)S(1)}, f32[48,128]{1,0:T(8,128)S(1)}, u32[]{:S(2)}, u32[]{:S(2)}) collective-permute-start(f32[48,128]{1,0:T(8,128)S(1)} %get-tuple-element.33), channel_id=1, source_target_pairs={{0,8},{8,16},{16,24},{1,9},{9,17},{17,25},{2,10},{10,18},{18,26},{... | collective-permute-start | bytes 73736 | tf_op jit(solution)/shard_map/ppermute | solution.py:760

commit v21 on v19

--- a/solution.py
+++ b/solution.py
@@ -507,15 +507,10 @@
                     spread_ref[base : base + cells_row, lanes] = jnp.where(
                         at_row, packed_rows(piece, cells_row), jnp.zeros((), BF16)
                     )
-    cover = jnp.concatenate([cover_ref[0:16, :], cover_ref[LANES - 16 :, :]], axis=0)
-    edges = times_turned(cover, spread_ref[0:stack_rows, :]) + times_turned(cover, spread_ref[stack_rows:, :])
-    side_ref[...] = jnp.zeros_like(side_ref)
-    for side, base in ((0, 0), (1, 32 - RIM)):
-        for column in range(RIM):
-            lanes = slice(column * LANES, column * LANES + stack_rows)
-            side_ref[side, 0:1, lanes] = edges[base + column : base + column + 1, :]
+    load = sum_halves(times_turned(spread_ref[...], cover_ref[...]))
+    spare = LANES - stack_rows
+    edge_columns(jnp.concatenate([load, jnp.zeros((spare, LANES), F32)], axis=0), side_ref)
     sides = start_sides(side_ref, out_ref, sent_sides)
-    load = sum_halves(times_turned(spread_ref[...], cover_ref[...]))
     load_ref[...] = load
     held_ref[0:stack_rows, :] = load
     count = stack_rows // (3 * TILE_X)

time: 57.1 us -> 57.1 us (level)
  no operation moved by 1% of the time
where the time goes in v21:
time: 57.1 us; the launch traced here: 56.7 us
  blocking collectives  22.9 us (40%)
  starting transfers between devices  21.6 us (38%)
  Pallas kernels  8.13 us (14%)
  waiting for transfers between devices  3.21 us (6%)
  between operations  0.8 us (1%)
    all_to_all x2, blocking collectives, exchange(): return lax.all_to_all(chunks, both, split_axis=0, concat_axis=0, tiled=True)  22.9 us
    all_to_all x2, starting transfers between devices, exchange(): return lax.all_to_all(chunks, both, split_axis=0, concat_axis=0, tiled=True)  9.89 us
    pallas_call x6, Pallas kernels, call_kernel(): pl.pallas_call(body, name=name, out_shape=outs, in_specs=[pl.BlockSpec(me...  8.13 us
    ppermute x1, starting transfers between devices, shards(): lower = lax.ppermute(high, 'gx', up)  4.55 us
    ppermute x1, starting transfers between devices, shards(): load_lower = lax.ppermute(load_high, 'gx', up)  4.55 us
    ppermute x1, waiting for transfers between devices, shards(): load_lower = lax.ppermute(load_high, 'gx', up)  1.49 us
    ppermute x1, starting transfers between devices, shards(): higher = lax.ppermute(low, 'gx', down)  1.29 us
    ppermute x1, starting transfers between devices, shards(): load_higher = lax.ppermute(load_low, 'gx', down)  1.29 us
  transfers between devices with their start and end apart: 6, of which 3 were waited for; matrix products, arithmetic and copies ran while one was open for 0% of the time, Pallas kernels for 1%

profile of v21, /device:TPU:0, one launch (start us, length us, event | category | flops | bytes accessed | tf_op | source)
XLA Modules:
  0.0 56.7 jit_solution(4259697121154875207)
XLA Ops:
  0.6 1.8 %pack_edges.1 = (f32[224,128]{1,0:T(8,128)}, f32[168,128]{1,0:T(8,128)}, f32[168,128]{1,0:T(8,128)}, f32[32,1,768]{2,1,0:T(1,128)}) custom-call(f32[144,128]{1,0:T(8,128)} %bitcast.20, f32[16,128]{1,0:T(8,128)} %bitcast.21, f32[16,128]{1,0:T(8,128)} %bitcast.22, f32[16,128]{1,0:T(8,128)} %bitcast.23, s32[1,64]{1,0:T(1,128)} %bitcast.24, f32[3,64]{1,0:T(4,128)} %refs_5_.1), custom_call_target="tpu_custom_call" | custom-call | tf_op jit(solution)/shard_map/pack_edges/pallas_call | solution.py:27
  2.4 0.0 copy-start.4
  2.4 0.0 copy-start.5
  2.4 7.3 %all-to-all-start = ((f32[32,1,768]{2,1,0:T(1,128)}), f32[32,1,768]{2,1,0:T(1,128)S(1)}, u32[]{:S(2)}, u32[]{:S(2)}) async-start(f32[32,1,768]{2,1,0:T(1,128)} %get-tuple-element.24), calls=%async_computation | async-start | bytes 196608 | tf_op jit(solution)/shard_map/all_to_all | solution.py:644
  9.8 1.3 %collective-permute-start = (f32[168,128]{1,0:T(8,128)}, f32[168,128]{1,0:T(8,128)S(1)}, u32[]{:S(2)}, u32[]{:S(2)}) collective-permute-start(f32[168,128]{1,0:T(8,128)} %get-tuple-element.22), channel_id=1, source_target_pairs={{8,0},{16,8},{24,16},{9,1},{17,9},{25,17},{10,2},{18,10},{26,18},{... | collective-permute-start | bytes 258056 | tf_op jit(solution)/shard_map/ppermute | solution.py:675
  11.1 0.0 copy-start.1
  11.1 4.5 %collective-permute-start.1 = (f32[168,128]{1,0:T(8,128)}, f32[168,128]{1,0:T(8,128)S(1)}, u32[]{:S(2)}, u32[]{:S(2)}) collective-permute-start(f32[168,128]{1,0:T(8,128)} %get-tuple-element.23), channel_id=1, source_target_pairs={{0,8},{8,16},{16,24},{1,9},{9,17},{17,25},{2,10},{10,18},{18,26},{... | collective-permute-start | bytes 258056 | tf_op jit(solution)/shard_map/ppermute | solution.py:674
  15.7 0.6 %segment_slots.1 = (s32[16,128]{1,0:T(8,128)S(1)}, s32[16,128]{1,0:T(8,128)S(1)}, bf16[128,2048]{1,0:T(8,128)(2,1)S(1)}, bf16[128,2048]{1,0:T(8,128)(2,1)S(1)}) custom-call(s32[16,128]{1,0:T(8,128)S(1)} %bitcast.18, s32[16,128]{1,0:T(8,128)S(1)} %bitcast.19), custom_call_target="tpu_custom_call" | custom-call | tf_op jit(solution)/shard_map/segment_slots/pallas_call | solution.py:27
  16.3 0.0 copy-start.3
  16.3 0.7 %collective-permute-done.higher_ref = f32[168,128]{1,0:T(8,128)S(1)} collective-permute-done((f32[168,128]{1,0:T(8,128)}, f32[168,128]{1,0:T(8,128)S(1)}, u32[]{:S(2)}, u32[]{:S(2)}) %collective-permute-start) | collective-permute-done | bytes 86048 | tf_op jit(solution)/shard_map/ppermute | solution.py:675
  17.0 1.0 %collective-permute-done.1.lower_ref = f32[168,128]{1,0:T(8,128)S(1)} collective-permute-done((f32[168,128]{1,0:T(8,128)}, f32[168,128]{1,0:T(8,128)S(1)}, u32[]{:S(2)}, u32[]{:S(2)}) %collective-permute-start.1) | collective-permute-done | bytes 86048 | tf_op jit(solution)/shard_map/ppermute | solution.py:674
  18.0 1.7 %forward_run.1 = (f32[128,128]{1,0:T(8,128)S(1)}, f32[288,128]{1,0:T(8,128)S(1)}, f32[12,16,256]{2,1,0:T(8,128)S(1)}) custom-call(f32[224,128]{1,0:T(8,128)S(1)} %copy-done, f32[168,128]{1,0:T(8,128)S(1)} %collective-permute-done.higher_ref, f32[168,128]{1,0:T(8,128)S(1)} %collective-permute-done.1.lower_ref, f32[32,1,768]{2,1,0:T(1,128)S(1)} %all-to-all-done.recv_ref, ...), custom_call_target="tpu_custom_call" | custom-call | tf_op jit(solution)/shard_map/forward_run/pallas_call | solution.py:27
  19.7 0.0 copy-start.2
  19.7 13.8 %all_to_all.20 = f32[32,4,128]{2,1,0:T(4,128)S(1)} all-to-all(f32[32,4,128]{2,1,0:T(4,128)S(1)} %bitcast.15), channel_id=1, replica_groups=mesh['gx'=4,'gy'=8] {'gx','gy'}, dimensions={0} | all-to-all | bytes 131072 | tf_op jit(solution)/shard_map/all_to_all | solution.py:644
  33.5 1.1 %channel_sums.1 = (f32[3,1024]{1,0:T(4,128)S(1)}, f32[128,128]{1,0:T(8,128)S(1)}) custom-call(f32[128,128]{1,0:T(8,128)S(1)} %bitcast.14, f32[3,1024]{1,0:T(4,128)S(1)} %copy-done.2), custom_call_target="tpu_custom_call" | custom-call | tf_op jit(solution)/shard_map/channel_sums/pallas_call | solution.py:27
  34.6 9.1 %all_to_all.21 = f32[32,4,128]{2,1,0:T(4,128)S(1)} all-to-all(f32[32,4,128]{2,1,0:T(4,128)S(1)} %bitcast.16), channel_id=1, replica_groups=mesh['gx'=4,'gy'=8] {'gx','gy'}, dimensions={0} | all-to-all | bytes 131072 | tf_op jit(solution)/shard_map/all_to_all | solution.py:644
  43.7 1.7 %segment_loads.1 = (f32[96,128]{1,0:T(8,128)S(1)}, f32[48,128]{1,0:T(8,128)S(1)}, f32[48,128]{1,0:T(8,128)S(1)}, f32[32,1,384]{2,1,0:T(1,128)}) custom-call(f32[128,128]{1,0:T(8,128)S(1)} %bitcast.13, s32[16,128]{1,0:T(8,128)S(1)} %get-tuple-element.25.slot_ref, s32[16,128]{1,0:T(8,128)S(1)} %get-tuple-element.26.row_ref, f32[2,2048]{1,0:T(2,128)S(1)} %copy-done.1, ...), custom_call_target="tpu_custom_call" | custom-call | tf_op jit(solution)/shard_map/segment_loads/pallas_call | solution.py:27
  45.4 2.6 %all-to-all-start.3 = ((f32[32,1,384]{2,1,0:T(1,128)}), f32[32,1,384]{2,1,0:T(1,128)S(1)}, u32[]{:S(2)}, u32[]{:S(2)}) async-start(f32[32,1,384]{2,1,0:T(1,128)} %get-tuple-element.34), calls=%async_computation.3 | async-start | bytes 98304 | tf_op jit(solution)/shard_map/all_to_all | solution.py:644
  48.0 1.3 %collective-permute-start.2 = (f32[48,128]{1,0:T(8,128)S(1)}, f32[48,128]{1,0:T(8,128)S(1)}, u32[]{:S(2)}, u32[]{:S(2)}) collective-permute-start(f32[48,128]{1,0:T(8,128)S(1)} %get-tuple-element.32), channel_id=1, source_target_pairs={{8,0},{16,8},{24,16},{9,1},{17,9},{25,17},{10,2},{18,10},{26,18},{... | collective-permute-start | bytes 73736 | tf_op jit(solution)/shard_map/ppermute | solution.py:752
  49.3 4.5 %collective-permute-start.3 = (f32[48,128]{1,0:T(8,128)S(1)}, f32[48,128]{1,0:T(8,128)S(1)}, u32[]{:S(2)}, u32[]{:S(2)}) collective-permute-start(f32[48,128]{1,0:T(8,128)S(1)} %get-tuple-element.33), channel_id=1, source_target_pairs={{0,8},{8,16},{16,24},{1,9},{9,17},{17,25},{2,10},{10,18},{18,26},{... | collective-permute-start | bytes 73736 | tf_op jit(solution)/shard_map/ppermute | solution.py:751
  53.9 0.0 collective-permute-done.2.higher_ref
  53.9 1.5 %collective-permute-done.3.lower_ref = f32[48,128]{1,0:T(8,128)S(1)} collective-permute-done((f32[48,128]{1,0:T(8,128)S(1)}, f32[48,128]{1,0:T(8,128)S(1)}, u32[]{:S(2)}, u32[]{:S(2)}) %collective-permute-start.3) | collective-permute-done | bytes 24608 | tf_op jit(solution)/shard_map/ppermute | solution.py:751
  55.4 0.0 all-to-all-done.3.recv_ref
  55.4 1.3 %adjoint_run.1 = (f32[32,128]{1,0:T(8,128)}, f32[3,1024]{1,0:T(4,128)}) custom-call(f32[96,128]{1,0:T(8,128)S(1)} %get-tuple-element.31.load_ref, f32[48,128]{1,0:T(8,128)S(1)} %collective-permute-done.2.higher_ref, f32[48,128]{1,0:T(8,128)S(1)} %collective-permute-done.3.lower_ref, f32[32,1,384]{2,1,0:T(1,128)S(1)} %all-to-all-done.3.recv_ref, ...), custom_call_target="tpu_custom_call" | custom-call | tf_op jit(solution)/shard_map/adjoint_run/pallas_call | solution.py:27
  (8 shorter events, 0.0 us)
Async XLA Ops:
  2.4 13.2 %copy-start.4 = (s32[2048,1]{0,1:T(1,128)S(1)}, s32[2048,1]{0,1:T(1,128)}, u32[]{:S(2)}) copy-start(s32[2048,1]{0,1:T(1,128)} %param.19) | copy-start | bytes 24580
  2.4 13.2 %copy-start.5 = (s32[2048]{0:T(1024)S(1)}, s32[2048]{0:T(1024)}, u32[]{:S(2)}) copy-start(s32[2048]{0:T(1024)} %param.17) | copy-start | bytes 24580
  2.4 15.6 %copy-start = (f32[224,128]{1,0:T(8,128)S(1)}, f32[224,128]{1,0:T(8,128)}, u32[]{:S(2)}) copy-start(f32[224,128]{1,0:T(8,128)} %get-tuple-element.21.fields_ref) | copy-start | bytes 344068
  2.4 15.6 %all-to-all-start = ((f32[32,1,768]{2,1,0:T(1,128)}), f32[32,1,768]{2,1,0:T(1,128)S(1)}, u32[]{:S(2)}, u32[]{:S(2)}) async-start(f32[32,1,768]{2,1,0:T(1,128)} %get-tuple-element.24), calls=%async_computation | async-start | bytes 196608 | tf_op jit(solution)/shard_map/all_to_all | solution.py:644
  9.8 7.2 %collective-permute-start = (f32[168,128]{1,0:T(8,128)}, f32[168,128]{1,0:T(8,128)S(1)}, u32[]{:S(2)}, u32[]{:S(2)}) collective-permute-start(f32[168,128]{1,0:T(8,128)} %get-tuple-element.22), channel_id=1, source_target_pairs={{8,0},{16,8},{24,16},{9,1},{17,9},{25,17},{10,2},{18,10},{26,18},{... | collective-permute-start | bytes 258056 | tf_op jit(solution)/shard_map/ppermute | solution.py:675
  11.1 7.0 %copy-start.1 = (f32[2,2048]{1,0:T(2,128)S(1)}, f32[2,2048]{1,0:T(2,128)}, u32[]{:S(2)}) copy-start(f32[2,2048]{1,0:T(2,128)} %weight_ref.3) | copy-start | bytes 49156
  11.1 6.9 %collective-permute-start.1 = (f32[168,128]{1,0:T(8,128)}, f32[168,128]{1,0:T(8,128)S(1)}, u32[]{:S(2)}, u32[]{:S(2)}) collective-permute-start(f32[168,128]{1,0:T(8,128)} %get-tuple-element.23), channel_id=1, source_target_pairs={{0,8},{8,16},{16,24},{1,9},{9,17},{17,25},{2,10},{10,18},{18,26},{... | collective-permute-start | bytes 258056 | tf_op jit(solution)/shard_map/ppermute | solution.py:674
  16.3 1.7 %copy-start.3 = (s32[2048]{0:T(1024)S(1)}, s32[2048]{0:T(1024)}, u32[]{:S(2)}) copy-start(s32[2048]{0:T(1024)} %param.20) | copy-start | bytes 24580
  19.7 13.8 %copy-start.2 = (f32[3,1024]{1,0:T(4,128)S(1)}, f32[3,1024]{1,0:T(4,128)}, u32[]{:S(2)}) copy-start(f32[3,1024]{1,0:T(4,128)} %observed_ref.1) | copy-start | bytes 36868
  45.4 9.9 %all-to-all-start.3 = ((f32[32,1,384]{2,1,0:T(1,128)}), f32[32,1,384]{2,1,0:T(1,128)S(1)}, u32[]{:S(2)}, u32[]{:S(2)}) async-start(f32[32,1,384]{2,1,0:T(1,128)} %get-tuple-element.34), calls=%async_computation.3 | async-start | bytes 98304 | tf_op jit(solution)/shard_map/all_to_all | solution.py:644
  48.0 5.9 %collective-permute-start.2 = (f32[48,128]{1,0:T(8,128)S(1)}, f32[48,128]{1,0:T(8,128)S(1)}, u32[]{:S(2)}, u32[]{:S(2)}) collective-permute-start(f32[48,128]{1,0:T(8,128)S(1)} %get-tuple-element.32), channel_id=1, source_target_pairs={{8,0},{16,8},{24,16},{9,1},{17,9},{25,17},{10,2},{18,10},{26,18},{... | collective-permute-start | bytes 73736 | tf_op jit(solution)/shard_map/ppermute | solution.py:752
  49.3 6.1 %collective-permute-start.3 = (f32[48,128]{1,0:T(8,128)S(1)}, f32[48,128]{1,0:T(8,128)S(1)}, u32[]{:S(2)}, u32[]{:S(2)}) collective-permute-start(f32[48,128]{1,0:T(8,128)S(1)} %get-tuple-element.33), channel_id=1, source_target_pairs={{0,8},{8,16},{16,24},{1,9},{9,17},{17,25},{2,10},{10,18},{18,26},{... | collective-permute-start | bytes 73736 | tf_op jit(solution)/shard_map/ppermute | solution.py:751

commit v22 on v19

--- a/solution.py
+++ b/solution.py
@@ -240,18 +240,21 @@
 def pack_body(*refs):
     inputs, outputs, scratch = refs[:6], refs[6:10], refs[10:]
     fields_ref, high_ref, low_ref, side_ref, cells_ref, wavelet_ref, arrived, sent, sent_sides = scratch
+    third = inputs[0].shape[0] // 3
+    sources = [inputs[0].at[part * third : (part + 1) * third] for part in range(3)] + list(inputs[1:4])
     targets, at = [], 0
-    for source in inputs[:4]:
+    for source in sources:
         targets.append(fields_ref.at[at : at + source.shape[0]])
         at = at + source.shape[0]
+    sources += inputs[4:]
     copies = [
         pltpu.make_async_copy(source, target, arrived.at[number])
-        for number, (source, target) in enumerate(zip(inputs, targets + [cells_ref, wavelet_ref]))
+        for number, (source, target) in enumerate(zip(sources, targets + [cells_ref, wavelet_ref]))
     ]
-    for copy in copies[4:] + copies[:4]:
+    for copy in copies[6:] + copies[:6]:
         copy.start()
-    copies[4].wait()
-    copies[5].wait()
+    copies[6].wait()
+    copies[7].wait()
     cells_row = inputs[1].shape[0]
     cells = cells_ref[...]
     count = cells.shape[1]
@@ -263,7 +266,7 @@
     maps = sum_thirds(
         times_turned(jnp.concatenate(stack, axis=0).astype(BF16), jnp.where(at_lane, 1.0, 0.0).astype(BF16))
     )
-    for copy in copies[:4]:
+    for copy in copies[:6]:
         copy.wait()
     total = at + 2 * cells_row
     fields_ref[at:total, :] = maps[cells_row:]
@@ -558,7 +561,6 @@
     lay_planes(first_ref, later_ref, LANES, *rims)
     for plane in range(3 * depth):
         near_ref[plane] = narrowed(medium_ref[plane])
-    gradient_ref[...] = jnp.zeros_like(gradient_ref)
     residual_out_ref[...] = residual_ref[...]
     state, near, medium = (
         fields_of(state_ref, 9, depth),
@@ -584,7 +586,8 @@
                 product = term if product is None else product + term
         for part, term in enumerate((dilation * dilation_back, 2.0 * doubled + product)):
             base = (part * depth + z) * TILE_X
-            gradient_ref[base : base + TILE_X, :] = gradient_ref[base : base + TILE_X, :] + term
+            rows = slice(base, base + TILE_X)
+            gradient_ref[rows, :] = gradient_ref[rows, :] + term if turn else term
 
     loads, velocity = fields_of(first_ref, 2, depth), fields_of(velocity_ref, 2, depth)
     for z in range(depth):
@@ -665,7 +668,7 @@
             pltpu.VMEM((2, 1, 2 * RIM * LANES), F32),
             pltpu.VMEM((1, source_cells.shape[0]), I32),
             pltpu.VMEM(source_wavelet.shape, F32),
-            pltpu.SemaphoreType.DMA((6,)),
+            pltpu.SemaphoreType.DMA((8,)),
             pltpu.SemaphoreType.DMA((3,)),
             pltpu.SemaphoreType.DMA((6,)),
         ],

time: 57.1 us -> 57.1 us (level)
  no operation moved by 1% of the time
where the time goes in v22:
time: 57.1 us; the launch traced here: 56.6 us
  blocking collectives  22.9 us (40%)
  starting transfers between devices  21.6 us (38%)
  Pallas kernels  8.1 us (14%)
  waiting for transfers between devices  3.21 us (6%)
  between operations  0.8 us (1%)
    all_to_all x2, blocking collectives, exchange(): return lax.all_to_all(chunks, both, split_axis=0, concat_axis=0, tiled=True)  22.9 us
    all_to_all x2, starting transfers between devices, exchange(): return lax.all_to_all(chunks, both, split_axis=0, concat_axis=0, tiled=True)  9.89 us
    pallas_call x6, Pallas kernels, call_kernel(): pl.pallas_call(body, name=name, out_shape=outs, in_specs=[pl.BlockSpec(me...  8.1 us
    ppermute x1, starting transfers between devices, shards(): lower = lax.ppermute(high, 'gx', up)  4.55 us
    ppermute x1, starting transfers between devices, shards(): load_lower = lax.ppermute(load_high, 'gx', up)  4.55 us
    ppermute x1, waiting for transfers between devices, shards(): load_lower = lax.ppermute(load_high, 'gx', up)  1.49 us
    ppermute x1, starting transfers between devices, shards(): higher = lax.ppermute(low, 'gx', down)  1.29 us
    ppermute x1, starting transfers between devices, shards(): load_higher = lax.ppermute(load_low, 'gx', down)  1.29 us
  transfers between devices with their start and end apart: 6, of which 3 were waited for; matrix products, arithmetic and copies ran while one was open for 0% of the time, Pallas kernels for 1%

profile of v22, /device:TPU:0, one launch (start us, length us, event | category | flops | bytes accessed | tf_op | source)
XLA Modules:
  0.0 56.6 jit_solution(15699228957768661960)
XLA Ops:
  0.6 1.8 %pack_edges.1 = (f32[224,128]{1,0:T(8,128)}, f32[168,128]{1,0:T(8,128)}, f32[168,128]{1,0:T(8,128)}, f32[32,1,768]{2,1,0:T(1,128)}) custom-call(f32[144,128]{1,0:T(8,128)} %bitcast.20, f32[16,128]{1,0:T(8,128)} %bitcast.21, f32[16,128]{1,0:T(8,128)} %bitcast.22, f32[16,128]{1,0:T(8,128)} %bitcast.23, s32[1,64]{1,0:T(1,128)} %bitcast.24, f32[3,64]{1,0:T(4,128)} %refs_5_.1), custom_call_target="tpu_custom_call" | custom-call | tf_op jit(solution)/shard_map/pack_edges/pallas_call | solution.py:27
  2.4 0.0 copy-start.4
  2.4 0.0 copy-start.5
  2.4 7.3 %all-to-all-start = ((f32[32,1,768]{2,1,0:T(1,128)}), f32[32,1,768]{2,1,0:T(1,128)S(1)}, u32[]{:S(2)}, u32[]{:S(2)}) async-start(f32[32,1,768]{2,1,0:T(1,128)} %get-tuple-element.24), calls=%async_computation | async-start | bytes 196608 | tf_op jit(solution)/shard_map/all_to_all | solution.py:652
  9.7 1.3 %collective-permute-start = (f32[168,128]{1,0:T(8,128)}, f32[168,128]{1,0:T(8,128)S(1)}, u32[]{:S(2)}, u32[]{:S(2)}) collective-permute-start(f32[168,128]{1,0:T(8,128)} %get-tuple-element.22), channel_id=1, source_target_pairs={{8,0},{16,8},{24,16},{9,1},{17,9},{25,17},{10,2},{18,10},{26,18},{... | collective-permute-start | bytes 258056 | tf_op jit(solution)/shard_map/ppermute | solution.py:683
  11.0 0.0 copy-start.1
  11.1 4.5 %collective-permute-start.1 = (f32[168,128]{1,0:T(8,128)}, f32[168,128]{1,0:T(8,128)S(1)}, u32[]{:S(2)}, u32[]{:S(2)}) collective-permute-start(f32[168,128]{1,0:T(8,128)} %get-tuple-element.23), channel_id=1, source_target_pairs={{0,8},{8,16},{16,24},{1,9},{9,17},{17,25},{2,10},{10,18},{18,26},{... | collective-permute-start | bytes 258056 | tf_op jit(solution)/shard_map/ppermute | solution.py:682
  15.6 0.6 %segment_slots.1 = (s32[16,128]{1,0:T(8,128)S(1)}, s32[16,128]{1,0:T(8,128)S(1)}, bf16[128,2048]{1,0:T(8,128)(2,1)S(1)}, bf16[128,2048]{1,0:T(8,128)(2,1)S(1)}) custom-call(s32[16,128]{1,0:T(8,128)S(1)} %bitcast.18, s32[16,128]{1,0:T(8,128)S(1)} %bitcast.19), custom_call_target="tpu_custom_call" | custom-call | tf_op jit(solution)/shard_map/segment_slots/pallas_call | solution.py:27
  16.3 0.0 copy-start.3
  16.3 0.7 %collective-permute-done.higher_ref = f32[168,128]{1,0:T(8,128)S(1)} collective-permute-done((f32[168,128]{1,0:T(8,128)}, f32[168,128]{1,0:T(8,128)S(1)}, u32[]{:S(2)}, u32[]{:S(2)}) %collective-permute-start) | collective-permute-done | bytes 86048 | tf_op jit(solution)/shard_map/ppermute | solution.py:683
  17.0 1.0 %collective-permute-done.1.lower_ref = f32[168,128]{1,0:T(8,128)S(1)} collective-permute-done((f32[168,128]{1,0:T(8,128)}, f32[168,128]{1,0:T(8,128)S(1)}, u32[]{:S(2)}, u32[]{:S(2)}) %collective-permute-start.1) | collective-permute-done | bytes 86048 | tf_op jit(solution)/shard_map/ppermute | solution.py:682
  18.0 0.0 all-to-all-done.recv_ref
  18.0 1.7 %forward_run.1 = (f32[128,128]{1,0:T(8,128)S(1)}, f32[288,128]{1,0:T(8,128)S(1)}, f32[12,16,256]{2,1,0:T(8,128)S(1)}) custom-call(f32[224,128]{1,0:T(8,128)S(1)} %copy-done, f32[168,128]{1,0:T(8,128)S(1)} %collective-permute-done.higher_ref, f32[168,128]{1,0:T(8,128)S(1)} %collective-permute-done.1.lower_ref, f32[32,1,768]{2,1,0:T(1,128)S(1)} %all-to-all-done.recv_ref, ...), custom_call_target="tpu_custom_call" | custom-call | tf_op jit(solution)/shard_map/forward_run/pallas_call | solution.py:27
  19.7 0.0 copy-start.2
  19.7 13.8 %all_to_all.20 = f32[32,4,128]{2,1,0:T(4,128)S(1)} all-to-all(f32[32,4,128]{2,1,0:T(4,128)S(1)} %bitcast.15), channel_id=1, replica_groups=mesh['gx'=4,'gy'=8] {'gx','gy'}, dimensions={0} | all-to-all | bytes 131072 | tf_op jit(solution)/shard_map/all_to_all | solution.py:652
  33.5 1.1 %channel_sums.1 = (f32[3,1024]{1,0:T(4,128)S(1)}, f32[128,128]{1,0:T(8,128)S(1)}) custom-call(f32[128,128]{1,0:T(8,128)S(1)} %bitcast.14, f32[3,1024]{1,0:T(4,128)S(1)} %copy-done.2), custom_call_target="tpu_custom_call" | custom-call | tf_op jit(solution)/shard_map/channel_sums/pallas_call | solution.py:27
  34.6 9.1 %all_to_all.21 = f32[32,4,128]{2,1,0:T(4,128)S(1)} all-to-all(f32[32,4,128]{2,1,0:T(4,128)S(1)} %bitcast.16), channel_id=1, replica_groups=mesh['gx'=4,'gy'=8] {'gx','gy'}, dimensions={0} | all-to-all | bytes 131072 | tf_op jit(solution)/shard_map/all_to_all | solution.py:652
  43.7 1.7 %segment_loads.1 = (f32[96,128]{1,0:T(8,128)S(1)}, f32[48,128]{1,0:T(8,128)S(1)}, f32[48,128]{1,0:T(8,128)S(1)}, f32[32,1,384]{2,1,0:T(1,128)}) custom-call(f32[128,128]{1,0:T(8,128)S(1)} %bitcast.13, s32[16,128]{1,0:T(8,128)S(1)} %get-tuple-element.25.slot_ref, s32[16,128]{1,0:T(8,128)S(1)} %get-tuple-element.26.row_ref, f32[2,2048]{1,0:T(2,128)S(1)} %copy-done.1, ...), custom_call_target="tpu_custom_call" | custom-call | tf_op jit(solution)/shard_map/segment_loads/pallas_call | solution.py:27
  45.4 2.6 %all-to-all-start.3 = ((f32[32,1,384]{2,1,0:T(1,128)}), f32[32,1,384]{2,1,0:T(1,128)S(1)}, u32[]{:S(2)}, u32[]{:S(2)}) async-start(f32[32,1,384]{2,1,0:T(1,128)} %get-tuple-element.34), calls=%async_computation.3 | async-start | bytes 98304 | tf_op jit(solution)/shard_map/all_to_all | solution.py:652
  48.0 1.3 %collective-permute-start.2 = (f32[48,128]{1,0:T(8,128)S(1)}, f32[48,128]{1,0:T(8,128)S(1)}, u32[]{:S(2)}, u32[]{:S(2)}) collective-permute-start(f32[48,128]{1,0:T(8,128)S(1)} %get-tuple-element.32), channel_id=1, source_target_pairs={{8,0},{16,8},{24,16},{9,1},{17,9},{25,17},{10,2},{18,10},{26,18},{... | collective-permute-start | bytes 73736 | tf_op jit(solution)/shard_map/ppermute | solution.py:760
  49.3 4.5 %collective-permute-start.3 = (f32[48,128]{1,0:T(8,128)S(1)}, f32[48,128]{1,0:T(8,128)S(1)}, u32[]{:S(2)}, u32[]{:S(2)}) collective-permute-start(f32[48,128]{1,0:T(8,128)S(1)} %get-tuple-element.33), channel_id=1, source_target_pairs={{0,8},{8,16},{16,24},{1,9},{9,17},{17,25},{2,10},{10,18},{18,26},{... | collective-permute-start | bytes 73736 | tf_op jit(solution)/shard_map/ppermute | solution.py:759
  53.8 0.0 collective-permute-done.2.higher_ref
  53.9 1.5 %collective-permute-done.3.lower_ref = f32[48,128]{1,0:T(8,128)S(1)} collective-permute-done((f32[48,128]{1,0:T(8,128)S(1)}, f32[48,128]{1,0:T(8,128)S(1)}, u32[]{:S(2)}, u32[]{:S(2)}) %collective-permute-start.3) | collective-permute-done | bytes 24608 | tf_op jit(solution)/shard_map/ppermute | solution.py:759
  55.4 1.3 %adjoint_run.1 = (f32[32,128]{1,0:T(8,128)}, f32[3,1024]{1,0:T(4,128)}) custom-call(f32[96,128]{1,0:T(8,128)S(1)} %get-tuple-element.31.load_ref, f32[48,128]{1,0:T(8,128)S(1)} %collective-permute-done.2.higher_ref, f32[48,128]{1,0:T(8,128)S(1)} %collective-permute-done.3.lower_ref, f32[32,1,384]{2,1,0:T(1,128)S(1)} %all-to-all-done.3.recv_ref, ...), custom_call_target="tpu_custom_call" | custom-call | tf_op jit(solution)/shard_map/adjoint_run/pallas_call | solution.py:27
  (8 shorter events, 0.0 us)
Async XLA Ops:
  2.4 13.2 %copy-start.4 = (s32[2048,1]{0,1:T(1,128)S(1)}, s32[2048,1]{0,1:T(1,128)}, u32[]{:S(2)}) copy-start(s32[2048,1]{0,1:T(1,128)} %param.19) | copy-start | bytes 24580
  2.4 13.2 %copy-start.5 = (s32[2048]{0:T(1024)S(1)}, s32[2048]{0:T(1024)}, u32[]{:S(2)}) copy-start(s32[2048]{0:T(1024)} %param.17) | copy-start | bytes 24580
  2.4 15.6 %copy-start = (f32[224,128]{1,0:T(8,128)S(1)}, f32[224,128]{1,0:T(8,128)}, u32[]{:S(2)}) copy-start(f32[224,128]{1,0:T(8,128)} %get-tuple-element.21.fields_ref) | copy-start | bytes 344068
  2.4 15.6 %all-to-all-start = ((f32[32,1,768]{2,1,0:T(1,128)}), f32[32,1,768]{2,1,0:T(1,128)S(1)}, u32[]{:S(2)}, u32[]{:S(2)}) async-start(f32[32,1,768]{2,1,0:T(1,128)} %get-tuple-element.24), calls=%async_computation | async-start | bytes 196608 | tf_op jit(solution)/shard_map/all_to_all | solution.py:652
  9.7 7.2 %collective-permute-start = (f32[168,128]{1,0:T(8,128)}, f32[168,128]{1,0:T(8,128)S(1)}, u32[]{:S(2)}, u32[]{:S(2)}) collective-permute-start(f32[168,128]{1,0:T(8,128)} %get-tuple-element.22), channel_id=1, source_target_pairs={{8,0},{16,8},{24,16},{9,1},{17,9},{25,17},{10,2},{18,10},{26,18},{... | collective-permute-start | bytes 258056 | tf_op jit(solution)/shard_map/ppermute | solution.py:683
  11.0 7.0 %copy-start.1 = (f32[2,2048]{1,0:T(2,128)S(1)}, f32[2,2048]{1,0:T(2,128)}, u32[]{:S(2)}) copy-start(f32[2,2048]{1,0:T(2,128)} %weight_ref.3) | copy-start | bytes 49156
  11.1 6.9 %collective-permute-start.1 = (f32[168,128]{1,0:T(8,128)}, f32[168,128]{1,0:T(8,128)S(1)}, u32[]{:S(2)}, u32[]{:S(2)}) collective-permute-start(f32[168,128]{1,0:T(8,128)} %get-tuple-element.23), channel_id=1, source_target_pairs={{0,8},{8,16},{16,24},{1,9},{9,17},{17,25},{2,10},{10,18},{18,26},{... | collective-permute-start | bytes 258056 | tf_op jit(solution)/shard_map/ppermute | solution.py:682
  16.3 1.7 %copy-start.3 = (s32[2048]{0:T(1024)S(1)}, s32[2048]{0:T(1024)}, u32[]{:S(2)}) copy-start(s32[2048]{0:T(1024)} %param.20) | copy-start | bytes 24580
  19.7 13.8 %copy-start.2 = (f32[3,1024]{1,0:T(4,128)S(1)}, f32[3,1024]{1,0:T(4,128)}, u32[]{:S(2)}) copy-start(f32[3,1024]{1,0:T(4,128)} %observed_ref.1) | copy-start | bytes 36868
  45.4 9.9 %all-to-all-start.3 = ((f32[32,1,384]{2,1,0:T(1,128)}), f32[32,1,384]{2,1,0:T(1,128)S(1)}, u32[]{:S(2)}, u32[]{:S(2)}) async-start(f32[32,1,384]{2,1,0:T(1,128)} %get-tuple-element.34), calls=%async_computation.3 | async-start | bytes 98304 | tf_op jit(solution)/shard_map/all_to_all | solution.py:652
  48.0 5.9 %collective-permute-start.2 = (f32[48,128]{1,0:T(8,128)S(1)}, f32[48,128]{1,0:T(8,128)S(1)}, u32[]{:S(2)}, u32[]{:S(2)}) collective-permute-start(f32[48,128]{1,0:T(8,128)S(1)} %get-tuple-element.32), channel_id=1, source_target_pairs={{8,0},{16,8},{24,16},{9,1},{17,9},{25,17},{10,2},{18,10},{26,18},{... | collective-permute-start | bytes 73736 | tf_op jit(solution)/shard_map/ppermute | solution.py:760
  49.3 6.1 %collective-permute-start.3 = (f32[48,128]{1,0:T(8,128)S(1)}, f32[48,128]{1,0:T(8,128)S(1)}, u32[]{:S(2)}, u32[]{:S(2)}) collective-permute-start(f32[48,128]{1,0:T(8,128)S(1)} %get-tuple-element.33), channel_id=1, source_target_pairs={{0,8},{8,16},{16,24},{1,9},{9,17},{17,25},{2,10},{10,18},{18,26},{... | collective-permute-start | bytes 73736 | tf_op jit(solution)/shard_map/ppermute | solution.py:759

commit v23 on v22

--- a/solution.py
+++ b/solution.py
@@ -251,7 +251,7 @@
         pltpu.make_async_copy(source, target, arrived.at[number])
         for number, (source, target) in enumerate(zip(sources, targets + [cells_ref, wavelet_ref]))
     ]
-    for copy in copies[6:] + copies[:6]:
+    for copy in copies:
         copy.start()
     copies[6].wait()
     copies[7].wait()

time: 57.1 us -> 57.2 us (level)
  no operation moved by 1% of the time
where the time goes in v23:
time: 57.2 us; the launch traced here: 56.7 us
  blocking collectives  22.9 us (40%)
  starting transfers between devices  21.6 us (38%)
  Pallas kernels  8.2 us (14%)
  waiting for transfers between devices  3.21 us (6%)
  between operations  0.8 us (1%)
    all_to_all x2, blocking collectives, exchange(): return lax.all_to_all(chunks, both, split_axis=0, concat_axis=0, tiled=True)  22.9 us
    all_to_all x2, starting transfers between devices, exchange(): return lax.all_to_all(chunks, both, split_axis=0, concat_axis=0, tiled=True)  9.89 us
    pallas_call x6, Pallas kernels, call_kernel(): pl.pallas_call(body, name=name, out_shape=outs, in_specs=[pl.BlockSpec(me...  8.2 us
    ppermute x1, starting transfers between devices, shards(): lower = lax.ppermute(high, 'gx', up)  4.55 us
    ppermute x1, starting transfers between devices, shards(): load_lower = lax.ppermute(load_high, 'gx', up)  4.55 us
    ppermute x1, waiting for transfers between devices, shards(): load_lower = lax.ppermute(load_high, 'gx', up)  1.49 us
    ppermute x1, starting transfers between devices, shards(): load_higher = lax.ppermute(load_low, 'gx', down)  1.29 us
    ppermute x1, starting transfers between devices, shards(): higher = lax.ppermute(low, 'gx', down)  1.29 us
  transfers between devices with their start and end apart: 6, of which 3 were waited for; matrix products, arithmetic and copies ran while one was open for 0% of the time, Pallas kernels for 1%

profile of v23, /device:TPU:0, one launch (start us, length us, event | category | flops | bytes accessed | tf_op | source)
XLA Modules:
  0.0 56.7 jit_solution(6317021653121973594)
XLA Ops:
  0.6 1.9 %pack_edges.1 = (f32[224,128]{1,0:T(8,128)}, f32[168,128]{1,0:T(8,128)}, f32[168,128]{1,0:T(8,128)}, f32[32,1,768]{2,1,0:T(1,128)}) custom-call(f32[144,128]{1,0:T(8,128)} %bitcast.20, f32[16,128]{1,0:T(8,128)} %bitcast.21, f32[16,128]{1,0:T(8,128)} %bitcast.22, f32[16,128]{1,0:T(8,128)} %bitcast.23, s32[1,64]{1,0:T(1,128)} %bitcast.24, f32[3,64]{1,0:T(4,128)} %refs_5_.1), custom_call_target="tpu_custom_call" | custom-call | tf_op jit(solution)/shard_map/pack_edges/pallas_call | solution.py:27
  2.5 0.0 copy-start.4
  2.5 0.0 copy-start.5
  2.5 7.3 %all-to-all-start = ((f32[32,1,768]{2,1,0:T(1,128)}), f32[32,1,768]{2,1,0:T(1,128)S(1)}, u32[]{:S(2)}, u32[]{:S(2)}) async-start(f32[32,1,768]{2,1,0:T(1,128)} %get-tuple-element.24), calls=%async_computation | async-start | bytes 196608 | tf_op jit(solution)/shard_map/all_to_all | solution.py:652
  9.8 1.3 %collective-permute-start = (f32[168,128]{1,0:T(8,128)}, f32[168,128]{1,0:T(8,128)S(1)}, u32[]{:S(2)}, u32[]{:S(2)}) collective-permute-start(f32[168,128]{1,0:T(8,128)} %get-tuple-element.22), channel_id=1, source_target_pairs={{8,0},{16,8},{24,16},{9,1},{17,9},{25,17},{10,2},{18,10},{26,18},{... | collective-permute-start | bytes 258056 | tf_op jit(solution)/shard_map/ppermute | solution.py:683
  11.1 0.0 copy-start.1
  11.2 4.5 %collective-permute-start.1 = (f32[168,128]{1,0:T(8,128)}, f32[168,128]{1,0:T(8,128)S(1)}, u32[]{:S(2)}, u32[]{:S(2)}) collective-permute-start(f32[168,128]{1,0:T(8,128)} %get-tuple-element.23), channel_id=1, source_target_pairs={{0,8},{8,16},{16,24},{1,9},{9,17},{17,25},{2,10},{10,18},{18,26},{... | collective-permute-start | bytes 258056 | tf_op jit(solution)/shard_map/ppermute | solution.py:682
  15.7 0.6 %segment_slots.1 = (s32[16,128]{1,0:T(8,128)S(1)}, s32[16,128]{1,0:T(8,128)S(1)}, bf16[128,2048]{1,0:T(8,128)(2,1)S(1)}, bf16[128,2048]{1,0:T(8,128)(2,1)S(1)}) custom-call(s32[16,128]{1,0:T(8,128)S(1)} %bitcast.18, s32[16,128]{1,0:T(8,128)S(1)} %bitcast.19), custom_call_target="tpu_custom_call" | custom-call | tf_op jit(solution)/shard_map/segment_slots/pallas_call | solution.py:27
  16.4 0.0 copy-start.3
  16.4 0.7 %collective-permute-done.higher_ref = f32[168,128]{1,0:T(8,128)S(1)} collective-permute-done((f32[168,128]{1,0:T(8,128)}, f32[168,128]{1,0:T(8,128)S(1)}, u32[]{:S(2)}, u32[]{:S(2)}) %collective-permute-start) | collective-permute-done | bytes 86048 | tf_op jit(solution)/shard_map/ppermute | solution.py:683
  17.1 1.0 %collective-permute-done.1.lower_ref = f32[168,128]{1,0:T(8,128)S(1)} collective-permute-done((f32[168,128]{1,0:T(8,128)}, f32[168,128]{1,0:T(8,128)S(1)}, u32[]{:S(2)}, u32[]{:S(2)}) %collective-permute-start.1) | collective-permute-done | bytes 86048 | tf_op jit(solution)/shard_map/ppermute | solution.py:682
  18.1 0.0 all-to-all-done.recv_ref
  18.1 1.7 %forward_run.1 = (f32[128,128]{1,0:T(8,128)S(1)}, f32[288,128]{1,0:T(8,128)S(1)}, f32[12,16,256]{2,1,0:T(8,128)S(1)}) custom-call(f32[224,128]{1,0:T(8,128)S(1)} %copy-done, f32[168,128]{1,0:T(8,128)S(1)} %collective-permute-done.higher_ref, f32[168,128]{1,0:T(8,128)S(1)} %collective-permute-done.1.lower_ref, f32[32,1,768]{2,1,0:T(1,128)S(1)} %all-to-all-done.recv_ref, ...), custom_call_target="tpu_custom_call" | custom-call | tf_op jit(solution)/shard_map/forward_run/pallas_call | solution.py:27
  19.8 0.0 copy-start.2
  19.8 13.8 %all_to_all.20 = f32[32,4,128]{2,1,0:T(4,128)S(1)} all-to-all(f32[32,4,128]{2,1,0:T(4,128)S(1)} %bitcast.15), channel_id=1, replica_groups=mesh['gx'=4,'gy'=8] {'gx','gy'}, dimensions={0} | all-to-all | bytes 131072 | tf_op jit(solution)/shard_map/all_to_all | solution.py:652
  33.6 1.1 %channel_sums.1 = (f32[3,1024]{1,0:T(4,128)S(1)}, f32[128,128]{1,0:T(8,128)S(1)}) custom-call(f32[128,128]{1,0:T(8,128)S(1)} %bitcast.14, f32[3,1024]{1,0:T(4,128)S(1)} %copy-done.2), custom_call_target="tpu_custom_call" | custom-call | tf_op jit(solution)/shard_map/channel_sums/pallas_call | solution.py:27
  34.7 9.1 %all_to_all.21 = f32[32,4,128]{2,1,0:T(4,128)S(1)} all-to-all(f32[32,4,128]{2,1,0:T(4,128)S(1)} %bitcast.16), channel_id=1, replica_groups=mesh['gx'=4,'gy'=8] {'gx','gy'}, dimensions={0} | all-to-all | bytes 131072 | tf_op jit(solution)/shard_map/all_to_all | solution.py:652
  43.8 1.7 %segment_loads.1 = (f32[96,128]{1,0:T(8,128)S(1)}, f32[48,128]{1,0:T(8,128)S(1)}, f32[48,128]{1,0:T(8,128)S(1)}, f32[32,1,384]{2,1,0:T(1,128)}) custom-call(f32[128,128]{1,0:T(8,128)S(1)} %bitcast.13, s32[16,128]{1,0:T(8,128)S(1)} %get-tuple-element.25.slot_ref, s32[16,128]{1,0:T(8,128)S(1)} %get-tuple-element.26.row_ref, f32[2,2048]{1,0:T(2,128)S(1)} %copy-done.1, ...), custom_call_target="tpu_custom_call" | custom-call | tf_op jit(solution)/shard_map/segment_loads/pallas_call | solution.py:27
  45.5 2.6 %all-to-all-start.3 = ((f32[32,1,384]{2,1,0:T(1,128)}), f32[32,1,384]{2,1,0:T(1,128)S(1)}, u32[]{:S(2)}, u32[]{:S(2)}) async-start(f32[32,1,384]{2,1,0:T(1,128)} %get-tuple-element.34), calls=%async_computation.3 | async-start | bytes 98304 | tf_op jit(solution)/shard_map/all_to_all | solution.py:652
  48.1 1.3 %collective-permute-start.2 = (f32[48,128]{1,0:T(8,128)S(1)}, f32[48,128]{1,0:T(8,128)S(1)}, u32[]{:S(2)}, u32[]{:S(2)}) collective-permute-start(f32[48,128]{1,0:T(8,128)S(1)} %get-tuple-element.32), channel_id=1, source_target_pairs={{8,0},{16,8},{24,16},{9,1},{17,9},{25,17},{10,2},{18,10},{26,18},{... | collective-permute-start | bytes 73736 | tf_op jit(solution)/shard_map/ppermute | solution.py:760
  49.4 4.5 %collective-permute-start.3 = (f32[48,128]{1,0:T(8,128)S(1)}, f32[48,128]{1,0:T(8,128)S(1)}, u32[]{:S(2)}, u32[]{:S(2)}) collective-permute-start(f32[48,128]{1,0:T(8,128)S(1)} %get-tuple-element.33), channel_id=1, source_target_pairs={{0,8},{8,16},{16,24},{1,9},{9,17},{17,25},{2,10},{10,18},{18,26},{... | collective-permute-start | bytes 73736 | tf_op jit(solution)/shard_map/ppermute | solution.py:759
  53.9 0.0 collective-permute-done.2.higher_ref
  54.0 1.5 %collective-permute-done.3.lower_ref = f32[48,128]{1,0:T(8,128)S(1)} collective-permute-done((f32[48,128]{1,0:T(8,128)S(1)}, f32[48,128]{1,0:T(8,128)S(1)}, u32[]{:S(2)}, u32[]{:S(2)}) %collective-permute-start.3) | collective-permute-done | bytes 24608 | tf_op jit(solution)/shard_map/ppermute | solution.py:759
  55.5 1.3 %adjoint_run.1 = (f32[32,128]{1,0:T(8,128)}, f32[3,1024]{1,0:T(4,128)}) custom-call(f32[96,128]{1,0:T(8,128)S(1)} %get-tuple-element.31.load_ref, f32[48,128]{1,0:T(8,128)S(1)} %collective-permute-done.2.higher_ref, f32[48,128]{1,0:T(8,128)S(1)} %collective-permute-done.3.lower_ref, f32[32,1,384]{2,1,0:T(1,128)S(1)} %all-to-all-done.3.recv_ref, ...), custom_call_target="tpu_custom_call" | custom-call | tf_op jit(solution)/shard_map/adjoint_run/pallas_call | solution.py:27
  (8 shorter events, 0.0 us)
Async XLA Ops:
  2.5 13.2 %copy-start.4 = (s32[2048,1]{0,1:T(1,128)S(1)}, s32[2048,1]{0,1:T(1,128)}, u32[]{:S(2)}) copy-start(s32[2048,1]{0,1:T(1,128)} %param.19) | copy-start | bytes 24580
  2.5 13.2 %copy-start.5 = (s32[2048]{0:T(1024)S(1)}, s32[2048]{0:T(1024)}, u32[]{:S(2)}) copy-start(s32[2048]{0:T(1024)} %param.17) | copy-start | bytes 24580
  2.5 15.6 %copy-start = (f32[224,128]{1,0:T(8,128)S(1)}, f32[224,128]{1,0:T(8,128)}, u32[]{:S(2)}) copy-start(f32[224,128]{1,0:T(8,128)} %get-tuple-element.21.fields_ref) | copy-start | bytes 344068
  2.5 15.6 %all-to-all-start = ((f32[32,1,768]{2,1,0:T(1,128)}), f32[32,1,768]{2,1,0:T(1,128)S(1)}, u32[]{:S(2)}, u32[]{:S(2)}) async-start(f32[32,1,768]{2,1,0:T(1,128)} %get-tuple-element.24), calls=%async_computation | async-start | bytes 196608 | tf_op jit(solution)/shard_map/all_to_all | solution.py:652
  9.8 7.2 %collective-permute-start = (f32[168,128]{1,0:T(8,128)}, f32[168,128]{1,0:T(8,128)S(1)}, u32[]{:S(2)}, u32[]{:S(2)}) collective-permute-start(f32[168,128]{1,0:T(8,128)} %get-tuple-element.22), channel_id=1, source_target_pairs={{8,0},{16,8},{24,16},{9,1},{17,9},{25,17},{10,2},{18,10},{26,18},{... | collective-permute-start | bytes 258056 | tf_op jit(solution)/shard_map/ppermute | solution.py:683
  11.1 7.0 %copy-start.1 = (f32[2,2048]{1,0:T(2,128)S(1)}, f32[2,2048]{1,0:T(2,128)}, u32[]{:S(2)}) copy-start(f32[2,2048]{1,0:T(2,128)} %weight_ref.3) | copy-start | bytes 49156
  11.2 6.9 %collective-permute-start.1 = (f32[168,128]{1,0:T(8,128)}, f32[168,128]{1,0:T(8,128)S(1)}, u32[]{:S(2)}, u32[]{:S(2)}) collective-permute-start(f32[168,128]{1,0:T(8,128)} %get-tuple-element.23), channel_id=1, source_target_pairs={{0,8},{8,16},{16,24},{1,9},{9,17},{17,25},{2,10},{10,18},{18,26},{... | collective-permute-start | bytes 258056 | tf_op jit(solution)/shard_map/ppermute | solution.py:682
  16.4 1.7 %copy-start.3 = (s32[2048]{0:T(1024)S(1)}, s32[2048]{0:T(1024)}, u32[]{:S(2)}) copy-start(s32[2048]{0:T(1024)} %param.20) | copy-start | bytes 24580
  19.8 13.8 %copy-start.2 = (f32[3,1024]{1,0:T(4,128)S(1)}, f32[3,1024]{1,0:T(4,128)}, u32[]{:S(2)}) copy-start(f32[3,1024]{1,0:T(4,128)} %observed_ref.1) | copy-start | bytes 36868
  45.5 9.9 %all-to-all-start.3 = ((f32[32,1,384]{2,1,0:T(1,128)}), f32[32,1,384]{2,1,0:T(1,128)S(1)}, u32[]{:S(2)}, u32[]{:S(2)}) async-start(f32[32,1,384]{2,1,0:T(1,128)} %get-tuple-element.34), calls=%async_computation.3 | async-start | bytes 98304 | tf_op jit(solution)/shard_map/all_to_all | solution.py:652
  48.1 5.9 %collective-permute-start.2 = (f32[48,128]{1,0:T(8,128)S(1)}, f32[48,128]{1,0:T(8,128)S(1)}, u32[]{:S(2)}, u32[]{:S(2)}) collective-permute-start(f32[48,128]{1,0:T(8,128)S(1)} %get-tuple-element.32), channel_id=1, source_target_pairs={{8,0},{16,8},{24,16},{9,1},{17,9},{25,17},{10,2},{18,10},{26,18},{... | collective-permute-start | bytes 73736 | tf_op jit(solution)/shard_map/ppermute | solution.py:760
  49.4 6.1 %collective-permute-start.3 = (f32[48,128]{1,0:T(8,128)S(1)}, f32[48,128]{1,0:T(8,128)S(1)}, u32[]{:S(2)}, u32[]{:S(2)}) collective-permute-start(f32[48,128]{1,0:T(8,128)S(1)} %get-tuple-element.33), channel_id=1, source_target_pairs={{0,8},{8,16},{16,24},{1,9},{9,17},{17,25},{2,10},{10,18},{18,26},{... | collective-permute-start | bytes 73736 | tf_op jit(solution)/shard_map/ppermute | solution.py:759
